TPU v7x, 32 devices: a whole 2x2x4 slice. The times are simulated.
32 devices in a mesh: dp: 8 (over y, x, core), seq: 4 (over z).
Axes of the slice: x: 2, y: 2, z: 4, core: 2. Of those that a mesh axis runs over, the one named last changes fastest.
Arguments:
- tokens: bfloat16 [8, 1024, 2048], P('dp', 'seq'), may hold values from -6 to 6
- cotangent: bfloat16 [8, 1024, 2048], P('dp', 'seq'), may hold values from -6 to 6
- doc_ids: int32 [8, 1024], P('dp'), may hold values from 0 to 64, as said below
- mix_in: float32 [2560, 2, 2048], P(('dp', 'seq')), may hold values from -0.125 to 0.125
- mix_out: float32 [2560, 2048], P(('dp', 'seq')), may hold values from -0.125 to 0.125
- gate_w: float32 [2560, 2, 160], P(('dp', 'seq')), may hold values from -0.5 to 0.5
- conv_w: float32 [4, 2560], P(None, ('dp', 'seq')), may hold values from -3 to 3
- conv_bias: float32 [2560], P(('dp', 'seq')), may hold values from -3 to 3
- gate_bias: float32 [2, 2560], P(None, ('dp', 'seq')), may hold values from -4 to 4
- decay_param: float32 [2560], P(('dp', 'seq')), may hold values from -13 to -4
- gain_one: float32 [2048], P(('dp', 'seq')), may hold values from 0.5 to 1.5
- gain_two: float32 [2048], P(('dp', 'seq')), may hold values from 0.5 to 1.5
- mlp_in: float32 [6144, 2, 2048], P(('dp', 'seq')), may hold values from -0.125 to 0.125
- mlp_out: float32 [6144, 2048], P(('dp', 'seq')), may hold values from -0.078125 to 0.078125
Outputs:
- layer_out: bfloat16 [8, 1024, 2048], P('dp', 'seq')
- input_grad: bfloat16 [8, 1024, 2048], P('dp', 'seq')
- grad_mix_in: float32 [2560, 2, 2048], P(('dp', 'seq'))
- grad_mix_out: float32 [2560, 2048], P(('dp', 'seq'))
- grad_gate_w: float32 [2560, 2, 160], P(('dp', 'seq'))
- grad_conv_w: float32 [4, 2560], P(None, ('dp', 'seq'))
- grad_conv_bias: float32 [2560], P(('dp', 'seq'))
- grad_gate_bias: float32 [2, 2560], P(None, ('dp', 'seq'))
- grad_decay: float32 [2560], P(('dp', 'seq'))
- grad_gain_one: float32 [2048], P(('dp', 'seq'))
- grad_gain_two: float32 [2048], P(('dp', 'seq'))
- grad_mlp_in: float32 [6144, 2, 2048], P(('dp', 'seq'))
- grad_mlp_out: float32 [6144, 2048], P(('dp', 'seq'))
Inputs may be any that keep to these rules, and one draw needn't show every extreme that they name: doc_ids[s, t] numbers the document of token t of sequence s: 0 at the first token, rising by 0 or 1 from each token to the next; every sequence opens exactly 256 / 4 further documents, all within the first and the last 256 / 2 tokens of the sequence.
All inputs are finite; a program needn't handle non-finite values.
Results may differ from a plain program's by a relative error of at most 0.012.
The roundings to bfloat16 on the way count: a program that leaves them out, or rounds other values in their place, can miss the bound.
Values may be sent and summed in bfloat16 or wider, within the bound.
No kernel may reach another device: no remote copies, remote signals or barrier semaphores. Data moves between devices by JAX's collectives and lax.ppermute only.
A program may use at most 832 MiB of HBM per device.

v0:
```python
import jax
import jax.numpy as jnp
from jax import lax
from jax.sharding import PartitionSpec as P

EPS = 1e-06
FLOOR = 0.0001
SHARP = 8.0


def passed_along(value, axis, steps):
    count = lax.axis_size(axis)
    initial, last = (max(0, -steps), min(count, count - steps))
    return lax.ppermute(value, axis, [(source, source + steps) for source in range(initial, last)])


def entering(value, axis, join, neutral, backward):
    count, mine = (lax.axis_size(axis), lax.axis_index(axis))
    pieces = jax.tree.map(lambda part: lax.all_gather(part, axis), value)
    if backward:
        pieces = jax.tree.map(lambda part: part[::-1], pieces)
        mine = count - 1 - mine
    so_far = jax.tree.map(
        lambda part, zero: jnp.full_like(part, 0) + jnp.asarray(zero, part.dtype), value, neutral
    )

    def hop(position, so_far):
        longer = join(so_far, jax.tree.map(lambda part: part[position], pieces))
        return jax.tree.map(lambda new, old: jnp.where(position < mine, new, old), longer, so_far)

    return lax.fori_loop(0, count - 1, hop, so_far)


def rms_norm(values, gain_vec):
    return values * lax.rsqrt(jnp.mean(values * values, axis=-1, keepdims=True) + EPS) * gain_vec


def gate_rule(conv_out, gate_pre, decay_raw, fresh_start):
    recur_gate = jax.nn.sigmoid(gate_pre[0])
    entry_gate = jax.nn.sigmoid(gate_pre[1])
    decays = jnp.exp(-SHARP * jax.nn.softplus(decay_raw) * recur_gate)
    scaling = jnp.where(fresh_start, 1.0, jnp.sqrt(jnp.maximum(1.0 - decays * decays, FLOOR)))
    carried = jnp.where(fresh_start, 0.0, decays)
    return (carried, conv_out * entry_gate * scaling)


def affine_join(earlier, later):
    return (earlier[0] * later[0], later[0] * earlier[1] + later[1])


def project(left_rows, weights):
    return jnp.einsum("td,rkd->ktr", left_rows, weights, preferred_element_type=jnp.float32)


def back_project(row_grads, weights):
    return jnp.einsum("ktr,rkd->td", row_grads, weights, preferred_element_type=jnp.float32)


def weight_grad(row_grads, left_rows):
    return jnp.einsum("ktr,td->rkd", row_grads, left_rows, preferred_element_type=jnp.float32)


def contract_last(left_rows, right_rows):
    return lax.dot_general(
        left_rows, right_rows, (((1,), (1,)), ((), ())), preferred_element_type=jnp.float32
    )


def contract_first(left_rows, right_rows):
    return lax.dot_general(
        left_rows, right_rows, (((0,), (0,)), ((), ())), preferred_element_type=jnp.float32
    )


def gelu_product(gate_vals, up_vals):
    return jax.nn.gelu(gate_vals) * up_vals


def doc_masks(padded_docs, first_token, length):
    own_docs = lax.dynamic_slice_in_dim(padded_docs, first_token + 3, length)
    masks = []
    for offset in range(4):
        earlier_docs = lax.dynamic_slice_in_dim(padded_docs, first_token + 3 - offset, length)
        masks.append(jnp.where(earlier_docs == own_docs, 1.0, 0.0)[:, None])
    return (masks, masks[1] == 0.0)


def conv_forward(u_ext, taps, bias_vec, masks, length):
    conv_out = bias_vec.astype(jnp.float32)[None, :] + jnp.zeros(
        (length, taps.shape[1]), jnp.float32
    )
    for offset in range(4):
        conv_out = conv_out + taps[offset] * u_ext[3 - offset : 3 - offset + length] * masks[offset]
    return conv_out


def gate_inputs(conv_low, gate_rows, bias_rows):
    length, width = conv_low.shape
    block_width = gate_rows.shape[2]
    count = width // block_width
    blocks = gate_rows.reshape(count, block_width, 2, block_width)
    conv_blocks = conv_low.reshape(length, count, block_width)
    pre = jnp.einsum("tbj,bokj->ktbo", conv_blocks, blocks, preferred_element_type=jnp.float32)
    pre = pre.reshape(2, length, width) + bias_rows.astype(jnp.float32)[:, None, :]
    return (pre, blocks, conv_blocks)


def recurrence_forward(conv_low, gate_pre, decay_vals, fresh_start):

    def local_gates(conv_in, pre_in, decay_in):
        return gate_rule(conv_in, pre_in, decay_in, fresh_start)

    (carried, inputs), gates_back = jax.vjp(
        local_gates, conv_low.astype(jnp.float32), gate_pre, decay_vals.astype(jnp.float32)
    )
    cum_keep, local_states = lax.associative_scan(affine_join, (carried, inputs), axis=0)
    return (carried, cum_keep, local_states, gates_back)


def head_backward(d_mixed, states, gelu_y, gelu_back, carried):
    d_y_pre = gelu_back(d_mixed * states)[0].astype(jnp.bfloat16)
    emitted = d_mixed * gelu_y
    next_keep = jnp.concatenate([carried[1:], jnp.ones((1, carried.shape[1]), jnp.float32)], 0)
    cum_back, local_back = lax.associative_scan(
        affine_join, (next_keep, emitted), reverse=True, axis=0
    )
    return (d_y_pre, cum_back, local_back)


def tail_backward(d_states, prev_states, gates_back, blocks, conv_blocks, masks, u_ext, taps):
    length, width = d_states.shape
    d_conv_direct, d_gate_pre, d_decay = gates_back((d_states * prev_states, d_states))
    d_gate_low = d_gate_pre.astype(jnp.bfloat16)
    d_gate_blocks = d_gate_low.reshape(2, length, blocks.shape[0], blocks.shape[1])
    d_conv = d_conv_direct + jnp.einsum(
        "ktbo,bokj->tbj", d_gate_blocks, blocks, preferred_element_type=jnp.float32
    ).reshape(length, width)
    grad_gate_w = jnp.einsum(
        "ktbo,tbj->bokj", d_gate_blocks, conv_blocks, preferred_element_type=jnp.float32
    ).reshape(width, 2, blocks.shape[1])
    grad_gate_bias = jnp.sum(d_gate_low.astype(jnp.float32), axis=1)
    grad_conv_bias = jnp.sum(d_conv, axis=0)
    tap_grads = []
    d_u_ext = jnp.zeros((length + 3, width), jnp.float32)
    for offset in range(4):
        masked = d_conv * masks[offset]
        tap_grads.append(jnp.sum(masked * u_ext[3 - offset : 3 - offset + length], axis=0))
        d_u_ext = d_u_ext + jnp.pad(masked * taps[offset], ((3 - offset, offset), (0, 0)))
    return (d_u_ext, grad_gate_w, grad_gate_bias, jnp.stack(tap_grads), grad_conv_bias, d_decay)


def per_device(
    tokens,
    cotangent,
    doc_ids,
    mix_in,
    mix_out,
    gate_w,
    conv_w,
    conv_bias,
    gate_bias,
    decay_param,
    gain_one,
    gain_two,
    mlp_in,
    mlp_out,
):
    run_len = tokens.shape[1]
    model_width = tokens.shape[2]
    x_zero = tokens.reshape(run_len, model_width).astype(jnp.float32)
    cot_rows = cotangent.reshape(run_len, model_width)
    cot_float = cot_rows.astype(jnp.float32)
    first_token = lax.axis_index("seq") * run_len
    padded_docs = jnp.concatenate([jnp.full((3,), -1, jnp.int32), doc_ids.reshape(-1)])
    w_in, w_out, w_gate, w_conv, b_conv, b_gate, w_decay, g_one, g_two = (
        lax.all_gather(mix_in.astype(jnp.bfloat16), ("dp", "seq"), axis=0, tiled=True),
        lax.all_gather(mix_out.astype(jnp.bfloat16), ("dp", "seq"), axis=0, tiled=True),
        lax.all_gather(gate_w.astype(jnp.bfloat16), ("dp", "seq"), axis=0, tiled=True),
        lax.all_gather(conv_w.astype(jnp.bfloat16), ("dp", "seq"), axis=1, tiled=True),
        lax.all_gather(conv_bias.astype(jnp.bfloat16), ("dp", "seq"), axis=0, tiled=True),
        lax.all_gather(gate_bias.astype(jnp.bfloat16), ("dp", "seq"), axis=1, tiled=True),
        lax.all_gather(decay_param.astype(jnp.bfloat16), ("dp", "seq"), axis=0, tiled=True),
        lax.all_gather(gain_one.astype(jnp.bfloat16), ("dp", "seq"), axis=0, tiled=True),
        lax.all_gather(gain_two.astype(jnp.bfloat16), ("dp", "seq"), axis=0, tiled=True),
    )
    n_one, norm_one_back = jax.vjp(rms_norm, x_zero, g_one.astype(jnp.float32))
    h_one = n_one.astype(jnp.bfloat16)
    taps = w_conv.astype(jnp.float32)
    masks, fresh_start = doc_masks(padded_docs, first_token, run_len)
    width = w_out.shape[0]
    both_pre = project(h_one, w_in)
    y_pre = both_pre[0]
    u_vals = both_pre[1].astype(jnp.bfloat16)
    u_lead = passed_along(u_vals[run_len - 3 :], "seq", 1)
    u_ext = jnp.concatenate([u_lead, u_vals], 0).astype(jnp.float32)
    conv_low = conv_forward(u_ext, taps, b_conv, masks, run_len).astype(jnp.bfloat16)
    gate_pre, gate_blocks, conv_blocks = gate_inputs(conv_low, w_gate, b_gate)
    carried, cum_keep, local_states, gates_back = recurrence_forward(
        conv_low, gate_pre, w_decay, fresh_start
    )
    unit_pair = (jnp.ones((width,), jnp.float32), jnp.zeros((width,), jnp.float32))
    state_in = entering(
        (cum_keep[run_len - 1], local_states[run_len - 1]), "seq", affine_join, unit_pair, False
    )[1]
    states = local_states + cum_keep * state_in[None, :]
    gelu_y, gelu_back = jax.vjp(jax.nn.gelu, y_pre)
    mixed_out = (gelu_y * states).astype(jnp.bfloat16)
    mixer_sum = jnp.dot(mixed_out, w_out, preferred_element_type=jnp.float32)
    x_one = x_zero + mixer_sum
    n_two, norm_two_back = jax.vjp(rms_norm, x_one, g_two.astype(jnp.float32))
    h_two = n_two.astype(jnp.bfloat16)
    rows_a = lax.all_gather(mlp_in.astype(jnp.bfloat16), ("dp", "seq"), axis=0, tiled=True)
    rows_b = lax.all_gather(mlp_out.astype(jnp.bfloat16), ("dp", "seq"), axis=0, tiled=True)
    piece_pre = project(h_two, rows_a)
    piece_hidden = gelu_product(piece_pre[0], piece_pre[1]).astype(jnp.bfloat16)
    mlp_sum = jnp.dot(piece_hidden, rows_b, preferred_element_type=jnp.float32)
    layer_out = (x_one + mlp_sum).astype(jnp.bfloat16).reshape(1, run_len, model_width)
    rows_a = lax.all_gather(mlp_in.astype(jnp.bfloat16), ("dp", "seq"), axis=0, tiled=True)
    rows_b = lax.all_gather(mlp_out.astype(jnp.bfloat16), ("dp", "seq"), axis=0, tiled=True)
    piece_pre = project(h_two, rows_a)
    piece_act, piece_back = jax.vjp(gelu_product, piece_pre[0], piece_pre[1])
    d_gate, d_up = piece_back(contract_last(cot_rows, rows_b))
    d_pre = jnp.stack([d_gate, d_up]).astype(jnp.bfloat16)
    keep_block = jnp.concatenate([d_pre, piece_act.astype(jnp.bfloat16)[None]], 0)
    d_h_two = back_project(d_pre, rows_a)
    gate_up = weight_grad(keep_block[0:2], h_two)
    down_grad = contract_first(keep_block[2], cot_rows)
    mlp_grad = lax.psum_scatter(
        jnp.concatenate([gate_up, down_grad[:, None, :]], 1),
        ("dp", "seq"),
        scatter_dimension=0,
        tiled=True,
    )
    grad_mlp_in = mlp_grad[:, 0:2]
    grad_mlp_out = mlp_grad[:, 2]
    d_x_norm, d_gain_two = norm_two_back(d_h_two)
    d_x_one = cot_float + d_x_norm
    d_mix = d_x_one.astype(jnp.bfloat16)
    grad_mix_out = contract_first(mixed_out, d_mix)
    d_mixed = contract_last(d_mix, w_out)
    d_y_pre, cum_back, local_back = head_backward(d_mixed, states, gelu_y, gelu_back, carried)
    from_later = entering(
        (carried[0] * cum_back[0], carried[0] * local_back[0]), "seq", affine_join, unit_pair, True
    )[1]
    d_states = local_back + cum_back * from_later[None, :]
    prev_states = jnp.concatenate([state_in[None, :], states[: run_len - 1]], 0)
    d_u_ext, grad_gate_w, grad_gate_bias, grad_conv_w, grad_conv_bias, d_decay = tail_backward(
        d_states, prev_states, gates_back, gate_blocks, conv_blocks, masks, u_ext, taps
    )
    from_next = passed_along(d_u_ext[0:3], "seq", -1)
    d_u = d_u_ext[3:] + jnp.pad(from_next, ((run_len - 3, 0), (0, 0)))
    d_both = jnp.stack([d_y_pre, d_u.astype(jnp.bfloat16)])
    grad_mix_in = weight_grad(d_both, h_one)
    d_h_one = back_project(d_both, w_in)
    d_x_zero, d_gain_one = norm_one_back(d_h_one)
    input_grad = (d_x_one + d_x_zero).astype(jnp.bfloat16).reshape(1, run_len, model_width)
    summed = (
        lax.psum_scatter(grad_mix_in, ("dp", "seq"), scatter_dimension=0, tiled=True),
        lax.psum_scatter(grad_mix_out, ("dp", "seq"), scatter_dimension=0, tiled=True),
        lax.psum_scatter(grad_gate_w, ("dp", "seq"), scatter_dimension=0, tiled=True),
        lax.psum_scatter(grad_conv_w, ("dp", "seq"), scatter_dimension=1, tiled=True),
        lax.psum_scatter(grad_conv_bias, ("dp", "seq"), scatter_dimension=0, tiled=True),
        lax.psum_scatter(grad_gate_bias, ("dp", "seq"), scatter_dimension=1, tiled=True),
        lax.psum_scatter(d_decay, ("dp", "seq"), scatter_dimension=0, tiled=True),
        lax.psum_scatter(d_gain_one, ("dp", "seq"), scatter_dimension=0, tiled=True),
        lax.psum_scatter(d_gain_two, ("dp", "seq"), scatter_dimension=0, tiled=True),
    )
    out_conv_w = summed[3]
    out_gate_bias = summed[5]
    return (
        layer_out,
        input_grad,
        summed[0],
        summed[1],
        summed[2],
        out_conv_w,
        summed[4],
        out_gate_bias,
        summed[6],
        summed[7],
        summed[8],
        grad_mlp_in,
        grad_mlp_out,
    )


def solution(mesh):
    placed = (
        P("dp", "seq", None),
        P("dp", "seq", None),
        P("dp", None),
        P(("dp", "seq"), None, None),
        P(("dp", "seq"), None),
        P(("dp", "seq"), None, None),
        P(None, ("dp", "seq")),
        P(("dp", "seq")),
        P(None, ("dp", "seq")),
        P(("dp", "seq")),
        P(("dp", "seq")),
        P(("dp", "seq")),
        P(("dp", "seq"), None, None),
        P(("dp", "seq"), None),
    )
    return jax.shard_map(
        per_device,
        mesh=mesh,
        in_specs=placed,
        out_specs=(
            P("dp", "seq", None),
            P("dp", "seq", None),
            P(("dp", "seq"), None, None),
            P(("dp", "seq"), None),
            P(("dp", "seq"), None, None),
            P(None, ("dp", "seq")),
            P(("dp", "seq")),
            P(None, ("dp", "seq")),
            P(("dp", "seq")),
            P(("dp", "seq")),
            P(("dp", "seq")),
            P(("dp", "seq"), None, None),
            P(("dp", "seq"), None),
        ),
        check_vma=False,
    )
```

profile of v0, /device:TPU:0, one launch (start us, length us, event | category | flops | bytes accessed | tf_op | source)
XLA Modules:
  0.0 3698.7 jit_solution(2631213903383564026)
XLA Ops:
  19.4 43.7 %all-reduce.84 = (bf16[2560]{0:T(1024)(128)(2,1)S(1)}, bf16[2048]{0:T(1024)(128)(2,1)S(1)}, bf16[2560]{0:T(1024)(128)(2,1)S(1)}, bf16[2048]{0:T(1024)(128)(2,1)S(1)}) all-reduce(bf16[2560]{0:T(1024)(128)(2,1)S(1)} %dynamic-update-slice.2, bf16[2048]{0:T(1024)(128)(2,1)S(1)} %dynamic-update-slice, ...), channel_id=1, replica_groups=mesh['dp'=8,'seq'=4] {'dp','seq'}, use_global_device_ids=true, to_apply=%add.76 | all-reduce | flops 9216 | bytes 36864
  63.2 66.0 %all-gather.1 = bf16[32,80,2]{1,2,0:T(2,128)(2,1)S(1)} all-gather(bf16[1,80,2]{1,2,0:T(2,128)(2,1)S(1)} %convert_bitcast_fusion.1), channel_id=1, replica_groups=mesh['dp'=8,'seq'=4] {'dp','seq'}, dimensions={0}, use_global_device_ids=true | all-gather | bytes 10560 | tf_op jit(solution)/shard_map/all_gather | solution.py:181
  129.3 63.8 %all-gather = bf16[32,80,4]{1,2,0:T(4,128)(2,1)S(1)} all-gather(bf16[1,80,4]{1,2,0:T(4,128)(2,1)S(1)} %convert_bitcast_fusion), channel_id=1, replica_groups=mesh['dp'=8,'seq'=4] {'dp','seq'}, dimensions={0}, use_global_device_ids=true | all-gather | bytes 21120 | tf_op jit(solution)/shard_map/all_gather | solution.py:179
  194.4 11.9 fusion.154
  377.8 13.6 all-gather.2
  404.0 14.0 all-gather.3
  418.4 10.9 slice.676
  457.2 119.0 %all-gather.18.cloned.1.call-done = bf16[6144,2,2048]{2,0,1:T(8,128)(2,1)} async-done(((bf16[192,2,2048]{2,0,1:T(8,128)(2,1)}), bf16[6144,2,2048]{2,0,1:T(8,128)(2,1)}) %all-gather.18.cloned.1.call-update) | async-done | bytes 50331664 | tf_op jit(solution)/shard_map/all_gather | solution.py:212
  576.2 24.6 convolution_bitcast_fusion.3
  600.8 131.6 %all-gather.20.cloned.1.call-done = bf16[6144,2048]{1,0:T(8,128)(2,1)} async-done(((bf16[192,2048]{1,0:T(8,128)(2,1)}), bf16[6144,2048]{1,0:T(8,128)(2,1)}) %all-gather.20.cloned.1.call-update) | async-done | bytes 25165840 | tf_op jit(solution)/shard_map/all_gather | solution.py:213
  732.4 18.3 fusion.28
  750.7 23.7 multiply_reduce_fusion.5
  776.8 11.0 fusion.84
  796.7 10.8 slice.671
  897.7 20.7 rev.14
  918.5 21.1 rev.15
  939.6 13.1 all-gather.5
  953.2 13.1 all-gather.4
  967.4 10.7 fusion.31
  1033.0 16.7 convolution_bitcast_fusion.2
  1049.7 61.4 %copy.98 = f32[2560,2,2048]{2,1,0:T(2,128)} copy(f32[2560,2,2048]{0,2,1:T(8,128)} %convolution_bitcast_fusion.2) | data formatting | bytes 83886080 | tf_op jit(solution)/shard_map/ktr,td->rkd/transpose | solution.py:60
  1112.3 22.0 convolution_bitcast_fusion.1
  1134.3 37.8 %convolution_bitcast_fusion = f32[6144,2,2048]{0,2,1:T(8,128)} fusion(bf16[1,256,6144]{2,1,0:T(8,128)(2,1)} %get-tuple-element.348, bf16[1,256,6144]{2,1,0:T(8,128)(2,1)} %copy-done.34, f32[256,2048]{1,0:T(8,128)S(1)} %copy-done.8, f32[2048]{0:T(1024)S(1)} %copy-done.37, f32[256]{0:T(256)S(1)} %copy-done.54), kind=kOutput, calls=%fused_computation.7 | convolution fusion | flops 12899057664 | bytes 109061120 | tf_op jit(solution)/shard_map/ktr,td->rkd/dot_general | solution.py:60
  1172.2 99.4 %pad_maximum_fusion = f32[6144,3,2048]{0,2,1:T(8,128)} fusion(f32[6144,1,2048]{0,2,1:T(8,128)} %convolution_bitcast_fusion.1, f32[6144,2,2048]{0,2,1:T(8,128)} %convolution_bitcast_fusion), kind=kLoop, calls=%fused_computation.6 | loop fusion | flops 37748736 | bytes 301989888 | tf_op jit(solution)/shard_map/concatenate | solution.py:229
  1271.5 146.7 %copy.125 = f32[6144,6144]{1,0:T(8,128)} copy(f32[6144,6144]{0,1:T(8,128)} %bitcast.72) | data formatting | bytes 301989888
  1420.3 9.3 fusion.94
  1430.4 21.7 fusion.65
  1452.3 11.2 fusion.72
  1463.5 40.2 %all-reduce.83 = (f32[2560]{0:T(1024)S(1)}, f32[2560]{0:T(1024)S(1)}, f32[2048]{0:T(1024)S(1)}, f32[2048]{0:T(1024)S(1)}) all-reduce(f32[2560]{0:T(1024)S(1)} %copy-done.72, f32[2560]{0:T(1024)S(1)} %fusion.116, f32[2048]{0:T(1024)S(1)} %get-tuple-element.297, ...), channel_id=6, replica_groups=mesh['dp'=8,'seq'=4] {'dp','seq'}, use_global_device_ids=true, to_apply=%region_17.18.clone | all-reduce | flops 9216 | bytes 73728
  1513.9 454.9 %all-reduce.87.cloned.1.call-done = f32[2560,2,2048]{2,1,0:T(2,128)} async-done(((f32[2560,2,2048]{2,1,0:T(2,128)}), f32[2560,2,2048]{2,1,0:T(2,128)}) %all-reduce.87.cloned.1.call-update) | async-done | bytes 41943056
  1971.3 1267.7 %reduce-scatter.22.cloned.1.call-done = f32[192,6144]{1,0:T(8,128)} async-done(((f32[6144,6144]{1,0:T(8,128)}), f32[192,6144]{1,0:T(8,128)}) %reduce-scatter.22.cloned.1.call-update) | async-done | bytes 4718608
  3259.4 432.4 %reduce-scatter.14.cloned.1.call-done = f32[80,2048]{1,0:T(8,128)} async-done(((f32[2560,2048]{1,0:T(8,128)}), f32[80,2048]{1,0:T(8,128)}) %reduce-scatter.14.cloned.1.call-update) | async-done | bytes 655376 | tf_op jit(solution)/shard_map/reduce_scatter | solution.py:259
  (604 shorter events, 419.2 us)
Async XLA Ops:
  7.2 187.2 %all-gather.12.cloned.1.call-start = ((), (), s32[]{:S(2)}) async-start(), calls=%async_computation.5 | async-start | bytes 21626880 | tf_op jit(solution)/shard_map/all_gather | solution.py:176
  10.3 208.4 %all-gather.14.cloned.1.call-start = ((), (), s32[]{:S(2)}) async-start(), calls=%async_computation.6 | async-start | bytes 2703360 | tf_op jit(solution)/shard_map/all_gather | solution.py:178
  11.1 440.0 %all-gather.16.cloned.1.call-start = ((), (), s32[]{:S(2)}) async-start(), calls=%async_computation.7 | async-start | bytes 10813440 | tf_op jit(solution)/shard_map/all_gather | solution.py:177
  13.0 563.3 %all-gather.18.cloned.1.call-start = ((), (), s32[]{:S(2)}) async-start(), calls=%async_computation.8 | async-start | bytes 51904512 | tf_op jit(solution)/shard_map/all_gather | solution.py:212
  15.9 113.4 %copy-start.99 = (f32[4,80]{1,0:T(4,128)S(1)}, f32[4,80]{1,0:T(4,128)}, u32[]{:S(2)}) copy-start(f32[4,80]{1,0:T(4,128)} %param.24) | copy-start | bytes 3844
  15.9 177.3 %copy-start.93 = (s32[1,1024]{1,0:T(1,128)S(1)}, s32[1,1024]{1,0:T(1,128)}, u32[]{:S(2)}) copy-start(s32[1,1024]{1,0:T(1,128)} %param.20) | copy-start | bytes 12292
  15.9 177.6 %copy-start.10 = (bf16[1,256,2048]{2,1,0:T(8,128)(2,1)S(1)}, bf16[1,256,2048]{2,1,0:T(8,128)(2,1)}, u32[]{:S(2)}) copy-start(bf16[1,256,2048]{2,1,0:T(8,128)(2,1)} %param.18) | copy-start | bytes 3145732
  15.9 716.5 %all-gather.20.cloned.1.call-start = ((), (), s32[]{:S(2)}) async-start(), calls=%async_computation.9 | async-start | bytes 25952256 | tf_op jit(solution)/shard_map/all_gather | solution.py:213
  18.3 1491.0 %reduce-scatter.20.cloned.1.call-start = ((), (), s32[]{:S(2)}) async-start(), calls=%async_computation.13 | async-start | bytes 1351680
  63.1 143.2 %copy-start.88 = (bf16[2560]{0:T(1024)(128)(2,1)}, bf16[2560]{0:T(1024)(128)(2,1)S(1)}, u32[]{:S(2)}) copy-start(bf16[2560]{0:T(1024)(128)(2,1)S(1)} %get-tuple-element.328) | copy-start | bytes 15364
  63.1 143.2 %copy-start.63 = (f32[2048]{0:T(1024)}, f32[2048]{0:T(1024)S(1)}, u32[]{:S(2)}) copy-start(f32[2048]{0:T(1024)S(1)} %convert_element_type.128) | copy-start | bytes 24580
  63.1 711.3 %copy-start.36 = (f32[2048]{0:T(1024)}, f32[2048]{0:T(1024)S(1)}, u32[]{:S(2)}) copy-start(f32[2048]{0:T(1024)S(1)} %convert_element_type.147) | copy-start | bytes 24580
  63.1 170.2 %copy-start.68 = (f32[2560]{0:T(1024)}, f32[2560]{0:T(1024)S(1)}, u32[]{:S(2)}) copy-start(f32[2560]{0:T(1024)S(1)} %convert_element_type.132) | copy-start | bytes 30724
  207.1 5.7 collective-permute-start
  457.2 317.2 %copy-start.7 = (f32[256,2048]{1,0:T(8,128)}, f32[256,2048]{1,0:T(8,128)S(1)}, u32[]{:S(2)}) copy-start(f32[256,2048]{1,0:T(8,128)S(1)} %get-tuple-element.434) | copy-start | bytes 6291460
  457.2 317.2 %copy-start.53 = (f32[256]{0:T(256)}, f32[256]{0:T(256)S(1)}, u32[]{:S(2)}) copy-start(f32[256]{0:T(256)S(1)} %fusion.129) | copy-start | bytes 3076
  576.2 156.2 %copy-start.31 = (bf16[1,256,2048]{2,1,0:T(8,128)(2,1)S(1)}, bf16[1,256,2048]{2,1,0:T(8,128)(2,1)}, u32[]{:S(2)}) copy-start(bf16[1,256,2048]{2,1,0:T(8,128)(2,1)} %param.19) | copy-start | bytes 3145732
  918.4 48.9 %copy-start.60 = (f32[2560]{0:T(1024)S(1)}, f32[2560]{0:T(1024)}, u32[]{:S(2)}) copy-start(f32[2560]{0:T(1024)} %copy-done.59) | copy-start | bytes 30724
  918.4 48.9 %copy-start.62 = (f32[2560]{0:T(1024)S(1)}, f32[2560]{0:T(1024)}, u32[]{:S(2)}) copy-start(f32[2560]{0:T(1024)} %copy-done.61) | copy-start | bytes 30724
  918.4 48.9 %copy-start.67 = (f32[2560]{0:T(1024)S(1)}, f32[2560]{0:T(1024)}, u32[]{:S(2)}) copy-start(f32[2560]{0:T(1024)} %copy-done.66) | copy-start | bytes 30724
  918.4 48.9 %copy-start.69 = (f32[2560]{0:T(1024)S(1)}, f32[2560]{0:T(1024)}, u32[]{:S(2)}) copy-start(f32[2560]{0:T(1024)} %copy-done.68) | copy-start | bytes 30724
  918.4 48.9 %copy-start.83 = (f32[256]{0:T(256)S(1)}, f32[256]{0:T(256)}, u32[]{:S(2)}) copy-start(f32[256]{0:T(256)} %copy-done.82) | copy-start | bytes 3076
  918.4 48.9 %copy-start.85 = (f32[256]{0:T(256)S(1)}, f32[256]{0:T(256)}, u32[]{:S(2)}) copy-start(f32[256]{0:T(256)} %copy-done.84) | copy-start | bytes 3076
  918.5 48.9 %copy-start.87 = (f32[256]{0:T(256)S(1)}, f32[256]{0:T(256)}, u32[]{:S(2)}) copy-start(f32[256]{0:T(256)} %copy-done.86) | copy-start | bytes 3076
  918.5 48.9 %copy-start.98 = (pred[256]{0:T(512)(128)(4,1)S(1)}, pred[256]{0:T(512)(128)(4,1)}, u32[]{:S(2)}) copy-start(pred[256]{0:T(512)(128)(4,1)} %copy-done.97) | copy-start | bytes 772
  983.8 526.8 %reduce-scatter.18.cloned.1.call-start = ((), (), s32[]{:S(2)}) async-start(), calls=%async_computation.12 | async-start | bytes 1351680
  1006.4 505.7 %reduce-scatter.16.cloned.1.call-start = ((), (), s32[]{:S(2)}) async-start(), calls=%async_computation.11 | async-start | bytes 4055040
  1022.9 945.9 %all-reduce.87.cloned.1.call-start = ((), (), s32[]{:S(2)}) async-start(), calls=%async_computation.15 | async-start | bytes 83886080
  1025.6 6.0 collective-permute-start.1
  1111.2 2127.9 %reduce-scatter.22.cloned.1.call-start = ((), (), s32[]{:S(2)}) async-start(), calls=%async_computation.14 | async-start | bytes 155713536
  1418.3 2273.4 %reduce-scatter.14.cloned.1.call-start = ((), (), s32[]{:S(2)}) async-start(), calls=%async_computation.10 | async-start | bytes 21626880 | tf_op jit(solution)/shard_map/reduce_scatter | solution.py:259
  1452.2 53.8 %copy-start.95 = (f32[256]{0:T(256)S(1)}, f32[256]{0:T(256)}, u32[]{:S(2)}) copy-start(f32[256]{0:T(256)} %copy-done.94) | copy-start | bytes 3076
  (86 other events, 1116.5 us)
Sparse Core Ops, SparseCore 0:
  11.5 138.4 all-gather.11
  153.4 56.2 all-gather.13
  212.6 85.6 all-gather.15
  301.7 274.5 all-gather.17
  579.5 152.8 all-gather.19
  984.0 134.3 reduce-scatter.19
  1120.7 132.7 reduce-scatter.17
  1259.0 100.5 reduce-scatter.15
  1366.0 602.8 all-reduce.86
  1975.1 1263.8 reduce-scatter.21
  3242.0 449.6 reduce-scatter.13
where the time goes:
time: 3720 us; the launch traced here: 3700 us
  waiting for transfers between devices  2410 us (65%)
  local copies, waits for them, and re-layouts  570 us (15%)
  blocking collectives  268 us (7%)
  matrix products  225 us (6%)
  other arithmetic  203 us (5%)
    unnamed x16, waiting for transfers between devices  1720 us
    reduce_scatter x1, waiting for transfers between devices, per_device(): lax.psum_scatter(grad_mix_out, ('dp', 'seq'), scatter_dimension=0, tiled=...  432 us
    unnamed x241, local copies, waits for them, and re-layouts  208 us
    all_gather x1, waiting for transfers between devices, per_device(): lax.all_gather(mlp_out.astype(jnp.bfloat16), ('dp', 'seq'), axis=0, tiled...  132 us
    all_gather x1, waiting for transfers between devices, per_device(): lax.all_gather(mlp_in.astype(jnp.bfloat16), ('dp', 'seq'), axis=0, tiled=...  119 us
    concatenate x1, other arithmetic, per_device(): jnp.concatenate([gate_up, down_grad[:, None, :]], 1)  99.4 us
    unnamed x2, blocking collectives  83.9 us
    slice x57, local copies, waits for them, and re-layouts, head_backward(): lax.associative_scan(affine_join, (next_keep, emitted), reverse=True, axi...  75.2 us
  transfers between devices with their start and end apart: 13, of which 7 were waited for; matrix products, arithmetic and copies ran while one was open for 21% of the time, Pallas kernels for 0%

commit v1 on v0

v1 whole, which is shorter than its diff:
```python
import functools

import jax
import jax.numpy as jnp
from jax import lax
from jax.experimental import pallas as pl
from jax.experimental.pallas import tpu as pltpu
from jax.sharding import PartitionSpec as P

EPS = 1e-06
FLOOR = 0.0001
SHARP = 8.0
HALO = 16
F32 = jnp.float32
BF16 = jnp.bfloat16
VMEM_LIMIT = 56 * 1024 * 1024
ANY = pl.BlockSpec(memory_space=pl.ANY)
ROOT = 0.7978845608028654
CUBE = 0.044715


def dot_nt(left, right):
    return lax.dot_general(left, right, (((1,), (1,)), ((), ())), preferred_element_type=F32)


def dot_nn(left, right):
    return lax.dot_general(left, right, (((1,), (0,)), ((), ())), preferred_element_type=F32)


def dot_tn(left, right):
    return lax.dot_general(left, right, (((0,), (0,)), ((), ())), preferred_element_type=F32)


def rms_norm(values, gain_vec):
    return values * lax.rsqrt(jnp.mean(values * values, axis=-1, keepdims=True) + EPS) * gain_vec


def gelu_parts(values):
    squared = values * values
    bend = jnp.tanh(ROOT * (values + CUBE * values * squared))
    half = 0.5 * (1.0 + bend)
    slope = half + 0.5 * values * (1.0 - bend * bend) * (ROOT * (1.0 + 3.0 * CUBE * squared))
    return values * half, slope


def gelu_value(values):
    bend = jnp.tanh(ROOT * (values + CUBE * values * values * values))
    return values * (0.5 * (1.0 + bend))


def plane_stages(count):
    bits = count.bit_length() - 1
    upper = list(range(1, bits))
    stages = []
    for place in range(len(upper)):
        pairs = []
        for source in range(count):
            shift = place if source % 2 == 0 else (place + 1) % len(upper)
            pairs.append((source, source ^ (1 << upper[shift])))
        stages.append(pairs)
    twin = [(source, source ^ 1) for source in range(count)]
    return stages, twin


def gather_rows(piece):
    stages, twin = plane_stages(lax.axis_size("dp"))
    held = [piece]
    other = [lax.ppermute(piece, "dp", twin)]
    for pairs in stages:
        arrived = [lax.ppermute(part, "dp", pairs) for part in held]
        held = held + arrived
        other = other + [lax.ppermute(part, "dp", twin) for part in arrived]
    return held + other


def scatter_rows(own, partner):
    stages, twin = plane_stages(lax.axis_size("dp"))
    held = own.astype(F32) + lax.ppermute(partner, "dp", twin).astype(F32)
    for pairs in reversed(stages):
        half = held.shape[0] // 2
        sent = held[half:].astype(BF16)
        held = held[:half] + lax.ppermute(sent, "dp", pairs).astype(F32)
    return held[0]


def hand_on(value, steps):
    count = lax.axis_size("seq")
    first, last = (max(0, -steps), min(count, count - steps))
    return lax.ppermute(value, "seq", [(source, source + steps) for source in range(first, last)])


def scan_into(keep, entry, cum_ref, state_ref, backward):
    rows, width = keep.shape
    groups = rows // 8
    mult = keep.reshape(groups, 8, width)
    total = entry.reshape(groups, 8, width)
    place = lax.broadcasted_iota(jnp.int32, (groups, 8, width), 1)
    for hop in (1, 2, 4):
        if backward:
            shift, valid = 8 - hop, place < 8 - hop
        else:
            shift, valid = hop, place >= hop
        near_mult = pltpu.roll(mult, shift, 1)
        near_total = pltpu.roll(total, shift, 1)
        total = jnp.where(valid, total + mult * near_total, total)
        mult = jnp.where(valid, mult * near_mult, mult)
    carry_total = jnp.zeros((1, width), F32)
    carry_mult = jnp.ones((1, width), F32)
    edge = 0 if backward else 7
    order = range(groups - 1, -1, -1) if backward else range(groups)
    for group in order:
        now_total = total[group] + mult[group] * carry_total
        now_mult = mult[group] * carry_mult
        state_ref[0, group * 8 : group * 8 + 8, :] = now_total
        cum_ref[0, group * 8 : group * 8 + 8, :] = now_mult
        carry_total = now_total[edge : edge + 1]
        carry_mult = now_mult[edge : edge + 1]
    return carry_mult, carry_total


def folded(refs):
    carry = refs[-1][0, 1:2, :]
    for ref in refs[-2::-1]:
        carry = ref[0, 1:2, :] + ref[0, 0:1, :] * carry
    return carry


def ends_block(mult, total):
    width = mult.shape[1]
    return jnp.concatenate([mult, total, jnp.zeros((6, width), F32)], 0)


def fetch_all(refs, buf, sems):
    for index, ref in enumerate(refs):
        pltpu.make_async_copy(ref, buf.at[index], sems.at[index]).start()


def fetched(refs, buf, sems, index):
    pltpu.make_async_copy(refs[0], buf.at[index], sems.at[index]).wait()


def mixer_enter_kernel(count, *refs):
    x_refs = refs[:count]
    (gain, wu, wy, wz, par, h_out, u_out, y_out, conv_out, r_out, e_out, k_out, m_out, a_out, s_out, ends, buf, sems) = refs[count:]
    step = pl.program_id(0)

    @pl.when(step == 0)
    def _():
        fetch_all(x_refs, buf, sems)

    fetched(x_refs, buf, sems, step)
    x_low = buf[step]
    rows = x_low.shape[0] - HALO
    width = wu.shape[0]
    x_val = x_low.astype(F32)
    h_low = rms_norm(x_val, gain[...]).astype(BF16)
    h_out[0] = h_low[HALO:]
    u_low = dot_nt(h_low, wu[...]).astype(BF16)
    u_out[0] = u_low
    y_out[0] = dot_nt(h_low[HALO:], wy[...])
    info = jnp.broadcast_to(x_val[0:1, :rows], (width, rows)).astype(BF16)
    across = lax.broadcasted_iota(jnp.int32, (rows, rows), 0)
    down = lax.broadcasted_iota(jnp.int32, (rows, rows), 1)
    same = dot_nt(jnp.where(across == down, 1.0, 0.0).astype(BF16), info)
    m_out[0] = same.astype(BF16)
    u_val = u_low.astype(F32)
    conv = par[4:5, :] + par[0:1, :] * u_val[HALO:]
    for back in (1, 2, 3):
        term = par[back : back + 1, :] * u_val[HALO - back : HALO - back + rows]
        conv = conv + jnp.where(same >= back, term, 0.0)
    conv_low = conv.astype(BF16)
    conv_out[0] = conv_low
    conv = conv_low.astype(F32)
    pre = dot_nt(conv_low, wz[...])
    recur = jax.nn.sigmoid(pre[:, :width] + par[5:6, :])
    enter = jax.nn.sigmoid(pre[:, width:] + par[6:7, :])
    keep = jnp.where(same >= 1.0, jnp.exp(par[7:8, :] * recur), 0.0)
    r_out[0] = recur
    e_out[0] = enter
    k_out[0] = keep
    inputs = conv * enter * jnp.sqrt(jnp.maximum(1.0 - keep * keep, FLOOR))
    mult, total = scan_into(keep, inputs, a_out, s_out, False)
    ends[0] = ends_block(mult, total)


def resident(shape):
    zeros = (0,) * len(shape)
    return pl.BlockSpec(shape, lambda step: zeros)


def per_piece(shape, first=0):
    rest = (0,) * len(shape)
    return pl.BlockSpec((1,) + shape, lambda step: (step + first,) + rest)


def call(kernel, grid, in_specs, out_specs, out_shape, scratch, flops, moved):
    return pl.pallas_call(
        kernel,
        grid=grid,
        in_specs=in_specs,
        out_specs=out_specs,
        out_shape=out_shape,
        scratch_shapes=scratch,
        compiler_params=pltpu.CompilerParams(
            vmem_limit_bytes=VMEM_LIMIT, dimension_semantics=("arbitrary",) * len(grid)
        ),
        cost_estimate=pl.CostEstimate(flops=int(flops), bytes_accessed=int(moved), transcendentals=0),
    )


def mixer_enter(pieces, gain, wu, wy, wz, par):
    count = len(pieces)
    tall, model = pieces[0].shape
    rows = tall - HALO
    width = wu.shape[0]

    def out(height, columns, dtype):
        return jax.ShapeDtypeStruct((count, height, columns), dtype)

    shapes = [
        out(rows, model, BF16),
        out(tall, width, BF16),
        out(rows, width, F32),
        out(rows, width, BF16),
        out(rows, width, F32),
        out(rows, width, F32),
        out(rows, width, F32),
        out(rows, width, BF16),
        out(rows, width, F32),
        out(rows, width, F32),
        out(8, width, F32),
    ]
    return call(
        functools.partial(mixer_enter_kernel, count),
        (count,),
        [ANY] * count + [resident(v.shape) for v in (gain, wu, wy, wz, par)],
        [per_piece(s.shape[1:]) for s in shapes],
        shapes,
        [pltpu.VMEM((count, tall, model), BF16), pltpu.SemaphoreType.DMA((count,))],
        2 * count * rows * model * width * 2,
        count * rows * (model * 4 + width * 34),
    )(*pieces, gain, wu, wy, wz, par)


def mixer_leave_kernel(hops, *refs):
    ends = refs[:hops]
    cum, local, y_pre, w_out, part = refs[hops:]
    states = local[0] + cum[0] * folded(ends)
    mixed = (gelu_value(y_pre[0]) * states).astype(BF16)
    part[0] = dot_nn(mixed, w_out[...]).astype(BF16)


def mixer_leave(ends, cum, local, y_pre, w_out, first, count):
    rows, width = cum.shape[1:]
    model = w_out.shape[1]
    return call(
        functools.partial(mixer_leave_kernel, len(ends)),
        (count,),
        [per_piece((8, width), first)] * len(ends)
        + [per_piece((rows, width), first)] * 3
        + [resident(w_out.shape)],
        per_piece((rows, model)),
        jax.ShapeDtypeStruct((count, rows, model), BF16),
        [],
        2 * count * rows * width * model,
        count * rows * (width * 12 + model * 2),
    )(*ends, cum, local, y_pre, w_out)


def head_back_kernel(count, hops, *refs):
    d_refs = refs[:count]
    ends = refs[count : count + hops]
    (cum, local, y_pre, keep_ref, w_out, dy_out, mixed_out, cb_out, lb_out, ends_out, buf, sems) = refs[count + hops :]
    step = pl.program_id(0)

    @pl.when(step == 0)
    def _():
        fetch_all(d_refs, buf, sems)

    fetched(d_refs, buf, sems, step)
    d_mixed = dot_nt(buf[step], w_out[...])
    states = local[0] + cum[0] * folded(ends)
    value, slope = gelu_parts(y_pre[0])
    mixed_out[0] = (value * states).astype(BF16)
    dy_out[0] = (slope * d_mixed * states).astype(BF16)
    keep = keep_ref[0]
    width = keep.shape[1]
    next_keep = jnp.concatenate([keep[1:], jnp.ones((1, width), F32)], 0)
    mult, total = scan_into(next_keep, d_mixed * value, cb_out, lb_out, True)
    ends_out[0] = ends_block(mult * keep[0:1], total * keep[0:1])


def head_back(pieces, ends, cum, local, y_pre, keep, w_out):
    count = len(pieces)
    rows, model = pieces[0].shape
    width = cum.shape[2]

    def out(height, dtype):
        return jax.ShapeDtypeStruct((count, height, width), dtype)

    shapes = [out(rows, BF16), out(rows, BF16), out(rows, F32), out(rows, F32), out(8, F32)]
    return call(
        functools.partial(head_back_kernel, count, len(ends)),
        (count,),
        [ANY] * count
        + [per_piece((8, width))] * len(ends)
        + [per_piece((rows, width))] * 4
        + [resident(w_out.shape)],
        [per_piece(s.shape[1:]) for s in shapes],
        shapes,
        [pltpu.VMEM((count, rows, model), BF16), pltpu.SemaphoreType.DMA((count,))],
        2 * count * rows * width * model,
        count * rows * (width * 28 + model * 2),
    )(*pieces, *ends, cum, local, y_pre, keep, w_out)


def tail_back_kernel(hops, *refs):
    ends = refs[:hops]
    later = refs[hops : 2 * hops]
    (cb, lb, cum, local, r_ref, e_ref, k_ref, conv_ref, u_ref, m_ref, wz, par, du_out, edge_out, gw_out, small_out) = refs[2 * hops :]
    step = pl.program_id(0)

    @pl.when(step == 0)
    def _():
        gw_out[...] = jnp.zeros_like(gw_out)
        small_out[...] = jnp.zeros_like(small_out)

    state_in = folded(ends)
    d_states = lb[0] + cb[0] * folded(later)
    states = local[0] + cum[0] * state_in
    prev = jnp.concatenate([state_in, states[:-1]], 0)
    recur, enter, keep = r_ref[0], e_ref[0], k_ref[0]
    conv_low = conv_ref[0]
    conv = conv_low.astype(F32)
    rows, width = conv.shape
    spare = 1.0 - keep * keep
    scaling = jnp.sqrt(jnp.maximum(spare, FLOOR))
    weight = jnp.where(spare > FLOOR, 0.5, jnp.where(spare == FLOOR, 0.25, 0.0)) / scaling
    d_enter_sum = d_states * conv
    d_spare = d_enter_sum * enter * weight
    d_expo = (d_states * prev - 2.0 * keep * d_spare) * keep
    d_recur = d_expo * par[7:8, :] * recur * (1.0 - recur)
    d_enter = d_enter_sum * scaling * enter * (1.0 - enter)
    d_pre = jnp.concatenate([d_recur.astype(BF16), d_enter.astype(BF16)], 1)
    d_conv = d_states * enter * scaling + dot_nn(d_pre, wz[...])
    gw_out[...] += dot_tn(d_pre, conv_low)
    d_pre_val = d_pre.astype(F32)
    same = m_ref[0].astype(F32)
    u_val = u_ref[0].astype(F32)
    sums = []
    d_u = jnp.zeros((rows, width), F32)
    head = jnp.zeros((8, width), F32)
    for back in range(4):
        masked = d_conv if back == 0 else jnp.where(same >= back, d_conv, 0.0)
        sums.append(jnp.sum(masked * u_val[HALO - back : HALO - back + rows], axis=0, keepdims=True))
        moved = masked * par[back : back + 1, :]
        if back == 0:
            d_u = d_u + moved
        else:
            nothing = jnp.zeros((back, width), F32)
            d_u = d_u + jnp.concatenate([moved[back:], nothing], 0)
            head = head + jnp.concatenate([jnp.zeros((8 - back, width), F32), moved[:back]], 0)
    sums.append(jnp.sum(d_conv, axis=0, keepdims=True))
    sums.append(jnp.sum(d_pre_val[:, :width], axis=0, keepdims=True))
    sums.append(jnp.sum(d_pre_val[:, width:], axis=0, keepdims=True))
    sums.append(jnp.sum(d_expo * recur, axis=0, keepdims=True))
    small_out[...] += jnp.concatenate(sums, 0)
    du_out[0] = d_u.astype(BF16)
    edge_out[0, 0:8, :] = head
    edge_out[0, 8:16, :] = d_u[rows - 8 :]


def tail_back(ends, later, cb, lb, cum, local, recur, enter, keep, conv, u_ext, same, wz, par):
    count, rows, width = cb.shape
    shapes = [
        jax.ShapeDtypeStruct((count, rows, width), BF16),
        jax.ShapeDtypeStruct((count, 16, width), F32),
        jax.ShapeDtypeStruct(wz.shape, F32),
        jax.ShapeDtypeStruct((8, width), F32),
    ]
    tall = u_ext.shape[1]
    return call(
        functools.partial(tail_back_kernel, len(ends)),
        (count,),
        [per_piece((8, width))] * (2 * len(ends))
        + [per_piece((rows, width))] * 8
        + [per_piece((tall, width)), per_piece((rows, width)), resident(wz.shape), resident(par.shape)],
        [per_piece((rows, width)), per_piece((16, width)), resident(wz.shape), resident((8, width))],
        shapes,
        [],
        8 * count * rows * width * width,
        count * rows * width * 36,
    )(*ends, *later, cb, lb, cum, local, recur, enter, keep, conv, u_ext, same, wz, par)


def rows_times_kernel(terms, *refs):
    total = dot_nn(refs[0][0], refs[terms][...])
    for term in range(1, terms):
        total = total + dot_nn(refs[term][0], refs[terms + term][...])
    refs[-1][0] = total.astype(BF16)


def rows_times(lefts, rights, first, count):
    rows = lefts[0].shape[1]
    model = rights[0].shape[1]
    inner = sum(right.shape[0] for right in rights)
    return call(
        functools.partial(rows_times_kernel, len(lefts)),
        (count,),
        [per_piece(left.shape[1:], first) for left in lefts] + [resident(r.shape) for r in rights],
        per_piece((rows, model)),
        jax.ShapeDtypeStruct((count, rows, model), BF16),
        [],
        2 * count * rows * inner * model,
        count * rows * 2 * (inner + model) + 2 * inner * model,
    )(*lefts, *rights)


def mlp_kernel(count, *refs):
    h_refs = refs[:count]
    c_refs = refs[count : 2 * count]
    wg, wu, wo, hid_out, dg_out, du_out, h_buf, c_buf, h_sems, c_sems = refs[2 * count :]
    step = pl.program_id(0)

    @pl.when(step == 0)
    def _():
        fetch_all(h_refs, h_buf, h_sems)
        fetch_all(c_refs, c_buf, c_sems)

    def one_piece(index, carry):
        @pl.when(step == 0)
        def _():
            fetched(h_refs, h_buf, h_sems, index)
            fetched(c_refs, c_buf, c_sems, index)

        h_low = h_buf[index]
        gate = dot_nt(h_low, wg[...])
        up = dot_nt(h_low, wu[...])
        d_hidden = dot_nt(c_buf[index], wo[...])
        value, slope = gelu_parts(gate)
        hid_out[index] = (value * up).astype(BF16)
        dg_out[index] = (d_hidden * up * slope).astype(BF16)
        du_out[index] = (d_hidden * value).astype(BF16)
        return carry

    lax.fori_loop(0, count, one_piece, 0)


def mlp_middle(h_pieces, c_pieces, wg, wu, wo):
    count = len(h_pieces)
    rows, model = h_pieces[0].shape
    hidden = wg.shape[0]
    tile = next(t for t in (256, 128, hidden) if hidden % t == 0)
    shape = jax.ShapeDtypeStruct((count, rows, hidden), BF16)
    w_spec = pl.BlockSpec((tile, model), lambda step: (step, 0))
    out_spec = pl.BlockSpec((count, rows, tile), lambda step: (0, 0, step))
    return call(
        functools.partial(mlp_kernel, count),
        (hidden // tile,),
        [ANY] * (2 * count) + [w_spec] * 3,
        [out_spec] * 3,
        [shape] * 3,
        [
            pltpu.VMEM((count, rows, model), BF16),
            pltpu.VMEM((count, rows, model), BF16),
            pltpu.SemaphoreType.DMA((count,)),
            pltpu.SemaphoreType.DMA((count,)),
        ],
        6 * count * rows * model * hidden,
        count * rows * (4 * model + 6 * hidden) + 6 * model * hidden,
    )(*h_pieces, *c_pieces, wg, wu, wo)


def weight_grad(rows_left, rows_right):
    left = rows_left.reshape(-1, rows_left.shape[-1])
    right = rows_right.reshape(-1, rows_right.shape[-1])
    return dot_tn(left, right).astype(BF16)


def seq_gather(shard):
    return lax.all_gather(shard, "seq", axis=0, tiled=True)


def seq_scatter(whole):
    return lax.psum_scatter(whole, "seq", scatter_dimension=0, tiled=True)


def per_device(
    tokens,
    cotangent,
    doc_ids,
    mix_in,
    mix_out,
    gate_w,
    conv_w,
    conv_bias,
    gate_bias,
    decay_param,
    gain_one,
    gain_two,
    mlp_in,
    mlp_out,
):
    run_len, model = tokens.shape[1:]
    n_seq = lax.axis_size("seq")
    n_dev = lax.axis_size("dp") * n_seq
    own = mix_out.shape[0]
    block = gate_w.shape[2]
    chan = own * n_seq
    width = -(-chan // 128) * 128
    blocks = chan // block

    x_low = tokens.reshape(run_len, model)
    x_zero = x_low.astype(F32)
    cot_low = cotangent.reshape(run_len, model)
    lead = hand_on(x_low[run_len - HALO :], 1)
    first_token = lax.axis_index("seq") * run_len
    padded = jnp.concatenate([jnp.full((3,), -1, jnp.int32), doc_ids.reshape(-1)])
    own_docs = lax.dynamic_slice_in_dim(padded, first_token + 3, run_len)
    same = sum(
        jnp.where(lax.dynamic_slice_in_dim(padded, first_token + 3 - back, run_len) == own_docs, 1.0, 0.0)
        for back in (1, 2, 3)
    )
    info = jnp.pad(same, (0, model - run_len)).astype(BF16)[None]
    x_piece = jnp.concatenate([info, lead[1:], x_low], 0)

    small = jnp.concatenate(
        [
            gate_w.reshape(own, 2 * block),
            conv_w.T,
            conv_bias[:, None],
            gate_bias.T,
            decay_param[:, None],
        ],
        1,
    )
    extra = -(-small.shape[1] // 128) * 128
    small = jnp.pad(small, ((0, 0), (0, extra - small.shape[1])))
    w_u_all = seq_gather(jnp.concatenate([mix_in[:, 1, :], small], 1).astype(BF16))
    w_y = seq_gather(mix_in[:, 0, :].astype(BF16))
    w_out = seq_gather(mix_out.astype(BF16))
    w_gate = seq_gather(mlp_in[:, 0, :].astype(BF16))
    w_up = seq_gather(mlp_in[:, 1, :].astype(BF16))
    w_down = seq_gather(mlp_out.astype(BF16))
    gains = jnp.concatenate([gain_one, gain_two]).astype(BF16)[None]
    gains = lax.all_gather(gains, ("dp", "seq"), axis=0, tiled=True).astype(F32)
    part = gain_one.shape[0]
    g_one = gains[:, :part].reshape(1, model)
    g_two = gains[:, part:].reshape(1, model)

    def widened(rows):
        return jnp.pad(rows, ((0, width - chan), (0, 0)))

    w_u = widened(w_u_all[:, :model])
    w_y = widened(w_y)
    w_out = widened(w_out)
    gate_rows = w_u_all[:, model : model + 2 * block].reshape(blocks, block, 2, block)
    eye = jnp.eye(blocks, dtype=BF16)
    w_z = jnp.einsum("bogj,bc->gbocj", gate_rows, eye).reshape(2, chan, chan)
    w_z = jnp.pad(w_z, ((0, 0), (0, width - chan), (0, width - chan))).reshape(2 * width, width)
    par = w_u_all[:, model + 2 * block : model + 2 * block + 8].astype(F32).T
    decay_rate = -SHARP * jax.nn.softplus(par[7])
    decay_slope = -SHARP * jax.nn.sigmoid(par[7])
    par = jnp.pad(jnp.concatenate([par[:7], decay_rate[None]], 0), ((0, 0), (0, width - chan)))

    x_pieces = gather_rows(x_piece)
    count = len(x_pieces)
    half = count // 2
    (h_one, u_ext, y_pre, conv, recur, enter, keep, same, cum, local, ends) = mixer_enter(
        x_pieces, g_one, w_u, w_y, w_z, par
    )
    earlier = [hand_on(ends, steps) for steps in range(1, n_seq)]
    partner = mixer_leave(earlier, cum, local, y_pre, w_out, half, half)
    mine = mixer_leave(earlier, cum, local, y_pre, w_out, 0, half)
    x_one = x_zero + scatter_rows(mine, partner)
    n_two, norm_two_back = jax.vjp(rms_norm, x_one, g_two)
    h_two = n_two.astype(BF16)

    c_pieces = gather_rows(cot_low)
    h_pieces = gather_rows(h_two)
    hidden, d_gate, d_up = mlp_middle(h_pieces, c_pieces, w_gate, w_up, w_down)
    partner = rows_times([d_gate, d_up], [w_gate, w_up], half, half)
    mine = rows_times([d_gate, d_up], [w_gate, w_up], 0, half)
    d_h_two = scatter_rows(mine, partner)
    h_all = jnp.concatenate(h_pieces, 0)
    c_all = jnp.concatenate(c_pieces, 0)
    grad_down = seq_scatter(weight_grad(hidden, c_all))
    grad_gate = seq_scatter(weight_grad(d_gate, h_all))
    grad_up = seq_scatter(weight_grad(d_up, h_all))
    partner = rows_times([hidden], [w_down], half, half)
    mine = rows_times([hidden], [w_down], 0, half)
    layer_out = (x_one + scatter_rows(mine, partner)).astype(BF16).reshape(1, run_len, model)
    d_x_norm, d_gain_two = norm_two_back(d_h_two)
    d_x_one = cot_low.astype(F32) + d_x_norm
    d_mix = d_x_one.astype(BF16)

    d_pieces = gather_rows(d_mix)
    d_y, mixed, cum_back, local_back, ends_back = head_back(
        d_pieces, earlier, cum, local, y_pre, keep, w_out
    )
    later = [hand_on(ends_back, -steps) for steps in range(1, n_seq)]
    grad_out = seq_scatter(weight_grad(mixed, jnp.concatenate(d_pieces, 0))[:chan])
    grad_y = seq_scatter(weight_grad(d_y, h_one)[:chan])
    d_u, edges, grad_z, sums = tail_back(
        earlier, later, cum_back, local_back, cum, local, recur, enter, keep, conv, u_ext, same, w_z, par
    )
    from_next = hand_on(edges[:, :8], -1)
    d_u = lax.dynamic_update_slice(d_u, (edges[:, 8:] + from_next).astype(BF16), (0, run_len - 8, 0))
    partner = rows_times([d_y, d_u], [w_y, w_u], half, half)
    mine = rows_times([d_y, d_u], [w_y, w_u], 0, half)
    d_h_one = scatter_rows(mine, partner)
    _, norm_one_back = jax.vjp(rms_norm, x_zero, g_one)
    d_x_zero, d_gain_one = norm_one_back(d_h_one)
    input_grad = (d_x_one + d_x_zero).astype(BF16).reshape(1, run_len, model)

    grad_u = weight_grad(d_u, h_one)[:chan]
    grad_z = grad_z.reshape(2, width, width)[:, :chan, :chan].reshape(2, blocks, block, blocks, block)
    grad_z = jnp.stack([grad_z[:, b, :, b, :] for b in range(blocks)], 1)
    grad_z = jnp.transpose(grad_z, (1, 2, 0, 3)).reshape(chan, 2 * block)
    sums = sums[:, :chan]
    sums = jnp.concatenate([sums[:7], (sums[7] * decay_slope)[None]], 0).T
    tail = jnp.concatenate([grad_z, sums], 1)
    tail = jnp.pad(tail, ((0, 0), (0, extra - tail.shape[1]))).astype(BF16)
    grad_u = seq_scatter(jnp.concatenate([grad_u, tail], 1))
    tail = grad_u[:, model:].astype(F32)
    grad_mix_in = jnp.stack([grad_y.astype(F32), grad_u[:, :model].astype(F32)], 1)
    at = 2 * block
    d_gains = jnp.concatenate([d_gain_one.reshape(n_dev, part), d_gain_two.reshape(n_dev, part)], 1)
    d_gains = lax.psum_scatter(d_gains, ("dp", "seq"), scatter_dimension=0, tiled=True)[0]
    return (
        layer_out,
        input_grad,
        grad_mix_in,
        grad_out.astype(F32),
        tail[:, :at].reshape(own, 2, block),
        tail[:, at : at + 4].T,
        tail[:, at + 4],
        tail[:, at + 5 : at + 7].T,
        tail[:, at + 7],
        d_gains[:part],
        d_gains[part:],
        jnp.stack([grad_gate.astype(F32), grad_up.astype(F32)], 1),
        grad_down.astype(F32),
    )


def solution(mesh):
    rows = P(("dp", "seq"))
    placed = (
        P("dp", "seq", None),
        P("dp", "seq", None),
        P("dp", None),
        P(("dp", "seq"), None, None),
        P(("dp", "seq"), None),
        P(("dp", "seq"), None, None),
        P(None, ("dp", "seq")),
        rows,
        P(None, ("dp", "seq")),
        rows,
        rows,
        rows,
        P(("dp", "seq"), None, None),
        P(("dp", "seq"), None),
    )
    return jax.shard_map(
        per_device,
        mesh=mesh,
        in_specs=placed,
        out_specs=placed[:2] + placed[3:],
        check_vma=False,
    )
```

time: 3720 us -> 778 us (0.21)
  waiting for transfers between devices: 2410 us -> 236 us
  local copies, waits for them, and re-layouts: 570 us -> 88.7 us
  matrix products: 225 us -> 52.5 us
  blocking collectives: 268 us -> 104 us
  Pallas kernels: 0 us -> 158 us
  other arithmetic: 203 us -> 64.8 us
  starting transfers between devices: 6.41 us -> 49.1 us
    unnamed x16 -> x12, waiting for transfers between devices: 1720 us -> 0.2 us
    reduce_scatter x1 -> x6, waiting for transfers between devices: 432 us -> 0.05 us  [seq_scatter(): return lax.psum_scatter(whole, 'seq', scatter_dimension=0, tiled=True)]
    all_gather x5 -> x6, waiting for transfers between devices: 251 us -> 14 us  [seq_gather(): return lax.all_gather(shard, 'seq', axis=0, tiled=True)]
    ppermute x2 -> x48, waiting for transfers between devices: 3.32 us -> 221 us  [the longest x12 104 us: gather_rows(): arrived = [lax.ppermute(part, 'dp', pairs) for part in held]]
    dot_general x14 -> x6, matrix products: 223 us -> 52.5 us  [dot_tn(): lax.dot_general(left, right, (((0,), (0,)), ((), ())), preferred_element_...]
    pallas_call x0 -> x12, Pallas kernels: none -> 158 us  [the longest x6 54.2 us: rows_times(): call(functools.partial(rows_times_kernel, len(lefts)), (count,), [per_pie...]
    unnamed x241 -> x131, local copies, waits for them, and re-layouts: 208 us -> 55.3 us
    slice x113 -> x27, local copies, waits for them, and re-layouts: 146 us -> 16.3 us  [the longest x8 7.44 us: scatter_rows(): sent = held[half:].astype(BF16)]
  transfers between devices with their start and end apart: 13 -> 60, of which waited for: 7 -> 22; matrix products, arithmetic and copies ran while one was open for 21% -> 23% of each run, Pallas kernels for 0% -> 15%
where the time goes in v1:
time: 778 us; the launch traced here: 768 us
  waiting for transfers between devices  236 us (30%)
  Pallas kernels  158 us (20%)
  blocking collectives  104 us (13%)
  local copies, waits for them, and re-layouts  88.7 us (11%)
  other arithmetic  64.8 us (8%)
  matrix products  52.5 us (7%)
  starting transfers between devices  49.1 us (6%)
  between operations  15.5 us (2%)
    ppermute x12, waiting for transfers between devices, gather_rows(): arrived = [lax.ppermute(part, 'dp', pairs) for part in held]  104 us
    ppermute x8, waiting for transfers between devices, scatter_rows(): held = held[:half] + lax.ppermute(sent, 'dp', pairs).astype(F32)  86 us
    all_gather x1, blocking collectives, per_device(): gains = lax.all_gather(gains, ('dp', 'seq'), axis=0, tiled=True).astype(F32)  66.4 us
    unnamed x131, local copies, waits for them, and re-layouts  55.3 us
    pallas_call x6, Pallas kernels, rows_times(): call(functools.partial(rows_times_kernel, len(lefts)), (count,), [per_pie...  54.2 us
    dot_general x6, matrix products, dot_tn(): lax.dot_general(left, right, (((0,), (0,)), ((), ())), preferred_element_...  52.5 us
    unnamed x1, blocking collectives  37.5 us
    pallas_call x1, Pallas kernels, mlp_middle(): call(functools.partial(mlp_kernel, count), (hidden // tile,), [ANY] * (2...  30.2 us
  transfers between devices with their start and end apart: 60, of which 22 were waited for; matrix products, arithmetic and copies ran while one was open for 23% of the time, Pallas kernels for 15%

profile of v1, /device:TPU:0, one launch (start us, length us, event | category | flops | bytes accessed | tf_op | source)
XLA Modules:
  0.0 767.7 jit_solution(13679794782584901639)
XLA Ops:
  23.0 24.7 %collective-permute-done.1.refs_1_ = bf16[272,2048]{1,0:T(8,128)(2,1)} collective-permute-done((bf16[272,2048]{1,0:T(8,128)(2,1)}, bf16[272,2048]{1,0:T(8,128)(2,1)}, u32[]{:S(2)}, u32[]{:S(2)}) %collective-permute-start.1) | collective-permute-done | bytes 1114144 | tf_op jit(solution)/shard_map/ppermute | solution.py:70
  52.8 66.4 %all-gather.3 = bf16[32,1,128]{2,1,0:T(2,128)(2,1)S(1)} all-gather(bf16[1,1,128]{2,1,0:T(2,128)(2,1)S(1)} %maximum_bitcast_fusion.2), channel_id=1, replica_groups=mesh['dp'=8,'seq'=4] {'dp','seq'}, dimensions={0}, use_global_device_ids=true | all-gather | bytes 8448 | tf_op jit(solution)/shard_map/all_gather | solution.py:546
  130.0 25.5 %shard_map.237 = (bf16[8,256,2048]{2,1,0:T(8,128)(2,1)}, bf16[8,272,384]{2,1,0:T(8,128)(2,1)}, f32[8,256,384]{2,1,0:T(8,128)}, bf16[8,256,384]{2,1,0:T(8,128)(2,...) custom-call(bf16[272,2048]{1,0:T(8,128)(2,1)} %pad_maximum_fusion.1., ...), custom_call_target="tpu_custom_call" | custom-call | flops 6442450944 | bytes 43515904 | tf_op jit(solution)/shard_map/pallas_call | solution.py:233
  178.9 7.1 shard_map.238
  193.2 24.6 %collective-permute-done.12 = bf16[2,256,2048]{2,1,0:T(8,128)(2,1)S(1)} collective-permute-done((bf16[2,256,2048]{2,1,0:T(8,128)(2,1)S(1)}, bf16[2,256,2048]{2,1,0:T(8,128)(2,1)S(1)}, u32[]{:S(2)}, u32[]{:S(2)}) %collective-permute-start.12) | collective-permute-done | bytes 2097184 | tf_op jit(solution)/shard_map/ppermute | solution.py:82
  225.3 18.9 %collective-permute-done.13 = bf16[1,256,2048]{2,1,0:T(8,128)(2,1)} collective-permute-done((bf16[1,256,2048]{2,1,0:T(8,128)(2,1)S(1)}, bf16[1,256,2048]{2,1,0:T(8,128)(2,1)}, u32[]{:S(2)}, u32[]{:S(2)}) %collective-permute-start.13) | collective-permute-done | bytes 1048608 | tf_op jit(solution)/shard_map/ppermute | solution.py:82
  249.6 8.4 %collective-permute-done.21.refs_9_ = bf16[256,2048]{1,0:T(8,128)(2,1)} collective-permute-done((bf16[256,2048]{1,0:T(8,128)(2,1)}, bf16[256,2048]{1,0:T(8,128)(2,1)}, u32[]{:S(2)}, u32[]{:S(2)}) %collective-permute-start.21) | collective-permute-done | bytes 1048608 | tf_op jit(solution)/shard_map/ppermute | solution.py:70
  260.6 18.0 %collective-permute-done.14.refs_1_ = bf16[256,2048]{1,0:T(8,128)(2,1)} collective-permute-done((bf16[256,2048]{1,0:T(8,128)(2,1)S(1)}, bf16[256,2048]{1,0:T(8,128)(2,1)}, u32[]{:S(2)}, u32[]{:S(2)}) %collective-permute-start.14) | collective-permute-done | bytes 1048608 | tf_op jit(solution)/shard_map/ppermute | solution.py:70
  281.1 9.4 %collective-permute-done.15.refs_2_ = bf16[256,2048]{1,0:T(8,128)(2,1)} collective-permute-done((bf16[256,2048]{1,0:T(8,128)(2,1)S(1)}, bf16[256,2048]{1,0:T(8,128)(2,1)}, u32[]{:S(2)}, u32[]{:S(2)}) %collective-permute-start.15) | collective-permute-done | bytes 1048608 | tf_op jit(solution)/shard_map/ppermute | solution.py:70
  291.8 9.9 %collective-permute-done.16.refs_3_ = bf16[256,2048]{1,0:T(8,128)(2,1)} collective-permute-done((bf16[256,2048]{1,0:T(8,128)(2,1)}, bf16[256,2048]{1,0:T(8,128)(2,1)}, u32[]{:S(2)}, u32[]{:S(2)}) %collective-permute-start.16) | collective-permute-done | bytes 1048608 | tf_op jit(solution)/shard_map/ppermute | solution.py:70
  303.1 14.0 %all-gather.15.cloned.1.call-done.refs_18_.refs_1_ = bf16[768,2048]{1,0:T(8,128)(2,1)} async-done(((bf16[192,2048]{1,0:T(8,128)(2,1)}), bf16[768,2048]{1,0:T(8,128)(2,1)}) %all-gather.15.cloned.1.call-update) | async-done | bytes 3145744 | tf_op jit(solution)/shard_map/all_gather | solution.py:481
  317.1 30.2 %shard_map.240 = (bf16[8,256,768]{2,1,0:T(8,128)(2,1)}, bf16[8,256,768]{2,1,0:T(8,128)(2,1)}, bf16[8,256,768]{2,1,0:T(8,128)(2,1)}) custom-call(bf16[256,2048]{1,0:T(8,128)(2,1)} %copy-done.21, bf16[256,2048]{1,0:T(8,128)(2,1)} %collective-permute-done.14.refs_1_, bf16[256,2048]{1,0:T(8,128)(2,1)} %collective-permute-done.15.refs_2_, ...), custom_call_target="tpu_custom_call" | custom-call | flops 19327352832 | bytes 35651584 | tf_op jit(solution)/shard_map/pallas_call | solution.py:457
  347.3 11.4 %shard_map.244 = bf16[4,256,2048]{2,1,0:T(8,128)(2,1)} custom-call(bf16[8,256,768]{2,1,0:T(8,128)(2,1)} %get-tuple-element.41.refs_0_, bf16[8,256,768]{2,1,0:T(8,128)(2,1)} %get-tuple-element.42.refs_1_, bf16[768,2048]{1,0:T(8,128)(2,1)} %bitcast.119, bf16[768,2048]{1,0:T(8,128)(2,1)} %bitcast.122), custom_call_target="tpu_custom_call" | custom-call | flops 6442450944 | bytes 13631488 | tf_op jit(solution)/shard_map/pallas_call | solution.py:407
  375.1 10.5 %convolution_convert_fusion.2 = bf16[768,2048]{1,0:T(8,128)(2,1)} fusion(bf16[2048,768]{1,0:T(8,128)(2,1)S(1)} %bitcast.127, bf16[2048,2048]{1,0:T(8,128)(2,1)} %constant_dynamic-update-slice_fusion.8), kind=kOutput, calls=%fused_computation.18 | convolution fusion | flops 6444023808 | bytes 14680064 | tf_op jit(solution)/shard_map/dot_general | solution.py:31
  385.8 11.4 %shard_map.243 = bf16[4,256,2048]{2,1,0:T(8,128)(2,1)} custom-call(bf16[8,256,768]{2,1,0:T(8,128)(2,1)} %get-tuple-element.41.refs_0_, bf16[8,256,768]{2,1,0:T(8,128)(2,1)} %get-tuple-element.42.refs_1_, bf16[768,2048]{1,0:T(8,128)(2,1)} %bitcast.120, bf16[768,2048]{1,0:T(8,128)(2,1)} %bitcast.123), custom_call_target="tpu_custom_call" | custom-call | flops 6442450944 | bytes 13631488 | tf_op jit(solution)/shard_map/pallas_call | solution.py:407
  404.5 24.6 %collective-permute-done.32 = bf16[2,256,2048]{2,1,0:T(8,128)(2,1)S(1)} collective-permute-done((bf16[2,256,2048]{2,1,0:T(8,128)(2,1)S(1)}, bf16[2,256,2048]{2,1,0:T(8,128)(2,1)S(1)}, u32[]{:S(2)}, u32[]{:S(2)}) %collective-permute-start.32) | collective-permute-done | bytes 2097184 | tf_op jit(solution)/shard_map/ppermute | solution.py:82
  434.5 8.4 %convolution_convert_fusion.1 = bf16[768,2048]{1,0:T(8,128)(2,1)} fusion(bf16[2048,768]{1,0:T(8,128)(2,1)S(1)} %bitcast.126, bf16[2048,2048]{1,0:T(8,128)(2,1)S(1)} %bitcast.114), kind=kOutput, calls=%fused_computation.17 | convolution fusion | flops 6444023808 | bytes 14680064 | tf_op jit(solution)/shard_map/dot_general | solution.py:31
  455.3 23.1 %collective-permute-done.34.refs_1_ = bf16[256,2048]{1,0:T(8,128)(2,1)S(1)} collective-permute-done((bf16[256,2048]{1,0:T(8,128)(2,1)S(1)}, bf16[256,2048]{1,0:T(8,128)(2,1)S(1)}, u32[]{:S(2)}, u32[]{:S(2)}) %collective-permute-start.34) | collective-permute-done | bytes 1048608 | tf_op jit(solution)/shard_map/ppermute | solution.py:70
  482.3 10.9 %collective-permute-done.36.refs_3_ = bf16[256,2048]{1,0:T(8,128)(2,1)S(1)} collective-permute-done((bf16[256,2048]{1,0:T(8,128)(2,1)S(1)}, bf16[256,2048]{1,0:T(8,128)(2,1)S(1)}, u32[]{:S(2)}, u32[]{:S(2)}) %collective-permute-start.36) | collective-permute-done | bytes 1048608 | tf_op jit(solution)/shard_map/ppermute | solution.py:70
  500.3 16.6 %shard_map.245 = (bf16[8,256,384]{2,1,0:T(8,128)(2,1)}, bf16[8,256,384]{2,1,0:T(8,128)(2,1)}, f32[8,256,384]{2,1,0:T(8,128)}, f32[8,256,384]{2,1,0:T(8,128)}, f32[8,8,384]{2,1,0:T(8,128)}) custom-call(bf16[256,2048]{1,0:T(8,128)(2,1)} %copy-done.9, bf16[256,2048]{1,0:T(8,128)(2,1)} %copy-done.10, bf16[256,2048]{1,0:T(8,128)(2,1)} %copy-done.11, ...), custom_call_target="tpu_custom_call" | custom-call | flops 3221225472 | bytes 30408704 | tf_op jit(solution)/shard_map/pallas_call | solution.py:302
  516.9 7.3 fusion.29
  533.8 10.4 %convolution_convert_fusion = bf16[768,2048]{1,0:T(8,128)(2,1)} fusion(bf16[2048,768]{1,0:T(8,128)(2,1)S(1)} %bitcast.125, bf16[2048,2048]{1,0:T(8,128)(2,1)} %constant_dynamic-update-slice_fusion.16), kind=kOutput, calls=%fused_computation.16 | convolution fusion | flops 6444023808 | bytes 14680064 | tf_op jit(solution)/shard_map/dot_general | solution.py:31
  544.3 7.3 shard_map.242
  566.2 16.9 %shard_map.246 = (bf16[8,256,384]{2,1,0:T(8,128)(2,1)}, f32[8,16,384]{2,1,0:T(8,128)}, f32[768,384]{1,0:T(8,128)}, f32[8,384]{1,0:T(8,128)}) custom-call(f32[8,8,384]{2,1,0:T(8,128)} %copy-done.18, f32[8,8,384]{2,1,0:T(8,128)} %copy-done.19, f32[8,8,384]{2,1,0:T(8,128)} %copy-done.17, f32[8,8,384]{2,1,0:T(8,128)} %copy-done.34, f32[8,8,384]{2,1,0:T(8,128)} %copy-done.35, ...), custom_call_target="tpu_custom_call" | custom-call | flops 2415919104 | bytes 28311552 | tf_op jit(solution)/shard_map/pallas_call | solution.py:382
  585.3 11.0 %collective-permute-done.44 = f32[8,8,384]{2,1,0:T(8,128)S(1)} collective-permute-done((f32[8,8,384]{2,1,0:T(8,128)S(1)}, f32[8,8,384]{2,1,0:T(8,128)S(1)}, u32[]{:S(2)}, u32[]{:S(2)}) %collective-permute-start.44) | collective-permute-done | bytes 98336 | tf_op jit(solution)/shard_map/ppermute | solution.py:89
  597.8 8.3 %shard_map.248 = bf16[4,256,2048]{2,1,0:T(8,128)(2,1)} custom-call(bf16[8,256,384]{2,1,0:T(8,128)(2,1)} %get-tuple-element.44.refs_0_, bf16[8,256,384]{2,1,0:T(8,128)(2,1)} %fusion.18.refs_1_, bf16[384,2048]{1,0:T(8,128)(2,1)} %pad.37.refs_10_.refs_2_, bf16[384,2048]{1,0:T(8,128)(2,1)} %pad.36.refs_9_.refs_3_), custom_call_target="tpu_custom_call" | custom-call | flops 3221225472 | bytes 8912896 | tf_op jit(solution)/shard_map/pallas_call | solution.py:407
  610.0 7.4 convolution_bitcast_fusion
  618.8 7.3 shard_map.241
  637.7 8.5 %shard_map.247 = bf16[4,256,2048]{2,1,0:T(8,128)(2,1)} custom-call(bf16[8,256,384]{2,1,0:T(8,128)(2,1)} %get-tuple-element.44.refs_0_, bf16[8,256,384]{2,1,0:T(8,128)(2,1)} %fusion.18.refs_1_, bf16[384,2048]{1,0:T(8,128)(2,1)} %pad.37.refs_10_.refs_2_, bf16[384,2048]{1,0:T(8,128)(2,1)} %pad.36.refs_9_.refs_3_), custom_call_target="tpu_custom_call" | custom-call | flops 3221225472 | bytes 8912896 | tf_op jit(solution)/shard_map/pallas_call | solution.py:407
  654.1 8.4 %convolution_bitcast_fusion.1 = bf16[384,2048]{1,0:T(8,128)(2,1)S(1)} fusion(bf16[8,256,384]{2,1,0:T(8,128)(2,1)S(1)} %copy-done.42, bf16[8,256,2048]{2,1,0:T(8,128)(2,1)} %get-tuple-element.55), kind=kOutput, calls=%fused_computation.24 | convolution fusion | flops 3221225472 | bytes 11534336 | tf_op jit(solution)/shard_map/dot_general | solution.py:31
  682.8 7.1 collective-permute-done.46
  716.2 37.5 %all-reduce.9 = f32[32,128]{1,0:T(8,128)S(1)} all-reduce(f32[32,128]{1,0:T(8,128)S(1)} %pad_maximum_fusion.2), channel_id=8, replica_groups=mesh['dp'=8,'seq'=4] {'dp','seq'}, use_global_device_ids=true, to_apply=%region_9.10.clone | all-reduce | flops 4096 | bytes 32768
  (359 shorter events, 240.8 us)
Async XLA Ops:
  7.3 113.7 %all-gather.17.cloned.1.call-start = ((), (), s32[]{:S(2)}) async-start(), calls=%async_computation.15 | async-start | bytes 1638400 | tf_op jit(solution)/shard_map/all_gather | solution.py:481
  10.3 113.5 %all-gather.11.cloned.1.call-start = ((), (), s32[]{:S(2)}) async-start(), calls=%async_computation.6 | async-start | bytes 1945600 | tf_op jit(solution)/shard_map/all_gather | solution.py:481
  12.0 147.5 %all-gather.13.cloned.1.call-start = ((), (), s32[]{:S(2)}) async-start(), calls=%async_computation.7 | async-start | bytes 1638400 | tf_op jit(solution)/shard_map/all_gather | solution.py:481
  17.8 285.3 %all-gather.19.cloned.1.call-start = ((), (), s32[]{:S(2)}) async-start(), calls=%async_computation.16 | async-start | bytes 3932160 | tf_op jit(solution)/shard_map/all_gather | solution.py:481
  20.0 27.7 %collective-permute-start.1 = (bf16[272,2048]{1,0:T(8,128)(2,1)}, bf16[272,2048]{1,0:T(8,128)(2,1)}, u32[]{:S(2)}, u32[]{:S(2)}) collective-permute-start(bf16[272,2048]{1,0:T(8,128)(2,1)} %pad_maximum_fusion.1.refs_0_), channel_id=1, source_target_pairs={{0,8},{4,20},{8,0},{12,28},{16,24},{20,4},{24,16},{28,12},{1,9},{5... | collective-permute-start | bytes 3342344 | tf_op jit(solution)/shard_map/ppermute | solution.py:70
  21.5 98.3 %collective-permute-start.2 = (bf16[272,2048]{1,0:T(8,128)(2,1)}, bf16[272,2048]{1,0:T(8,128)(2,1)}, u32[]{:S(2)}, u32[]{:S(2)}) collective-permute-start(bf16[272,2048]{1,0:T(8,128)(2,1)} %pad_maximum_fusion.1.refs_0_), channel_id=1, source_target_pairs={{0,16},{4,12},{8,24},{12,4},{16,0},{20,28},{24,8},{28,20},{1,17},{... | collective-permute-start | bytes 3342344 | tf_op jit(solution)/shard_map/ppermute | solution.py:70
  47.7 72.1 %collective-permute-start.3 = (bf16[272,2048]{1,0:T(8,128)(2,1)}, bf16[272,2048]{1,0:T(8,128)(2,1)}, u32[]{:S(2)}, u32[]{:S(2)}) collective-permute-start(bf16[272,2048]{1,0:T(8,128)(2,1)} %collective-permute-done.1.refs_1_), channel_id=1, source_target_pairs={{0,16},{4,12},{8,24},{12,4},{16,0},{20,28},{24,8},{28,20},{1,17},{... | collective-permute-start | bytes 3342344 | tf_op jit(solution)/shard_map/ppermute | solution.py:70
  52.6 250.5 %all-gather.21.cloned.1.call-start = ((), (), s32[]{:S(2)}) async-start(), calls=%async_computation.17 | async-start | bytes 3932160 | tf_op jit(solution)/shard_map/all_gather | solution.py:481
  178.4 138.7 %all-gather.15.cloned.1.call-start = ((), (), s32[]{:S(2)}) async-start(), calls=%async_computation.8 | async-start | bytes 3932160 | tf_op jit(solution)/shard_map/all_gather | solution.py:481
  191.7 26.1 %collective-permute-start.12 = (bf16[2,256,2048]{2,1,0:T(8,128)(2,1)S(1)}, bf16[2,256,2048]{2,1,0:T(8,128)(2,1)S(1)}, u32[]{:S(2)}, u32[]{:S(2)}) collective-permute-start(bf16[2,256,2048]{2,1,0:T(8,128)(2,1)S(1)} %slice.330), channel_id=1, source_target_pairs={{0,16},{4,12},{8,24},{12,4},{16,0},{20,28},{24,8},{28,20},{1,17},{... | collective-permute-start | bytes 6291464 | tf_op jit(solution)/shard_map/ppermute | solution.py:82
  222.9 440.9 %reduce-scatter.13.cloned.1.call-start = ((), (), s32[]{:S(2)}) async-start(), calls=%async_computation.12 | async-start | bytes 3932160 | tf_op jit(solution)/shard_map/reduce_scatter | solution.py:485
  222.9 35.1 %collective-permute-start.21 = (bf16[256,2048]{1,0:T(8,128)(2,1)}, bf16[256,2048]{1,0:T(8,128)(2,1)}, u32[]{:S(2)}, u32[]{:S(2)}) collective-permute-start(bf16[256,2048]{1,0:T(8,128)(2,1)} %bitcast.17.refs_8_), channel_id=1, source_target_pairs={{0,8},{4,20},{8,0},{12,28},{16,24},{20,4},{24,16},{28,12},{1,9},{5... | collective-permute-start | bytes 3145736 | tf_op jit(solution)/shard_map/ppermute | solution.py:70
  224.0 35.5 %collective-permute-start.22 = (bf16[256,2048]{1,0:T(8,128)(2,1)}, bf16[256,2048]{1,0:T(8,128)(2,1)}, u32[]{:S(2)}, u32[]{:S(2)}) collective-permute-start(bf16[256,2048]{1,0:T(8,128)(2,1)} %bitcast.17.refs_8_), channel_id=1, source_target_pairs={{0,16},{4,12},{8,24},{12,4},{16,0},{20,28},{24,8},{28,20},{1,17},{... | collective-permute-start | bytes 3145736 | tf_op jit(solution)/shard_map/ppermute | solution.py:70
  225.3 34.7 %collective-permute-start.24 = (bf16[256,2048]{1,0:T(8,128)(2,1)}, bf16[256,2048]{1,0:T(8,128)(2,1)}, u32[]{:S(2)}, u32[]{:S(2)}) collective-permute-start(bf16[256,2048]{1,0:T(8,128)(2,1)} %bitcast.17.refs_8_), channel_id=1, source_target_pairs={{0,4},{4,0},{8,12},{12,8},{16,20},{20,16},{24,28},{28,24},{1,5},{5... | collective-permute-start | bytes 3145736 | tf_op jit(solution)/shard_map/ppermute | solution.py:68
  248.0 30.6 %collective-permute-start.14 = (bf16[256,2048]{1,0:T(8,128)(2,1)S(1)}, bf16[256,2048]{1,0:T(8,128)(2,1)}, u32[]{:S(2)}, u32[]{:S(2)}) collective-permute-start(bf16[256,2048]{1,0:T(8,128)(2,1)S(1)} %get-tuple-element.118.refs_0_), channel_id=1, source_target_pairs={{0,8},{4,20},{8,0},{12,28},{16,24},{20,4},{24,16},{28,12},{1,9},{5... | collective-permute-start | bytes 3145736 | tf_op jit(solution)/shard_map/ppermute | solution.py:70
  260.0 30.5 %collective-permute-start.15 = (bf16[256,2048]{1,0:T(8,128)(2,1)S(1)}, bf16[256,2048]{1,0:T(8,128)(2,1)}, u32[]{:S(2)}, u32[]{:S(2)}) collective-permute-start(bf16[256,2048]{1,0:T(8,128)(2,1)S(1)} %get-tuple-element.118.refs_0_), channel_id=1, source_target_pairs={{0,16},{4,12},{8,24},{12,4},{16,0},{20,28},{24,8},{28,20},{1,17},{... | collective-permute-start | bytes 3145736 | tf_op jit(solution)/shard_map/ppermute | solution.py:70
  280.6 36.5 %collective-permute-start.17 = (bf16[256,2048]{1,0:T(8,128)(2,1)S(1)}, bf16[256,2048]{1,0:T(8,128)(2,1)}, u32[]{:S(2)}, u32[]{:S(2)}) collective-permute-start(bf16[256,2048]{1,0:T(8,128)(2,1)S(1)} %get-tuple-element.118.refs_0_), channel_id=1, source_target_pairs={{0,4},{4,0},{8,12},{12,8},{16,20},{20,16},{24,28},{28,24},{1,5},{5... | collective-permute-start | bytes 3145736 | tf_op jit(solution)/shard_map/ppermute | solution.py:68
  280.7 36.4 %collective-permute-start.18 = (bf16[256,2048]{1,0:T(8,128)(2,1)}, bf16[256,2048]{1,0:T(8,128)(2,1)}, u32[]{:S(2)}, u32[]{:S(2)}) collective-permute-start(bf16[256,2048]{1,0:T(8,128)(2,1)} %collective-permute-done.14.refs_1_), channel_id=1, source_target_pairs={{0,4},{4,0},{8,12},{12,8},{16,20},{20,16},{24,28},{28,24},{1,5},{5... | collective-permute-start | bytes 3145736 | tf_op jit(solution)/shard_map/ppermute | solution.py:72
  290.5 26.6 %collective-permute-start.19 = (bf16[256,2048]{1,0:T(8,128)(2,1)}, bf16[256,2048]{1,0:T(8,128)(2,1)}, u32[]{:S(2)}, u32[]{:S(2)}) collective-permute-start(bf16[256,2048]{1,0:T(8,128)(2,1)} %collective-permute-done.15.refs_2_), channel_id=1, source_target_pairs={{0,4},{4,0},{8,12},{12,8},{16,20},{20,16},{24,28},{28,24},{1,5},{5... | collective-permute-start | bytes 3145736 | tf_op jit(solution)/shard_map/ppermute | solution.py:72
  358.7 38.5 %collective-permute-start.31 = (bf16[4,256,2048]{2,1,0:T(8,128)(2,1)}, bf16[4,256,2048]{2,1,0:T(8,128)(2,1)}, u32[]{:S(2)}, u32[]{:S(2)}) collective-permute-start(bf16[4,256,2048]{2,1,0:T(8,128)(2,1)} %shard_map.244), channel_id=1, source_target_pairs={{0,4},{4,0},{8,12},{12,8},{16,20},{20,16},{24,28},{28,24},{1,5},{5... | collective-permute-start | bytes 12582920 | tf_op jit(solution)/shard_map/ppermute | solution.py:78
  385.6 278.2 %reduce-scatter.15.cloned.1.call-start = ((), (), s32[]{:S(2)}) async-start(), calls=%async_computation.13 | async-start | bytes 3932160 | tf_op jit(solution)/shard_map/reduce_scatter | solution.py:485
  403.0 26.1 %collective-permute-start.32 = (bf16[2,256,2048]{2,1,0:T(8,128)(2,1)S(1)}, bf16[2,256,2048]{2,1,0:T(8,128)(2,1)S(1)}, u32[]{:S(2)}, u32[]{:S(2)}) collective-permute-start(bf16[2,256,2048]{2,1,0:T(8,128)(2,1)S(1)} %slice.328), channel_id=1, source_target_pairs={{0,16},{4,12},{8,24},{12,4},{16,0},{20,28},{24,8},{28,20},{1,17},{... | collective-permute-start | bytes 6291464 | tf_op jit(solution)/shard_map/ppermute | solution.py:82
  442.9 234.7 %reduce-scatter.11.cloned.1.call-start = ((), (), s32[]{:S(2)}) async-start(), calls=%async_computation.11 | async-start | bytes 1638400 | tf_op jit(solution)/shard_map/reduce_scatter | solution.py:485
  453.9 27.8 %collective-permute-start.35 = (bf16[256,2048]{1,0:T(8,128)(2,1)S(1)}, bf16[256,2048]{1,0:T(8,128)(2,1)S(1)}, u32[]{:S(2)}, u32[]{:S(2)}) collective-permute-start(bf16[256,2048]{1,0:T(8,128)(2,1)S(1)} %get-tuple-element.120.refs_0_), channel_id=1, source_target_pairs={{0,16},{4,12},{8,24},{12,4},{16,0},{20,28},{24,8},{28,20},{1,17},{... | collective-permute-start | bytes 3145736 | tf_op jit(solution)/shard_map/ppermute | solution.py:70
  525.5 153.9 %reduce-scatter.17.cloned.1.call-start = ((), (), s32[]{:S(2)}) async-start(), calls=%async_computation.14 | async-start | bytes 3932160 | tf_op jit(solution)/shard_map/reduce_scatter | solution.py:485
  544.2 137.7 %reduce-scatter.9.cloned.1.call-start = ((), (), s32[]{:S(2)}) async-start(), calls=%async_computation.10 | async-start | bytes 1945600 | tf_op jit(solution)/shard_map/reduce_scatter | solution.py:485
  551.6 74.5 %collective-permute-start.28 = (bf16[4,256,2048]{2,1,0:T(8,128)(2,1)}, bf16[4,256,2048]{2,1,0:T(8,128)(2,1)}, u32[]{:S(2)}, u32[]{:S(2)}) collective-permute-start(bf16[4,256,2048]{2,1,0:T(8,128)(2,1)} %shard_map.242), channel_id=1, source_target_pairs={{0,4},{4,0},{8,12},{12,8},{16,20},{20,16},{24,28},{28,24},{1,5},{5... | collective-permute-start | bytes 12582920 | tf_op jit(solution)/shard_map/ppermute | solution.py:78
  606.1 40.0 %collective-permute-start.45 = (bf16[4,256,2048]{2,1,0:T(8,128)(2,1)}, bf16[4,256,2048]{2,1,0:T(8,128)(2,1)}, u32[]{:S(2)}, u32[]{:S(2)}) collective-permute-start(bf16[4,256,2048]{2,1,0:T(8,128)(2,1)} %shard_map.248), channel_id=1, source_target_pairs={{0,4},{4,0},{8,12},{12,8},{16,20},{20,16},{24,28},{28,24},{1,5},{5... | collective-permute-start | bytes 12582920 | tf_op jit(solution)/shard_map/ppermute | solution.py:78
  618.7 82.7 %reduce-scatter.7.cloned.1.call-start = ((), (), s32[]{:S(2)}) async-start(), calls=%async_computation.9 | async-start | bytes 1638400 | tf_op jit(solution)/shard_map/reduce_scatter | solution.py:485
  636.6 32.9 %collective-permute-start.29 = (bf16[2,256,2048]{2,1,0:T(8,128)(2,1)}, bf16[2,256,2048]{2,1,0:T(8,128)(2,1)}, u32[]{:S(2)}, u32[]{:S(2)}) collective-permute-start(bf16[2,256,2048]{2,1,0:T(8,128)(2,1)} %slice.329), channel_id=1, source_target_pairs={{0,16},{4,12},{8,24},{12,4},{16,0},{20,28},{24,8},{28,20},{1,17},{... | collective-permute-start | bytes 6291464 | tf_op jit(solution)/shard_map/ppermute | solution.py:82
  653.2 36.7 %collective-permute-start.46 = (bf16[2,256,2048]{2,1,0:T(8,128)(2,1)}, bf16[2,256,2048]{2,1,0:T(8,128)(2,1)S(1)}, u32[]{:S(2)}, u32[]{:S(2)}) collective-permute-start(bf16[2,256,2048]{2,1,0:T(8,128)(2,1)} %slice.327), channel_id=1, source_target_pairs={{0,16},{4,12},{8,24},{12,4},{16,0},{20,28},{24,8},{28,20},{1,17},{... | collective-permute-start | bytes 6291464 | tf_op jit(solution)/shard_map/ppermute | solution.py:82
  676.1 78.2 %collective-permute-start.30 = (bf16[1,256,2048]{2,1,0:T(8,128)(2,1)}, bf16[1,256,2048]{2,1,0:T(8,128)(2,1)}, u32[]{:S(2)}, u32[]{:S(2)}) collective-permute-start(bf16[1,256,2048]{2,1,0:T(8,128)(2,1)} %slice.336), channel_id=1, source_target_pairs={{0,8},{4,20},{8,0},{12,28},{16,24},{20,4},{24,16},{28,12},{1,9},{5... | collective-permute-start | bytes 3145736 | tf_op jit(solution)/shard_map/ppermute | solution.py:82
  (82 other events, 852.0 us)
Sparse Core Ops, SparseCore 0:
  10.4 35.3 all-gather.16
  48.0 35.9 all-gather.10
  86.1 31.6 all-gather.12
  119.2 64.9 all-gather.18
  185.6 67.8 all-gather.20
  254.9 62.1 all-gather.14
  385.7 59.0 reduce-scatter.12
  447.1 60.2 reduce-scatter.14
  525.7 28.9 reduce-scatter.10
  556.8 62.1 reduce-scatter.16
  621.3 34.1 reduce-scatter.8
  663.9 29.8 reduce-scatter.6

commit v2 on v1

v2 whole, which is shorter than its diff:
```python
import functools

import jax
import jax.numpy as jnp
from jax import lax
from jax.experimental import pallas as pl
from jax.experimental.pallas import tpu as pltpu
from jax.sharding import PartitionSpec as P

EPS = 1e-06
FLOOR = 0.0001
SHARP = 8.0
HALO = 16
F32 = jnp.float32
BF16 = jnp.bfloat16
VMEM_LIMIT = 56 * 1024 * 1024
ANY = pl.BlockSpec(memory_space=pl.ANY)
ROOT = 0.7978845608028654
CUBE = 0.044715


def dot_nt(left, right):
    return lax.dot_general(left, right, (((1,), (1,)), ((), ())), preferred_element_type=F32)


def dot_nn(left, right):
    return lax.dot_general(left, right, (((1,), (0,)), ((), ())), preferred_element_type=F32)


def dot_tn(left, right):
    return lax.dot_general(left, right, (((0,), (0,)), ((), ())), preferred_element_type=F32)


def rms_norm(values, gain_vec):
    return values * lax.rsqrt(jnp.mean(values * values, axis=-1, keepdims=True) + EPS) * gain_vec


def gelu_parts(values):
    squared = values * values
    bend = jnp.tanh(ROOT * (values + CUBE * values * squared))
    half = 0.5 * (1.0 + bend)
    slope = half + 0.5 * values * (1.0 - bend * bend) * (ROOT * (1.0 + 3.0 * CUBE * squared))
    return values * half, slope


def gelu_value(values):
    bend = jnp.tanh(ROOT * (values + CUBE * values * values * values))
    return values * (0.5 * (1.0 + bend))


def plane_stages(count):
    bits = count.bit_length() - 1
    upper = list(range(1, bits))
    stages = []
    for place in range(len(upper)):
        pairs = []
        for source in range(count):
            shift = place if source % 2 == 0 else (place + 1) % len(upper)
            pairs.append((source, source ^ (1 << upper[shift])))
        stages.append(pairs)
    twin = [(source, source ^ 1) for source in range(count)]
    return stages, twin


def gather_rows(piece, fills=(), filled=None):
    stages, twin = plane_stages(lax.axis_size("dp"))
    held = [piece] + [None] * (2 ** len(stages) - 1)
    for wave in range(1, len(stages) + 1):
        members = [m for m in range(len(held)) if bin(m).count("1") == wave]
        tops = [m.bit_length() - 1 for m in members]
        sent = [held[m ^ (1 << top)] for m, top in zip(members, tops)]
        arrived = [lax.ppermute(part, "dp", stages[top]) for part, top in zip(sent, tops)]
        if wave <= len(fills):
            arrived, made = lax.optimization_barrier((arrived, fills[wave - 1](sent)))
            if filled is not None:
                filled.append(made)
        for m, part in zip(members, arrived):
            held[m] = part
    return held + [lax.ppermute(part, "dp", twin) for part in held]


def after(value, *others):
    return lax.optimization_barrier((value, others))[0]


def total_of(terms):
    return sum(term.astype(F32) for term in terms)


def scatter_tail(terms, stages, waits):
    for place, pairs in enumerate(reversed(stages)):
        split = len(terms) // 2
        sent = [total_of(those).astype(BF16) for those in terms[split:]]
        got = [lax.ppermute(part, "dp", pairs) for part in sent]
        if place < len(waits):
            got = waits[place](sent, got)
        terms = [[*those, one] for those, one in zip(terms, got)]
    return total_of(terms[0])


def scatter_rows(make, count, wait):
    stages, twin = plane_stages(lax.axis_size("dp"))
    quarter = count // 4
    theirs = make([3], quarter, ())[0]
    there = lax.ppermute(theirs, "dp", twin)
    far = make([1], quarter, (theirs,))[0]
    sent = [total_of([far[k], there[k]]).astype(BF16) for k in range(quarter)]
    got = [lax.ppermute(part, "dp", stages[-1]) for part in sent]
    split = quarter // 2
    theirs, near = make([2, 0], quarter, (sent,))
    theirs, near, got[split:] = lax.optimization_barrier((theirs, near, got[split:]))
    there = lax.ppermute(theirs, "dp", twin)
    terms = [[near[k], there[k], got[k]] for k in range(quarter)]
    return scatter_tail(terms, stages[:-1], [wait] if wait else [])


def beside(work):
    def wait(sent, got):
        return after(got, work(sent))

    return wait


def piece_order(count):
    stages, twin = plane_stages(count)
    orders = []
    for device in range(count):
        held, other = [device], [twin[device][1]]
        for pairs in stages:
            held = held + [pairs[place][1] for place in held]
            other = other + [pairs[place][1] for place in other]
        orders.append(held + other)
    return orders


def hand_on(value, steps):
    count = lax.axis_size("seq")
    first, last = (max(0, -steps), min(count, count - steps))
    return lax.ppermute(value, "seq", [(source, source + steps) for source in range(first, last)])


def scan_into(keep, entry, cum_ref, state_ref, backward):
    rows, width = keep.shape
    groups = rows // 8
    mult = keep.reshape(groups, 8, width)
    total = entry.reshape(groups, 8, width)
    place = lax.broadcasted_iota(jnp.int32, (groups, 8, width), 1)
    for hop in (1, 2, 4):
        if backward:
            shift, valid = 8 - hop, place < 8 - hop
        else:
            shift, valid = hop, place >= hop
        near_mult = pltpu.roll(mult, shift, 1)
        near_total = pltpu.roll(total, shift, 1)
        total = jnp.where(valid, total + mult * near_total, total)
        mult = jnp.where(valid, mult * near_mult, mult)
    carry_total = jnp.zeros((1, width), F32)
    carry_mult = jnp.ones((1, width), F32)
    edge = 0 if backward else 7
    order = range(groups - 1, -1, -1) if backward else range(groups)
    for group in order:
        now_total = total[group] + mult[group] * carry_total
        now_mult = mult[group] * carry_mult
        state_ref[0, group * 8 : group * 8 + 8, :] = now_total
        cum_ref[0, group * 8 : group * 8 + 8, :] = now_mult
        carry_total = now_total[edge : edge + 1]
        carry_mult = now_mult[edge : edge + 1]
    return carry_mult, carry_total


def folded(refs):
    carry = refs[-1][0, 1:2, :]
    for ref in refs[-2::-1]:
        carry = ref[0, 1:2, :] + ref[0, 0:1, :] * carry
    return carry


def ends_block(mult, total):
    width = mult.shape[1]
    return jnp.concatenate([mult, total, jnp.zeros((6, width), F32)], 0)


def fetch_all(refs, buf, sems):
    for index, ref in enumerate(refs):
        pltpu.make_async_copy(ref, buf.at[index], sems.at[index]).start()


def fetched(refs, buf, sems, index):
    pltpu.make_async_copy(refs[0], buf.at[index], sems.at[index]).wait()


def put(buf, whole, sems, index):
    return pltpu.make_async_copy(buf.at[index], whole.at[index], sems.at[index])


def padded_rows(rows, width):
    missing = width - rows.shape[0]
    return jnp.concatenate([rows, jnp.zeros((missing, rows.shape[1]), rows.dtype)], 0) if missing else rows


def first_norm_kernel(count, *refs):
    x_refs, top_refs = refs[:count], refs[count : 2 * count]
    gain, all_out, h_out, m_out, buf, top, sems, top_sems = refs[2 * count :]
    step = pl.program_id(0)

    @pl.when(step == 0)
    def _():
        fetch_all(top_refs, top, top_sems)
        fetch_all(x_refs, buf, sems)

    fetched(top_refs, top, top_sems, step)
    fetched(x_refs, buf, sems, step)
    rows, width = m_out.shape[1:]
    top_val = top[step].astype(F32)
    info = jnp.broadcast_to(top_val[0:1, :rows], (width, rows)).astype(BF16)
    across = lax.broadcasted_iota(jnp.int32, (rows, rows), 0)
    down = lax.broadcasted_iota(jnp.int32, (rows, rows), 1)
    m_out[0] = dot_nt(jnp.where(across == down, 1.0, 0.0).astype(BF16), info).astype(BF16)
    all_out[0, :HALO] = rms_norm(top_val, gain[...]).astype(BF16)
    h_low = rms_norm(buf[step].astype(F32), gain[...]).astype(BF16)
    all_out[0, HALO:] = h_low
    h_out[0] = h_low


def first_norm(pieces, tops, gain, width):
    count = len(pieces)
    rows, model = pieces[0].shape
    shapes = [
        jax.ShapeDtypeStruct((count, rows + HALO, model), BF16),
        jax.ShapeDtypeStruct((count, rows, model), BF16),
        jax.ShapeDtypeStruct((count, rows, width), BF16),
    ]
    return call(
        functools.partial(first_norm_kernel, count),
        (count,),
        [ANY] * (2 * count) + [resident(gain.shape)],
        [per_piece(s.shape[1:]) for s in shapes],
        shapes,
        [
            pltpu.VMEM((count, rows, model), BF16),
            pltpu.VMEM((count, HALO, model), BF16),
            pltpu.SemaphoreType.DMA((count,)),
            pltpu.SemaphoreType.DMA((count,)),
        ],
        count * rows * model * 8,
        count * rows * model * 6,
    )(*pieces, *tops, gain)


def mixer_enter_kernel(
    h_ref, m_ref, wu, wy, wz, par, u_out, y_out, conv_out, r_out, e_out, k_out, a_out, s_out, ends, wu_all, wy_all
):
    width = wz.shape[1]

    @pl.when(pl.program_id(0) == 0)
    def _():
        wu_all[...] = padded_rows(wu[...], width)
        wy_all[...] = padded_rows(wy[...], width)

    h_low = h_ref[0]
    rows = h_low.shape[0] - HALO
    u_low = dot_nt(h_low, wu_all[...]).astype(BF16)
    u_out[0] = u_low
    y_out[0] = dot_nt(h_low[HALO:], wy_all[...])
    same = m_ref[0].astype(F32)
    u_val = u_low.astype(F32)
    conv = par[4:5, :] + par[0:1, :] * u_val[HALO:]
    for back in (1, 2, 3):
        term = par[back : back + 1, :] * u_val[HALO - back : HALO - back + rows]
        conv = conv + jnp.where(same >= back, term, 0.0)
    conv_low = conv.astype(BF16)
    conv_out[0] = conv_low
    conv = conv_low.astype(F32)
    pre = dot_nt(conv_low, wz[...])
    recur = jax.nn.sigmoid(pre[:, :width] + par[5:6, :])
    enter = jax.nn.sigmoid(pre[:, width:] + par[6:7, :])
    keep = jnp.where(same >= 1.0, jnp.exp(par[7:8, :] * recur), 0.0)
    r_out[0] = recur
    e_out[0] = enter
    k_out[0] = keep
    inputs = conv * enter * jnp.sqrt(jnp.maximum(1.0 - keep * keep, FLOOR))
    mult, total = scan_into(keep, inputs, a_out, s_out, False)
    ends[0] = ends_block(mult, total)


def resident(shape):
    zeros = (0,) * len(shape)
    return pl.BlockSpec(shape, lambda step: zeros)


def per_piece(shape, first=0):
    rest = (0,) * len(shape)
    return pl.BlockSpec((1,) + shape, lambda step: (step + first,) + rest)


def call(kernel, grid, in_specs, out_specs, out_shape, scratch, flops, moved):
    return pl.pallas_call(
        kernel,
        grid=grid,
        in_specs=in_specs,
        out_specs=out_specs,
        out_shape=out_shape,
        scratch_shapes=scratch,
        compiler_params=pltpu.CompilerParams(
            vmem_limit_bytes=VMEM_LIMIT, dimension_semantics=("arbitrary",) * len(grid)
        ),
        cost_estimate=pl.CostEstimate(flops=int(flops), bytes_accessed=int(moved), transcendentals=0),
    )


def mixer_enter(h_all, same, w_in, wz, par):
    count, tall, model = h_all.shape
    rows = tall - HALO
    chan = w_in.shape[0]
    width = wz.shape[1]

    def out(height, columns, dtype):
        return jax.ShapeDtypeStruct((count, height, columns), dtype)

    shapes = [out(tall, width, BF16), out(rows, width, F32), out(rows, width, BF16)]
    shapes += [out(rows, width, F32)] * 5 + [out(8, width, F32)]
    return call(
        mixer_enter_kernel,
        (count,),
        [
            per_piece((tall, model)),
            per_piece((rows, width)),
            pl.BlockSpec((chan, model), lambda step: (0, 0)),
            pl.BlockSpec((chan, model), lambda step: (0, 1)),
            resident(wz.shape),
            resident(par.shape),
        ],
        [per_piece(s.shape[1:]) for s in shapes],
        shapes,
        [pltpu.VMEM((width, model), BF16), pltpu.VMEM((width, model), BF16)],
        2 * count * rows * model * width * 2,
        count * rows * (model * 2 + width * 32),
    )(h_all, same, w_in, w_in, wz, par)


def column_tile(model):
    return next(t for t in (512, 256, 128) if model % t == 0)


def group_of(shape, blocks, pieces):
    first, stride = blocks[0], (blocks[-1] - blocks[0]) // max(1, len(blocks) - 1)
    rest = (0,) * len(shape)
    return pl.BlockSpec((pieces,) + shape, lambda group, step: (first + stride * group,) + rest)


def group_outs(rows, tile, steps, blocks, pieces):
    def spec(place):
        def index(group, step):
            at = jnp.clip((group - place) * steps + step, 0, steps - 1)
            return (0, 0, at)

        return pl.BlockSpec((pieces, rows, tile), index)

    return [spec(place) for place in range(len(blocks))]


def put_group(outs, total):
    for place, out in enumerate(outs):

        @pl.when(pl.program_id(0) == place)
        def _(out=out):
            out[...] = total.reshape(out.shape)


def fold_piece(refs, index):
    carry = refs[-1][index, 1:2, :]
    for ref in refs[-2::-1]:
        carry = ref[index, 1:2, :] + ref[index, 0:1, :] * carry
    return carry


def mixer_leave_kernel(hops, pieces, groups, *refs):
    ends = refs[:hops]
    cum, local, y_pre, w_out = refs[hops : hops + 4]
    mixed = refs[-1]
    rows = cum.shape[1]

    @pl.when(pl.program_id(1) == 0)
    def _():
        for index in range(pieces):
            states = local[index] + cum[index] * fold_piece(ends, index)
            mixed[index * rows : index * rows + rows, :] = (gelu_value(y_pre[index]) * states).astype(BF16)

    right = padded_rows(w_out[...], mixed.shape[1])
    put_group(refs[hops + 4 : hops + 4 + groups], dot_nn(mixed[...], right).astype(BF16))


def mixer_leave(ends, cum, local, y_pre, w_out, blocks, pieces):
    rows, width = cum.shape[1:]
    model = w_out.shape[1]
    tile = column_tile(model)
    steps = model // tile
    groups = len(blocks)
    return call(
        functools.partial(mixer_leave_kernel, len(ends), pieces, groups),
        (groups, steps),
        [group_of((8, width), blocks, pieces)] * len(ends)
        + [group_of((rows, width), blocks, pieces)] * 3
        + [pl.BlockSpec((w_out.shape[0], tile), lambda group, step: (0, step))],
        group_outs(rows, tile, steps, blocks, pieces),
        [jax.ShapeDtypeStruct((pieces, rows, model), BF16)] * groups,
        [pltpu.VMEM((pieces * rows, width), BF16)],
        2 * groups * pieces * rows * width * model,
        groups * pieces * rows * (width * 12 + model * 2),
    )(*ends, cum, local, y_pre, w_out)


def head_back_kernel(count, hops, *refs):
    d_refs = refs[:count]
    ends = refs[count : count + hops]
    (cum, local, y_pre, keep_ref, w_out, dy_out, mixed_out, cb_out, lb_out, ends_out, all_out, buf, w_all, sems, all_sems) = refs[count + hops :]
    step = pl.program_id(0)

    @pl.when(step == 0)
    def _():
        fetch_all(d_refs, buf, sems)
        w_all[...] = padded_rows(w_out[...], w_all.shape[0])

    fetched(d_refs, buf, sems, step)
    put(buf, all_out, all_sems, step).start()
    d_mixed = dot_nt(buf[step], w_all[...])
    states = local[0] + cum[0] * folded(ends)
    value, slope = gelu_parts(y_pre[0])
    mixed_out[0] = (value * states).astype(BF16)
    dy_out[0] = (slope * d_mixed * states).astype(BF16)
    keep = keep_ref[0]
    width = keep.shape[1]
    next_keep = jnp.concatenate([keep[1:], jnp.ones((1, width), F32)], 0)
    mult, total = scan_into(next_keep, d_mixed * value, cb_out, lb_out, True)
    ends_out[0] = ends_block(mult * keep[0:1], total * keep[0:1])

    @pl.when(step == count - 1)
    def _():
        for index in range(count):
            put(buf, all_out, all_sems, index).wait()


def head_back(pieces, ends, cum, local, y_pre, keep, w_out):
    count = len(pieces)
    rows, model = pieces[0].shape
    width = cum.shape[2]

    def out(height, dtype):
        return jax.ShapeDtypeStruct((count, height, width), dtype)

    shapes = [out(rows, BF16), out(rows, BF16), out(rows, F32), out(rows, F32), out(8, F32)]
    return call(
        functools.partial(head_back_kernel, count, len(ends)),
        (count,),
        [ANY] * count
        + [per_piece((8, width))] * len(ends)
        + [per_piece((rows, width))] * 4
        + [resident(w_out.shape)],
        [per_piece(s.shape[1:]) for s in shapes] + [ANY],
        shapes + [jax.ShapeDtypeStruct((count, rows, model), BF16)],
        [
            pltpu.VMEM((count, rows, model), BF16),
            pltpu.VMEM((width, model), BF16),
            pltpu.SemaphoreType.DMA((count,)),
            pltpu.SemaphoreType.DMA((count,)),
        ],
        2 * count * rows * width * model,
        count * rows * (width * 28 + model * 2),
    )(*pieces, *ends, cum, local, y_pre, keep, w_out)


def tail_back_kernel(hops, *refs):
    ends = refs[:hops]
    later = refs[hops : 2 * hops]
    (cb, lb, cum, local, r_ref, e_ref, k_ref, conv_ref, u_ref, m_ref, wz, par, du_out, edge_out, fold_out, small_out, gw_out) = refs[2 * hops :]
    step = pl.program_id(0)

    @pl.when(step == 0)
    def _():
        gw_out[...] = jnp.zeros_like(gw_out)
        small_out[...] = jnp.zeros_like(small_out)

    state_in = folded(ends)
    d_states = lb[0] + cb[0] * folded(later)
    states = local[0] + cum[0] * state_in
    prev = jnp.concatenate([state_in, states[:-1]], 0)
    recur, enter, keep = r_ref[0], e_ref[0], k_ref[0]
    conv_low = conv_ref[0]
    conv = conv_low.astype(F32)
    rows, width = conv.shape
    spare = 1.0 - keep * keep
    scaling = jnp.sqrt(jnp.maximum(spare, FLOOR))
    weight = jnp.where(spare > FLOOR, 0.5, jnp.where(spare == FLOOR, 0.25, 0.0)) / scaling
    d_enter_sum = d_states * conv
    d_spare = d_enter_sum * enter * weight
    d_expo = (d_states * prev - 2.0 * keep * d_spare) * keep
    d_recur = d_expo * par[7:8, :] * recur * (1.0 - recur)
    d_enter = d_enter_sum * scaling * enter * (1.0 - enter)
    d_pre = jnp.concatenate([d_recur.astype(BF16), d_enter.astype(BF16)], 1)
    d_conv = d_states * enter * scaling + dot_nn(d_pre, wz[...])
    gw_out[...] += dot_tn(d_pre, conv_low)
    d_pre_val = d_pre.astype(F32)
    same = m_ref[0].astype(F32)
    u_val = u_ref[0].astype(F32)
    sums = []
    d_u = jnp.zeros((rows, width), F32)
    head = jnp.zeros((8, width), F32)
    for back in range(4):
        masked = d_conv if back == 0 else jnp.where(same >= back, d_conv, 0.0)
        sums.append(jnp.sum(masked * u_val[HALO - back : HALO - back + rows], axis=0, keepdims=True))
        moved = masked * par[back : back + 1, :]
        if back == 0:
            d_u = d_u + moved
        else:
            nothing = jnp.zeros((back, width), F32)
            d_u = d_u + jnp.concatenate([moved[back:], nothing], 0)
            head = head + jnp.concatenate([jnp.zeros((8 - back, width), F32), moved[:back]], 0)
    sums.append(jnp.sum(d_conv, axis=0, keepdims=True))
    sums.append(jnp.sum(d_pre_val[:, :width], axis=0, keepdims=True))
    sums.append(jnp.sum(d_pre_val[:, width:], axis=0, keepdims=True))
    sums.append(jnp.sum(d_expo * recur, axis=0, keepdims=True))
    small_out[...] += jnp.concatenate(sums, 0)
    du_out[0] = d_u.astype(BF16)
    edge_out[0, 0:8, :] = head
    edge_out[0, 8:16, :] = d_u[rows - 8 :]

    @pl.when(step == pl.num_programs(0) - 1)
    def _():
        block = fold_out.shape[1]
        row = lax.broadcasted_iota(jnp.int32, (width, width), 0)
        column = lax.broadcasted_iota(jnp.int32, (width, width), 1)
        inside = None
        for start in range(0, width, block):
            here = (row >= start) & (row < start + block) & (column >= start) & (column < start + block)
            inside = here if inside is None else inside | here
        row = lax.broadcasted_iota(jnp.int32, (width, block), 0)
        column = lax.broadcasted_iota(jnp.int32, (width, block), 1)
        fold = None
        for start in range(0, width, block):
            here = row - start == column
            fold = here if fold is None else fold | here
        fold = jnp.where(fold, 1.0, 0.0).astype(BF16)
        for gate in (0, 1):
            whole = jnp.where(inside, gw_out[gate * width : gate * width + width, :], 0.0).astype(BF16)
            fold_out[gate * width : gate * width + width, :] = dot_nn(whole, fold).astype(BF16)


def tail_back(ends, later, cb, lb, cum, local, recur, enter, keep, conv, u_ext, same, wz, par, block):
    count, rows, width = cb.shape
    shapes = [
        jax.ShapeDtypeStruct((count, rows, width), BF16),
        jax.ShapeDtypeStruct((count, 16, width), F32),
        jax.ShapeDtypeStruct((2 * width, block), BF16),
        jax.ShapeDtypeStruct((8, width), F32),
    ]
    tall = u_ext.shape[1]
    return call(
        functools.partial(tail_back_kernel, len(ends)),
        (count,),
        [per_piece((8, width))] * (2 * len(ends))
        + [per_piece((rows, width))] * 8
        + [per_piece((tall, width)), per_piece((rows, width)), resident(wz.shape), resident(par.shape)],
        [per_piece((rows, width)), per_piece((16, width)), resident((2 * width, block)), resident((8, width))],
        shapes,
        [pltpu.VMEM(wz.shape, F32)],
        8 * count * rows * width * width,
        count * rows * width * 36,
    )(*ends, *later, cb, lb, cum, local, recur, enter, keep, conv, u_ext, same, wz, par)


def rows_times_kernel(terms, gained, *refs):
    lefts, rights = refs[:terms], refs[terms : 2 * terms]
    outs = refs[2 * terms + gained :]
    total = None
    for left, right in zip(lefts, rights):
        pieces, rows, inner = left.shape
        term = dot_nn(left[...].reshape(pieces * rows, inner), padded_rows(right[...], inner))
        total = term if total is None else total + term
    if gained:
        factor = refs[2 * terms][...].reshape(total.shape).astype(F32)
        outs[-1][0] = jnp.sum(total * factor, axis=0, keepdims=True)
        outs = outs[:-1]
    put_group(outs, total.astype(BF16))


def rows_times(lefts, rights, blocks, pieces, factor=None):
    rows = lefts[0].shape[1]
    model = rights[0][2]
    tile = column_tile(model)
    steps = model // tile
    groups = len(blocks)
    inner = sum(right.shape[0] for right, _, _ in rights)
    gained = 0 if factor is None else 1

    def right_spec(right, place):
        return pl.BlockSpec((right.shape[0], tile), lambda group, step: (0, place * steps + step))

    out_specs = group_outs(rows, tile, steps, blocks, pieces)
    shapes = [jax.ShapeDtypeStruct((pieces, rows, model), BF16)] * groups
    extra_specs = []
    if gained:
        first, stride = blocks[0], (blocks[-1] - blocks[0]) // max(1, groups - 1)
        out_specs.append(pl.BlockSpec((1, 1, tile), lambda group, step: (group, 0, step)))
        shapes.append(jax.ShapeDtypeStruct((groups, 1, model), F32))
        extra_specs.append(
            pl.BlockSpec((pieces, rows, tile), lambda group, step: (first + stride * group, 0, step))
        )
    return call(
        functools.partial(rows_times_kernel, len(lefts), gained),
        (groups, steps),
        [group_of(left.shape[1:], blocks, pieces) for left in lefts]
        + [right_spec(right, place) for right, place, _ in rights]
        + extra_specs,
        out_specs,
        shapes,
        [],
        2 * groups * pieces * rows * inner * model,
        groups * pieces * rows * 2 * (inner + model) + 2 * inner * model,
    )(*lefts, *[right for right, _, _ in rights], *([factor] if gained else []))


def assemble_kernel(count, *refs):
    parts, whole, buf, sems, all_sems = refs[:count], refs[count], *refs[count + 1 :]
    fetch_all(parts, buf, sems)
    for index in range(count):
        fetched(parts, buf, sems, index)
        put(buf, whole, all_sems, index).start()
    for index in range(count):
        put(buf, whole, all_sems, index).wait()


def assemble(pieces):
    count = len(pieces)
    shape = (count,) + pieces[0].shape
    return call(
        functools.partial(assemble_kernel, count),
        (1,),
        [ANY] * count,
        ANY,
        jax.ShapeDtypeStruct(shape, pieces[0].dtype),
        [pltpu.VMEM(shape, pieces[0].dtype), pltpu.SemaphoreType.DMA((count,)), pltpu.SemaphoreType.DMA((count,))],
        0,
        4 * count * pieces[0].size,
    )(*pieces)


def mlp_enter_kernel(count, *refs):
    h_refs = refs[:count]
    wg, wu, hid_out, turn_out, value_out, all_out, buf, sems, all_sems = refs[count:]
    step = pl.program_id(0)
    pair = 2 if count % 2 == 0 else 1
    rows, tile = hid_out.shape[1:]

    @pl.when(step == 0)
    def _():
        fetch_all(h_refs, buf, sems)

    def some_pieces(index, carry):
        @pl.when(step == 0)
        def _():
            for place in range(pair):
                fetched(h_refs, buf, sems, index * pair + place)
                put(buf, all_out, all_sems, index * pair + place).start()

        span = pl.ds(index * pair, pair)
        h_low = buf[span].reshape(pair * rows, buf.shape[2])
        gate = dot_nt(h_low, wg[...])
        up = dot_nt(h_low, wu[...])
        value, slope = gelu_parts(gate)
        shape = (pair, rows, tile)
        hid_out[span] = (value * up).astype(BF16).reshape(shape)
        turn_out[span] = (up * slope).reshape(shape)
        value_out[span] = value.reshape(shape)
        return carry

    lax.fori_loop(0, count // pair, some_pieces, 0)

    @pl.when(step == pl.num_programs(0) - 1)
    def _():
        for index in range(count):
            put(buf, all_out, all_sems, index).wait()


def hidden_tile(hidden):
    return next(t for t in (256, 128, hidden) if hidden % t == 0)


def mlp_enter(h_pieces, w_both):
    count = len(h_pieces)
    rows, model = h_pieces[0].shape
    hidden = w_both.shape[0]
    tile = hidden_tile(hidden)
    out_spec = pl.BlockSpec((count, rows, tile), lambda step: (0, 0, step))
    return call(
        functools.partial(mlp_enter_kernel, count),
        (hidden // tile,),
        [ANY] * count
        + [pl.BlockSpec((tile, model), lambda step: (step, 0)), pl.BlockSpec((tile, model), lambda step: (step, 1))],
        [out_spec] * 3 + [ANY],
        [
            jax.ShapeDtypeStruct((count, rows, hidden), BF16),
            jax.ShapeDtypeStruct((count, rows, hidden), F32),
            jax.ShapeDtypeStruct((count, rows, hidden), F32),
            jax.ShapeDtypeStruct((count, rows, model), BF16),
        ],
        [
            pltpu.VMEM((count, rows, model), BF16),
            pltpu.SemaphoreType.DMA((count,)),
            pltpu.SemaphoreType.DMA((count,)),
        ],
        4 * count * rows * model * hidden,
        count * rows * (4 * model + 10 * hidden) + 4 * model * hidden,
    )(*h_pieces, w_both, w_both)


def mlp_back_kernel(c_ref, wo, turn, value, dg_out, du_out):
    count, rows, tile = dg_out.shape
    pair = 2 if count % 2 == 0 else 1

    def some_pieces(index, carry):
        span = pl.ds(index * pair, pair)
        d_hidden = dot_nt(c_ref[span].reshape(pair * rows, c_ref.shape[2]), wo[...])
        d_hidden = d_hidden.reshape(pair, rows, tile)
        dg_out[span] = (d_hidden * turn[span]).astype(BF16)
        du_out[span] = (d_hidden * value[span]).astype(BF16)
        return carry

    lax.fori_loop(0, count // pair, some_pieces, 0)


def mlp_back(c_all, w_down, turn, value):
    count, rows, model = c_all.shape
    hidden = w_down.shape[0]
    tile = hidden_tile(hidden)
    spec = pl.BlockSpec((count, rows, tile), lambda step: (0, 0, step))
    return call(
        mlp_back_kernel,
        (hidden // tile,),
        [resident(c_all.shape), pl.BlockSpec((tile, model), lambda step: (step, 0)), spec, spec],
        [spec] * 2,
        [jax.ShapeDtypeStruct((count, rows, hidden), BF16)] * 2,
        [],
        2 * count * rows * model * hidden,
        count * rows * (2 * model + 12 * hidden) + 2 * model * hidden,
    )(c_all, w_down, turn, value)


def weight_grad(rows_left, rows_right):
    left = rows_left.reshape(-1, rows_left.shape[-1])
    right = rows_right.reshape(-1, rows_right.shape[-1])
    return dot_tn(left, right).astype(BF16)


def seq_gather(shard):
    return lax.all_gather(shard, "seq", axis=0, tiled=True)


def seq_scatter(whole):
    return lax.psum_scatter(whole, "seq", scatter_dimension=0, tiled=True)


def per_device(
    tokens,
    cotangent,
    doc_ids,
    mix_in,
    mix_out,
    gate_w,
    conv_w,
    conv_bias,
    gate_bias,
    decay_param,
    gain_one,
    gain_two,
    mlp_in,
    mlp_out,
):
    run_len, model = tokens.shape[1:]
    n_seq = lax.axis_size("seq")
    n_dev = lax.axis_size("dp") * n_seq
    own = mix_out.shape[0]
    block = gate_w.shape[2]
    chan = own * n_seq
    width = -(-chan // 128) * 128
    blocks = chan // block

    x_low = tokens.reshape(run_len, model)
    x_pieces = gather_rows(x_low)
    x_zero = x_low.astype(F32)
    cot_low = cotangent.reshape(run_len, model)
    lead = hand_on(x_low[run_len - HALO :], 1)
    part = gain_one.shape[0]
    gains = jnp.concatenate([gain_one, gain_two]).astype(BF16)[None]
    my_run = lax.axis_index("seq")
    first_token = my_run * run_len
    places = lax.broadcasted_iota(jnp.int32, (n_seq, 1), 0)
    gain_rows = jnp.where(places == my_run, gains, jnp.zeros((), BF16))
    for hop in range(1, n_seq):
        ring = [(source, (source + hop) % n_seq) for source in range(n_seq)]
        arrived = lax.ppermute(gains, "seq", ring)
        gain_rows = jnp.where(places == (my_run - hop) % n_seq, arrived, gain_rows)
    gain_rows = jnp.pad(gain_rows.reshape(1, -1), ((0, 0), (0, model - 2 * part * n_seq)))
    padded = jnp.concatenate([jnp.full((3,), -1, jnp.int32), doc_ids.reshape(-1)])
    own_docs = lax.dynamic_slice_in_dim(padded, first_token + 3, run_len)
    same = sum(
        jnp.where(lax.dynamic_slice_in_dim(padded, first_token + 3 - back, run_len) == own_docs, 1.0, 0.0)
        for back in (1, 2, 3)
    )
    info = jnp.pad(same, (0, model - run_len)).astype(BF16)[None]
    tops = gather_rows(jnp.concatenate([info, gain_rows, lead[2:]], 0))
    count = len(tops)
    half = count // 2

    small = jnp.concatenate(
        [
            gate_w.reshape(own, 2 * block),
            conv_w.T,
            conv_bias[:, None],
            gate_bias.T,
            decay_param[:, None],
        ],
        1,
    )
    extra = -(-small.shape[1] // 128) * 128
    small = jnp.pad(small, ((0, 0), (0, extra - small.shape[1])))
    w_in = seq_gather(jnp.concatenate([mix_in[:, 1, :], mix_in[:, 0, :], small], 1).astype(BF16))
    w_out = seq_gather(mix_out.astype(BF16))
    mlp_in, mlp_out = after((mlp_in, mlp_out), lead)
    both_shard = mlp_in.astype(BF16).reshape(-1, 2 * model)
    down_shard = mlp_out.astype(BF16)
    w_both = seq_gather(both_shard)
    w_down = seq_gather(down_shard)

    w_small = w_in[:, 2 * model :]
    gate_rows = w_small[:, : 2 * block].reshape(blocks, block, 2, block)
    eye = jnp.eye(blocks, dtype=BF16)
    w_z = jnp.einsum("bogj,bc->gbocj", gate_rows, eye).reshape(2, chan, chan)
    w_z = jnp.pad(w_z, ((0, 0), (0, width - chan), (0, width - chan))).reshape(2 * width, width)
    par = w_small[:, 2 * block : 2 * block + 8].astype(F32).T
    decay_rate = -SHARP * jax.nn.softplus(par[7])
    decay_slope = -SHARP * jax.nn.sigmoid(par[7])
    par = jnp.pad(jnp.concatenate([par[:7], decay_rate[None]], 0), ((0, 0), (0, width - chan)))

    orders = jnp.asarray(piece_order(count), jnp.int32)
    order = lax.dynamic_index_in_dim(after(orders, lead), lax.axis_index("dp"), 0, False)
    places = lax.broadcasted_iota(jnp.int32, (count, 1), 0)
    gain_rows = jnp.zeros((count, 2 * part * n_seq), F32)
    for index, piece in enumerate(tops):
        row = piece[1:2, : 2 * part * n_seq].astype(F32)
        gain_rows = jnp.where(places == order[index], row, gain_rows)
    gain_rows = gain_rows.reshape(n_dev, 2 * part)
    g_one = gain_rows[:, :part].reshape(1, model)
    g_two = gain_rows[:, part:].reshape(1, model)

    h_all, h_one, same = first_norm(x_pieces, tops, g_one, width)
    entered = mixer_enter(after(h_all, both_shard, down_shard), same, w_in, w_z, par)
    (u_ext, y_pre, conv, recur, enter, keep, cum, local, ends) = entered
    c_pieces = gather_rows(after(cot_low, *x_pieces), [lambda sent: ends])
    ends = after(ends, w_out)
    earlier = [hand_on(ends, steps) for steps in range(1, n_seq)]
    earlier, c_pieces = lax.optimization_barrier((earlier, c_pieces[:half])), c_pieces
    earlier, c_pieces[:half] = earlier

    def leaving(blocks_at, pieces, before):
        return mixer_leave(earlier, cum, local, after(y_pre, *before), w_out, blocks_at, pieces)

    kept = []
    x_one = x_zero + scatter_rows(leaving, count, None)
    n_two, norm_two_back = jax.vjp(rms_norm, x_one, g_two)
    h_two = n_two.astype(BF16)

    h_pieces = gather_rows(h_two, [lambda sent: assemble(after(c_pieces, *sent))], kept)
    c_all = kept.pop()
    hidden, turn, value, h_all = mlp_enter(h_pieces, w_both)
    grad_down = weight_grad(hidden, c_all)
    turn = after(turn, grad_down)
    grad_down = seq_scatter(grad_down)
    d_gate, d_up = mlp_back(c_all, w_down, turn, value)

    def d_entering(blocks_at, pieces, before):
        d_one = after(d_gate, *before)
        return rows_times([d_one, d_up], [(w_both, 0, model), (w_both, 1, model)], blocks_at, pieces)

    def gate_grad(sent):
        kept.append(weight_grad(after(d_gate, sent), h_all))
        return kept[-1]

    def up_grad(sent):
        kept.append(weight_grad(after(d_up, sent), h_all))
        return kept[-1]

    d_h_two = scatter_rows(d_entering, count, beside(gate_grad))
    grad_gate = seq_scatter(kept[-1])
    d_x_norm, d_gain_two = norm_two_back(d_h_two)
    d_x_one = cot_low.astype(F32) + d_x_norm
    d_mix = d_x_one.astype(BF16)

    def mlp_leaving(blocks_at, pieces, before):
        return rows_times([after(hidden, *before)], [(w_down, 0, model)], blocks_at, pieces)

    stages, twin = plane_stages(lax.axis_size("dp"))

    def mlp_out_rows(sent):
        nonlocal hidden
        hidden = after(hidden, sent)
        return mlp_leaving([1, 0], half, ())

    def up_grad_and_sums(sent):
        theirs, mine = kept.pop()
        there = lax.ppermute(theirs, "dp", twin)
        far = [total_of([mine[k], there[k]]).astype(BF16) for k in range(half // 2, half)]
        kept.append((mine, there, far))
        return up_grad(sent), far

    d_pieces = gather_rows(d_mix, [mlp_out_rows, up_grad_and_sums], kept)
    kept.pop()
    grad_up = kept.pop()
    mine, there, far = kept.pop()
    d_y, mixed, cum_back, local_back, ends_back, d_all = head_back(
        after(d_pieces, far), earlier, cum, local, y_pre, keep, w_out
    )
    got = [lax.ppermute(part, "dp", stages[-1]) for part in far]
    ends_back, got = lax.optimization_barrier((ends_back, got))
    later = [hand_on(ends_back, -steps) for steps in range(1, n_seq)]
    grad_y = weight_grad(after(d_y, ends_back), h_one)[:chan]
    grad_out = weight_grad(after(mixed, ends_back), d_all)[:chan]
    grad_y_out = jnp.concatenate([grad_y, grad_out], 1)
    later, grad_y_out = lax.optimization_barrier((later, grad_y_out))
    grad_up = seq_scatter(grad_up)
    grad_y_out = seq_scatter(grad_y_out)

    def tail_work(sent, got):
        nonlocal tailed
        tailed = tail_back(
            earlier, after(later, sent), cum_back, local_back, cum, local, recur, enter, keep, conv, u_ext, same, w_z, par, block
        )
        tailed, got = lax.optimization_barrier((tailed, got))
        return got

    tailed = None
    terms = [[mine[k], there[k], got[k]] for k in range(half // 2)]
    layer_out = x_one + scatter_tail(terms, stages[:-1], [tail_work])
    layer_out = layer_out.astype(BF16).reshape(1, run_len, model)
    d_u, edges, grad_z, sums = tailed
    from_next = hand_on(edges[:, :8], -1)
    grad_z = jnp.concatenate([grad_z[:chan], grad_z[width : width + chan]], 1)
    sums = sums[:, :chan]
    sums = jnp.concatenate([sums[:7], (sums[7] * decay_slope)[None]], 0).T
    tail = jnp.concatenate([grad_z, sums.astype(BF16)], 1)
    tail = jnp.pad(tail, ((0, 0), (0, extra - tail.shape[1])))
    from_next, layer_out = lax.optimization_barrier((from_next, layer_out))
    d_u = lax.dynamic_update_slice(d_u, (edges[:, 8:] + from_next).astype(BF16), (0, run_len - 8, 0))
    gain_terms = []

    def d_leaving(blocks_at, pieces, before):
        *part_rows, gain_term = rows_times(
            [after(d_y, *before), d_u], [(w_in, 1, model), (w_in, 0, model)], blocks_at, pieces, h_one
        )
        gain_terms.append(gain_term.sum(0))
        return part_rows

    def u_grad(sent):
        kept.append(weight_grad(after(d_u, sent, grad_down, grad_gate, grad_up, grad_y_out), h_one))
        return kept[-1]

    d_h_one = scatter_rows(d_leaving, count, beside(u_grad))
    grad_u = seq_scatter(jnp.concatenate([kept[-1][:chan], tail], 1))
    _, norm_one_back = jax.vjp(lambda values: rms_norm(values, g_one), x_zero)
    input_grad = (d_x_one + norm_one_back(d_h_one)[0]).astype(BF16)
    d_gain_one = sum(gain_terms) / g_one
    d_gains = jnp.concatenate([d_gain_one.reshape(n_dev, part), d_gain_two.reshape(n_dev, part)], 1)
    grads = lax.optimization_barrier((kept[-1], grad_gate, grad_up, grad_down, grad_y_out))[1:]
    rest = (d_gains, *grads)
    input_grad, rest = lax.optimization_barrier((input_grad, rest))
    (d_gains, grad_gate, grad_up, grad_down, grad_y_out) = rest
    input_grad = input_grad.reshape(1, run_len, model)
    d_gains = lax.all_to_all(d_gains, ("dp", "seq"), 0, 0, tiled=True).sum(0)

    tail = grad_u[:, model:].astype(F32)
    grad_mix_in = jnp.stack([grad_y_out[:, :model].astype(F32), grad_u[:, :model].astype(F32)], 1)
    at = 2 * block
    return (
        layer_out,
        input_grad,
        grad_mix_in,
        grad_y_out[:, model:].astype(F32),
        tail[:, :at].reshape(own, 2, block),
        tail[:, at : at + 4].T,
        tail[:, at + 4],
        tail[:, at + 5 : at + 7].T,
        tail[:, at + 7],
        d_gains[:part],
        d_gains[part:],
        jnp.stack([grad_gate.astype(F32), grad_up.astype(F32)], 1),
        grad_down.astype(F32),
    )


def solution(mesh):
    rows = P(("dp", "seq"))
    placed = (
        P("dp", "seq", None),
        P("dp", "seq", None),
        P("dp", None),
        P(("dp", "seq"), None, None),
        P(("dp", "seq"), None),
        P(("dp", "seq"), None, None),
        P(None, ("dp", "seq")),
        rows,
        P(None, ("dp", "seq")),
        rows,
        rows,
        rows,
        P(("dp", "seq"), None, None),
        P(("dp", "seq"), None),
    )
    return jax.shard_map(
        per_device,
        mesh=mesh,
        in_specs=placed,
        out_specs=placed[:2] + placed[3:],
        check_vma=False,
    )
```

time: 778 us -> 655 us (0.84)
  blocking collectives: 104 us -> 0 us
  local copies, waits for them, and re-layouts: 88.7 us -> 34.1 us
  Pallas kernels: 158 us -> 203 us
  waiting for transfers between devices: 236 us -> 194 us
  starting transfers between devices: 49.1 us -> 66 us
  other arithmetic: 64.8 us -> 81.4 us
    ppermute x40 -> x57, waiting for transfers between devices: 192 us -> 100 us  [the longest x15 58.1 us: gather_rows(): lax.ppermute(part, 'dp', stages[top])]
    all_gather x1 -> x0, blocking collectives: 66.4 us -> none  [per_device(): gains = lax.all_gather(gains, ('dp', 'seq'), axis=0, tiled=True).astype(F32)]
    pallas_call x10 -> x15, Pallas kernels: 124 us -> 167 us  [the longest x7 65.9 us: rows_times(): call(functools.partial(rows_times_kernel, len(lefts), gained), (groups, s...]
    unnamed x131 -> x121, local copies, waits for them, and re-layouts: 55.3 us -> 17.6 us
    unnamed x1 -> x0, blocking collectives: 37.5 us -> none
    convert_element_type x4 -> x15, other arithmetic: 9.28 us -> 44.7 us  [the longest x4 14 us: scatter_tail(): sent = [total_of(those).astype(BF16) for those in terms[split:]]]
    reduce_scatter x6 -> x5, waiting for transfers between devices: 0.05 us -> 35.2 us  [seq_scatter(): return lax.psum_scatter(whole, 'seq', scatter_dimension=0, tiled=True)]
    all_gather x6 -> x4, waiting for transfers between devices: 14 us -> 45.6 us  [seq_gather(): return lax.all_gather(shard, 'seq', axis=0, tiled=True)]
  transfers between devices with their start and end apart: 60 -> 75, of which waited for: 22 -> 30; matrix products, arithmetic and copies ran while one was open for 23% -> 22% of each run, Pallas kernels for 15% -> 27%
where the time goes in v2:
time: 655 us; the launch traced here: 645 us
  Pallas kernels  203 us (31%)
  waiting for transfers between devices  194 us (30%)
  other arithmetic  81.4 us (12%)
  starting transfers between devices  66 us (10%)
  matrix products  51.2 us (8%)
  local copies, waits for them, and re-layouts  34.1 us (5%)
  between operations  15.2 us (2%)
    pallas_call x7, Pallas kernels, rows_times(): call(functools.partial(rows_times_kernel, len(lefts), gained), (groups, s...  65.9 us
    ppermute x15, waiting for transfers between devices, gather_rows(): lax.ppermute(part, 'dp', stages[top])  58.1 us
    dot_general x6, matrix products, dot_tn(): lax.dot_general(left, right, (((0,), (0,)), ((), ())), preferred_element_...  51.2 us
    all_gather x4, waiting for transfers between devices, seq_gather(): return lax.all_gather(shard, 'seq', axis=0, tiled=True)  45.6 us
    reduce_scatter x5, waiting for transfers between devices, seq_scatter(): return lax.psum_scatter(whole, 'seq', scatter_dimension=0, tiled=True)  35.2 us
    pallas_call x1, Pallas kernels, mlp_enter(): call(functools.partial(mlp_enter_kernel, count), (hidden // tile,), [ANY]...  24 us
    pallas_call x3, Pallas kernels, mixer_leave(): call(functools.partial(mixer_leave_kernel, len(ends), pieces, groups), (g...  21.8 us
    pallas_call x1, Pallas kernels, mixer_enter(): call(mixer_enter_kernel, (count,), [per_piece((tall, model)), per_piece((...  21.7 us
  transfers between devices with their start and end apart: 75, of which 30 were waited for; matrix products, arithmetic and copies ran while one was open for 22% of the time, Pallas kernels for 27%

profile of v2, /device:TPU:0, one launch (start us, length us, event | category | flops | bytes accessed | tf_op | source)
XLA Modules:
  0.0 644.9 jit_solution(14082704705971082368)
XLA Ops:
  39.7 8.5 %collective-permute-done.refs_1_ = bf16[256,2048]{1,0:T(8,128)(2,1)} collective-permute-done((bf16[256,2048]{1,0:T(8,128)(2,1)S(1)}, bf16[256,2048]{1,0:T(8,128)(2,1)}, u32[]{:S(2)}, u32[]{:S(2)}) %collective-permute-start) | collective-permute-done | bytes 1048608 | tf_op jit(solution)/shard_map/ppermute | solution.py:72
  79.2 10.9 %shard_map.246 = (bf16[8,272,2048]{2,1,0:T(8,128)(2,1)}, bf16[8,256,2048]{2,1,0:T(8,128)(2,1)}, bf16[8,256,384]{2,1,0:T(8,128)(2,1)}) custom-call(bf16[256,2048]{1,0:T(8,128)(2,1)} %bitcast.176, bf16[256,2048]{1,0:T(8,128)(2,1)} %collective-permute-done.refs_1_, bf16[256,2048]{1,0:T(8,128)(2,1)} %collective-permute-done.1.refs_2_, ...), custom_call_target="tpu_custom_call" | custom-call | flops 33554432 | bytes 25165824 | tf_op jit(solution)/shard_map/pallas_call | solution.py:233
  95.9 21.7 %shard_map.247 = (bf16[8,272,384]{2,1,0:T(8,128)(2,1)}, f32[8,256,384]{2,1,0:T(8,128)}, bf16[8,256,384]{2,1,0:T(8,128)(2,1)}, f32[8,256,384]{2,1,0:T(8,128)}, f3...) custom-call(bf16[8,272,2048]{2,1,0:T(8,128)(2,1)} %get-tuple-element, ...), custom_call_target="tpu_custom_call" | custom-call | flops 6442450944 | bytes 33554432 | tf_op jit(solution)/shard_map/pallas_call | solution.py:322
  148.5 10.4 %shard_map.250 = (bf16[2,256,2048]{2,1,0:T(8,128)(2,1)}, bf16[2,256,2048]{2,1,0:T(8,128)(2,1)}) custom-call(f32[8,8,384]{2,1,0:T(8,128)} %copy-done.11, f32[8,8,384]{2,1,0:T(8,128)} %copy-done.10, f32[8,8,384]{2,1,0:T(8,128)} %copy-done.9, f32[8,256,384]{2,1,0:T(8,128)} %get-tuple-element.158.refs_3_.refs_11_.refs_8_, ...), custom_call_target="tpu_custom_call" | custom-call | flops 1610612736 | bytes 8912896 | tf_op jit(solution)/shard_map/pallas_call | solution.py:399
  171.6 8.8 %collective-permute-done.27 = bf16[256,2048]{1,0:T(8,128)(2,1)S(1)} collective-permute-done((bf16[256,2048]{1,0:T(8,128)(2,1)S(1)}, bf16[256,2048]{1,0:T(8,128)(2,1)S(1)}, u32[]{:S(2)}, u32[]{:S(2)}) %collective-permute-start.27) | collective-permute-done | bytes 1048608 | tf_op jit(solution)/shard_map/ppermute | solution.py:108
  181.4 6.0 collective-permute-done.28
  196.0 6.5 %shard_map.251.c_ref = bf16[8,256,2048]{2,1,0:T(8,128)(2,1)} custom-call(bf16[256,2048]{1,0:T(8,128)(2,1)} %bitcast.40.refs_0_, bf16[256,2048]{1,0:T(8,128)(2,1)} %collective-permute-done.21.refs_1_, bf16[256,2048]{1,0:T(8,128)(2,1)} %collective-permute-done.22.refs_2_, bf16[256,2048]{1,0:T(8,128)(2,1)} %collective-permute-done.23.refs_3_, ...), custom_call_target="tpu_custom_call" | custom-call | bytes 16777216 | tf_op jit(solution)/shard_map/pallas_call | solution.py:635
  202.5 15.5 %collective-permute-done.30.refs_2_ = bf16[256,2048]{1,0:T(8,128)(2,1)} collective-permute-done((bf16[256,2048]{1,0:T(8,128)(2,1)}, bf16[256,2048]{1,0:T(8,128)(2,1)}, u32[]{:S(2)}, u32[]{:S(2)}) %collective-permute-start.30) | collective-permute-done | bytes 1048608 | tf_op jit(solution)/shard_map/ppermute | solution.py:72
  220.1 13.0 %collective-permute-done.35.refs_3_ = bf16[256,2048]{1,0:T(8,128)(2,1)} collective-permute-done((bf16[256,2048]{1,0:T(8,128)(2,1)}, bf16[256,2048]{1,0:T(8,128)(2,1)}, u32[]{:S(2)}, u32[]{:S(2)}) %collective-permute-start.35) | collective-permute-done | bytes 1048608 | tf_op jit(solution)/shard_map/ppermute | solution.py:72
  233.1 18.5 %all-gather.11.cloned.1.call-done.refs_8_.refs_9_.refs_2_.refs_3_ = bf16[768,4096]{1,0:T(8,128)(2,1)} async-done(((bf16[192,4096]{1,0:T(8,128)(2,1)}), bf16[768,4096]{1,0:T(8,128)(2,1)}) %all-gather.11.cloned.1.call-update) | async-done | bytes 6291472 | tf_op jit(solution)/shard_map/all_gather | solution.py:755
  251.6 24.0 %shard_map.252 = (bf16[8,256,768]{2,1,0:T(8,128)(2,1)}, f32[8,256,768]{2,1,0:T(8,128)}, f32[8,256,768]{2,1,0:T(8,128)}, bf16[8,256,2048]{2,1,0:T(8,128)(2,1)}) custom-call(bf16[256,2048]{1,0:T(8,128)(2,1)} %multiply_convert_fusion.refs_0_, bf16[256,2048]{1,0:T(8,128)(2,1)} %collective-permute-done.29.refs_1_, ...), custom_call_target="tpu_custom_call" | custom-call | flops 12884901888 | bytes 38797312 | tf_op jit(solution)/shard_map/pallas_call | solution.py:694
  275.6 12.1 %bitcast_convert_fusion.2 = bf16[768,2048]{1,0:T(8,128)(2,1)} fusion(bf16[8,256,768]{2,1,0:T(8,128)(2,1)} %get-tuple-element.199.refs_0_, bf16[8,256,2048]{2,1,0:T(8,128)(2,1)} %shard_map.251.c_ref), kind=kOutput, calls=%fused_computation.2 | convolution fusion | flops 6444023808 | bytes 14680064 | tf_op jit(solution)/shard_map/dot_general | solution.py:31
  287.7 27.1 %all-gather.9.cloned.1.call-done.wo.refs_1_ = bf16[768,2048]{1,0:T(8,128)(2,1)} async-done(((bf16[192,2048]{1,0:T(8,128)(2,1)}), bf16[768,2048]{1,0:T(8,128)(2,1)}) %all-gather.9.cloned.1.call-update) | async-done | bytes 3145744 | tf_op jit(solution)/shard_map/all_gather | solution.py:755
  314.8 16.4 %shard_map.253 = (bf16[8,256,768]{2,1,0:T(8,128)(2,1)}, bf16[8,256,768]{2,1,0:T(8,128)(2,1)}) custom-call(bf16[8,256,2048]{2,1,0:T(8,128)(2,1)} %shard_map.251.c_ref, bf16[768,2048]{1,0:T(8,128)(2,1)} %all-gather.9.cloned.1.call-done.wo.refs_1_, f32[8,256,768]{2,1,0:T(8,128)} %get-tuple-element.185.turn, f32[8,256,768]{2,1,0:T(8,128)} %get-tuple-element.186.value), custom_call_target="tpu_custom_call" | custom-call | flops 6442450944 | bytes 30408704 | tf_op jit(solution)/shard_map/pallas_call | solution.py:736
  331.2 7.4 %shard_map.254 = bf16[2,256,2048]{2,1,0:T(8,128)(2,1)} custom-call(bf16[8,256,768]{2,1,0:T(8,128)(2,1)} %get-tuple-element.196.refs_0_, bf16[8,256,768]{2,1,0:T(8,128)(2,1)} %get-tuple-element.204.refs_1_, bf16[768,4096]{1,0:T(8,128)(2,1)} %all-gather.11.cloned.1.call-done.refs_8_.refs_9_.refs_2_.refs_3_, ...), custom_call_target="tpu_custom_call" | custom-call | flops 3221225472 | bytes 9961472 | tf_op jit(solution)/shard_map/pallas_call | solution.py:608
  338.8 7.8 %shard_map.255 = bf16[2,256,2048]{2,1,0:T(8,128)(2,1)} custom-call(bf16[8,256,768]{2,1,0:T(8,128)(2,1)} %get-tuple-element.196.refs_0_, bf16[8,256,768]{2,1,0:T(8,128)(2,1)} %get-tuple-element.204.refs_1_, bf16[768,4096]{1,0:T(8,128)(2,1)} %all-gather.11.cloned.1.call-done.refs_8_.refs_9_.refs_2_.refs_3_, ...), custom_call_target="tpu_custom_call" | custom-call | flops 3221225472 | bytes 9961472 | tf_op jit(solution)/shard_map/pallas_call | solution.py:608
  352.1 13.5 %shard_map.256 = (bf16[2,256,2048]{2,1,0:T(8,128)(2,1)}, bf16[2,256,2048]{2,1,0:T(8,128)(2,1)}) custom-call(bf16[8,256,768]{2,1,0:T(8,128)(2,1)} %get-tuple-element.196.refs_0_, bf16[8,256,768]{2,1,0:T(8,128)(2,1)} %get-tuple-element.204.refs_1_, bf16[768,4096]{1,0:T(8,128)(2,1)} %all-gather.11.cloned.1.call-done.refs_8_.refs_9_.refs_2_.refs_3_, ...), custom_call_target="tpu_custom_call" | custom-call | flops 6442450944 | bytes 13631488 | tf_op jit(solution)/shard_map/pallas_call | solution.py:608
  375.1 10.4 %bitcast_convert_fusion.1 = bf16[768,2048]{1,0:T(8,128)(2,1)} fusion(bf16[8,256,768]{2,1,0:T(8,128)(2,1)S(1)} %copy-done.6, bf16[8,256,2048]{2,1,0:T(8,128)(2,1)} %get-tuple-element.197), kind=kOutput, calls=%fused_computation.1 | convolution fusion | flops 6444023808 | bytes 14680064 | tf_op jit(solution)/shard_map/dot_general | solution.py:31
  385.5 6.1 collective-permute-done.44
  401.2 13.7 %shard_map.257 = (bf16[4,256,2048]{2,1,0:T(8,128)(2,1)}, bf16[4,256,2048]{2,1,0:T(8,128)(2,1)}) custom-call(bf16[8,256,768]{2,1,0:T(8,128)(2,1)} %get-tuple-element.199.refs_0_, bf16[768,2048]{1,0:T(8,128)(2,1)} %all-gather.9.cloned.1.call-done.wo.refs_1_), custom_call_target="tpu_custom_call" | custom-call | flops 6442450944 | bytes 14680064 | tf_op jit(solution)/shard_map/pallas_call | solution.py:608
  414.9 9.1 %collective-permute-done.46.refs_2_ = bf16[256,2048]{1,0:T(8,128)(2,1)} collective-permute-done((bf16[256,2048]{1,0:T(8,128)(2,1)}, bf16[256,2048]{1,0:T(8,128)(2,1)}, u32[]{:S(2)}, u32[]{:S(2)}) %collective-permute-start.46) | collective-permute-done | bytes 1048608 | tf_op jit(solution)/shard_map/ppermute | solution.py:72
  426.8 10.4 %bitcast_convert_fusion = bf16[768,2048]{1,0:T(8,128)(2,1)} fusion(bf16[8,256,768]{2,1,0:T(8,128)(2,1)S(1)} %copy-done.5, bf16[8,256,2048]{2,1,0:T(8,128)(2,1)} %get-tuple-element.197), kind=kOutput, calls=%fused_computation | convolution fusion | flops 6444023808 | bytes 14680064 | tf_op jit(solution)/shard_map/dot_general | solution.py:31
  444.8 18.8 %shard_map.258 = (bf16[8,256,384]{2,1,0:T(8,128)(2,1)}, bf16[8,256,384]{2,1,0:T(8,128)(2,1)}, f32[8,256,384]{2,1,0:T(8,128)}, f32[8,256,384]{2,1,0:T(8,128)}, f3...) custom-call(bf16[256,2048]{1,0:T(8,128)(2,1)} %fusion.43.refs_0_, bf16[256,2048]{1,0:T(8,128)(2,1)} %collective-permute-done.45.refs_1_, ...), custom_call_target="tpu_custom_call" | custom-call | flops 3221225472 | bytes 30408704 | tf_op jit(solution)/shard_map/pallas_call | solution.py:452
  477.6 7.5 %convolution_bitcast_fusion = bf16[384,2048]{1,0:T(8,128)(2,1)S(1)} fusion(bf16[8,256,384]{2,1,0:T(8,128)(2,1)} %get-tuple-element.223, bf16[8,256,2048]{2,1,0:T(8,128)(2,1)} %get-tuple-element.224), kind=kOutput, calls=%fused_computation.10 | convolution fusion | flops 3221225472 | bytes 11534336 | tf_op jit(solution)/shard_map/dot_general | solution.py:31
  492.4 17.4 %shard_map.259 = (bf16[8,256,384]{2,1,0:T(8,128)(2,1)}, f32[8,16,384]{2,1,0:T(8,128)}, bf16[768,160]{1,0:T(8,128)(2,1)}, f32[8,384]{1,0:T(8,128)}) custom-call(f32[8,8,384]{2,1,0:T(8,128)} %copy-done.11, f32[8,8,384]{2,1,0:T(8,128)} %copy-done.10, f32[8,8,384]{2,1,0:T(8,128)} %copy-done.9, f32[8,8,384]{2,1,0:T(8,128)} %copy-done.34, ...), custom_call_target="tpu_custom_call" | custom-call | flops 2415919104 | bytes 28311552 | tf_op jit(solution)/shard_map/pallas_call | solution.py:557
  516.2 6.8 %collective-permute-done.59 = f32[8,8,384]{2,1,0:T(8,128)S(1)} collective-permute-done((f32[8,8,384]{2,1,0:T(8,128)S(1)}, f32[8,8,384]{2,1,0:T(8,128)S(1)}, u32[]{:S(2)}, u32[]{:S(2)}) %collective-permute-start.59) | collective-permute-done | bytes 98336 | tf_op jit(solution)/shard_map/ppermute | solution.py:139
  523.6 6.1 shard_map.260
  530.2 6.2 shard_map.261
  541.6 11.3 %shard_map.262 = (bf16[2,256,2048]{2,1,0:T(8,128)(2,1)}, bf16[2,256,2048]{2,1,0:T(8,128)(2,1)}, f32[2,1,2048]{2,1,0:T(1,128)}) custom-call(bf16[8,256,384]{2,1,0:T(8,128)(2,1)} %get-tuple-element.251.refs_0_, bf16[8,256,384]{2,1,0:T(8,128)(2,1)} %fusion.37.refs_1_, bf16[320,4480]{1,0:T(8,128)(2,1)} %all-gather.5.cloned.1.call-done.wu.wy.refs_2_.refs_3_, ...), custom_call_target="tpu_custom_call" | custom-call | flops 2684354560 | bytes 8126464 | tf_op jit(solution)/shard_map/pallas_call | solution.py:608
  564.7 22.4 %reduce-scatter.12.cloned.1.call-done = bf16[80,4096]{1,0:T(8,128)(2,1)} async-done(((bf16[320,4096]{1,0:T(8,128)(2,1)}), bf16[80,4096]{1,0:T(8,128)(2,1)}) %reduce-scatter.12.cloned.1.call-update) | async-done | bytes 655376 | tf_op jit(solution)/shard_map/reduce_scatter | solution.py:759
  587.0 7.3 %bitcast_convert_fusion.3 = bf16[384,2048]{1,0:T(8,128)(2,1)S(1)} fusion(bf16[8,256,384]{2,1,0:T(8,128)(2,1)} %fusion.37.refs_1_, bf16[8,256,2048]{2,1,0:T(8,128)(2,1)} %get-tuple-element.221.refs_4_), kind=kOutput, calls=%fused_computation.7 | convolution fusion | flops 3222011904 | bytes 11534336 | tf_op jit(solution)/shard_map/dot_general | solution.py:31
  618.3 12.9 %reduce-scatter.14.cloned.1.call-done = bf16[80,2432]{1,0:T(8,128)(2,1)} async-done(((bf16[320,2432]{1,0:T(8,128)(2,1)}), bf16[80,2432]{1,0:T(8,128)(2,1)}) %reduce-scatter.14.cloned.1.call-update) | async-done | bytes 389136 | tf_op jit(solution)/shard_map/reduce_scatter | solution.py:759
  (411 shorter events, 235.5 us)
Async XLA Ops:
  7.2 82.9 %all-gather.5.cloned.1.call-start = ((), (), s32[]{:S(2)}) async-start(), calls=%async_computation.6 | async-start | bytes 3584000 | tf_op jit(solution)/shard_map/all_gather | solution.py:755
  14.7 104.5 %all-gather.7.cloned.1.call-start = ((), (), s32[]{:S(2)}) async-start(), calls=%async_computation.7 | async-start | bytes 1638400 | tf_op jit(solution)/shard_map/all_gather | solution.py:755
  21.8 54.3 %collective-permute-start.3 = (bf16[256,2048]{1,0:T(8,128)(2,1)S(1)}, bf16[256,2048]{1,0:T(8,128)(2,1)}, u32[]{:S(2)}, u32[]{:S(2)}) collective-permute-start(bf16[256,2048]{1,0:T(8,128)(2,1)S(1)} %bitcast.177), channel_id=1, source_target_pairs={{0,4},{4,0},{8,12},{12,8},{16,20},{20,16},{24,28},{28,24},{1,5},{5... | collective-permute-start | bytes 3145736 | tf_op jit(solution)/shard_map/ppermute | solution.py:79
  21.8 49.2 %collective-permute-start.1 = (bf16[256,2048]{1,0:T(8,128)(2,1)S(1)}, bf16[256,2048]{1,0:T(8,128)(2,1)}, u32[]{:S(2)}, u32[]{:S(2)}) collective-permute-start(bf16[256,2048]{1,0:T(8,128)(2,1)S(1)} %bitcast.178), channel_id=1, source_target_pairs={{0,16},{4,12},{8,24},{12,4},{16,0},{20,28},{24,8},{28,20},{1,17},{... | collective-permute-start | bytes 3145736 | tf_op jit(solution)/shard_map/ppermute | solution.py:72
  25.2 226.3 %all-gather.11.cloned.1.call-start = ((), (), s32[]{:S(2)}) async-start(), calls=%async_computation.9 | async-start | bytes 7864320 | tf_op jit(solution)/shard_map/all_gather | solution.py:755
  33.8 31.7 %collective-permute-start.14 = (bf16[16,2048]{1,0:T(8,128)(2,1)S(1)}, bf16[16,2048]{1,0:T(8,128)(2,1)S(1)}, u32[]{:S(2)}, u32[]{:S(2)}) collective-permute-start(bf16[16,2048]{1,0:T(8,128)(2,1)S(1)} %fusion.36.refs_8_), channel_id=1, source_target_pairs={{0,4},{4,0},{8,12},{12,8},{16,20},{20,16},{24,28},{28,24},{1,5},{5... | collective-permute-start | bytes 196616 | tf_op jit(solution)/shard_map/ppermute | solution.py:79
  33.9 27.3 %collective-permute-start.12 = (bf16[16,2048]{1,0:T(8,128)(2,1)S(1)}, bf16[16,2048]{1,0:T(8,128)(2,1)S(1)}, u32[]{:S(2)}, u32[]{:S(2)}) collective-permute-start(bf16[16,2048]{1,0:T(8,128)(2,1)S(1)} %fusion.36.refs_8_), channel_id=1, source_target_pairs={{0,16},{4,12},{8,24},{12,4},{16,0},{20,28},{24,8},{28,20},{1,17},{... | collective-permute-start | bytes 196616 | tf_op jit(solution)/shard_map/ppermute | solution.py:72
  48.2 23.4 %collective-permute-start.2 = (bf16[256,2048]{1,0:T(8,128)(2,1)}, bf16[256,2048]{1,0:T(8,128)(2,1)}, u32[]{:S(2)}, u32[]{:S(2)}) collective-permute-start(bf16[256,2048]{1,0:T(8,128)(2,1)} %collective-permute-done.refs_1_), channel_id=1, source_target_pairs={{0,16},{4,12},{8,24},{12,4},{16,0},{20,28},{24,8},{28,20},{1,17},{... | collective-permute-start | bytes 3145736 | tf_op jit(solution)/shard_map/ppermute | solution.py:72
  77.1 40.5 %collective-permute-start.22 = (bf16[256,2048]{1,0:T(8,128)(2,1)}, bf16[256,2048]{1,0:T(8,128)(2,1)}, u32[]{:S(2)}, u32[]{:S(2)}) collective-permute-start(bf16[256,2048]{1,0:T(8,128)(2,1)} %bitcast.40.refs_0_), channel_id=1, source_target_pairs={{0,16},{4,12},{8,24},{12,4},{16,0},{20,28},{24,8},{28,20},{1,17},{... | collective-permute-start | bytes 3145736 | tf_op jit(solution)/shard_map/ppermute | solution.py:72
  77.8 39.8 %collective-permute-start.21 = (bf16[256,2048]{1,0:T(8,128)(2,1)}, bf16[256,2048]{1,0:T(8,128)(2,1)}, u32[]{:S(2)}, u32[]{:S(2)}) collective-permute-start(bf16[256,2048]{1,0:T(8,128)(2,1)} %bitcast.40.refs_0_), channel_id=1, source_target_pairs={{0,8},{4,20},{8,0},{12,28},{16,24},{20,4},{24,16},{28,12},{1,9},{5... | collective-permute-start | bytes 3145736 | tf_op jit(solution)/shard_map/ppermute | solution.py:72
  138.5 176.3 %all-gather.9.cloned.1.call-start = ((), (), s32[]{:S(2)}) async-start(), calls=%async_computation.8 | async-start | bytes 3932160 | tf_op jit(solution)/shard_map/all_gather | solution.py:755
  170.4 22.9 %collective-permute-start.31 = (bf16[256,2048]{1,0:T(8,128)(2,1)}, bf16[256,2048]{1,0:T(8,128)(2,1)S(1)}, u32[]{:S(2)}, u32[]{:S(2)}) collective-permute-start(bf16[256,2048]{1,0:T(8,128)(2,1)} %bitcast.40.refs_0_), channel_id=1, source_target_pairs={{0,4},{4,0},{8,12},{12,8},{16,20},{20,16},{24,28},{28,24},{1,5},{5... | collective-permute-start | bytes 3145736 | tf_op jit(solution)/shard_map/ppermute | solution.py:79
  171.1 22.6 %collective-permute-start.33 = (bf16[256,2048]{1,0:T(8,128)(2,1)}, bf16[256,2048]{1,0:T(8,128)(2,1)S(1)}, u32[]{:S(2)}, u32[]{:S(2)}) collective-permute-start(bf16[256,2048]{1,0:T(8,128)(2,1)} %collective-permute-done.22.refs_2_), channel_id=1, source_target_pairs={{0,4},{4,0},{8,12},{12,8},{16,20},{20,16},{24,28},{28,24},{1,5},{5... | collective-permute-start | bytes 3145736 | tf_op jit(solution)/shard_map/ppermute | solution.py:79
  171.1 22.6 %collective-permute-start.32 = (bf16[256,2048]{1,0:T(8,128)(2,1)}, bf16[256,2048]{1,0:T(8,128)(2,1)S(1)}, u32[]{:S(2)}, u32[]{:S(2)}) collective-permute-start(bf16[256,2048]{1,0:T(8,128)(2,1)} %collective-permute-done.21.refs_1_), channel_id=1, source_target_pairs={{0,4},{4,0},{8,12},{12,8},{16,20},{20,16},{24,28},{28,24},{1,5},{5... | collective-permute-start | bytes 3145736 | tf_op jit(solution)/shard_map/ppermute | solution.py:79
  191.6 26.3 %collective-permute-start.30 = (bf16[256,2048]{1,0:T(8,128)(2,1)}, bf16[256,2048]{1,0:T(8,128)(2,1)}, u32[]{:S(2)}, u32[]{:S(2)}) collective-permute-start(bf16[256,2048]{1,0:T(8,128)(2,1)} %multiply_convert_fusion.refs_0_), channel_id=1, source_target_pairs={{0,16},{4,12},{8,24},{12,4},{16,0},{20,28},{24,8},{28,20},{1,17},{... | collective-permute-start | bytes 3145736 | tf_op jit(solution)/shard_map/ppermute | solution.py:72
  193.2 24.7 %collective-permute-start.29 = (bf16[256,2048]{1,0:T(8,128)(2,1)}, bf16[256,2048]{1,0:T(8,128)(2,1)}, u32[]{:S(2)}, u32[]{:S(2)}) collective-permute-start(bf16[256,2048]{1,0:T(8,128)(2,1)} %multiply_convert_fusion.refs_0_), channel_id=1, source_target_pairs={{0,8},{4,20},{8,0},{12,28},{16,24},{20,4},{24,16},{28,12},{1,9},{5... | collective-permute-start | bytes 3145736 | tf_op jit(solution)/shard_map/ppermute | solution.py:72
  219.4 345.3 %reduce-scatter.6.cloned.1.call-start = ((), (), s32[]{:S(2)}) async-start(), calls=%async_computation.10 | async-start | bytes 3932160 | tf_op jit(solution)/shard_map/reduce_scatter | solution.py:759
  219.4 32.2 %collective-permute-start.36 = (bf16[256,2048]{1,0:T(8,128)(2,1)}, bf16[256,2048]{1,0:T(8,128)(2,1)}, u32[]{:S(2)}, u32[]{:S(2)}) collective-permute-start(bf16[256,2048]{1,0:T(8,128)(2,1)} %multiply_convert_fusion.refs_0_), channel_id=1, source_target_pairs={{0,4},{4,0},{8,12},{12,8},{16,20},{20,16},{24,28},{28,24},{1,5},{5... | collective-permute-start | bytes 3145736 | tf_op jit(solution)/shard_map/ppermute | solution.py:79
  219.5 32.1 %collective-permute-start.37 = (bf16[256,2048]{1,0:T(8,128)(2,1)}, bf16[256,2048]{1,0:T(8,128)(2,1)}, u32[]{:S(2)}, u32[]{:S(2)}) collective-permute-start(bf16[256,2048]{1,0:T(8,128)(2,1)} %collective-permute-done.29.refs_1_), channel_id=1, source_target_pairs={{0,4},{4,0},{8,12},{12,8},{16,20},{20,16},{24,28},{28,24},{1,5},{5... | collective-permute-start | bytes 3145736 | tf_op jit(solution)/shard_map/ppermute | solution.py:79
  220.0 31.6 %collective-permute-start.38 = (bf16[256,2048]{1,0:T(8,128)(2,1)}, bf16[256,2048]{1,0:T(8,128)(2,1)}, u32[]{:S(2)}, u32[]{:S(2)}) collective-permute-start(bf16[256,2048]{1,0:T(8,128)(2,1)} %collective-permute-done.30.refs_2_), channel_id=1, source_target_pairs={{0,4},{4,0},{8,12},{12,8},{16,20},{20,16},{24,28},{28,24},{1,5},{5... | collective-permute-start | bytes 3145736 | tf_op jit(solution)/shard_map/ppermute | solution.py:79
  338.6 226.1 %reduce-scatter.8.cloned.1.call-start = ((), (), s32[]{:S(2)}) async-start(), calls=%async_computation.11 | async-start | bytes 3932160 | tf_op jit(solution)/shard_map/reduce_scatter | solution.py:759
  366.0 25.6 %collective-permute-start.43 = (bf16[256,2048]{1,0:T(8,128)(2,1)}, bf16[256,2048]{1,0:T(8,128)(2,1)}, u32[]{:S(2)}, u32[]{:S(2)}) collective-permute-start(bf16[256,2048]{1,0:T(8,128)(2,1)} %get-tuple-element.341), channel_id=1, source_target_pairs={{0,16},{4,12},{8,24},{12,4},{16,0},{20,28},{24,8},{28,20},{1,17},{... | collective-permute-start | bytes 3145736 | tf_op jit(solution)/shard_map/ppermute | solution.py:108
  385.5 179.2 %reduce-scatter.10.cloned.1.call-start = ((), (), s32[]{:S(2)}) async-start(), calls=%async_computation.12 | async-start | bytes 3932160 | tf_op jit(solution)/shard_map/reduce_scatter | solution.py:759
  398.6 25.4 %collective-permute-start.46 = (bf16[256,2048]{1,0:T(8,128)(2,1)}, bf16[256,2048]{1,0:T(8,128)(2,1)}, u32[]{:S(2)}, u32[]{:S(2)}) collective-permute-start(bf16[256,2048]{1,0:T(8,128)(2,1)} %fusion.43.refs_0_), channel_id=1, source_target_pairs={{0,16},{4,12},{8,24},{12,4},{16,0},{20,28},{24,8},{28,20},{1,17},{... | collective-permute-start | bytes 3145736 | tf_op jit(solution)/shard_map/ppermute | solution.py:72
  399.9 25.0 %collective-permute-start.45 = (bf16[256,2048]{1,0:T(8,128)(2,1)}, bf16[256,2048]{1,0:T(8,128)(2,1)}, u32[]{:S(2)}, u32[]{:S(2)}) collective-permute-start(bf16[256,2048]{1,0:T(8,128)(2,1)} %fusion.43.refs_0_), channel_id=1, source_target_pairs={{0,8},{4,20},{8,0},{12,28},{16,24},{20,4},{24,16},{28,12},{1,9},{5... | collective-permute-start | bytes 3145736 | tf_op jit(solution)/shard_map/ppermute | solution.py:72
  442.9 25.6 %collective-permute-start.53 = (bf16[256,2048]{1,0:T(8,128)(2,1)}, bf16[256,2048]{1,0:T(8,128)(2,1)}, u32[]{:S(2)}, u32[]{:S(2)}) collective-permute-start(bf16[256,2048]{1,0:T(8,128)(2,1)} %get-tuple-element.337), channel_id=1, source_target_pairs={{0,16},{4,12},{8,24},{12,4},{16,0},{20,28},{24,8},{28,20},{1,17},{... | collective-permute-start | bytes 3145736 | tf_op jit(solution)/shard_map/ppermute | solution.py:922
  444.3 142.8 %reduce-scatter.12.cloned.1.call-start = ((), (), s32[]{:S(2)}) async-start(), calls=%async_computation.13 | async-start | bytes 3276800 | tf_op jit(solution)/shard_map/reduce_scatter | solution.py:759
  468.6 23.2 %collective-permute-start.57 = (f32[8,8,384]{2,1,0:T(8,128)}, f32[8,8,384]{2,1,0:T(8,128)S(1)}, u32[]{:S(2)}, u32[]{:S(2)}) collective-permute-start(f32[8,8,384]{2,1,0:T(8,128)} %get-tuple-element.218), channel_id=1, source_target_pairs={{3,0},{7,4},{11,8},{15,12},{19,16},{23,20},{27,24},{31,28}} | collective-permute-start | bytes 294920 | tf_op jit(solution)/shard_map/ppermute | solution.py:139
  476.2 33.6 %collective-permute-start.58 = (bf16[256,2048]{1,0:T(8,128)(2,1)}, bf16[256,2048]{1,0:T(8,128)(2,1)}, u32[]{:S(2)}, u32[]{:S(2)}) collective-permute-start(bf16[256,2048]{1,0:T(8,128)(2,1)} %fusion.11), channel_id=1, source_target_pairs={{0,8},{4,20},{8,0},{12,28},{16,24},{20,4},{24,16},{28,12},{1,9},{5... | collective-permute-start | bytes 3145736 | tf_op jit(solution)/shard_map/ppermute | solution.py:94
  529.7 101.4 %reduce-scatter.14.cloned.1.call-start = ((), (), s32[]{:S(2)}) async-start(), calls=%async_computation.14 | async-start | bytes 1945600 | tf_op jit(solution)/shard_map/reduce_scatter | solution.py:759
  556.8 40.2 %collective-permute-start.63 = (bf16[256,2048]{1,0:T(8,128)(2,1)}, bf16[256,2048]{1,0:T(8,128)(2,1)}, u32[]{:S(2)}, u32[]{:S(2)}) collective-permute-start(bf16[256,2048]{1,0:T(8,128)(2,1)} %get-tuple-element.339), channel_id=1, source_target_pairs={{0,16},{4,12},{8,24},{12,4},{16,0},{20,28},{24,8},{28,20},{1,17},{... | collective-permute-start | bytes 3145736 | tf_op jit(solution)/shard_map/ppermute | solution.py:108
  563.2 33.7 %collective-permute-start.64 = (bf16[256,2048]{1,0:T(8,128)(2,1)}, bf16[256,2048]{1,0:T(8,128)(2,1)}, u32[]{:S(2)}, u32[]{:S(2)}) collective-permute-start(bf16[256,2048]{1,0:T(8,128)(2,1)} %fusion.5), channel_id=1, source_target_pairs={{0,8},{4,20},{8,0},{12,28},{16,24},{20,4},{24,16},{28,12},{1,9},{5... | collective-permute-start | bytes 3145736 | tf_op jit(solution)/shard_map/ppermute | solution.py:94
  (101 other events, 941.9 us)
Sparse Core Ops, SparseCore 0:
  14.8 61.5 all-gather.4
  78.0 32.6 all-gather.6
  138.6 112.8 all-gather.10
  253.0 61.7 all-gather.8
  338.7 59.0 reduce-scatter.5
  400.0 60.2 reduce-scatter.7
  462.6 68.5 reduce-scatter.9
  534.1 52.9 reduce-scatter.11
  596.0 35.1 reduce-scatter.13

commit v3 on v2

--- a/solution.py
+++ b/solution.py
@@ -17,6 +17,9 @@
 ANY = pl.BlockSpec(memory_space=pl.ANY)
 ROOT = 0.7978845608028654
 CUBE = 0.044715
+SLOW = 4.5
+RATE = 650e6
+SWEEP = 25e-6
 
 
 def dot_nt(left, right):
@@ -62,21 +65,28 @@
     return stages, twin
 
 
-def gather_rows(piece, fills=(), filled=None):
+def gather_rows(piece, beside=()):
     stages, twin = plane_stages(lax.axis_size("dp"))
     held = [piece] + [None] * (2 ** len(stages) - 1)
-    for wave in range(1, len(stages) + 1):
-        members = [m for m in range(len(held)) if bin(m).count("1") == wave]
-        tops = [m.bit_length() - 1 for m in members]
-        sent = [held[m ^ (1 << top)] for m, top in zip(members, tops)]
-        arrived = [lax.ppermute(part, "dp", stages[top]) for part, top in zip(sent, tops)]
-        if wave <= len(fills):
-            arrived, made = lax.optimization_barrier((arrived, fills[wave - 1](sent)))
-            if filled is not None:
-                filled.append(made)
+    done = []
+    before = ()
+
+    def arrival(m):
+        top = m.bit_length() - 1
+        return lax.ppermute(held[m ^ (1 << top)], "dp", stages[top])
+
+    for members, work in beside:
+        arrived = [arrival(m) for m in members]
+        sent = [held[m ^ (1 << (m.bit_length() - 1))] for m in members]
+        arrived, made = lax.optimization_barrier((arrived, work((sent, before), done)))
+        before = arrived
+        done.append(made)
         for m, part in zip(members, arrived):
             held[m] = part
-    return held + [lax.ppermute(part, "dp", twin) for part in held]
+    for m in range(1, len(held)):
+        if held[m] is None:
+            held[m] = arrival(m)
+    return held + [lax.ppermute(part, "dp", twin) for part in held], done
 
 
 def after(value, *others):
@@ -84,39 +94,47 @@
 
 
 def total_of(terms):
-    return sum(term.astype(F32) for term in terms)
+    return sum(array[place].astype(F32) for array, place in terms)
 
 
 def scatter_tail(terms, stages, waits):
     for place, pairs in enumerate(reversed(stages)):
         split = len(terms) // 2
-        sent = [total_of(those).astype(BF16) for those in terms[split:]]
+        sent = add_rows(terms[split:])
         got = [lax.ppermute(part, "dp", pairs) for part in sent]
         if place < len(waits):
             got = waits[place](sent, got)
-        terms = [[*those, one] for those, one in zip(terms, got)]
-    return total_of(terms[0])
-
-
-def scatter_rows(make, count, wait):
+        terms = [[*those, (one[None], 0)] for those, one in zip(terms, got)]
+    return terms[0]
+
+
+def scatter_terms(make, count, wait, low_wait=None):
     stages, twin = plane_stages(lax.axis_size("dp"))
     quarter = count // 4
     theirs = make([3], quarter, ())[0]
     there = lax.ppermute(theirs, "dp", twin)
     far = make([1], quarter, (theirs,))[0]
-    sent = [total_of([far[k], there[k]]).astype(BF16) for k in range(quarter)]
+    sent = add_rows([[(far, k), (there, k)] for k in range(quarter)])
     got = [lax.ppermute(part, "dp", stages[-1]) for part in sent]
     split = quarter // 2
     theirs, near = make([2, 0], quarter, (sent,))
     theirs, near, got[split:] = lax.optimization_barrier((theirs, near, got[split:]))
     there = lax.ppermute(theirs, "dp", twin)
-    terms = [[near[k], there[k], got[k]] for k in range(quarter)]
+    if low_wait is not None:
+        got[:split] = low_wait(sent, got[:split])
+    terms = [[(near, k), (there, k), (got[k][None], 0)] for k in range(quarter)]
     return scatter_tail(terms, stages[:-1], [wait] if wait else [])
 
 
-def beside(work):
+def scatter_rows(make, count, wait):
+    return total_of(scatter_terms(make, count, wait))
+
+
+def beside(work, done):
     def wait(sent, got):
-        return after(got, work(sent))
+        got, made = lax.optimization_barrier((got, work(sent)))
+        done.append(made)
+        return got
 
     return wait
 
@@ -168,16 +186,17 @@
     return carry_mult, carry_total
 
 
-def folded(refs):
-    carry = refs[-1][0, 1:2, :]
+def folded(refs, piece):
+    at = pl.ds(piece, 1)
+    carry = refs[-1][1, at, :]
     for ref in refs[-2::-1]:
-        carry = ref[0, 1:2, :] + ref[0, 0:1, :] * carry
+        carry = ref[1, at, :] + ref[0, at, :] * carry
     return carry
 
 
-def ends_block(mult, total):
-    width = mult.shape[1]
-    return jnp.concatenate([mult, total, jnp.zeros((6, width), F32)], 0)
+def put_ends(ref, piece, mult, total):
+    ref[0, pl.ds(piece, 1), :] = mult
+    ref[1, pl.ds(piece, 1), :] = total
 
 
 def fetch_all(refs, buf, sems):
@@ -242,13 +261,53 @@
             pltpu.SemaphoreType.DMA((count,)),
             pltpu.SemaphoreType.DMA((count,)),
         ],
-        count * rows * model * 8,
-        count * rows * model * 6,
+        2.6e-6 * count * rows * model,
     )(*pieces, *tops, gain)
 
 
+def block_masks(width, block):
+    row = lax.broadcasted_iota(jnp.int32, (width, width), 0)
+    column = lax.broadcasted_iota(jnp.int32, (width, width), 1)
+    inside = None
+    for start in range(0, width, block):
+        here = (row >= start) & (row < start + block) & (column >= start) & (column < start + block)
+        inside = here if inside is None else inside | here
+    row = lax.broadcasted_iota(jnp.int32, (width, block), 0)
+    column = lax.broadcasted_iota(jnp.int32, (width, block), 1)
+    fold = None
+    for start in range(0, width, block):
+        here = row - start == column
+        fold = here if fold is None else fold | here
+    return inside, jnp.where(fold, 1.0, 0.0).astype(BF16)
+
+
+def softplus(values):
+    small = jnp.exp(-jnp.abs(values))
+    grown = 1.0 + small
+    exact = jnp.where(grown == 1.0, small, jnp.log(grown) * small / jnp.where(grown == 1.0, 1.0, grown - 1.0))
+    return jnp.maximum(values, 0.0) + exact
+
+
 def mixer_enter_kernel(
-    h_ref, m_ref, wu, wy, wz, par, u_out, y_out, conv_out, r_out, e_out, k_out, a_out, s_out, ends, wu_all, wy_all
+    block,
+    h_ref,
+    m_ref,
+    wu,
+    wy,
+    small,
+    u_out,
+    y_out,
+    conv_out,
+    r_out,
+    e_out,
+    k_out,
+    a_out,
+    s_out,
+    ends,
+    wz,
+    par,
+    wu_all,
+    wy_all,
 ):
     width = wz.shape[1]
 
@@ -256,6 +315,18 @@
     def _():
         wu_all[...] = padded_rows(wu[...], width)
         wy_all[...] = padded_rows(wy[...], width)
+        rows = padded_rows(small[...], width)
+        inside, fold = block_masks(width, block)
+        for gate in (0, 1):
+            spread = dot_nt(rows[:, gate * block : gate * block + block], fold)
+            wz[gate * width : gate * width + width, :] = jnp.where(inside, spread, 0.0).astype(BF16)
+        row = lax.broadcasted_iota(jnp.int32, (width, width), 0)
+        column = lax.broadcasted_iota(jnp.int32, (width, width), 1)
+        same = jnp.where(row == column, 1.0, 0.0).astype(BF16)
+        turned = dot_tn(rows[:, 2 * block : 2 * block + 8], same)
+        par[0:8, :] = turned
+        par[8:16, :] = turned
+        par[7:8, :] = -SHARP * softplus(turned[7:8, :])
 
     h_low = h_ref[0]
     rows = h_low.shape[0] - HALO
@@ -280,7 +351,7 @@
     k_out[0] = keep
     inputs = conv * enter * jnp.sqrt(jnp.maximum(1.0 - keep * keep, FLOOR))
     mult, total = scan_into(keep, inputs, a_out, s_out, False)
-    ends[0] = ends_block(mult, total)
+    put_ends(ends, pl.program_id(0), mult, total)
 
 
 def resident(shape):
@@ -293,7 +364,7 @@
     return pl.BlockSpec((1,) + shape, lambda step: (step + first,) + rest)
 
 
-def call(kernel, grid, in_specs, out_specs, out_shape, scratch, flops, moved):
+def call(kernel, grid, in_specs, out_specs, out_shape, scratch, micros):
     return pl.pallas_call(
         kernel,
         grid=grid,
@@ -304,38 +375,38 @@
         compiler_params=pltpu.CompilerParams(
             vmem_limit_bytes=VMEM_LIMIT, dimension_semantics=("arbitrary",) * len(grid)
         ),
-        cost_estimate=pl.CostEstimate(flops=int(flops), bytes_accessed=int(moved), transcendentals=0),
+        cost_estimate=pl.CostEstimate(flops=int(micros / SLOW * 1.15e9), bytes_accessed=1024, transcendentals=0),
     )
 
 
-def mixer_enter(h_all, same, w_in, wz, par):
+def mixer_enter(h_all, same, w_in, extra, block):
     count, tall, model = h_all.shape
     rows = tall - HALO
     chan = w_in.shape[0]
-    width = wz.shape[1]
+    width = same.shape[2]
 
     def out(height, columns, dtype):
         return jax.ShapeDtypeStruct((count, height, columns), dtype)
 
     shapes = [out(tall, width, BF16), out(rows, width, F32), out(rows, width, BF16)]
-    shapes += [out(rows, width, F32)] * 5 + [out(8, width, F32)]
-    return call(
-        mixer_enter_kernel,
+    shapes += [out(rows, width, F32)] * 5
+    fixed = [jax.ShapeDtypeStruct((2, count, width), F32)]
+    fixed += [jax.ShapeDtypeStruct((2 * width, width), BF16), jax.ShapeDtypeStruct((16, width), F32)]
+    return call(
+        functools.partial(mixer_enter_kernel, block),
         (count,),
         [
             per_piece((tall, model)),
             per_piece((rows, width)),
             pl.BlockSpec((chan, model), lambda step: (0, 0)),
             pl.BlockSpec((chan, model), lambda step: (0, 1)),
-            resident(wz.shape),
-            resident(par.shape),
+            pl.BlockSpec((chan, extra), lambda step: (0, 3 * model // extra)),
         ],
-        [per_piece(s.shape[1:]) for s in shapes],
-        shapes,
+        [per_piece(s.shape[1:]) for s in shapes] + [resident(s.shape) for s in fixed],
+        shapes + fixed,
         [pltpu.VMEM((width, model), BF16), pltpu.VMEM((width, model), BF16)],
-        2 * count * rows * model * width * 2,
-        count * rows * (model * 2 + width * 32),
-    )(h_all, same, w_in, w_in, wz, par)
+        SWEEP * count * rows * width,
+    )(h_all, same, w_in, w_in, w_in)
 
 
 def column_tile(model):
@@ -367,14 +438,9 @@
             out[...] = total.reshape(out.shape)
 
 
-def fold_piece(refs, index):
-    carry = refs[-1][index, 1:2, :]
-    for ref in refs[-2::-1]:
-        carry = ref[index, 1:2, :] + ref[index, 0:1, :] * carry
-    return carry
-
-
-def mixer_leave_kernel(hops, pieces, groups, *refs):
+def mixer_leave_kernel(hops, pieces, blocks, *refs):
+    groups = len(blocks)
+    first, stride = blocks[0], (blocks[-1] - blocks[0]) // max(1, groups - 1)
     ends = refs[:hops]
     cum, local, y_pre, w_out = refs[hops : hops + 4]
     mixed = refs[-1]
@@ -383,31 +449,30 @@
     @pl.when(pl.program_id(1) == 0)
     def _():
         for index in range(pieces):
-            states = local[index] + cum[index] * fold_piece(ends, index)
+            piece = (first + stride * pl.program_id(0)) * pieces + index
+            states = local[index] + cum[index] * folded(ends, piece)
             mixed[index * rows : index * rows + rows, :] = (gelu_value(y_pre[index]) * states).astype(BF16)
 
     right = padded_rows(w_out[...], mixed.shape[1])
     put_group(refs[hops + 4 : hops + 4 + groups], dot_nn(mixed[...], right).astype(BF16))
 
 
-def mixer_leave(ends, cum, local, y_pre, w_out, blocks, pieces):
+def mixer_leave(ends, cum, local, y_pre, w_in, model, blocks, pieces):
     rows, width = cum.shape[1:]
-    model = w_out.shape[1]
     tile = column_tile(model)
     steps = model // tile
     groups = len(blocks)
     return call(
-        functools.partial(mixer_leave_kernel, len(ends), pieces, groups),
+        functools.partial(mixer_leave_kernel, len(ends), pieces, blocks),
         (groups, steps),
-        [group_of((8, width), blocks, pieces)] * len(ends)
+        [pl.BlockSpec(ends[0].shape, lambda group, step: (0, 0, 0))] * len(ends)
         + [group_of((rows, width), blocks, pieces)] * 3
-        + [pl.BlockSpec((w_out.shape[0], tile), lambda group, step: (0, step))],
+        + [pl.BlockSpec((w_in.shape[0], tile), lambda group, step: (0, 2 * steps + step))],
         group_outs(rows, tile, steps, blocks, pieces),
         [jax.ShapeDtypeStruct((pieces, rows, model), BF16)] * groups,
         [pltpu.VMEM((pieces * rows, width), BF16)],
-        2 * groups * pieces * rows * width * model,
-        groups * pieces * rows * (width * 12 + model * 2),
-    )(*ends, cum, local, y_pre, w_out)
+        3.5 + 3.5 * groups * pieces / 2,
+    )(*ends, cum, local, y_pre, w_in)
 
 
 def head_back_kernel(count, hops, *refs):
@@ -424,7 +489,7 @@
     fetched(d_refs, buf, sems, step)
     put(buf, all_out, all_sems, step).start()
     d_mixed = dot_nt(buf[step], w_all[...])
-    states = local[0] + cum[0] * folded(ends)
+    states = local[0] + cum[0] * folded(ends, step)
     value, slope = gelu_parts(y_pre[0])
     mixed_out[0] = (value * states).astype(BF16)
     dy_out[0] = (slope * d_mixed * states).astype(BF16)
@@ -432,7 +497,7 @@
     width = keep.shape[1]
     next_keep = jnp.concatenate([keep[1:], jnp.ones((1, width), F32)], 0)
     mult, total = scan_into(next_keep, d_mixed * value, cb_out, lb_out, True)
-    ends_out[0] = ends_block(mult * keep[0:1], total * keep[0:1])
+    put_ends(ends_out, step, mult * keep[0:1], total * keep[0:1])
 
     @pl.when(step == count - 1)
     def _():
@@ -440,7 +505,7 @@
             put(buf, all_out, all_sems, index).wait()
 
 
-def head_back(pieces, ends, cum, local, y_pre, keep, w_out):
+def head_back(pieces, ends, cum, local, y_pre, keep, w_in):
     count = len(pieces)
     rows, model = pieces[0].shape
     width = cum.shape[2]
@@ -448,25 +513,25 @@
     def out(height, dtype):
         return jax.ShapeDtypeStruct((count, height, width), dtype)
 
-    shapes = [out(rows, BF16), out(rows, BF16), out(rows, F32), out(rows, F32), out(8, F32)]
+    shapes = [out(rows, BF16), out(rows, BF16), out(rows, F32), out(rows, F32)]
+    ends_shape = jax.ShapeDtypeStruct((2, count, width), F32)
     return call(
         functools.partial(head_back_kernel, count, len(ends)),
         (count,),
         [ANY] * count
-        + [per_piece((8, width))] * len(ends)
+        + [resident(ends[0].shape)] * len(ends)
         + [per_piece((rows, width))] * 4
-        + [resident(w_out.shape)],
-        [per_piece(s.shape[1:]) for s in shapes] + [ANY],
-        shapes + [jax.ShapeDtypeStruct((count, rows, model), BF16)],
+        + [pl.BlockSpec((w_in.shape[0], model), lambda step: (0, 2))],
+        [per_piece(s.shape[1:]) for s in shapes] + [resident(ends_shape.shape), ANY],
+        shapes + [ends_shape, jax.ShapeDtypeStruct((count, rows, model), BF16)],
         [
             pltpu.VMEM((count, rows, model), BF16),
             pltpu.VMEM((width, model), BF16),
             pltpu.SemaphoreType.DMA((count,)),
             pltpu.SemaphoreType.DMA((count,)),
         ],
-        2 * count * rows * width * model,
-        count * rows * (width * 28 + model * 2),
-    )(*pieces, *ends, cum, local, y_pre, keep, w_out)
+        SWEEP * count * rows * width,
+    )(*pieces, *ends, cum, local, y_pre, keep, w_in)
 
 
 def tail_back_kernel(hops, *refs):
@@ -480,8 +545,8 @@
         gw_out[...] = jnp.zeros_like(gw_out)
         small_out[...] = jnp.zeros_like(small_out)
 
-    state_in = folded(ends)
-    d_states = lb[0] + cb[0] * folded(later)
+    state_in = folded(ends, step)
+    d_states = lb[0] + cb[0] * folded(later, step)
     states = local[0] + cum[0] * state_in
     prev = jnp.concatenate([state_in, states[:-1]], 0)
     recur, enter, keep = r_ref[0], e_ref[0], k_ref[0]
@@ -526,20 +591,7 @@
 
     @pl.when(step == pl.num_programs(0) - 1)
     def _():
-        block = fold_out.shape[1]
-        row = lax.broadcasted_iota(jnp.int32, (width, width), 0)
-        column = lax.broadcasted_iota(jnp.int32, (width, width), 1)
-        inside = None
-        for start in range(0, width, block):
-            here = (row >= start) & (row < start + block) & (column >= start) & (column < start + block)
-            inside = here if inside is None else inside | here
-        row = lax.broadcasted_iota(jnp.int32, (width, block), 0)
-        column = lax.broadcasted_iota(jnp.int32, (width, block), 1)
-        fold = None
-        for start in range(0, width, block):
-            here = row - start == column
-            fold = here if fold is None else fold | here
-        fold = jnp.where(fold, 1.0, 0.0).astype(BF16)
+        inside, fold = block_masks(width, fold_out.shape[1])
         for gate in (0, 1):
             whole = jnp.where(inside, gw_out[gate * width : gate * width + width, :], 0.0).astype(BF16)
             fold_out[gate * width : gate * width + width, :] = dot_nn(whole, fold).astype(BF16)
@@ -557,14 +609,13 @@
     return call(
         functools.partial(tail_back_kernel, len(ends)),
         (count,),
-        [per_piece((8, width))] * (2 * len(ends))
+        [resident(ends[0].shape)] * (2 * len(ends))
         + [per_piece((rows, width))] * 8
         + [per_piece((tall, width)), per_piece((rows, width)), resident(wz.shape), resident(par.shape)],
         [per_piece((rows, width)), per_piece((16, width)), resident((2 * width, block)), resident((8, width))],
         shapes,
         [pltpu.VMEM(wz.shape, F32)],
-        8 * count * rows * width * width,
-        count * rows * width * 36,
+        SWEEP * count * rows * width,
     )(*ends, *later, cb, lb, cum, local, recur, enter, keep, conv, u_ext, same, wz, par)
 
 
@@ -614,8 +665,7 @@
         out_specs,
         shapes,
         [],
-        2 * groups * pieces * rows * inner * model,
-        groups * pieces * rows * 2 * (inner + model) + 2 * inner * model,
+        3 + 2 * groups * pieces * rows * inner * model / RATE,
     )(*lefts, *[right for right, _, _ in rights], *([factor] if gained else []))
 
 
@@ -639,116 +689,270 @@
         ANY,
         jax.ShapeDtypeStruct(shape, pieces[0].dtype),
         [pltpu.VMEM(shape, pieces[0].dtype), pltpu.SemaphoreType.DMA((count,)), pltpu.SemaphoreType.DMA((count,))],
-        0,
-        4 * count * pieces[0].size,
+        6.5,
     )(*pieces)
 
 
-def mlp_enter_kernel(count, *refs):
-    h_refs = refs[:count]
-    wg, wu, hid_out, turn_out, value_out, all_out, buf, sems, all_sems = refs[count:]
+def mlp_kernel(count, first, *refs):
+    sources = count if first else 1
+    h_refs = refs[:count] if first else [refs[0].at[index] for index in range(count)]
+    c_ref, wg, wu, wo, hid_out, dg_out, du_out = refs[sources : sources + 7]
+    rest = refs[sources + 7 :]
+    all_out = rest[0] if first else None
+    h_buf, c_buf, h_sems, c_sems, all_sems = rest[-5:]
     step = pl.program_id(0)
     pair = 2 if count % 2 == 0 else 1
     rows, tile = hid_out.shape[1:]
+    model = h_buf.shape[2]
 
     @pl.when(step == 0)
     def _():
-        fetch_all(h_refs, buf, sems)
+        for index in range(count):
+            pltpu.make_async_copy(h_refs[index], h_buf.at[index], h_sems.at[index]).start()
+            pltpu.make_async_copy(c_ref.at[index], c_buf.at[index], c_sems.at[index]).start()
 
     def some_pieces(index, carry):
         @pl.when(step == 0)
         def _():
             for place in range(pair):
-                fetched(h_refs, buf, sems, index * pair + place)
-                put(buf, all_out, all_sems, index * pair + place).start()
+                at = index * pair + place
+                fetched(h_refs, h_buf, h_sems, at)
+                pltpu.make_async_copy(c_ref.at[0], c_buf.at[at], c_sems.at[at]).wait()
+                if first:
+                    put(h_buf, all_out, all_sems, at).start()
 
         span = pl.ds(index * pair, pair)
-        h_low = buf[span].reshape(pair * rows, buf.shape[2])
+        h_low = h_buf[span].reshape(pair * rows, model)
         gate = dot_nt(h_low, wg[...])
         up = dot_nt(h_low, wu[...])
+        d_hidden = dot_nt(c_buf[span].reshape(pair * rows, model), wo[...])
         value, slope = gelu_parts(gate)
         shape = (pair, rows, tile)
         hid_out[span] = (value * up).astype(BF16).reshape(shape)
-        turn_out[span] = (up * slope).reshape(shape)
-        value_out[span] = value.reshape(shape)
+        dg_out[span] = (d_hidden * up * slope).astype(BF16).reshape(shape)
+        du_out[span] = (d_hidden * value).astype(BF16).reshape(shape)
         return carry
 
     lax.fori_loop(0, count // pair, some_pieces, 0)
 
-    @pl.when(step == pl.num_programs(0) - 1)
-    def _():
-        for index in range(count):
-            put(buf, all_out, all_sems, index).wait()
+    if first:
+
+        @pl.when(step == pl.num_programs(0) - 1)
+        def _():
+            for index in range(count):
+                put(h_buf, all_out, all_sems, index).wait()
 
 
 def hidden_tile(hidden):
     return next(t for t in (256, 128, hidden) if hidden % t == 0)
 
 
-def mlp_enter(h_pieces, w_both):
-    count = len(h_pieces)
-    rows, model = h_pieces[0].shape
-    hidden = w_both.shape[0]
+def mlp_part(h_rows, c_all, weights):
+    first = isinstance(h_rows, list)
+    count, rows, model = c_all.shape
+    hidden = weights.shape[0]
     tile = hidden_tile(hidden)
-    out_spec = pl.BlockSpec((count, rows, tile), lambda step: (0, 0, step))
-    return call(
-        functools.partial(mlp_enter_kernel, count),
+    spec = pl.BlockSpec((count, rows, tile), lambda step: (0, 0, step))
+    whole = jax.ShapeDtypeStruct((count, rows, model), BF16)
+    sources = h_rows if first else [h_rows]
+
+    def column(place):
+        return pl.BlockSpec((tile, model), lambda step: (step, place))
+
+    return call(
+        functools.partial(mlp_kernel, count, first),
         (hidden // tile,),
-        [ANY] * count
-        + [pl.BlockSpec((tile, model), lambda step: (step, 0)), pl.BlockSpec((tile, model), lambda step: (step, 1))],
-        [out_spec] * 3 + [ANY],
+        [ANY] * (len(sources) + 1) + [column(0), column(1), column(2)],
+        [spec] * 3 + [ANY] * first,
+        [jax.ShapeDtypeStruct((count, rows, hidden), BF16)] * 3 + [whole] * first,
         [
-            jax.ShapeDtypeStruct((count, rows, hidden), BF16),
-            jax.ShapeDtypeStruct((count, rows, hidden), F32),
-            jax.ShapeDtypeStruct((count, rows, hidden), F32),
-            jax.ShapeDtypeStruct((count, rows, model), BF16),
-        ],
-        [
+            pltpu.VMEM((count, rows, model), BF16),
             pltpu.VMEM((count, rows, model), BF16),
             pltpu.SemaphoreType.DMA((count,)),
             pltpu.SemaphoreType.DMA((count,)),
+            pltpu.SemaphoreType.DMA((count,)),
         ],
-        4 * count * rows * model * hidden,
-        count * rows * (4 * model + 10 * hidden) + 4 * model * hidden,
-    )(*h_pieces, w_both, w_both)
-
-
-def mlp_back_kernel(c_ref, wo, turn, value, dg_out, du_out):
-    count, rows, tile = dg_out.shape
-    pair = 2 if count % 2 == 0 else 1
-
-    def some_pieces(index, carry):
-        span = pl.ds(index * pair, pair)
-        d_hidden = dot_nt(c_ref[span].reshape(pair * rows, c_ref.shape[2]), wo[...])
-        d_hidden = d_hidden.reshape(pair, rows, tile)
-        dg_out[span] = (d_hidden * turn[span]).astype(BF16)
-        du_out[span] = (d_hidden * value[span]).astype(BF16)
-        return carry
-
-    lax.fori_loop(0, count // pair, some_pieces, 0)
-
-
-def mlp_back(c_all, w_down, turn, value):
-    count, rows, model = c_all.shape
-    hidden = w_down.shape[0]
-    tile = hidden_tile(hidden)
-    spec = pl.BlockSpec((count, rows, tile), lambda step: (0, 0, step))
-    return call(
-        mlp_back_kernel,
-        (hidden // tile,),
-        [resident(c_all.shape), pl.BlockSpec((tile, model), lambda step: (step, 0)), spec, spec],
-        [spec] * 2,
-        [jax.ShapeDtypeStruct((count, rows, hidden), BF16)] * 2,
+        2 + 6 * count * rows * model * hidden / RATE,
+    )(*sources, c_all, weights, weights, weights)
+
+
+def mlp_grads_kernel(tiles, dg, du, hid, h_tile, c_tile, out, turned):
+    step = pl.program_id(0)
+    for place, left in enumerate((dg, du, hid)):
+
+        @pl.when(step == place * tiles)
+        def _(left=left):
+            turned[...] = left[...].T
+
+    @pl.when(step < 2 * tiles)
+    def _():
+        out[...] = dot_nn(turned[...], h_tile[...]).astype(BF16)
+
+    @pl.when(step >= 2 * tiles)
+    def _():
+        out[...] = dot_nn(turned[...], c_tile[...]).astype(BF16)
+
+
+def mlp_grads(d_gate, d_up, hidden, h_all, c_all):
+    model = h_all.shape[2]
+    lefts = [v.reshape(-1, v.shape[2]) for v in (d_gate, d_up, hidden)]
+    rights = [v.reshape(-1, model) for v in (h_all, c_all)]
+    inner, tall = lefts[0].shape
+    tile = column_tile(model)
+    tiles = model // tile
+    return call(
+        functools.partial(mlp_grads_kernel, tiles),
+        (3 * tiles,),
+        [resident((inner, tall))] * 3
+        + [
+            pl.BlockSpec((inner, tile), lambda step: (0, jnp.where(step < 2 * tiles, step % tiles, tiles - 1))),
+            pl.BlockSpec((inner, tile), lambda step: (0, jnp.maximum(step - 2 * tiles, 0))),
+        ],
+        pl.BlockSpec((tall, tile), lambda step: (0, step)),
+        jax.ShapeDtypeStruct((tall, 3 * model), BF16),
+        [pltpu.VMEM((tall, inner), BF16)],
+        3 + 6 * inner * tall * model / RATE,
+    )(*lefts, *rights)
+
+
+def weight_grads_kernel(tiles, count, *refs):
+    lefts, rights, out, turned = refs[:count], refs[count : 2 * count], refs[2 * count], refs[2 * count + 1]
+    step = pl.program_id(0)
+    for place in range(count):
+
+        @pl.when(step == place * tiles)
+        def _(left=lefts[place]):
+            turned[...] = left[...].T
+
+        @pl.when((step >= place * tiles) & (step < (place + 1) * tiles))
+        def _(right=rights[place]):
+            out[...] = dot_nn(turned[...], right[...])[: out.shape[0]].astype(BF16)
+
+
+def weight_grads(pairs, kept):
+    lefts = [left.reshape(-1, left.shape[-1]) for left, _ in pairs]
+    rights = [right.reshape(-1, right.shape[-1]) for _, right in pairs]
+    count = len(pairs)
+    inner, tall = lefts[0].shape
+    model = rights[0].shape[1]
+    tile = column_tile(model)
+    tiles = model // tile
+
+    def right_spec(place):
+        return pl.BlockSpec((inner, tile), lambda step: (0, jnp.clip(step - place * tiles, 0, tiles - 1)))
+
+    return call(
+        functools.partial(weight_grads_kernel, tiles, count),
+        (count * tiles,),
+        [resident((inner, tall))] * count + [right_spec(place) for place in range(count)],
+        pl.BlockSpec((kept, tile), lambda step: (0, step)),
+        jax.ShapeDtypeStruct((kept, count * model), BF16),
+        [pltpu.VMEM((tall, inner), BF16)],
+        3 + 2 * count * inner * tall * model / RATE,
+    )(*lefts, *rights)
+
+
+def add_kernel(counts, *refs):
+    at = 0
+    for count, out in zip(counts, refs[sum(counts) :]):
+        total = refs[at][0].astype(F32)
+        for ref in refs[at + 1 : at + count]:
+            total = total + ref[0].astype(F32)
+        out[...] = total.astype(BF16)
+        at += count
+
+
+def add_rows(sums):
+    arrays = [array for terms in sums for array, _ in terms]
+    places = [index for terms in sums for _, index in terms]
+    _, rows, width = arrays[0].shape
+    steps = 4
+    tall = rows // steps
+
+    def spec(place):
+        return pl.BlockSpec((1, tall, width), lambda step: (place, step, 0))
+
+    counts = [len(terms) for terms in sums]
+    return call(
+        functools.partial(add_kernel, counts),
+        (steps,),
+        [spec(place) for place in places],
+        [pl.BlockSpec((tall, width), lambda step: (step, 0))] * len(sums),
+        [jax.ShapeDtypeStruct((rows, width), BF16)] * len(sums),
         [],
-        2 * count * rows * model * hidden,
-        count * rows * (2 * model + 12 * hidden) + 2 * model * hidden,
-    )(c_all, w_down, turn, value)
-
-
-def weight_grad(rows_left, rows_right):
-    left = rows_left.reshape(-1, rows_left.shape[-1])
-    right = rows_right.reshape(-1, rows_right.shape[-1])
-    return dot_tn(left, right).astype(BF16)
+        1 + 0.6 * len(arrays),
+    )(*arrays)
+
+
+def last_kernel(terms, *refs):
+    rows, base, gain, out = refs[terms:]
+    total = refs[0][0].astype(F32)
+    for ref in refs[1:terms]:
+        total = total + ref[0].astype(F32)
+    if gain is not None:
+        x_val = rows[...].astype(F32)
+        root = lax.rsqrt(jnp.mean(x_val * x_val, axis=-1, keepdims=True) + EPS)
+        x_val = x_val * root
+        total = total * gain[...]
+        total = root * (total - x_val * jnp.mean(total * x_val, axis=-1, keepdims=True))
+    out[...] = (base[...] + total).astype(BF16)
+
+
+def last_rows(terms, base, rows=None, gain=None):
+    tall, model = base.shape
+    steps = 4
+    block = pl.BlockSpec((tall // steps, model), lambda step: (step, 0))
+
+    def spec(place):
+        return pl.BlockSpec((1, tall // steps, model), lambda step: (place, step, 0))
+
+    extra = [] if gain is None else [rows]
+    kernel = last_kernel if gain is not None else lambda count, *refs: last_kernel(
+        count, *refs[:count], None, refs[count], None, refs[count + 1]
+    )
+    return call(
+        functools.partial(kernel, len(terms)),
+        (steps,),
+        [spec(place) for _, place in terms]
+        + [block] * (len(extra) + 1)
+        + ([] if gain is None else [resident(gain.shape)]),
+        block,
+        jax.ShapeDtypeStruct((tall, model), BF16),
+        [],
+        6.0,
+    )(*[array for array, _ in terms], *extra, base, *([] if gain is None else [gain]))
+
+
+def split_grads_kernel(one_gate, one_up, one_down, two_gate, two_up, two_down, both, down):
+    cut = one_gate.shape[0]
+    both[:cut, 0, :] = one_gate[...].astype(F32)
+    both[:cut, 1, :] = one_up[...].astype(F32)
+    both[cut:, 0, :] = two_gate[...].astype(F32)
+    both[cut:, 1, :] = two_up[...].astype(F32)
+    down[:cut, :] = one_down[...].astype(F32)
+    down[cut:, :] = two_down[...].astype(F32)
+
+
+def split_grads(one, two, model):
+    rows = one.shape[0] + two.shape[0]
+    tile = column_tile(model)
+    steps = model // tile
+
+    def spec(part, place):
+        return pl.BlockSpec((part.shape[0], tile), lambda step: (0, place * steps + step))
+
+    return call(
+        split_grads_kernel,
+        (steps,),
+        [spec(part, place) for part in (one, two) for place in range(3)],
+        [
+            pl.BlockSpec((rows, 2, tile), lambda step: (0, 0, step)),
+            pl.BlockSpec((rows, tile), lambda step: (0, step)),
+        ],
+        [jax.ShapeDtypeStruct((rows, 2, model), F32), jax.ShapeDtypeStruct((rows, model), F32)],
+        [],
+        6.0,
+    )(one, one, one, two, two, two)
 
 
 def seq_gather(shard):
@@ -785,7 +989,7 @@
     blocks = chan // block
 
     x_low = tokens.reshape(run_len, model)
-    x_pieces = gather_rows(x_low)
+    x_pieces, _ = gather_rows(x_low)
     x_zero = x_low.astype(F32)
     cot_low = cotangent.reshape(run_len, model)
     lead = hand_on(x_low[run_len - HALO :], 1)
@@ -807,7 +1011,7 @@
         for back in (1, 2, 3)
     )
     info = jnp.pad(same, (0, model - run_len)).astype(BF16)[None]
-    tops = gather_rows(jnp.concatenate([info, gain_rows, lead[2:]], 0))
+    tops, _ = gather_rows(jnp.concatenate([info, gain_rows, lead[2:]], 0))
     count = len(tops)
     half = count // 2
 
@@ -823,23 +1027,13 @@
     )
     extra = -(-small.shape[1] // 128) * 128
     small = jnp.pad(small, ((0, 0), (0, extra - small.shape[1])))
-    w_in = seq_gather(jnp.concatenate([mix_in[:, 1, :], mix_in[:, 0, :], small], 1).astype(BF16))
-    w_out = seq_gather(mix_out.astype(BF16))
+    w_in = jnp.concatenate([mix_in[:, 1, :], mix_in[:, 0, :], mix_out, small], 1).astype(BF16)
+    w_in = seq_gather(w_in)
     mlp_in, mlp_out = after((mlp_in, mlp_out), lead)
-    both_shard = mlp_in.astype(BF16).reshape(-1, 2 * model)
-    down_shard = mlp_out.astype(BF16)
-    w_both = seq_gather(both_shard)
-    w_down = seq_gather(down_shard)
-
-    w_small = w_in[:, 2 * model :]
-    gate_rows = w_small[:, : 2 * block].reshape(blocks, block, 2, block)
-    eye = jnp.eye(blocks, dtype=BF16)
-    w_z = jnp.einsum("bogj,bc->gbocj", gate_rows, eye).reshape(2, chan, chan)
-    w_z = jnp.pad(w_z, ((0, 0), (0, width - chan), (0, width - chan))).reshape(2 * width, width)
-    par = w_small[:, 2 * block : 2 * block + 8].astype(F32).T
-    decay_rate = -SHARP * jax.nn.softplus(par[7])
-    decay_slope = -SHARP * jax.nn.sigmoid(par[7])
-    par = jnp.pad(jnp.concatenate([par[:7], decay_rate[None]], 0), ((0, 0), (0, width - chan)))
+    shard = jnp.concatenate([mlp_in.astype(BF16).reshape(-1, 2 * model), mlp_out.astype(BF16)], 1)
+    cut = 2 * shard.shape[0] // 3
+    shards = [shard[:cut], shard[cut:]]
+    w_one, w_two = [seq_gather(rows) for rows in shards]
 
     orders = jnp.asarray(piece_order(count), jnp.int32)
     order = lax.dynamic_index_in_dim(after(orders, lead), lax.axis_index("dp"), 0, False)
@@ -853,102 +1047,83 @@
     g_two = gain_rows[:, part:].reshape(1, model)
 
     h_all, h_one, same = first_norm(x_pieces, tops, g_one, width)
-    entered = mixer_enter(after(h_all, both_shard, down_shard), same, w_in, w_z, par)
-    (u_ext, y_pre, conv, recur, enter, keep, cum, local, ends) = entered
-    c_pieces = gather_rows(after(cot_low, *x_pieces), [lambda sent: ends])
-    ends = after(ends, w_out)
+    c_pieces, (same, entered) = gather_rows(
+        after(cot_low, *x_pieces),
+        [
+            ((1,), lambda sent, done: same),
+            ((2, 3), lambda sent, done: mixer_enter(after(h_all, shards), done[0], w_in, extra, block)),
+        ],
+    )
+    (u_ext, y_pre, conv, recur, enter, keep, cum, local, ends, w_z, par) = entered
     earlier = [hand_on(ends, steps) for steps in range(1, n_seq)]
-    earlier, c_pieces = lax.optimization_barrier((earlier, c_pieces[:half])), c_pieces
-    earlier, c_pieces[:half] = earlier
 
     def leaving(blocks_at, pieces, before):
-        return mixer_leave(earlier, cum, local, after(y_pre, *before), w_out, blocks_at, pieces)
+        return mixer_leave(earlier, cum, local, after(y_pre, *before), w_in, model, blocks_at, pieces)
 
     kept = []
     x_one = x_zero + scatter_rows(leaving, count, None)
     n_two, norm_two_back = jax.vjp(rms_norm, x_one, g_two)
     h_two = n_two.astype(BF16)
 
-    h_pieces = gather_rows(h_two, [lambda sent: assemble(after(c_pieces, *sent))], kept)
-    c_all = kept.pop()
-    hidden, turn, value, h_all = mlp_enter(h_pieces, w_both)
-    grad_down = weight_grad(hidden, c_all)
-    turn = after(turn, grad_down)
-    grad_down = seq_scatter(grad_down)
-    d_gate, d_up = mlp_back(c_all, w_down, turn, value)
+    h_pieces, (c_all,) = gather_rows(h_two, [((1, 2), lambda sent, done: assemble(after(c_pieces, sent)))])
+    hid_one, gate_one, up_one, h_all = mlp_part(h_pieces, c_all, w_one)
+    grad_one = mlp_grads(gate_one, up_one, hid_one, h_all, c_all)
+    hid_two, gate_two, up_two = mlp_part(after(h_all, grad_one), c_all, w_two)
+    grad_one = seq_scatter(grad_one)
 
     def d_entering(blocks_at, pieces, before):
-        d_one = after(d_gate, *before)
-        return rows_times([d_one, d_up], [(w_both, 0, model), (w_both, 1, model)], blocks_at, pieces)
-
-    def gate_grad(sent):
-        kept.append(weight_grad(after(d_gate, sent), h_all))
-        return kept[-1]
-
-    def up_grad(sent):
-        kept.append(weight_grad(after(d_up, sent), h_all))
-        return kept[-1]
-
-    d_h_two = scatter_rows(d_entering, count, beside(gate_grad))
-    grad_gate = seq_scatter(kept[-1])
+        lefts = [after(gate_one, *before), up_one, gate_two, up_two]
+        rights = [(w_one, 0, model), (w_one, 1, model), (w_two, 0, model), (w_two, 1, model)]
+        return rows_times(lefts, rights, blocks_at, pieces)
+
+    def second_grads(sent, done):
+        return mlp_grads(after(gate_two, sent), up_two, hid_two, h_all, c_all)
+
+    def mlp_leaving(blocks_at, pieces, before):
+        return rows_times([after(hid_one, *before), hid_two], [(w_one, 2, model), (w_two, 2, model)], blocks_at, pieces)
+
+    def mlp_out_rows(sent):
+        return mlp_leaving([1, 0], half, (sent,))
+
+    d_h_two = scatter_rows(d_entering, count, beside(mlp_out_rows, kept))
     d_x_norm, d_gain_two = norm_two_back(d_h_two)
     d_x_one = cot_low.astype(F32) + d_x_norm
     d_mix = d_x_one.astype(BF16)
 
-    def mlp_leaving(blocks_at, pieces, before):
-        return rows_times([after(hidden, *before)], [(w_down, 0, model)], blocks_at, pieces)
-
     stages, twin = plane_stages(lax.axis_size("dp"))
 
-    def mlp_out_rows(sent):
-        nonlocal hidden
-        hidden = after(hidden, sent)
-        return mlp_leaving([1, 0], half, ())
-
-    def up_grad_and_sums(sent):
-        theirs, mine = kept.pop()
+    def mlp_out_sums(sent, done):
+        theirs, mine = after(kept.pop(), sent)
         there = lax.ppermute(theirs, "dp", twin)
-        far = [total_of([mine[k], there[k]]).astype(BF16) for k in range(half // 2, half)]
-        kept.append((mine, there, far))
-        return up_grad(sent), far
-
-    d_pieces = gather_rows(d_mix, [mlp_out_rows, up_grad_and_sums], kept)
-    kept.pop()
-    grad_up = kept.pop()
-    mine, there, far = kept.pop()
+        return mine, there, add_rows([[(mine, k), (there, k)] for k in range(half // 2, half)])
+
+    d_pieces, done = gather_rows(d_mix, [((1, 2), second_grads), ((3,), mlp_out_sums)])
+    grad_two, (mine, there, far) = done
+    grad_two = seq_scatter(after(grad_two, grad_one))
     d_y, mixed, cum_back, local_back, ends_back, d_all = head_back(
-        after(d_pieces, far), earlier, cum, local, y_pre, keep, w_out
+        after(d_pieces, far), earlier, cum, local, y_pre, keep, w_in
     )
     got = [lax.ppermute(part, "dp", stages[-1]) for part in far]
-    ends_back, got = lax.optimization_barrier((ends_back, got))
+    mixed, got = lax.optimization_barrier((mixed, got))
     later = [hand_on(ends_back, -steps) for steps in range(1, n_seq)]
-    grad_y = weight_grad(after(d_y, ends_back), h_one)[:chan]
-    grad_out = weight_grad(after(mixed, ends_back), d_all)[:chan]
-    grad_y_out = jnp.concatenate([grad_y, grad_out], 1)
+    grad_y_out = weight_grads([(after(d_y, ends_back), h_one), (mixed, d_all)], chan)
     later, grad_y_out = lax.optimization_barrier((later, grad_y_out))
-    grad_up = seq_scatter(grad_up)
-    grad_y_out = seq_scatter(grad_y_out)
-
-    def tail_work(sent, got):
-        nonlocal tailed
-        tailed = tail_back(
-            earlier, after(later, sent), cum_back, local_back, cum, local, recur, enter, keep, conv, u_ext, same, w_z, par, block
-        )
-        tailed, got = lax.optimization_barrier((tailed, got))
-        return got
-
-    tailed = None
-    terms = [[mine[k], there[k], got[k]] for k in range(half // 2)]
-    layer_out = x_one + scatter_tail(terms, stages[:-1], [tail_work])
-    layer_out = layer_out.astype(BF16).reshape(1, run_len, model)
-    d_u, edges, grad_z, sums = tailed
+    grad_y_out = seq_scatter(after(grad_y_out, grad_two))
+    d_u, edges, grad_z, sums = tail_back(
+        earlier, later, cum_back, local_back, cum, local, recur, enter, keep, conv, u_ext, same, w_z, par, block
+    )
     from_next = hand_on(edges[:, :8], -1)
+    terms = [[(mine, k), (there, k), (got[k][None], 0)] for k in range(half // 2)]
+    held = terms[half // 4 :]
+    arrays = after([[array for array, _ in those] for those in held], edges)
+    layer_sums = add_rows([[(v, at) for v, (_, at) in zip(vs, those)] for vs, those in zip(arrays, held)])
+    from_next, layer_sums = lax.optimization_barrier((from_next, layer_sums))
+    layer_got = [lax.ppermute(part, "dp", stages[-2]) for part in layer_sums]
     grad_z = jnp.concatenate([grad_z[:chan], grad_z[width : width + chan]], 1)
     sums = sums[:, :chan]
-    sums = jnp.concatenate([sums[:7], (sums[7] * decay_slope)[None]], 0).T
+    sums = jnp.concatenate([sums[:7], (sums[7] * (-SHARP * jax.nn.sigmoid(par[15, :chan])))[None]], 0).T
     tail = jnp.concatenate([grad_z, sums.astype(BF16)], 1)
     tail = jnp.pad(tail, ((0, 0), (0, extra - tail.shape[1])))
-    from_next, layer_out = lax.optimization_barrier((from_next, layer_out))
     d_u = lax.dynamic_update_slice(d_u, (edges[:, 8:] + from_next).astype(BF16), (0, run_len - 8, 0))
     gain_terms = []
 
@@ -957,24 +1132,23 @@
             [after(d_y, *before), d_u], [(w_in, 1, model), (w_in, 0, model)], blocks_at, pieces, h_one
         )
         gain_terms.append(gain_term.sum(0))
+        if blocks_at == [1]:
+            part_rows[0], layer_got[:] = lax.optimization_barrier((part_rows[0], layer_got))
         return part_rows
 
     def u_grad(sent):
-        kept.append(weight_grad(after(d_u, sent, grad_down, grad_gate, grad_up, grad_y_out), h_one))
-        return kept[-1]
-
-    d_h_one = scatter_rows(d_leaving, count, beside(u_grad))
-    grad_u = seq_scatter(jnp.concatenate([kept[-1][:chan], tail], 1))
-    _, norm_one_back = jax.vjp(lambda values: rms_norm(values, g_one), x_zero)
-    input_grad = (d_x_one + norm_one_back(d_h_one)[0]).astype(BF16)
+        return weight_grads([(after(d_u, sent), h_one)], chan)
+
+    d_h_one = scatter_terms(d_leaving, count, None, beside(u_grad, kept))
+    grad_u = seq_scatter(after(jnp.concatenate([kept.pop(), tail], 1), grad_y_out))
+    input_grad = last_rows(d_h_one, d_x_one, x_low, g_one).reshape(1, run_len, model)
+    terms = [[*those, (one[None], 0)] for those, one in zip(terms, layer_got)]
+    layer_terms = scatter_tail(terms, stages[:-2], [])
+    layer_out = last_rows(layer_terms, x_one).reshape(1, run_len, model)
     d_gain_one = sum(gain_terms) / g_one
     d_gains = jnp.concatenate([d_gain_one.reshape(n_dev, part), d_gain_two.reshape(n_dev, part)], 1)
-    grads = lax.optimization_barrier((kept[-1], grad_gate, grad_up, grad_down, grad_y_out))[1:]
-    rest = (d_gains, *grads)
-    input_grad, rest = lax.optimization_barrier((input_grad, rest))
-    (d_gains, grad_gate, grad_up, grad_down, grad_y_out) = rest
-    input_grad = input_grad.reshape(1, run_len, model)
-    d_gains = lax.all_to_all(d_gains, ("dp", "seq"), 0, 0, tiled=True).sum(0)
+    d_gains = lax.all_to_all(after(d_gains, input_grad), ("dp", "seq"), 0, 0, tiled=True).sum(0)
+    grad_mlp_in, grad_mlp_out = split_grads(after(grad_one, input_grad), grad_two, model)
 
     tail = grad_u[:, model:].astype(F32)
     grad_mix_in = jnp.stack([grad_y_out[:, :model].astype(F32), grad_u[:, :model].astype(F32)], 1)
@@ -991,8 +1165,8 @@
         tail[:, at + 7],
         d_gains[:part],
         d_gains[part:],
-        jnp.stack([grad_gate.astype(F32), grad_up.astype(F32)], 1),
-        grad_down.astype(F32),
+        grad_mlp_in,
+        grad_mlp_out,
     )
 
 

time: 655 us -> 617 us (0.942)
  Pallas kernels: 203 us -> 311 us
  matrix products: 51.2 us -> 0 us
  waiting for transfers between devices: 194 us -> 150 us
  other arithmetic: 81.4 us -> 38.2 us
  starting transfers between devices: 66 us -> 58.7 us
    pallas_call x7 -> x22, Pallas kernels: 101 us -> 210 us  [the longest x2 43.1 us: mlp_grads(): call(functools.partial(mlp_grads_kernel, tiles), (3 * tiles,), [resident(...]
    dot_general x6 -> x0, matrix products: 51.2 us -> none  [dot_tn(): lax.dot_general(left, right, (((0,), (0,)), ((), ())), preferred_element_...]
    all_gather x4 -> x3, waiting for transfers between devices: 45.6 us -> 0.02 us  [seq_gather(): return lax.all_gather(shard, 'seq', axis=0, tiled=True)]
    convert_element_type x14 -> x2, other arithmetic: 41 us -> 3.47 us  [the longest x1 3.37 us: per_device(): mlp_in.astype(BF16).reshape(-1, 2 * model)]
    reduce_scatter x5 -> x4, waiting for transfers between devices: 35.2 us -> 4.9 us  [seq_scatter(): return lax.psum_scatter(whole, 'seq', scatter_dimension=0, tiled=True)]
    ppermute x48 -> x49, waiting for transfers between devices: 83.5 us -> 105 us  [the longest x15 64.4 us: arrival(): return lax.ppermute(held[m ^ 1 << top], 'dp', stages[top])]
    ppermute x4 -> x3, waiting for transfers between devices: 12.1 us -> 25.3 us  [scatter_tail(): got = [lax.ppermute(part, 'dp', pairs) for part in sent]]
    unnamed x121 -> x128, local copies, waits for them, and re-layouts: 17.6 us -> 22.8 us
  transfers between devices with their start and end apart: 75 -> 73, of which waited for: 30 -> 30; matrix products, arithmetic and copies ran while one was open for 22% -> 6% of each run, Pallas kernels for 27% -> 51%
where the time goes in v3:
time: 617 us; the launch traced here: 606 us
  Pallas kernels  311 us (50%)
  waiting for transfers between devices  150 us (24%)
  starting transfers between devices  58.7 us (10%)
  other arithmetic  38.2 us (6%)
  local copies, waits for them, and re-layouts  32.6 us (5%)
  between operations  15.7 us (3%)
    pallas_call x7, Pallas kernels, rows_times(): call(functools.partial(rows_times_kernel, len(lefts), gained), (groups, s...  65.7 us
    ppermute x15, waiting for transfers between devices, arrival(): return lax.ppermute(held[m ^ 1 << top], 'dp', stages[top])  64.4 us
    pallas_call x2, Pallas kernels, mlp_grads(): call(functools.partial(mlp_grads_kernel, tiles), (3 * tiles,), [resident(...  43.1 us
    pallas_call x2, Pallas kernels, mlp_part(): call(functools.partial(mlp_kernel, count, first), (hidden // tile,), [ANY...  34.4 us
    pallas_call x8, Pallas kernels, add_rows(): call(functools.partial(add_kernel, counts), (steps,), [spec(place) for pl...  32.4 us
    ppermute x3, waiting for transfers between devices, scatter_tail(): got = [lax.ppermute(part, 'dp', pairs) for part in sent]  25.3 us
    pallas_call x2, Pallas kernels, weight_grads(): call(functools.partial(weight_grads_kernel, tiles, count), (count * tiles...  23.4 us
    unnamed x128, local copies, waits for them, and re-layouts  22.8 us
  transfers between devices with their start and end apart: 73, of which 30 were waited for; matrix products, arithmetic and copies ran while one was open for 6% of the time, Pallas kernels for 51%

profile of v3, /device:TPU:0, one launch (start us, length us, event | category | flops | bytes accessed | tf_op | source)
XLA Modules:
  0.0 606.0 jit_solution(2320323327039085445)
XLA Ops:
  38.9 11.1 %collective-permute-done.refs_1_ = bf16[256,2048]{1,0:T(8,128)(2,1)} collective-permute-done((bf16[256,2048]{1,0:T(8,128)(2,1)S(1)}, bf16[256,2048]{1,0:T(8,128)(2,1)}, u32[]{:S(2)}, u32[]{:S(2)}) %collective-permute-start) | collective-permute-done | bytes 1048608 | tf_op jit(solution)/shard_map/ppermute | solution.py:76
  81.0 10.7 %shard_map.246 = (bf16[8,272,2048]{2,1,0:T(8,128)(2,1)}, bf16[8,256,2048]{2,1,0:T(8,128)(2,1)}, bf16[8,256,384]{2,1,0:T(8,128)(2,1)}) custom-call(bf16[256,2048]{1,0:T(8,128)(2,1)} %bitcast.126, bf16[256,2048]{1,0:T(8,128)(2,1)} %collective-permute-done.refs_1_, bf16[256,2048]{1,0:T(8,128)(2,1)} %collective-permute-done.1.refs_2_, ...), custom_call_target="tpu_custom_call" | custom-call | flops 2786882048 | bytes 1024 | tf_op jit(solution)/shard_map/pallas_call | solution.py:252
  91.7 9.6 %collective-permute-done.8.refs_1_ = bf16[256,2048]{1,0:T(8,128)(2,1)} collective-permute-done((bf16[256,2048]{1,0:T(8,128)(2,1)}, bf16[256,2048]{1,0:T(8,128)(2,1)}, u32[]{:S(2)}, u32[]{:S(2)}) %collective-permute-start.8) | collective-permute-done | bytes 1048608 | tf_op jit(solution)/shard_map/ppermute | solution.py:76
  104.1 22.1 %shard_map.247 = (bf16[8,272,384]{2,1,0:T(8,128)(2,1)}, f32[8,256,384]{2,1,0:T(8,128)}, bf16[8,256,384]{2,1,0:T(8,128)(2,1)}, f32[8,256,384]{2,1,0:T(8,128)}, f3...) custom-call(bf16[8,272,2048]{2,1,0:T(8,128)(2,1)} %get-tuple-element, ...), custom_call_target="tpu_custom_call" | custom-call | flops 5024426496 | bytes 1024 | tf_op jit(solution)/shard_map/pallas_call | solution.py:395
  135.1 5.6 shard_map.248
  140.7 5.7 shard_map.249.refs_0_.refs_2_
  152.0 10.4 %shard_map.251 = (bf16[2,256,2048]{2,1,0:T(8,128)(2,1)}, bf16[2,256,2048]{2,1,0:T(8,128)(2,1)}) custom-call(f32[2,8,384]{2,1,0:T(8,128)} %copy-done.37, f32[2,8,384]{2,1,0:T(8,128)} %copy-done.36, f32[2,8,384]{2,1,0:T(8,128)} %copy-done.35, f32[8,256,384]{2,1,0:T(8,128)} %get-tuple-element.181.refs_3_.refs_11_.refs_8_, ...), custom_call_target="tpu_custom_call" | custom-call | flops 2683333376 | bytes 1024 | tf_op jit(solution)/shard_map/pallas_call | solution.py:465
  184.9 7.6 %collective-permute-done.28 = bf16[256,2048]{1,0:T(8,128)(2,1)} collective-permute-done((bf16[256,2048]{1,0:T(8,128)(2,1)}, bf16[256,2048]{1,0:T(8,128)(2,1)}, u32[]{:S(2)}, u32[]{:S(2)}) %collective-permute-start.28) | collective-permute-done | bytes 1048608 | tf_op jit(solution)/shard_map/ppermute | solution.py:104
  199.9 6.4 %shard_map.253.refs_8_.refs_1_ = bf16[8,256,2048]{2,1,0:T(8,128)(2,1)} custom-call(bf16[256,2048]{1,0:T(8,128)(2,1)} %bitcast.refs_0_, bf16[256,2048]{1,0:T(8,128)(2,1)} %collective-permute-done.8.refs_1_, bf16[256,2048]{1,0:T(8,128)(2,1)} %collective-permute-done.7.refs_2_, bf16[256,2048]{1,0:T(8,128)(2,1)} %collective-permute-done.20.refs_3_, ...), custom_call_target="tpu_custom_call" | custom-call | flops 1661111168 | bytes 1024 | tf_op jit(solution)/shard_map/pallas_call | solution.py:685
  206.3 14.8 %collective-permute-done.30.refs_2_ = bf16[256,2048]{1,0:T(8,128)(2,1)} collective-permute-done((bf16[256,2048]{1,0:T(8,128)(2,1)S(1)}, bf16[256,2048]{1,0:T(8,128)(2,1)}, u32[]{:S(2)}, u32[]{:S(2)}) %collective-permute-start.30) | collective-permute-done | bytes 1048608 | tf_op jit(solution)/shard_map/ppermute | solution.py:76
  223.8 13.1 %collective-permute-done.35.refs_3_ = bf16[256,2048]{1,0:T(8,128)(2,1)} collective-permute-done((bf16[256,2048]{1,0:T(8,128)(2,1)}, bf16[256,2048]{1,0:T(8,128)(2,1)}, u32[]{:S(2)}, u32[]{:S(2)}) %collective-permute-start.35) | collective-permute-done | bytes 1048608 | tf_op jit(solution)/shard_map/ppermute | solution.py:76
  239.8 21.2 %shard_map.254 = (bf16[8,256,512]{2,1,0:T(8,128)(2,1)}, bf16[8,256,512]{2,1,0:T(8,128)(2,1)}, bf16[8,256,512]{2,1,0:T(8,128)(2,1)}, bf16[8,256,2048]{2,1,0:T(8,128)(2,1)}) custom-call(bf16[256,2048]{1,0:T(8,128)(2,1)} %copy-done.13, bf16[256,2048]{1,0:T(8,128)(2,1)} %collective-permute-done.29.refs_1_, bf16[256,2048]{1,0:T(8,128)(2,1)} %collective-permute-done.30.refs_2_, ...), custom_call_target="tpu_custom_call" | custom-call | flops 5576969728 | bytes 1024 | tf_op jit(solution)/shard_map/pallas_call | solution.py:762
  261.0 24.6 %shard_map.255 = bf16[512,6144]{1,0:T(8,128)(2,1)} custom-call(bf16[2048,512]{1,0:T(8,128)(2,1)} %bitcast.115, bf16[2048,512]{1,0:T(8,128)(2,1)} %bitcast.116, bf16[2048,512]{1,0:T(8,128)(2,1)} %bitcast.123, bf16[2048,2048]{1,0:T(8,128)(2,1)} %bitcast.113, bf16[2048,2048]{1,0:T(8,128)(2,1)} %bitcast.111), custom_call_target="tpu_custom_call" | custom-call | flops 5832525312 | bytes 1024 | tf_op jit(solution)/shard_map/pallas_call | solution.py:803
  285.9 13.3 %shard_map.256 = (bf16[8,256,256]{2,1,0:T(8,128)(2,1)}, bf16[8,256,256]{2,1,0:T(8,128)(2,1)}, bf16[8,256,256]{2,1,0:T(8,128)(2,1)}) custom-call(bf16[8,256,2048]{2,1,0:T(8,128)(2,1)} %get-tuple-element.210.refs_0_, bf16[8,256,2048]{2,1,0:T(8,128)(2,1)} %shard_map.253.refs_8_.refs_1_, ...), custom_call_target="tpu_custom_call" | custom-call | flops 3044040448 | bytes 1024 | tf_op jit(solution)/shard_map/pallas_call | solution.py:762
  299.2 7.5 %shard_map.257 = bf16[2,256,2048]{2,1,0:T(8,128)(2,1)} custom-call(bf16[8,256,512]{2,1,0:T(8,128)(2,1)} %get-tuple-element.216.refs_0_, bf16[8,256,512]{2,1,0:T(8,128)(2,1)} %get-tuple-element.207.refs_1_, bf16[8,256,256]{2,1,0:T(8,128)(2,1)} %get-tuple-element.227.refs_2_, bf16[8,256,256]{2,1,0:T(8,128)(2,1)} %get-tuple-element.212.refs_3_, ...), custom_call_target="tpu_custom_call" | custom-call | flops 2033131392 | bytes 1024 | tf_op jit(solution)/shard_map/pallas_call | solution.py:659
  306.8 7.5 %shard_map.258.refs_0_.refs_2_ = bf16[2,256,2048]{2,1,0:T(8,128)(2,1)} custom-call(bf16[8,256,512]{2,1,0:T(8,128)(2,1)} %get-tuple-element.216.refs_0_, bf16[8,256,512]{2,1,0:T(8,128)(2,1)} %get-tuple-element.207.refs_1_, bf16[8,256,256]{2,1,0:T(8,128)(2,1)} %get-tuple-element.227.refs_2_, bf16[8,256,256]{2,1,0:T(8,128)(2,1)} %get-tuple-element.212.refs_3_, ...), custom_call_target="tpu_custom_call" | custom-call | flops 2033131392 | bytes 1024 | tf_op jit(solution)/shard_map/pallas_call | solution.py:659
  320.1 13.4 %shard_map.260 = (bf16[2,256,2048]{2,1,0:T(8,128)(2,1)}, bf16[2,256,2048]{2,1,0:T(8,128)(2,1)}) custom-call(bf16[8,256,512]{2,1,0:T(8,128)(2,1)} %get-tuple-element.216.refs_0_, bf16[8,256,512]{2,1,0:T(8,128)(2,1)} %get-tuple-element.207.refs_1_, bf16[8,256,256]{2,1,0:T(8,128)(2,1)} %get-tuple-element.227.refs_2_, ...), custom_call_target="tpu_custom_call" | custom-call | flops 3299596032 | bytes 1024 | tf_op jit(solution)/shard_map/pallas_call | solution.py:659
  346.7 13.8 %shard_map.262 = (bf16[4,256,2048]{2,1,0:T(8,128)(2,1)}, bf16[4,256,2048]{2,1,0:T(8,128)(2,1)}) custom-call(bf16[8,256,512]{2,1,0:T(8,128)(2,1)} %get-tuple-element.222.refs_0_, bf16[8,256,256]{2,1,0:T(8,128)(2,1)} %get-tuple-element.223.refs_1_, bf16[512,6144]{1,0:T(8,128)(2,1)} %all-gather.6.cloned.1.call-done.refs_9_.refs_10_.refs_11_.refs_4_.refs_5_.refs_2_, ...), custom_call_target="tpu_custom_call" | custom-call | flops 3299596032 | bytes 1024 | tf_op jit(solution)/shard_map/pallas_call | solution.py:659
  360.5 9.6 %collective-permute-done.44 = bf16[256,2048]{1,0:T(8,128)(2,1)S(1)} collective-permute-done((bf16[256,2048]{1,0:T(8,128)(2,1)}, bf16[256,2048]{1,0:T(8,128)(2,1)S(1)}, u32[]{:S(2)}, u32[]{:S(2)}) %collective-permute-start.44) | collective-permute-done | bytes 1048608 | tf_op jit(solution)/shard_map/ppermute | solution.py:104
  379.9 18.6 %shard_map.263 = bf16[256,6144]{1,0:T(8,128)(2,1)} custom-call(bf16[2048,256]{1,0:T(8,128)(2,1)} %bitcast.119, bf16[2048,256]{1,0:T(8,128)(2,1)} %bitcast.120, bf16[2048,256]{1,0:T(8,128)(2,1)} %bitcast.131, bf16[2048,2048]{1,0:T(8,128)(2,1)} %bitcast.114, bf16[2048,2048]{1,0:T(8,128)(2,1)} %bitcast.112), custom_call_target="tpu_custom_call" | custom-call | flops 3299596032 | bytes 1024 | tf_op jit(solution)/shard_map/pallas_call | solution.py:803
  404.5 7.1 %collective-permute-done.48.refs_1_.refs_3_ = bf16[4,256,2048]{2,1,0:T(8,128)(2,1)S(1)} collective-permute-done((bf16[4,256,2048]{2,1,0:T(8,128)(2,1)}, bf16[4,256,2048]{2,1,0:T(8,128)(2,1)S(1)}, u32[]{:S(2)}, u32[]{:S(2)}) %collective-permute-start.48) | collective-permute-done | bytes 4194336 | tf_op jit(solution)/shard_map/ppermute | solution.py:1097
  422.1 18.5 %shard_map.265 = (bf16[8,256,384]{2,1,0:T(8,128)(2,1)}, bf16[8,256,384]{2,1,0:T(8,128)(2,1)}, f32[8,256,384]{2,1,0:T(8,128)}, f32[8,256,384]{2,1,0:T(8,128)}, f3...) custom-call(bf16[256,2048]{1,0:T(8,128)(2,1)} %copy-done.12, bf16[256,2048]{1,0:T(8,128)(2,1)} %copy-done.20, ...), custom_call_target="tpu_custom_call" | custom-call | flops 5024426496 | bytes 1024 | tf_op jit(solution)/shard_map/pallas_call | solution.py:518
  445.8 15.3 %shard_map.266 = bf16[320,4096]{1,0:T(8,128)(2,1)} custom-call(bf16[2048,384]{1,0:T(8,128)(2,1)} %bitcast.118, bf16[2048,384]{1,0:T(8,128)(2,1)} %bitcast.132, bf16[2048,2048]{1,0:T(8,128)(2,1)} %bitcast.109, bf16[2048,2048]{1,0:T(8,128)(2,1)} %bitcast.124), custom_call_target="tpu_custom_call" | custom-call | flops 3299596032 | bytes 1024 | tf_op jit(solution)/shard_map/pallas_call | solution.py:844
  466.1 17.9 %shard_map.267 = (bf16[8,256,384]{2,1,0:T(8,128)(2,1)}, f32[8,16,384]{2,1,0:T(8,128)}, bf16[768,160]{1,0:T(8,128)(2,1)}, f32[8,384]{1,0:T(8,128)}) custom-call(f32[2,8,384]{2,1,0:T(8,128)} %copy-done.37, f32[2,8,384]{2,1,0:T(8,128)} %copy-done.36, f32[2,8,384]{2,1,0:T(8,128)} %copy-done.35, f32[2,8,384]{2,1,0:T(8,128)} %copy-done.44, ...), custom_call_target="tpu_custom_call" | custom-call | flops 5024426496 | bytes 1024 | tf_op jit(solution)/shard_map/pallas_call | solution.py:609
  490.2 6.9 %collective-permute-done.58 = f32[8,8,384]{2,1,0:T(8,128)S(1)} collective-permute-done((f32[8,8,384]{2,1,0:T(8,128)S(1)}, f32[8,8,384]{2,1,0:T(8,128)S(1)}, u32[]{:S(2)}, u32[]{:S(2)}) %collective-permute-start.58) | collective-permute-done | bytes 98336 | tf_op jit(solution)/shard_map/ppermute | solution.py:157
  497.7 6.2 %shard_map.269 = (bf16[2,256,2048]{2,1,0:T(8,128)(2,1)}, f32[1,1,2048]{2,1,0:T(1,128)}) custom-call(bf16[8,256,384]{2,1,0:T(8,128)(2,1)} %get-tuple-element.284.refs_0_, bf16[8,256,384]{2,1,0:T(8,128)(2,1)} %fusion.16.refs_1_, bf16[320,6528]{1,0:T(8,128)(2,1)} %all-gather.4.cloned.1.call-done.wu.wy.small.refs_6_.refs_15_.refs_2_.refs_3_, ...), custom_call_target="tpu_custom_call" | custom-call | flops 1294360320 | bytes 1024 | tf_op jit(solution)/shard_map/pallas_call | solution.py:659
  505.4 6.1 %shard_map.270 = (bf16[2,256,2048]{2,1,0:T(8,128)(2,1)}, f32[1,1,2048]{2,1,0:T(1,128)}) custom-call(bf16[8,256,384]{2,1,0:T(8,128)(2,1)} %get-tuple-element.284.refs_0_, bf16[8,256,384]{2,1,0:T(8,128)(2,1)} %fusion.16.refs_1_, bf16[320,6528]{1,0:T(8,128)(2,1)} %all-gather.4.cloned.1.call-done.wu.wy.small.refs_6_.refs_15_.refs_2_.refs_3_, ...), custom_call_target="tpu_custom_call" | custom-call | flops 1294360320 | bytes 1024 | tf_op jit(solution)/shard_map/pallas_call | solution.py:659
  511.5 7.3 %collective-permute-done.59 = bf16[256,2048]{1,0:T(8,128)(2,1)S(1)} collective-permute-done((bf16[256,2048]{1,0:T(8,128)(2,1)S(1)}, bf16[256,2048]{1,0:T(8,128)(2,1)S(1)}, u32[]{:S(2)}, u32[]{:S(2)}) %collective-permute-start.59) | collective-permute-done | bytes 1048608 | tf_op jit(solution)/shard_map/ppermute | solution.py:1121
  526.3 11.2 %shard_map.273 = (bf16[2,256,2048]{2,1,0:T(8,128)(2,1)}, bf16[2,256,2048]{2,1,0:T(8,128)(2,1)}, f32[2,1,2048]{2,1,0:T(1,128)}) custom-call(bf16[8,256,384]{2,1,0:T(8,128)(2,1)} %get-tuple-element.284.refs_0_, bf16[8,256,384]{2,1,0:T(8,128)(2,1)} %fusion.16.refs_1_, ...), custom_call_target="tpu_custom_call" | custom-call | flops 1822053888 | bytes 1024 | tf_op jit(solution)/shard_map/pallas_call | solution.py:659
  542.3 8.1 %shard_map.274 = bf16[320,2048]{1,0:T(8,128)(2,1)} custom-call(bf16[2048,384]{1,0:T(8,128)(2,1)} %bitcast.117, bf16[2048,2048]{1,0:T(8,128)(2,1)} %bitcast.110), custom_call_target="tpu_custom_call" | custom-call | flops 2033131392 | bytes 1024 | tf_op jit(solution)/shard_map/pallas_call | solution.py:844
  565.8 8.0 %collective-permute-done.64 = bf16[256,2048]{1,0:T(8,128)(2,1)S(1)} collective-permute-done((bf16[256,2048]{1,0:T(8,128)(2,1)}, bf16[256,2048]{1,0:T(8,128)(2,1)S(1)}, u32[]{:S(2)}, u32[]{:S(2)}) %collective-permute-start.64) | collective-permute-done | bytes 1048608 | tf_op jit(solution)/shard_map/ppermute | solution.py:104
  574.8 5.3 shard_map.276
  (389 shorter events, 225.8 us)
Async XLA Ops:
  7.2 97.0 %all-gather.4.cloned.1.call-start = ((), (), s32[]{:S(2)}) async-start(), calls=%async_computation.5 | async-start | bytes 5222400 | tf_op jit(solution)/shard_map/all_gather | solution.py:959
  16.6 220.3 %all-gather.6.cloned.1.call-start = ((), (), s32[]{:S(2)}) async-start(), calls=%async_computation.6 | async-start | bytes 7864320 | tf_op jit(solution)/shard_map/all_gather | solution.py:959
  23.7 52.3 %collective-permute-start.3 = (bf16[256,2048]{1,0:T(8,128)(2,1)S(1)}, bf16[256,2048]{1,0:T(8,128)(2,1)}, u32[]{:S(2)}, u32[]{:S(2)}) collective-permute-start(bf16[256,2048]{1,0:T(8,128)(2,1)S(1)} %bitcast.128), channel_id=1, source_target_pairs={{0,4},{4,0},{8,12},{12,8},{16,20},{20,16},{24,28},{28,24},{1,5},{5... | collective-permute-start | bytes 3145736 | tf_op jit(solution)/shard_map/ppermute | solution.py:89
  23.7 36.0 %collective-permute-start.1 = (bf16[256,2048]{1,0:T(8,128)(2,1)S(1)}, bf16[256,2048]{1,0:T(8,128)(2,1)}, u32[]{:S(2)}, u32[]{:S(2)}) collective-permute-start(bf16[256,2048]{1,0:T(8,128)(2,1)S(1)} %bitcast.129), channel_id=1, source_target_pairs={{0,16},{4,12},{8,24},{12,4},{16,0},{20,28},{24,8},{28,20},{1,17},{... | collective-permute-start | bytes 3145736 | tf_op jit(solution)/shard_map/ppermute | solution.py:76
  25.4 24.6 %collective-permute-start = (bf16[256,2048]{1,0:T(8,128)(2,1)S(1)}, bf16[256,2048]{1,0:T(8,128)(2,1)}, u32[]{:S(2)}, u32[]{:S(2)}) collective-permute-start(bf16[256,2048]{1,0:T(8,128)(2,1)S(1)} %bitcast.130), channel_id=1, source_target_pairs={{0,8},{4,20},{8,0},{12,28},{16,24},{20,4},{24,16},{28,12},{1,9},{5... | collective-permute-start | bytes 3145736 | tf_op jit(solution)/shard_map/ppermute | solution.py:76
  33.1 26.4 %collective-permute-start.16 = (bf16[16,2048]{1,0:T(8,128)(2,1)S(1)}, bf16[16,2048]{1,0:T(8,128)(2,1)}, u32[]{:S(2)}, u32[]{:S(2)}) collective-permute-start(bf16[16,2048]{1,0:T(8,128)(2,1)S(1)} %fusion.15.refs_8_), channel_id=1, source_target_pairs={{0,4},{4,0},{8,12},{12,8},{16,20},{20,16},{24,28},{28,24},{1,5},{5... | collective-permute-start | bytes 196616 | tf_op jit(solution)/shard_map/ppermute | solution.py:89
  33.2 32.7 %collective-permute-start.14 = (bf16[16,2048]{1,0:T(8,128)(2,1)S(1)}, bf16[16,2048]{1,0:T(8,128)(2,1)}, u32[]{:S(2)}, u32[]{:S(2)}) collective-permute-start(bf16[16,2048]{1,0:T(8,128)(2,1)S(1)} %fusion.15.refs_8_), channel_id=1, source_target_pairs={{0,16},{4,12},{8,24},{12,4},{16,0},{20,28},{24,8},{28,20},{1,17},{... | collective-permute-start | bytes 196616 | tf_op jit(solution)/shard_map/ppermute | solution.py:76
  59.5 226.4 %all-gather.8.cloned.1.call-start = ((), (), s32[]{:S(2)}) async-start(), calls=%async_computation.7 | async-start | bytes 3932160 | tf_op jit(solution)/shard_map/all_gather | solution.py:959
  59.6 17.0 %collective-permute-start.4 = (bf16[256,2048]{1,0:T(8,128)(2,1)}, bf16[256,2048]{1,0:T(8,128)(2,1)S(1)}, u32[]{:S(2)}, u32[]{:S(2)}) collective-permute-start(bf16[256,2048]{1,0:T(8,128)(2,1)} %collective-permute-done.refs_1_), channel_id=1, source_target_pairs={{0,4},{4,0},{8,12},{12,8},{16,20},{20,16},{24,28},{28,24},{1,5},{5... | collective-permute-start | bytes 3145736 | tf_op jit(solution)/shard_map/ppermute | solution.py:89
  76.6 24.7 %collective-permute-start.8 = (bf16[256,2048]{1,0:T(8,128)(2,1)}, bf16[256,2048]{1,0:T(8,128)(2,1)}, u32[]{:S(2)}, u32[]{:S(2)}) collective-permute-start(bf16[256,2048]{1,0:T(8,128)(2,1)} %bitcast.refs_0_), channel_id=1, source_target_pairs={{0,8},{4,20},{8,0},{12,28},{16,24},{20,4},{24,16},{28,12},{1,9},{5... | collective-permute-start | bytes 3145736 | tf_op jit(solution)/shard_map/ppermute | solution.py:76
  79.4 46.9 %collective-permute-start.7 = (bf16[256,2048]{1,0:T(8,128)(2,1)}, bf16[256,2048]{1,0:T(8,128)(2,1)}, u32[]{:S(2)}, u32[]{:S(2)}) collective-permute-start(bf16[256,2048]{1,0:T(8,128)(2,1)} %bitcast.refs_0_), channel_id=1, source_target_pairs={{0,16},{4,12},{8,24},{12,4},{16,0},{20,28},{24,8},{28,20},{1,17},{... | collective-permute-start | bytes 3145736 | tf_op jit(solution)/shard_map/ppermute | solution.py:76
  101.3 25.0 %collective-permute-start.20 = (bf16[256,2048]{1,0:T(8,128)(2,1)}, bf16[256,2048]{1,0:T(8,128)(2,1)}, u32[]{:S(2)}, u32[]{:S(2)}) collective-permute-start(bf16[256,2048]{1,0:T(8,128)(2,1)} %collective-permute-done.8.refs_1_), channel_id=1, source_target_pairs={{0,16},{4,12},{8,24},{12,4},{16,0},{20,28},{24,8},{28,20},{1,17},{... | collective-permute-start | bytes 3145736 | tf_op jit(solution)/shard_map/ppermute | solution.py:76
  166.9 17.1 %collective-permute-start.27 = (bf16[256,2048]{1,0:T(8,128)(2,1)S(1)}, bf16[256,2048]{1,0:T(8,128)(2,1)S(1)}, u32[]{:S(2)}, u32[]{:S(2)}) collective-permute-start(bf16[256,2048]{1,0:T(8,128)(2,1)S(1)} %copy-done.60), channel_id=1, source_target_pairs={{0,16},{4,12},{8,24},{12,4},{16,0},{20,28},{24,8},{28,20},{1,17},{... | collective-permute-start | bytes 3145736 | tf_op jit(solution)/shard_map/ppermute | solution.py:118
  178.1 225.1 %reduce-scatter.5.cloned.1.call-start = ((), (), s32[]{:S(2)}) async-start(), calls=%async_computation.8 | async-start | bytes 7864320 | tf_op jit(solution)/shard_map/reduce_scatter | solution.py:963
  178.2 17.9 %collective-permute-start.31 = (bf16[256,2048]{1,0:T(8,128)(2,1)}, bf16[256,2048]{1,0:T(8,128)(2,1)S(1)}, u32[]{:S(2)}, u32[]{:S(2)}) collective-permute-start(bf16[256,2048]{1,0:T(8,128)(2,1)} %bitcast.refs_0_), channel_id=1, source_target_pairs={{0,4},{4,0},{8,12},{12,8},{16,20},{20,16},{24,28},{28,24},{1,5},{5... | collective-permute-start | bytes 3145736 | tf_op jit(solution)/shard_map/ppermute | solution.py:89
  178.2 19.3 %collective-permute-start.32 = (bf16[256,2048]{1,0:T(8,128)(2,1)}, bf16[256,2048]{1,0:T(8,128)(2,1)S(1)}, u32[]{:S(2)}, u32[]{:S(2)}) collective-permute-start(bf16[256,2048]{1,0:T(8,128)(2,1)} %collective-permute-done.8.refs_1_), channel_id=1, source_target_pairs={{0,4},{4,0},{8,12},{12,8},{16,20},{20,16},{24,28},{28,24},{1,5},{5... | collective-permute-start | bytes 3145736 | tf_op jit(solution)/shard_map/ppermute | solution.py:89
  178.7 18.9 %collective-permute-start.33 = (bf16[256,2048]{1,0:T(8,128)(2,1)}, bf16[256,2048]{1,0:T(8,128)(2,1)S(1)}, u32[]{:S(2)}, u32[]{:S(2)}) collective-permute-start(bf16[256,2048]{1,0:T(8,128)(2,1)} %collective-permute-done.7.refs_2_), channel_id=1, source_target_pairs={{0,4},{4,0},{8,12},{12,8},{16,20},{20,16},{24,28},{28,24},{1,5},{5... | collective-permute-start | bytes 3145736 | tf_op jit(solution)/shard_map/ppermute | solution.py:89
  195.8 25.3 %collective-permute-start.30 = (bf16[256,2048]{1,0:T(8,128)(2,1)S(1)}, bf16[256,2048]{1,0:T(8,128)(2,1)}, u32[]{:S(2)}, u32[]{:S(2)}) collective-permute-start(bf16[256,2048]{1,0:T(8,128)(2,1)S(1)} %multiply_convert_fusion.refs_0_), channel_id=1, source_target_pairs={{0,16},{4,12},{8,24},{12,4},{16,0},{20,28},{24,8},{28,20},{1,17},{... | collective-permute-start | bytes 3145736 | tf_op jit(solution)/shard_map/ppermute | solution.py:76
  196.1 25.7 %collective-permute-start.29 = (bf16[256,2048]{1,0:T(8,128)(2,1)S(1)}, bf16[256,2048]{1,0:T(8,128)(2,1)}, u32[]{:S(2)}, u32[]{:S(2)}) collective-permute-start(bf16[256,2048]{1,0:T(8,128)(2,1)S(1)} %multiply_convert_fusion.refs_0_), channel_id=1, source_target_pairs={{0,8},{4,20},{8,0},{12,28},{16,24},{20,4},{24,16},{28,12},{1,9},{5... | collective-permute-start | bytes 3145736 | tf_op jit(solution)/shard_map/ppermute | solution.py:76
  285.6 180.4 %reduce-scatter.7.cloned.1.call-start = ((), (), s32[]{:S(2)}) async-start(), calls=%async_computation.9 | async-start | bytes 3932160 | tf_op jit(solution)/shard_map/reduce_scatter | solution.py:963
  344.5 25.7 %collective-permute-start.44 = (bf16[256,2048]{1,0:T(8,128)(2,1)}, bf16[256,2048]{1,0:T(8,128)(2,1)S(1)}, u32[]{:S(2)}, u32[]{:S(2)}) collective-permute-start(bf16[256,2048]{1,0:T(8,128)(2,1)} %shard_map.261), channel_id=1, source_target_pairs={{0,8},{4,20},{8,0},{12,28},{16,24},{20,4},{24,16},{28,12},{1,9},{5... | collective-permute-start | bytes 3145736 | tf_op jit(solution)/shard_map/ppermute | solution.py:104
  346.2 24.0 %collective-permute-start.43 = (bf16[256,2048]{1,0:T(8,128)(2,1)}, bf16[256,2048]{1,0:T(8,128)(2,1)}, u32[]{:S(2)}, u32[]{:S(2)}) collective-permute-start(bf16[256,2048]{1,0:T(8,128)(2,1)} %get-tuple-element.214), channel_id=1, source_target_pairs={{0,16},{4,12},{8,24},{12,4},{16,0},{20,28},{24,8},{28,20},{1,17},{... | collective-permute-start | bytes 3145736 | tf_op jit(solution)/shard_map/ppermute | solution.py:118
  377.4 25.8 %collective-permute-start.46 = (bf16[256,2048]{1,0:T(8,128)(2,1)S(1)}, bf16[256,2048]{1,0:T(8,128)(2,1)S(1)}, u32[]{:S(2)}, u32[]{:S(2)}) collective-permute-start(bf16[256,2048]{1,0:T(8,128)(2,1)S(1)} %get-tuple-element.241.refs_0_), channel_id=1, source_target_pairs={{0,16},{4,12},{8,24},{12,4},{16,0},{20,28},{24,8},{28,20},{1,17},{... | collective-permute-start | bytes 3145736 | tf_op jit(solution)/shard_map/ppermute | solution.py:76
  377.8 25.3 %collective-permute-start.45 = (bf16[256,2048]{1,0:T(8,128)(2,1)S(1)}, bf16[256,2048]{1,0:T(8,128)(2,1)S(1)}, u32[]{:S(2)}, u32[]{:S(2)}) collective-permute-start(bf16[256,2048]{1,0:T(8,128)(2,1)S(1)} %get-tuple-element.241.refs_0_), channel_id=1, source_target_pairs={{0,8},{4,20},{8,0},{12,28},{16,24},{20,4},{24,16},{28,12},{1,9},{5... | collective-permute-start | bytes 3145736 | tf_op jit(solution)/shard_map/ppermute | solution.py:76
  403.2 150.3 %reduce-scatter.9.cloned.1.call-start = ((), (), s32[]{:S(2)}) async-start(), calls=%async_computation.10 | async-start | bytes 3276800 | tf_op jit(solution)/shard_map/reduce_scatter | solution.py:963
  418.3 26.5 %collective-permute-start.53 = (bf16[256,2048]{1,0:T(8,128)(2,1)}, bf16[256,2048]{1,0:T(8,128)(2,1)S(1)}, u32[]{:S(2)}, u32[]{:S(2)}) collective-permute-start(bf16[256,2048]{1,0:T(8,128)(2,1)} %get-tuple-element.239), channel_id=1, source_target_pairs={{0,16},{4,12},{8,24},{12,4},{16,0},{20,28},{24,8},{28,20},{1,17},{... | collective-permute-start | bytes 3145736 | tf_op jit(solution)/shard_map/ppermute | solution.py:1106
  418.7 26.1 %collective-permute-start.54 = (bf16[256,2048]{1,0:T(8,128)(2,1)}, bf16[256,2048]{1,0:T(8,128)(2,1)S(1)}, u32[]{:S(2)}, u32[]{:S(2)}) collective-permute-start(bf16[256,2048]{1,0:T(8,128)(2,1)} %get-tuple-element.240), channel_id=1, source_target_pairs={{0,16},{4,12},{8,24},{12,4},{16,0},{20,28},{24,8},{28,20},{1,17},{... | collective-permute-start | bytes 3145736 | tf_op jit(solution)/shard_map/ppermute | solution.py:1106
  440.7 20.4 %collective-permute-start.57 = (f32[2,8,384]{2,1,0:T(8,128)}, f32[2,8,384]{2,1,0:T(8,128)S(1)}, u32[]{:S(2)}, u32[]{:S(2)}) collective-permute-start(f32[2,8,384]{2,1,0:T(8,128)} %get-tuple-element.253), channel_id=1, source_target_pairs={{3,0},{7,4},{11,8},{15,12},{19,16},{23,20},{27,24},{31,28}} | collective-permute-start | bytes 73736 | tf_op jit(solution)/shard_map/ppermute | solution.py:157
  442.0 19.1 %collective-permute-start.56 = (f32[2,8,384]{2,1,0:T(8,128)}, f32[2,8,384]{2,1,0:T(8,128)S(1)}, u32[]{:S(2)}, u32[]{:S(2)}) collective-permute-start(f32[2,8,384]{2,1,0:T(8,128)} %get-tuple-element.253), channel_id=1, source_target_pairs={{2,0},{3,1},{6,4},{7,5},{10,8},{11,9},{14,12},{15,13},{18,16},{19,... | collective-permute-start | bytes 73736 | tf_op jit(solution)/shard_map/ppermute | solution.py:157
  443.3 17.8 %collective-permute-start.55 = (f32[2,8,384]{2,1,0:T(8,128)}, f32[2,8,384]{2,1,0:T(8,128)S(1)}, u32[]{:S(2)}, u32[]{:S(2)}) collective-permute-start(f32[2,8,384]{2,1,0:T(8,128)} %get-tuple-element.253), channel_id=1, source_target_pairs={{1,0},{2,1},{3,2},{5,4},{6,5},{7,6},{9,8},{10,9},{11,10},{13,12},{... | collective-permute-start | bytes 73736 | tf_op jit(solution)/shard_map/ppermute | solution.py:157
  466.1 125.7 %reduce-scatter.11.cloned.1.call-start = ((), (), s32[]{:S(2)}) async-start(), calls=%async_computation.11 | async-start | bytes 1945600 | tf_op jit(solution)/shard_map/reduce_scatter | solution.py:963
  525.7 24.8 %collective-permute-start.63 = (bf16[256,2048]{1,0:T(8,128)(2,1)}, bf16[256,2048]{1,0:T(8,128)(2,1)S(1)}, u32[]{:S(2)}, u32[]{:S(2)}) collective-permute-start(bf16[256,2048]{1,0:T(8,128)(2,1)} %get-tuple-element.282), channel_id=1, source_target_pairs={{0,16},{4,12},{8,24},{12,4},{16,0},{20,28},{24,8},{28,20},{1,17},{... | collective-permute-start | bytes 3145736 | tf_op jit(solution)/shard_map/ppermute | solution.py:118
  (102 other events, 1043.4 us)
Sparse Core Ops, SparseCore 0:
  16.7 83.2 all-gather.3
  101.5 114.5 all-gather.5
  217.6 63.6 all-gather.7
  285.7 112.5 reduce-scatter.4
  403.3 62.6 reduce-scatter.6
  468.8 54.1 reduce-scatter.8
  553.7 33.7 reduce-scatter.10

commit v4 on v3

--- a/solution.py
+++ b/solution.py
@@ -13,7 +13,7 @@
 HALO = 16
 F32 = jnp.float32
 BF16 = jnp.bfloat16
-VMEM_LIMIT = 56 * 1024 * 1024
+MEBI = 1024 * 1024
 ANY = pl.BlockSpec(memory_space=pl.ANY)
 ROOT = 0.7978845608028654
 CUBE = 0.044715
@@ -97,10 +97,14 @@
     return sum(array[place].astype(F32) for array, place in terms)
 
 
-def scatter_tail(terms, stages, waits):
+def scatter_tail(terms, stages, waits, late=()):
     for place, pairs in enumerate(reversed(stages)):
         split = len(terms) // 2
         sent = add_rows(terms[split:])
+        if late:
+            sent, late = lax.optimization_barrier((sent, late))
+            terms = [[*those, (one[None], 0)] for those, one in zip(terms, late)] + terms[split:]
+            late = ()
         got = [lax.ppermute(part, "dp", pairs) for part in sent]
         if place < len(waits):
             got = waits[place](sent, got)
@@ -120,10 +124,12 @@
     theirs, near = make([2, 0], quarter, (sent,))
     theirs, near, got[split:] = lax.optimization_barrier((theirs, near, got[split:]))
     there = lax.ppermute(theirs, "dp", twin)
+    terms = [[(near, k), (there, k)] for k in range(quarter)]
+    terms = terms[:split] + [[*terms[k], (got[k][None], 0)] for k in range(split, quarter)]
+    late = got[:split]
     if low_wait is not None:
-        got[:split] = low_wait(sent, got[:split])
-    terms = [[(near, k), (there, k), (got[k][None], 0)] for k in range(quarter)]
-    return scatter_tail(terms, stages[:-1], [wait] if wait else [])
+        late = low_wait(sent, late)
+    return scatter_tail(terms, stages[:-1], [wait] if wait else [], late)
 
 
 def scatter_rows(make, count, wait):
@@ -262,6 +268,7 @@
             pltpu.SemaphoreType.DMA((count,)),
         ],
         2.6e-6 * count * rows * model,
+        60,
     )(*pieces, *tops, gain)
 
 
@@ -279,6 +286,10 @@
         here = row - start == column
         fold = here if fold is None else fold | here
     return inside, jnp.where(fold, 1.0, 0.0).astype(BF16)
+
+
+def sigmoid(values):
+    return 0.5 * jnp.tanh(0.5 * values) + 0.5
 
 
 def softplus(values):
@@ -306,33 +317,38 @@
     ends,
     wz,
     par,
-    wu_all,
-    wy_all,
+    w_all,
+    both,
 ):
     width = wz.shape[1]
+    some, tall, model = h_ref.shape
+    rows = tall - HALO
+    place = pl.program_id(0) % some
 
     @pl.when(pl.program_id(0) == 0)
     def _():
-        wu_all[...] = padded_rows(wu[...], width)
-        wy_all[...] = padded_rows(wy[...], width)
-        rows = padded_rows(small[...], width)
+        w_all[:width, :] = padded_rows(wu[...], width)
+        w_all[width:, :] = padded_rows(wy[...], width)
+        params = padded_rows(small[...], width)
         inside, fold = block_masks(width, block)
         for gate in (0, 1):
-            spread = dot_nt(rows[:, gate * block : gate * block + block], fold)
+            spread = dot_nt(params[:, gate * block : gate * block + block], fold)
             wz[gate * width : gate * width + width, :] = jnp.where(inside, spread, 0.0).astype(BF16)
         row = lax.broadcasted_iota(jnp.int32, (width, width), 0)
         column = lax.broadcasted_iota(jnp.int32, (width, width), 1)
         same = jnp.where(row == column, 1.0, 0.0).astype(BF16)
-        turned = dot_tn(rows[:, 2 * block : 2 * block + 8], same)
+        turned = dot_tn(params[:, 2 * block : 2 * block + 8], same)
         par[0:8, :] = turned
         par[8:16, :] = turned
         par[7:8, :] = -SHARP * softplus(turned[7:8, :])
 
-    h_low = h_ref[0]
-    rows = h_low.shape[0] - HALO
-    u_low = dot_nt(h_low, wu_all[...]).astype(BF16)
+    @pl.when(place == 0)
+    def _():
+        both[...] = dot_nt(h_ref[...].reshape(some * tall, model), w_all[...]).reshape(both.shape)
+
+    u_low = both[place, :, :width].astype(BF16)
     u_out[0] = u_low
-    y_out[0] = dot_nt(h_low[HALO:], wy_all[...])
+    y_out[0] = both[place, HALO:, width:]
     same = m_ref[0].astype(F32)
     u_val = u_low.astype(F32)
     conv = par[4:5, :] + par[0:1, :] * u_val[HALO:]
@@ -343,13 +359,14 @@
     conv_out[0] = conv_low
     conv = conv_low.astype(F32)
     pre = dot_nt(conv_low, wz[...])
-    recur = jax.nn.sigmoid(pre[:, :width] + par[5:6, :])
-    enter = jax.nn.sigmoid(pre[:, width:] + par[6:7, :])
+    recur = sigmoid(pre[:, :width] + par[5:6, :])
+    enter = sigmoid(pre[:, width:] + par[6:7, :])
     keep = jnp.where(same >= 1.0, jnp.exp(par[7:8, :] * recur), 0.0)
     r_out[0] = recur
     e_out[0] = enter
     k_out[0] = keep
-    inputs = conv * enter * jnp.sqrt(jnp.maximum(1.0 - keep * keep, FLOOR))
+    spare = jnp.maximum(1.0 - keep * keep, FLOOR)
+    inputs = conv * enter * (spare * lax.rsqrt(spare))
     mult, total = scan_into(keep, inputs, a_out, s_out, False)
     put_ends(ends, pl.program_id(0), mult, total)
 
@@ -364,7 +381,20 @@
     return pl.BlockSpec((1,) + shape, lambda step: (step + first,) + rest)
 
 
-def call(kernel, grid, in_specs, out_specs, out_shape, scratch, micros):
+def grown(memory, count, usual=8):
+    return min(60, memory * max(count, usual) // usual)
+
+
+def settings(micros, axes, memory):
+    return dict(
+        compiler_params=pltpu.CompilerParams(
+            vmem_limit_bytes=memory * MEBI, dimension_semantics=("arbitrary",) * axes if axes else None
+        ),
+        cost_estimate=pl.CostEstimate(flops=int(micros / SLOW * 1.15e9), bytes_accessed=1024, transcendentals=0),
+    )
+
+
+def call(kernel, grid, in_specs, out_specs, out_shape, scratch, micros, memory, aliases={}):
     return pl.pallas_call(
         kernel,
         grid=grid,
@@ -372,10 +402,22 @@
         out_specs=out_specs,
         out_shape=out_shape,
         scratch_shapes=scratch,
-        compiler_params=pltpu.CompilerParams(
-            vmem_limit_bytes=VMEM_LIMIT, dimension_semantics=("arbitrary",) * len(grid)
-        ),
-        cost_estimate=pl.CostEstimate(flops=int(micros / SLOW * 1.15e9), bytes_accessed=1024, transcendentals=0),
+        input_output_aliases=aliases,
+        **settings(micros, len(grid), memory),
+    )
+
+
+def stream(kernel, grid, in_specs, out_specs, out_shape, micros):
+    def outer(*refs):
+        pltpu.emit_pipeline(kernel, grid=grid, in_specs=in_specs, out_specs=[out_specs])(*refs)
+
+    here = pl.BlockSpec(memory_space=pltpu.HBM)
+    return pl.pallas_call(
+        outer,
+        in_specs=[here] * len(in_specs),
+        out_specs=here,
+        out_shape=out_shape,
+        **settings(micros, 0, 16),
     )
 
 
@@ -384,6 +426,7 @@
     rows = tall - HALO
     chan = w_in.shape[0]
     width = same.shape[2]
+    some = 1
 
     def out(height, columns, dtype):
         return jax.ShapeDtypeStruct((count, height, columns), dtype)
@@ -396,7 +439,7 @@
         functools.partial(mixer_enter_kernel, block),
         (count,),
         [
-            per_piece((tall, model)),
+            pl.BlockSpec((some, tall, model), lambda step: (step // some, 0, 0)),
             per_piece((rows, width)),
             pl.BlockSpec((chan, model), lambda step: (0, 0)),
             pl.BlockSpec((chan, model), lambda step: (0, 1)),
@@ -404,8 +447,9 @@
         ],
         [per_piece(s.shape[1:]) for s in shapes] + [resident(s.shape) for s in fixed],
         shapes + fixed,
-        [pltpu.VMEM((width, model), BF16), pltpu.VMEM((width, model), BF16)],
+        [pltpu.VMEM((2 * width, model), BF16), pltpu.VMEM((some, tall, 2 * width), F32)],
         SWEEP * count * rows * width,
+        grown(26, count),
     )(h_all, same, w_in, w_in, w_in)
 
 
@@ -472,13 +516,15 @@
         [jax.ShapeDtypeStruct((pieces, rows, model), BF16)] * groups,
         [pltpu.VMEM((pieces * rows, width), BF16)],
         3.5 + 3.5 * groups * pieces / 2,
+        grown(20, pieces, 2),
     )(*ends, cum, local, y_pre, w_in)
 
 
 def head_back_kernel(count, hops, *refs):
     d_refs = refs[:count]
     ends = refs[count : count + hops]
-    (cum, local, y_pre, keep_ref, w_out, dy_out, mixed_out, cb_out, lb_out, ends_out, all_out, buf, w_all, sems, all_sems) = refs[count + hops :]
+    (cum, local, y_pre, keep_ref, w_out, dy_out, mixed_out, cb_out, lb_out, ends_out, all_out, buf, w_all, d_some, sems, all_sems) = refs[count + hops :]
+    some = 1
     step = pl.program_id(0)
 
     @pl.when(step == 0)
@@ -486,9 +532,15 @@
         fetch_all(d_refs, buf, sems)
         w_all[...] = padded_rows(w_out[...], w_all.shape[0])
 
-    fetched(d_refs, buf, sems, step)
-    put(buf, all_out, all_sems, step).start()
-    d_mixed = dot_nt(buf[step], w_all[...])
+    @pl.when(step % some == 0)
+    def _():
+        for place in range(some):
+            fetched(d_refs, buf, sems, step + place)
+            put(buf, all_out, all_sems, step + place).start()
+        rows, model = buf.shape[1:]
+        d_some[...] = dot_nt(buf[pl.ds(step, some)].reshape(some * rows, model), w_all[...]).reshape(d_some.shape)
+
+    d_mixed = d_some[step % some]
     states = local[0] + cum[0] * folded(ends, step)
     value, slope = gelu_parts(y_pre[0])
     mixed_out[0] = (value * states).astype(BF16)
@@ -527,17 +579,19 @@
         [
             pltpu.VMEM((count, rows, model), BF16),
             pltpu.VMEM((width, model), BF16),
+            pltpu.VMEM((1, rows, width), F32),
             pltpu.SemaphoreType.DMA((count,)),
             pltpu.SemaphoreType.DMA((count,)),
         ],
         SWEEP * count * rows * width,
+        grown(25, count),
     )(*pieces, *ends, cum, local, y_pre, keep, w_in)
 
 
-def tail_back_kernel(hops, *refs):
+def tail_back_kernel(hops, block, *refs):
     ends = refs[:hops]
     later = refs[hops : 2 * hops]
-    (cb, lb, cum, local, r_ref, e_ref, k_ref, conv_ref, u_ref, m_ref, wz, par, du_out, edge_out, fold_out, small_out, gw_out) = refs[2 * hops :]
+    (cb, lb, cum, local, r_ref, e_ref, k_ref, conv_ref, u_ref, m_ref, wz, par, du_out, edge_out, tail_out, small_out, gw_out) = refs[2 * hops :]
     step = pl.program_id(0)
 
     @pl.when(step == 0)
@@ -554,8 +608,10 @@
     conv = conv_low.astype(F32)
     rows, width = conv.shape
     spare = 1.0 - keep * keep
-    scaling = jnp.sqrt(jnp.maximum(spare, FLOOR))
-    weight = jnp.where(spare > FLOOR, 0.5, jnp.where(spare == FLOOR, 0.25, 0.0)) / scaling
+    floored = jnp.maximum(spare, FLOOR)
+    root = lax.rsqrt(floored)
+    scaling = floored * root
+    weight = jnp.where(spare > FLOOR, 0.5, jnp.where(spare == FLOOR, 0.25, 0.0)) * root
     d_enter_sum = d_states * conv
     d_spare = d_enter_sum * enter * weight
     d_expo = (d_states * prev - 2.0 * keep * d_spare) * keep
@@ -591,31 +647,42 @@
 
     @pl.when(step == pl.num_programs(0) - 1)
     def _():
-        inside, fold = block_masks(width, fold_out.shape[1])
+        kept, wide = tail_out.shape
+        inside, fold = block_masks(width, block)
+        parts = []
         for gate in (0, 1):
             whole = jnp.where(inside, gw_out[gate * width : gate * width + width, :], 0.0).astype(BF16)
-            fold_out[gate * width : gate * width + width, :] = dot_nn(whole, fold).astype(BF16)
-
-
-def tail_back(ends, later, cb, lb, cum, local, recur, enter, keep, conv, u_ext, same, wz, par, block):
+            parts.append(dot_nn(whole, fold))
+        sums = small_out[...]
+        slope = -SHARP * sigmoid(par[15:16, :])
+        sums = jnp.concatenate([sums[:7], sums[7:8] * slope], 0).astype(BF16)
+        row = lax.broadcasted_iota(jnp.int32, (width, width), 0)
+        column = lax.broadcasted_iota(jnp.int32, (width, width), 1)
+        parts.append(dot_nt(jnp.where(row == column, 1.0, 0.0).astype(BF16), sums))
+        parts.append(jnp.zeros((width, wide - 2 * block - 8), F32))
+        tail_out[...] = jnp.concatenate(parts, 1)[:kept].astype(BF16)
+
+
+def tail_back(ends, later, cb, lb, cum, local, recur, enter, keep, conv, u_ext, same, wz, par, block, into, wide):
     count, rows, width = cb.shape
     shapes = [
         jax.ShapeDtypeStruct((count, rows, width), BF16),
         jax.ShapeDtypeStruct((count, 16, width), F32),
-        jax.ShapeDtypeStruct((2 * width, block), BF16),
-        jax.ShapeDtypeStruct((8, width), F32),
+        jax.ShapeDtypeStruct(into.shape, BF16),
     ]
+    last = into.shape[1] // wide - 1
     tall = u_ext.shape[1]
     return call(
-        functools.partial(tail_back_kernel, len(ends)),
+        functools.partial(tail_back_kernel, len(ends), block),
         (count,),
         [resident(ends[0].shape)] * (2 * len(ends))
         + [per_piece((rows, width))] * 8
         + [per_piece((tall, width)), per_piece((rows, width)), resident(wz.shape), resident(par.shape)],
-        [per_piece((rows, width)), per_piece((16, width)), resident((2 * width, block)), resident((8, width))],
+        [per_piece((rows, width)), per_piece((16, width)), pl.BlockSpec((into.shape[0], wide), lambda step: (0, last))],
         shapes,
-        [pltpu.VMEM(wz.shape, F32)],
+        [pltpu.VMEM((8, width), F32), pltpu.VMEM(wz.shape, F32)],
         SWEEP * count * rows * width,
+        60,
     )(*ends, *later, cb, lb, cum, local, recur, enter, keep, conv, u_ext, same, wz, par)
 
 
@@ -666,6 +733,7 @@
         shapes,
         [],
         3 + 2 * groups * pieces * rows * inner * model / RATE,
+        grown(20, pieces, 4),
     )(*lefts, *[right for right, _, _ in rights], *([factor] if gained else []))
 
 
@@ -690,6 +758,7 @@
         jax.ShapeDtypeStruct(shape, pieces[0].dtype),
         [pltpu.VMEM(shape, pieces[0].dtype), pltpu.SemaphoreType.DMA((count,)), pltpu.SemaphoreType.DMA((count,))],
         6.5,
+        grown(16, count),
     )(*pieces)
 
 
@@ -773,24 +842,43 @@
             pltpu.SemaphoreType.DMA((count,)),
         ],
         2 + 6 * count * rows * model * hidden / RATE,
+        grown(42, count) if first else 60,
     )(*sources, c_all, weights, weights, weights)
 
 
-def mlp_grads_kernel(tiles, dg, du, hid, h_tile, c_tile, out, turned):
+def mlp_grads_kernel(dg, du, hid, h_tile, c_tile, out, turned, slots, sems):
     step = pl.program_id(0)
-    for place, left in enumerate((dg, du, hid)):
-
-        @pl.when(step == place * tiles)
-        def _(left=left):
-            turned[...] = left[...].T
-
-    @pl.when(step < 2 * tiles)
-    def _():
-        out[...] = dot_nn(turned[...], h_tile[...]).astype(BF16)
-
-    @pl.when(step >= 2 * tiles)
-    def _():
-        out[...] = dot_nn(turned[...], c_tile[...]).astype(BF16)
+    steps = pl.num_programs(0)
+    tall, tile = slots.shape[2:]
+    model = steps * tile
+    slot = step % 2
+
+    def sending(place, at, slot):
+        columns = pl.ds(pl.multiple_of(place * model + at * tile, tile), tile)
+        return pltpu.make_async_copy(slots.at[slot, place], out.at[:, columns], sems.at[slot, place])
+
+    @pl.when(step == 0)
+    def _():
+        for place, left in enumerate((dg, du, hid)):
+            turned[place * tall : place * tall + tall, :] = left[...].T
+
+    @pl.when(step >= 2)
+    def _():
+        for place in range(3):
+            sending(place, step - 2, slot).wait()
+
+    both = dot_nn(turned[: 2 * tall, :], h_tile[...]).astype(BF16)
+    slots[slot, 0] = both[:tall]
+    slots[slot, 1] = both[tall:]
+    slots[slot, 2] = dot_nn(turned[2 * tall :, :], c_tile[...]).astype(BF16)
+    for place in range(3):
+        sending(place, step, slot).start()
+
+    @pl.when(step == steps - 1)
+    def _():
+        for place in range(3):
+            sending(place, step - 1, 1 - slot).wait()
+            sending(place, step, slot).wait()
 
 
 def mlp_grads(d_gate, d_up, hidden, h_all, c_all):
@@ -798,58 +886,53 @@
     lefts = [v.reshape(-1, v.shape[2]) for v in (d_gate, d_up, hidden)]
     rights = [v.reshape(-1, model) for v in (h_all, c_all)]
     inner, tall = lefts[0].shape
+    tile = min(column_tile(model), model // 2)
+    return call(
+        mlp_grads_kernel,
+        (model // tile,),
+        [resident((inner, tall))] * 3 + [pl.BlockSpec((inner, tile), lambda step: (0, step))] * 2,
+        ANY,
+        jax.ShapeDtypeStruct((tall, 3 * model), BF16),
+        [
+            pltpu.VMEM((3 * tall, inner), BF16),
+            pltpu.VMEM((2, 3, tall, tile), BF16),
+            pltpu.SemaphoreType.DMA((2, 3)),
+        ],
+        3 + 6 * inner * tall * model / RATE,
+        grown(40, inner, 2048),
+    )(*lefts, *rights)
+
+
+def weight_grad_kernel(left, right, *refs):
+    out, turned = refs[-2:]
+
+    @pl.when(pl.program_id(0) == 0)
+    def _():
+        turned[...] = left[...].T
+
+    out[...] = dot_nn(turned[...], right[...])[: out.shape[0]].astype(BF16)
+
+
+def weight_grad(rows_left, rows_right, kept, wide=None, into=None, place=0):
+    left = rows_left.reshape(-1, rows_left.shape[-1])
+    right = rows_right.reshape(-1, rows_right.shape[-1])
+    inner, tall = left.shape
+    model = right.shape[1]
     tile = column_tile(model)
-    tiles = model // tile
-    return call(
-        functools.partial(mlp_grads_kernel, tiles),
-        (3 * tiles,),
-        [resident((inner, tall))] * 3
-        + [
-            pl.BlockSpec((inner, tile), lambda step: (0, jnp.where(step < 2 * tiles, step % tiles, tiles - 1))),
-            pl.BlockSpec((inner, tile), lambda step: (0, jnp.maximum(step - 2 * tiles, 0))),
-        ],
-        pl.BlockSpec((tall, tile), lambda step: (0, step)),
-        jax.ShapeDtypeStruct((tall, 3 * model), BF16),
-        [pltpu.VMEM((tall, inner), BF16)],
-        3 + 6 * inner * tall * model / RATE,
-    )(*lefts, *rights)
-
-
-def weight_grads_kernel(tiles, count, *refs):
-    lefts, rights, out, turned = refs[:count], refs[count : 2 * count], refs[2 * count], refs[2 * count + 1]
-    step = pl.program_id(0)
-    for place in range(count):
-
-        @pl.when(step == place * tiles)
-        def _(left=lefts[place]):
-            turned[...] = left[...].T
-
-        @pl.when((step >= place * tiles) & (step < (place + 1) * tiles))
-        def _(right=rights[place]):
-            out[...] = dot_nn(turned[...], right[...])[: out.shape[0]].astype(BF16)
-
-
-def weight_grads(pairs, kept):
-    lefts = [left.reshape(-1, left.shape[-1]) for left, _ in pairs]
-    rights = [right.reshape(-1, right.shape[-1]) for _, right in pairs]
-    count = len(pairs)
-    inner, tall = lefts[0].shape
-    model = rights[0].shape[1]
-    tile = column_tile(model)
-    tiles = model // tile
-
-    def right_spec(place):
-        return pl.BlockSpec((inner, tile), lambda step: (0, jnp.clip(step - place * tiles, 0, tiles - 1)))
-
-    return call(
-        functools.partial(weight_grads_kernel, tiles, count),
-        (count * tiles,),
-        [resident((inner, tall))] * count + [right_spec(place) for place in range(count)],
-        pl.BlockSpec((kept, tile), lambda step: (0, step)),
-        jax.ShapeDtypeStruct((kept, count * model), BF16),
-        [pltpu.VMEM((tall, inner), BF16)],
-        3 + 2 * count * inner * tall * model / RATE,
-    )(*lefts, *rights)
+    steps = model // tile
+    extra = [] if into is None else [into]
+    wide = model if wide is None else wide
+    shape = (kept, wide) if into is None else into.shape
+    return pl.pallas_call(
+        weight_grad_kernel,
+        grid=(steps,),
+        in_specs=[resident(left.shape), pl.BlockSpec((inner, tile), lambda step: (0, step))] + [ANY] * len(extra),
+        out_specs=pl.BlockSpec((kept, tile), lambda step: (0, place * steps + step)),
+        out_shape=jax.ShapeDtypeStruct(shape, BF16),
+        scratch_shapes=[pltpu.VMEM((tall, inner), BF16)],
+        input_output_aliases={2: 0} if extra else {},
+        **settings(3 + 2 * inner * tall * model / RATE, 1, grown(16, inner, 2048)),
+    )(left, right, *extra)
 
 
 def add_kernel(counts, *refs):
@@ -881,6 +964,7 @@
         [jax.ShapeDtypeStruct((rows, width), BF16)] * len(sums),
         [],
         1 + 0.6 * len(arrays),
+        12,
     )(*arrays)
 
 
@@ -910,7 +994,7 @@
     kernel = last_kernel if gain is not None else lambda count, *refs: last_kernel(
         count, *refs[:count], None, refs[count], None, refs[count + 1]
     )
-    return call(
+    return stream(
         functools.partial(kernel, len(terms)),
         (steps,),
         [spec(place) for _, place in terms]
@@ -918,12 +1002,11 @@
         + ([] if gain is None else [resident(gain.shape)]),
         block,
         jax.ShapeDtypeStruct((tall, model), BF16),
-        [],
         6.0,
     )(*[array for array, _ in terms], *extra, base, *([] if gain is None else [gain]))
 
 
-def split_grads_kernel(one_gate, one_up, one_down, two_gate, two_up, two_down, both, down):
+def finish_grads_kernel(one_gate, one_up, one_down, two_gate, two_up, two_down, second, both, down, out):
     cut = one_gate.shape[0]
     both[:cut, 0, :] = one_gate[...].astype(F32)
     both[:cut, 1, :] = one_up[...].astype(F32)
@@ -931,28 +1014,68 @@
     both[cut:, 1, :] = two_up[...].astype(F32)
     down[:cut, :] = one_down[...].astype(F32)
     down[cut:, :] = two_down[...].astype(F32)
-
-
-def split_grads(one, two, model):
+    out[...] = second[...].astype(F32)
+
+
+def finish_grads(one, two, mix, model):
     rows = one.shape[0] + two.shape[0]
+    own = mix.shape[0]
     tile = column_tile(model)
     steps = model // tile
 
-    def spec(part, place):
-        return pl.BlockSpec((part.shape[0], tile), lambda step: (0, place * steps + step))
+    def spec(tall, place):
+        return pl.BlockSpec((tall, tile), lambda step: (0, place * steps + step))
 
     return call(
-        split_grads_kernel,
+        finish_grads_kernel,
         (steps,),
-        [spec(part, place) for part in (one, two) for place in range(3)],
+        [spec(part.shape[0], place) for part in (one, two) for place in range(3)] + [spec(own, 1)],
+        [pl.BlockSpec((rows, 2, tile), lambda step: (0, 0, step)), spec(rows, 0), spec(own, 0)],
         [
-            pl.BlockSpec((rows, 2, tile), lambda step: (0, 0, step)),
-            pl.BlockSpec((rows, tile), lambda step: (0, step)),
+            jax.ShapeDtypeStruct((rows, 2, model), F32),
+            jax.ShapeDtypeStruct((rows, model), F32),
+            jax.ShapeDtypeStruct((own, model), F32),
         ],
-        [jax.ShapeDtypeStruct((rows, 2, model), F32), jax.ShapeDtypeStruct((rows, model), F32)],
         [],
-        6.0,
-    )(one, one, one, two, two, two)
+        5.0,
+        16,
+    )(one, one, one, two, two, two, mix)
+
+
+def part_grads_kernel(block, first, second, tail, both, gate_w, rows):
+    both[:, 0, :] = first[...].astype(F32)
+    both[:, 1, :] = second[...].astype(F32)
+
+    @pl.when(pl.program_id(0) == 0)
+    def _():
+        held = tail[...]
+        gate_w[:, 0, :] = held[:, :block].astype(F32)
+        gate_w[:, 1, :] = held[:, block : 2 * block].astype(F32)
+        count = held.shape[0]
+        row = lax.broadcasted_iota(jnp.int32, (count, count), 0)
+        column = lax.broadcasted_iota(jnp.int32, (count, count), 1)
+        rows[...] = dot_tn(held[:, 2 * block : 2 * block + 8], jnp.where(row == column, 1.0, 0.0).astype(BF16))
+
+
+def part_grads(grads, last, model, wide, block):
+    rows = grads.shape[0]
+    tile = column_tile(model)
+    steps = model // tile
+    spec = pl.BlockSpec((rows, tile), lambda step: (0, step))
+    return call(
+        functools.partial(part_grads_kernel, block),
+        (steps,),
+        [spec, spec, pl.BlockSpec((rows, wide), lambda step: (0, model // wide))],
+        [pl.BlockSpec((rows, 2, tile), lambda step: (0, 0, step)), resident((rows, 2, block)), resident((8, rows))],
+        [
+            jax.ShapeDtypeStruct((rows, 2, model), F32),
+            jax.ShapeDtypeStruct((rows, 2, block), F32),
+            jax.ShapeDtypeStruct((8, rows), F32),
+        ],
+        [],
+        3.0,
+        16,
+    )(grads, last, last)
 
 
 def seq_gather(shard):
@@ -1050,8 +1173,8 @@
     c_pieces, (same, entered) = gather_rows(
         after(cot_low, *x_pieces),
         [
-            ((1,), lambda sent, done: same),
-            ((2, 3), lambda sent, done: mixer_enter(after(h_all, shards), done[0], w_in, extra, block)),
+            ((1, 2), lambda sent, done: same),
+            ((3,), lambda sent, done: mixer_enter(after(h_all, shards), done[0], w_in, extra, block)),
         ],
     )
     (u_ext, y_pre, conv, recur, enter, keep, cum, local, ends, w_z, par) = entered
@@ -1077,7 +1200,7 @@
         return rows_times(lefts, rights, blocks_at, pieces)
 
     def second_grads(sent, done):
-        return mlp_grads(after(gate_two, sent), up_two, hid_two, h_all, c_all)
+        return mlp_grads(after(gate_two, sent), up_two, hid_two, h_all, c_all), grad_one
 
     def mlp_leaving(blocks_at, pieces, before):
         return rows_times([after(hid_one, *before), hid_two], [(w_one, 2, model), (w_two, 2, model)], blocks_at, pieces)
@@ -1098,7 +1221,7 @@
         return mine, there, add_rows([[(mine, k), (there, k)] for k in range(half // 2, half)])
 
     d_pieces, done = gather_rows(d_mix, [((1, 2), second_grads), ((3,), mlp_out_sums)])
-    grad_two, (mine, there, far) = done
+    (grad_two, grad_one), (mine, there, far) = done
     grad_two = seq_scatter(after(grad_two, grad_one))
     d_y, mixed, cum_back, local_back, ends_back, d_all = head_back(
         after(d_pieces, far), earlier, cum, local, y_pre, keep, w_in
@@ -1106,24 +1229,41 @@
     got = [lax.ppermute(part, "dp", stages[-1]) for part in far]
     mixed, got = lax.optimization_barrier((mixed, got))
     later = [hand_on(ends_back, -steps) for steps in range(1, n_seq)]
-    grad_y_out = weight_grads([(after(d_y, ends_back), h_one), (mixed, d_all)], chan)
-    later, grad_y_out = lax.optimization_barrier((later, grad_y_out))
-    grad_y_out = seq_scatter(after(grad_y_out, grad_two))
-    d_u, edges, grad_z, sums = tail_back(
-        earlier, later, cum_back, local_back, cum, local, recur, enter, keep, conv, u_ext, same, w_z, par, block
+    wide = next(t for t in (128, 256, 512, 1024) if t >= 2 * block + 8 and model % t == 0)
+    terms = [[(mine, k), (there, k), (got[k][None], 0)] for k in range(half // 2)]
+    layer_sums = add_rows(terms[half // 4 :])
+    grad_mix = weight_grad(after(d_y, ends_back, layer_sums), h_one, chan, 2 * model)
+    grad_mix = weight_grad(mixed, d_all, chan, into=grad_mix, place=1)
+    later, grad_mix, grad_two = lax.optimization_barrier((later, grad_mix, grad_two))
+    grad_mix = seq_scatter(grad_mix)
+    layer_got = [lax.ppermute(part, "dp", stages[-2]) for part in layer_sums]
+    tailed = tail_back(
+        earlier,
+        later,
+        cum_back,
+        local_back,
+        cum,
+        local,
+        recur,
+        enter,
+        keep,
+        conv,
+        u_ext,
+        same,
+        w_z,
+        par,
+        block,
+        jax.ShapeDtypeStruct((chan, model + wide), BF16),
+        wide,
     )
+    (d_u, edges, grad_u), layer_got = lax.optimization_barrier((tailed, layer_got))
+    terms = [[*those, (one[None], 0)] for those, one in zip(terms, layer_got)]
     from_next = hand_on(edges[:, :8], -1)
-    terms = [[(mine, k), (there, k), (got[k][None], 0)] for k in range(half // 2)]
-    held = terms[half // 4 :]
-    arrays = after([[array for array, _ in those] for those in held], edges)
-    layer_sums = add_rows([[(v, at) for v, (_, at) in zip(vs, those)] for vs, those in zip(arrays, held)])
-    from_next, layer_sums = lax.optimization_barrier((from_next, layer_sums))
-    layer_got = [lax.ppermute(part, "dp", stages[-2]) for part in layer_sums]
-    grad_z = jnp.concatenate([grad_z[:chan], grad_z[width : width + chan]], 1)
-    sums = sums[:, :chan]
-    sums = jnp.concatenate([sums[:7], (sums[7] * (-SHARP * jax.nn.sigmoid(par[15, :chan])))[None]], 0).T
-    tail = jnp.concatenate([grad_z, sums.astype(BF16)], 1)
-    tail = jnp.pad(tail, ((0, 0), (0, extra - tail.shape[1])))
+    layer_terms = scatter_tail(terms, stages[:-2], [])
+    arrays = after([array for array, _ in layer_terms], edges)
+    layer_out = last_rows([(v, at) for v, (_, at) in zip(arrays, layer_terms)], x_one)
+    from_next, layer_out = lax.optimization_barrier((from_next, layer_out))
+    layer_out = layer_out.reshape(1, run_len, model)
     d_u = lax.dynamic_update_slice(d_u, (edges[:, 8:] + from_next).astype(BF16), (0, run_len - 8, 0))
     gain_terms = []
 
@@ -1132,37 +1272,33 @@
             [after(d_y, *before), d_u], [(w_in, 1, model), (w_in, 0, model)], blocks_at, pieces, h_one
         )
         gain_terms.append(gain_term.sum(0))
-        if blocks_at == [1]:
-            part_rows[0], layer_got[:] = lax.optimization_barrier((part_rows[0], layer_got))
         return part_rows
 
     def u_grad(sent):
-        return weight_grads([(after(d_u, sent), h_one)], chan)
-
-    d_h_one = scatter_terms(d_leaving, count, None, beside(u_grad, kept))
-    grad_u = seq_scatter(after(jnp.concatenate([kept.pop(), tail], 1), grad_y_out))
-    input_grad = last_rows(d_h_one, d_x_one, x_low, g_one).reshape(1, run_len, model)
-    terms = [[*those, (one[None], 0)] for those, one in zip(terms, layer_got)]
-    layer_terms = scatter_tail(terms, stages[:-2], [])
-    layer_out = last_rows(layer_terms, x_one).reshape(1, run_len, model)
+        return weight_grad(after(d_u, sent), h_one, chan, into=grad_u, place=0)
+
+    def finished(sent):
+        return finish_grads(after(grad_one, sent), grad_two, grad_mix, model)
+
+    ready = []
+    d_h_one = scatter_terms(d_leaving, count, beside(finished, ready), beside(u_grad, kept))
+    grad_mlp_in, grad_mlp_out, grad_out = ready.pop()
+    grad_u = seq_scatter(after(kept.pop(), grad_mix))
+    input_grad = last_rows(d_h_one, d_x_one, x_low, g_one)
     d_gain_one = sum(gain_terms) / g_one
     d_gains = jnp.concatenate([d_gain_one.reshape(n_dev, part), d_gain_two.reshape(n_dev, part)], 1)
     d_gains = lax.all_to_all(after(d_gains, input_grad), ("dp", "seq"), 0, 0, tiled=True).sum(0)
-    grad_mlp_in, grad_mlp_out = split_grads(after(grad_one, input_grad), grad_two, model)
-
-    tail = grad_u[:, model:].astype(F32)
-    grad_mix_in = jnp.stack([grad_y_out[:, :model].astype(F32), grad_u[:, :model].astype(F32)], 1)
-    at = 2 * block
+    grad_mix_in, grad_gate_w, rows = part_grads(after(grad_mix, grad_out), grad_u, model, wide, block)
     return (
         layer_out,
-        input_grad,
+        input_grad.reshape(1, run_len, model),
         grad_mix_in,
-        grad_y_out[:, model:].astype(F32),
-        tail[:, :at].reshape(own, 2, block),
-        tail[:, at : at + 4].T,
-        tail[:, at + 4],
-        tail[:, at + 5 : at + 7].T,
-        tail[:, at + 7],
+        grad_out,
+        grad_gate_w,
+        rows[:4],
+        rows[4],
+        rows[5:7],
+        rows[7],
         d_gains[:part],
         d_gains[part:],
         grad_mlp_in,

time: 617 us -> 594 us (0.963)
  Pallas kernels: 311 us -> 220 us
  waiting for transfers between devices: 150 us -> 189 us
  local copies, waits for them, and re-layouts: 32.6 us -> 70.8 us
  other arithmetic: 38.2 us -> 30.8 us
    unnamed x128 -> x213, local copies, waits for them, and re-layouts: 22.8 us -> 63.2 us
    ppermute x6, waiting for transfers between devices: 13 us -> 38.8 us  [scatter_terms(): got = [lax.ppermute(part, 'dp', stages[-1]) for part in sent]]
    pallas_call x9 -> x11, Pallas kernels: 121 us -> 95.8 us  [the longest x2 31.1 us: mlp_grads(): call(mlp_grads_kernel, (model // tile,), [resident((inner, tall))] * 3 +...]
    pallas_call x8, Pallas kernels: 32.4 us -> 7.55 us  [add_rows(): call(functools.partial(add_kernel, counts), (steps,), [spec(place) for pl...]
    pallas_call x7, Pallas kernels: 65.7 us -> 45 us  [rows_times(): call(functools.partial(rows_times_kernel, len(lefts), gained), (groups, s...]
    ppermute x15, waiting for transfers between devices: 64.4 us -> 75.4 us  [arrival(): return lax.ppermute(held[m ^ 1 << top], 'dp', stages[top])]
    pallas_call x3, Pallas kernels: 21.7 us -> 10.7 us  [mixer_leave(): call(functools.partial(mixer_leave_kernel, len(ends), pieces, blocks), (g...]
    reduce_scatter x4, waiting for transfers between devices: 4.9 us -> 12.8 us  [seq_scatter(): return lax.psum_scatter(whole, 'seq', scatter_dimension=0, tiled=True)]
  transfers between devices with their start and end apart: 73 -> 73, of which waited for: 30 -> 32; matrix products, arithmetic and copies ran while one was open for 6% -> 5% of each run, Pallas kernels for 51% -> 37%
where the time goes in v4:
time: 594 us; the launch traced here: 585 us
  Pallas kernels  220 us (37%)
  waiting for transfers between devices  189 us (32%)
  local copies, waits for them, and re-layouts  70.8 us (12%)
  starting transfers between devices  58.4 us (10%)
  other arithmetic  30.8 us (5%)
  between operations  16.1 us (3%)
    ppermute x15, waiting for transfers between devices, arrival(): return lax.ppermute(held[m ^ 1 << top], 'dp', stages[top])  75.4 us
    unnamed x213, local copies, waits for them, and re-layouts  63.2 us
    pallas_call x7, Pallas kernels, rows_times(): call(functools.partial(rows_times_kernel, len(lefts), gained), (groups, s...  45 us
    ppermute x6, waiting for transfers between devices, scatter_terms(): got = [lax.ppermute(part, 'dp', stages[-1]) for part in sent]  38.8 us
    pallas_call x2, Pallas kernels, mlp_part(): call(functools.partial(mlp_kernel, count, first), (hidden // tile,), [ANY...  33.5 us
    pallas_call x2, Pallas kernels, mlp_grads(): call(mlp_grads_kernel, (model // tile,), [resident((inner, tall))] * 3 +...  31.1 us
    ppermute x3, waiting for transfers between devices, scatter_tail(): got = [lax.ppermute(part, 'dp', pairs) for part in sent]  24.5 us
    pallas_call x1, Pallas kernels, tail_back(): call(functools.partial(tail_back_kernel, len(ends), block), (count,), [re...  17.6 us
  transfers between devices with their start and end apart: 73, of which 32 were waited for; matrix products, arithmetic and copies ran while one was open for 5% of the time, Pallas kernels for 37%

profile of v4, /device:TPU:0, one launch (start us, length us, event | category | flops | bytes accessed | tf_op | source)
XLA Modules:
  0.0 584.8 jit_solution(15253388092177726954)
XLA Ops:
  39.0 11.1 %collective-permute-done.refs_1_ = bf16[256,2048]{1,0:T(8,128)(2,1)} collective-permute-done((bf16[256,2048]{1,0:T(8,128)(2,1)S(1)}, bf16[256,2048]{1,0:T(8,128)(2,1)}, u32[]{:S(2)}, u32[]{:S(2)}) %collective-permute-start) | collective-permute-done | bytes 1048608 | tf_op jit(solution)/shard_map/ppermute | solution.py:76
  82.3 10.8 %shard_map.246 = (bf16[8,272,2048]{2,1,0:T(8,128)(2,1)}, bf16[8,256,2048]{2,1,0:T(8,128)(2,1)}, bf16[8,256,384]{2,1,0:T(8,128)(2,1)}) custom-call(bf16[256,2048]{1,0:T(8,128)(2,1)} %bitcast.121, bf16[256,2048]{1,0:T(8,128)(2,1)} %collective-permute-done.refs_1_, bf16[256,2048]{1,0:T(8,128)(2,1)} %collective-permute-done.1.refs_2_, ...), custom_call_target="tpu_custom_call" | custom-call | flops 2786882048 | bytes 1024 | tf_op jit(solution)/shard_map/pallas_call | solution.py:258
  93.2 10.5 %collective-permute-done.8.refs_2_ = bf16[256,2048]{1,0:T(8,128)(2,1)S(1)} collective-permute-done((bf16[256,2048]{1,0:T(8,128)(2,1)}, bf16[256,2048]{1,0:T(8,128)(2,1)S(1)}, u32[]{:S(2)}, u32[]{:S(2)}) %collective-permute-start.8) | collective-permute-done | bytes 1048608 | tf_op jit(solution)/shard_map/ppermute | solution.py:76
  109.9 16.4 %shard_map.247 = (bf16[8,272,384]{2,1,0:T(8,128)(2,1)S(1)}, f32[8,256,384]{2,1,0:T(8,128)S(1)}, bf16[8,256,384]{2,1,0:T(8,128)(2,1)S(1)}, f32[8,256,384]{2,1,0:T...) custom-call(bf16[8,272,2048]{2,1,0:T(8,128)(2,1)} %get-tuple-element, ...), custom_call_target="tpu_custom_call" | custom-call | flops 5024426496 | bytes 1024 | tf_op jit(solution)/shard_map/pallas_call | solution.py:438
  146.5 5.6 shard_map.251
  152.1 8.8 %collective-permute-done.25 = bf16[256,2048]{1,0:T(8,128)(2,1)S(1)} collective-permute-done((bf16[256,2048]{1,0:T(8,128)(2,1)S(1)}, bf16[256,2048]{1,0:T(8,128)(2,1)S(1)}, u32[]{:S(2)}, u32[]{:S(2)}) %collective-permute-start.25) | collective-permute-done | bytes 1048608 | tf_op jit(solution)/shard_map/ppermute | solution.py:122
  166.8 8.9 %collective-permute-done.27 = bf16[256,2048]{1,0:T(8,128)(2,1)S(1)} collective-permute-done((bf16[256,2048]{1,0:T(8,128)(2,1)S(1)}, bf16[256,2048]{1,0:T(8,128)(2,1)S(1)}, u32[]{:S(2)}, u32[]{:S(2)}) %collective-permute-start.27) | collective-permute-done | bytes 1048608 | tf_op jit(solution)/shard_map/ppermute | solution.py:122
  178.8 12.9 %collective-permute-done.28 = bf16[256,2048]{1,0:T(8,128)(2,1)} collective-permute-done((bf16[256,2048]{1,0:T(8,128)(2,1)}, bf16[256,2048]{1,0:T(8,128)(2,1)}, u32[]{:S(2)}, u32[]{:S(2)}) %collective-permute-start.28) | collective-permute-done | bytes 1048608 | tf_op jit(solution)/shard_map/ppermute | solution.py:108
  202.2 17.3 %collective-permute-done.30.refs_2_ = bf16[256,2048]{1,0:T(8,128)(2,1)S(1)} collective-permute-done((bf16[256,2048]{1,0:T(8,128)(2,1)S(1)}, bf16[256,2048]{1,0:T(8,128)(2,1)S(1)}, u32[]{:S(2)}, u32[]{:S(2)}) %collective-permute-start.30) | collective-permute-done | bytes 1048608 | tf_op jit(solution)/shard_map/ppermute | solution.py:76
  220.5 13.9 %collective-permute-done.35.refs_3_ = bf16[256,2048]{1,0:T(8,128)(2,1)} collective-permute-done((bf16[256,2048]{1,0:T(8,128)(2,1)S(1)}, bf16[256,2048]{1,0:T(8,128)(2,1)}, u32[]{:S(2)}, u32[]{:S(2)}) %collective-permute-start.35) | collective-permute-done | bytes 1048608 | tf_op jit(solution)/shard_map/ppermute | solution.py:76
  237.4 20.1 %shard_map.254 = (bf16[8,256,512]{2,1,0:T(8,128)(2,1)S(1)}, bf16[8,256,512]{2,1,0:T(8,128)(2,1)}, bf16[8,256,512]{2,1,0:T(8,128)(2,1)}, bf16[8,256,2048]{2,1,0:T(8,128)(2,1)}) custom-call(bf16[256,2048]{1,0:T(8,128)(2,1)S(1)} %multiply_convert_fusion.refs_0_, bf16[256,2048]{1,0:T(8,128)(2,1)S(1)} %collective-permute-done.29.refs_1_, ...), custom_call_target="tpu_custom_call" | custom-call | flops 5576969728 | bytes 1024 | tf_op jit(solution)/shard_map/pallas_call | solution.py:831
  260.8 18.8 %shard_map.255 = bf16[512,6144]{1,0:T(8,128)(2,1)S(1)} custom-call(bf16[2048,512]{1,0:T(8,128)(2,1)S(1)} %bitcast.111, bf16[2048,512]{1,0:T(8,128)(2,1)S(1)} %bitcast.112, bf16[2048,512]{1,0:T(8,128)(2,1)S(1)} %bitcast.117, bf16[2048,2048]{1,0:T(8,128)(2,1)} %bitcast.134, bf16[2048,2048]{1,0:T(8,128)(2,1)} %bitcast.109), custom_call_target="tpu_custom_call" | custom-call | flops 5832525312 | bytes 1024 | tf_op jit(solution)/shard_map/pallas_call | solution.py:890
  283.8 13.4 %shard_map.256 = (bf16[8,256,256]{2,1,0:T(8,128)(2,1)}, bf16[8,256,256]{2,1,0:T(8,128)(2,1)}, bf16[8,256,256]{2,1,0:T(8,128)(2,1)}) custom-call(bf16[8,256,2048]{2,1,0:T(8,128)(2,1)} %get-tuple-element.230.refs_0_, bf16[8,256,2048]{2,1,0:T(8,128)(2,1)} %copy-done.6, bf16[256,6144]{1,0:T(8,128)(2,1)} %all-gather.8.cloned.1.call-done.refs_2_.refs_3_.refs_4_.refs_6_.refs_7_, ...), custom_call_target="tpu_custom_call" | custom-call | flops 3044040448 | bytes 1024 | tf_op jit(solution)/shard_map/pallas_call | solution.py:831
  310.5 4.7 shard_map.258.refs_0_.refs_2_
  316.8 9.8 %shard_map.260 = (bf16[2,256,2048]{2,1,0:T(8,128)(2,1)S(1)}, bf16[2,256,2048]{2,1,0:T(8,128)(2,1)S(1)}) custom-call(bf16[8,256,512]{2,1,0:T(8,128)(2,1)S(1)} %copy-done.24, bf16[8,256,512]{2,1,0:T(8,128)(2,1)S(1)} %copy-done.26, bf16[8,256,256]{2,1,0:T(8,128)(2,1)S(1)} %copy-done.32, bf16[8,256,256]{2,1,0:T(8,128)(2,1)S(1)} %copy-done.34, ...), custom_call_target="tpu_custom_call" | custom-call | flops 3299596032 | bytes 1024 | tf_op jit(solution)/shard_map/pallas_call | solution.py:726
  335.3 10.2 %collective-permute-done.43 = bf16[256,2048]{1,0:T(8,128)(2,1)S(1)} collective-permute-done((bf16[256,2048]{1,0:T(8,128)(2,1)S(1)}, bf16[256,2048]{1,0:T(8,128)(2,1)S(1)}, u32[]{:S(2)}, u32[]{:S(2)}) %collective-permute-start.43) | collective-permute-done | bytes 1048608 | tf_op jit(solution)/shard_map/ppermute | solution.py:122
  346.5 10.0 %shard_map.262 = (bf16[4,256,2048]{2,1,0:T(8,128)(2,1)S(1)}, bf16[4,256,2048]{2,1,0:T(8,128)(2,1)S(1)}) custom-call(bf16[8,256,512]{2,1,0:T(8,128)(2,1)S(1)} %copy-done.38, bf16[8,256,256]{2,1,0:T(8,128)(2,1)S(1)} %copy-done.54, bf16[512,6144]{1,0:T(8,128)(2,1)S(1)} %copy-done.3, bf16[256,6144]{1,0:T(8,128)(2,1)S(1)} %copy-done.4), custom_call_target="tpu_custom_call" | custom-call | flops 3299596032 | bytes 1024 | tf_op jit(solution)/shard_map/pallas_call | solution.py:726
  366.9 12.2 %shard_map.263 = bf16[256,6144]{1,0:T(8,128)(2,1)} custom-call(bf16[2048,256]{1,0:T(8,128)(2,1)S(1)} %bitcast.115, bf16[2048,256]{1,0:T(8,128)(2,1)S(1)} %bitcast.116, bf16[2048,256]{1,0:T(8,128)(2,1)S(1)} %bitcast.126, bf16[2048,2048]{1,0:T(8,128)(2,1)} %bitcast.135, bf16[2048,2048]{1,0:T(8,128)(2,1)} %bitcast.110), custom_call_target="tpu_custom_call" | custom-call | flops 3299596032 | bytes 1024 | tf_op jit(solution)/shard_map/pallas_call | solution.py:890
  379.2 11.2 %collective-permute-done.46.refs_2_ = bf16[256,2048]{1,0:T(8,128)(2,1)S(1)} collective-permute-done((bf16[256,2048]{1,0:T(8,128)(2,1)S(1)}, bf16[256,2048]{1,0:T(8,128)(2,1)S(1)}, u32[]{:S(2)}, u32[]{:S(2)}) %collective-permute-start.46) | collective-permute-done | bytes 1048608 | tf_op jit(solution)/shard_map/ppermute | solution.py:76
  390.4 6.3 %reduce-scatter.5.cloned.1.call-done.one_gate.one_up.one_down = bf16[128,6144]{1,0:T(8,128)(2,1)} async-done(((bf16[512,6144]{1,0:T(8,128)(2,1)}), bf16[128,6144]{1,0:T(8,128)(2,1)}) %reduce-scatter.5.cloned.1.call-update) | async-done | bytes 1572880 | tf_op jit(solution)/shard_map/reduce_scatter | solution.py:1086
  399.3 5.2 collective-permute-done.48.refs_1_.refs_3_
  414.7 13.8 %shard_map.265 = (bf16[8,256,384]{2,1,0:T(8,128)(2,1)S(1)}, bf16[8,256,384]{2,1,0:T(8,128)(2,1)S(1)}, f32[8,256,384]{2,1,0:T(8,128)S(1)}, f32[8,256,384]{2,1,0:T...) custom-call(bf16[256,2048]{1,0:T(8,128)(2,1)S(1)} %get-tuple-element.261.refs_0_, ...), custom_call_target="tpu_custom_call" | custom-call | flops 5024426496 | bytes 1024 | tf_op jit(solution)/shard_map/pallas_call | solution.py:570
  432.5 5.6 collective-permute-done.57
  442.9 5.9 %shard_map.267.refs_0_ = bf16[320,4096]{1,0:T(8,128)(2,1)} custom-call(bf16[2048,384]{1,0:T(8,128)(2,1)S(1)} %bitcast.113, bf16[2048,2048]{1,0:T(8,128)(2,1)S(1)} %bitcast.105), custom_call_target="tpu_custom_call" | custom-call | flops 2033131392 | bytes 1024 | tf_op jit(solution)/shard_map/pallas_call | solution.py:926
  448.8 5.9 %shard_map.268 = bf16[320,4096]{1,0:T(8,128)(2,1)} custom-call(bf16[2048,384]{1,0:T(8,128)(2,1)S(1)} %bitcast.127, bf16[2048,2048]{1,0:T(8,128)(2,1)S(1)} %bitcast.120, bf16[320,4096]{1,0:T(8,128)(2,1)} %shard_map.267.refs_0_), custom_call_target="tpu_custom_call", output_to_operand_aliasing={{}: (2, {})} | custom-call | flops 2033131392 | bytes 1024 | tf_op jit(solution)/shard_map/pallas_call | solution.py:926
  454.7 6.5 %reduce-scatter.7.cloned.1.call-done.two_gate.two_up.two_down = bf16[64,6144]{1,0:T(8,128)(2,1)} async-done(((bf16[256,6144]{1,0:T(8,128)(2,1)}), bf16[64,6144]{1,0:T(8,128)(2,1)}) %reduce-scatter.7.cloned.1.call-update) | async-done | bytes 786448 | tf_op jit(solution)/shard_map/reduce_scatter | solution.py:1086
  462.8 17.6 %shard_map.269 = (bf16[8,256,384]{2,1,0:T(8,128)(2,1)}, f32[8,16,384]{2,1,0:T(8,128)}, bf16[320,2560]{1,0:T(8,128)(2,1)}) custom-call(f32[2,8,384]{2,1,0:T(8,128)} %copy-done.71, f32[2,8,384]{2,1,0:T(8,128)} %copy-done.70, f32[2,8,384]{2,1,0:T(8,128)} %copy-done.69, f32[2,8,384]{2,1,0:T(8,128)} %copy-done.87, f32[2,8,384]{2,1,0:T(8,128)} %copy-done.86, ...), custom_call_target="tpu_custom_call" | custom-call | flops 5024426496 | bytes 1024 | tf_op jit(solution)/shard_map/pallas_call | solution.py:675
  508.2 8.5 %shard_map.274 = (bf16[2,256,2048]{2,1,0:T(8,128)(2,1)}, bf16[2,256,2048]{2,1,0:T(8,128)(2,1)S(1)}, f32[2,1,2048]{2,1,0:T(1,128)S(1)}) custom-call(bf16[8,256,384]{2,1,0:T(8,128)(2,1)S(1)} %copy-done.28, bf16[8,256,384]{2,1,0:T(8,128)(2,1)S(1)} %fusion.11.refs_1_, bf16[320,6528]{1,0:T(8,128)(2,1)S(1)} %copy-done.2, bf16[320,6528]{1,0:T(8,128)(2,1)S(1)} %copy-done.2, ...), custom_call_target="tpu_custom_call" | custom-call | flops 1822053888 | bytes 1024 | tf_op jit(solution)/shard_map/pallas_call | solution.py:726
  521.9 5.2 shard_map.276
  545.0 9.8 %collective-permute-done.64 = bf16[256,2048]{1,0:T(8,128)(2,1)} collective-permute-done((bf16[256,2048]{1,0:T(8,128)(2,1)}, bf16[256,2048]{1,0:T(8,128)(2,1)}, u32[]{:S(2)}, u32[]{:S(2)}) %collective-permute-start.64) | collective-permute-done | bytes 1048608 | tf_op jit(solution)/shard_map/ppermute | solution.py:108
  559.2 5.8 all-to-all-start
  565.0 7.1 %all-to-all-done = f32[32,1,128]{2,1,0:T(1,128)S(1)} async-done(((f32[32,1,128]{2,1,0:T(1,128)}), f32[32,1,128]{2,1,0:T(1,128)S(1)}, u32[]{:S(2)}, u32[]{:S(2)}) %all-to-all-start) | async-done | bytes 16416 | tf_op jit(solution)/shard_map/all_to_all | solution.py:1290
  (467 shorter events, 238.9 us)
Async XLA Ops:
  7.2 100.0 %all-gather.4.cloned.1.call-start = ((), (), s32[]{:S(2)}) async-start(), calls=%async_computation.5 | async-start | bytes 5222400 | tf_op jit(solution)/shard_map/all_gather | solution.py:1082
  16.7 217.8 %all-gather.6.cloned.1.call-start = ((), (), s32[]{:S(2)}) async-start(), calls=%async_computation.6 | async-start | bytes 7864320 | tf_op jit(solution)/shard_map/all_gather | solution.py:1082
  23.8 52.3 %collective-permute-start.3 = (bf16[256,2048]{1,0:T(8,128)(2,1)S(1)}, bf16[256,2048]{1,0:T(8,128)(2,1)}, u32[]{:S(2)}, u32[]{:S(2)}) collective-permute-start(bf16[256,2048]{1,0:T(8,128)(2,1)S(1)} %bitcast.122), channel_id=1, source_target_pairs={{0,4},{4,0},{8,12},{12,8},{16,20},{20,16},{24,28},{28,24},{1,5},{5... | collective-permute-start | bytes 3145736 | tf_op jit(solution)/shard_map/ppermute | solution.py:89
  23.8 37.1 %collective-permute-start.1 = (bf16[256,2048]{1,0:T(8,128)(2,1)S(1)}, bf16[256,2048]{1,0:T(8,128)(2,1)}, u32[]{:S(2)}, u32[]{:S(2)}) collective-permute-start(bf16[256,2048]{1,0:T(8,128)(2,1)S(1)} %bitcast.123), channel_id=1, source_target_pairs={{0,16},{4,12},{8,24},{12,4},{16,0},{20,28},{24,8},{28,20},{1,17},{... | collective-permute-start | bytes 3145736 | tf_op jit(solution)/shard_map/ppermute | solution.py:76
  25.6 24.6 %collective-permute-start = (bf16[256,2048]{1,0:T(8,128)(2,1)S(1)}, bf16[256,2048]{1,0:T(8,128)(2,1)}, u32[]{:S(2)}, u32[]{:S(2)}) collective-permute-start(bf16[256,2048]{1,0:T(8,128)(2,1)S(1)} %bitcast.124), channel_id=1, source_target_pairs={{0,8},{4,20},{8,0},{12,28},{16,24},{20,4},{24,16},{28,12},{1,9},{5... | collective-permute-start | bytes 3145736 | tf_op jit(solution)/shard_map/ppermute | solution.py:76
  33.2 27.6 %collective-permute-start.16 = (bf16[16,2048]{1,0:T(8,128)(2,1)S(1)}, bf16[16,2048]{1,0:T(8,128)(2,1)}, u32[]{:S(2)}, u32[]{:S(2)}) collective-permute-start(bf16[16,2048]{1,0:T(8,128)(2,1)S(1)} %fusion.10.refs_8_), channel_id=1, source_target_pairs={{0,4},{4,0},{8,12},{12,8},{16,20},{20,16},{24,28},{28,24},{1,5},{5... | collective-permute-start | bytes 196616 | tf_op jit(solution)/shard_map/ppermute | solution.py:89
  33.3 32.7 %collective-permute-start.14 = (bf16[16,2048]{1,0:T(8,128)(2,1)S(1)}, bf16[16,2048]{1,0:T(8,128)(2,1)}, u32[]{:S(2)}, u32[]{:S(2)}) collective-permute-start(bf16[16,2048]{1,0:T(8,128)(2,1)S(1)} %fusion.10.refs_8_), channel_id=1, source_target_pairs={{0,16},{4,12},{8,24},{12,4},{16,0},{20,28},{24,8},{28,20},{1,17},{... | collective-permute-start | bytes 196616 | tf_op jit(solution)/shard_map/ppermute | solution.py:76
  60.7 223.1 %all-gather.8.cloned.1.call-start = ((), (), s32[]{:S(2)}) async-start(), calls=%async_computation.7 | async-start | bytes 3932160 | tf_op jit(solution)/shard_map/all_gather | solution.py:1082
  60.8 15.9 %collective-permute-start.4 = (bf16[256,2048]{1,0:T(8,128)(2,1)}, bf16[256,2048]{1,0:T(8,128)(2,1)S(1)}, u32[]{:S(2)}, u32[]{:S(2)}) collective-permute-start(bf16[256,2048]{1,0:T(8,128)(2,1)} %collective-permute-done.refs_1_), channel_id=1, source_target_pairs={{0,4},{4,0},{8,12},{12,8},{16,20},{20,16},{24,28},{28,24},{1,5},{5... | collective-permute-start | bytes 3145736 | tf_op jit(solution)/shard_map/ppermute | solution.py:89
  60.9 15.8 %collective-permute-start.5 = (bf16[256,2048]{1,0:T(8,128)(2,1)}, bf16[256,2048]{1,0:T(8,128)(2,1)S(1)}, u32[]{:S(2)}, u32[]{:S(2)}) collective-permute-start(bf16[256,2048]{1,0:T(8,128)(2,1)} %collective-permute-done.1.refs_2_), channel_id=1, source_target_pairs={{0,4},{4,0},{8,12},{12,8},{16,20},{20,16},{24,28},{28,24},{1,5},{5... | collective-permute-start | bytes 3145736 | tf_op jit(solution)/shard_map/ppermute | solution.py:89
  77.7 26.0 %collective-permute-start.8 = (bf16[256,2048]{1,0:T(8,128)(2,1)}, bf16[256,2048]{1,0:T(8,128)(2,1)S(1)}, u32[]{:S(2)}, u32[]{:S(2)}) collective-permute-start(bf16[256,2048]{1,0:T(8,128)(2,1)} %bitcast.refs_0_), channel_id=1, source_target_pairs={{0,16},{4,12},{8,24},{12,4},{16,0},{20,28},{24,8},{28,20},{1,17},{... | collective-permute-start | bytes 3145736 | tf_op jit(solution)/shard_map/ppermute | solution.py:76
  79.2 24.4 %collective-permute-start.7 = (bf16[256,2048]{1,0:T(8,128)(2,1)}, bf16[256,2048]{1,0:T(8,128)(2,1)}, u32[]{:S(2)}, u32[]{:S(2)}) collective-permute-start(bf16[256,2048]{1,0:T(8,128)(2,1)} %bitcast.refs_0_), channel_id=1, source_target_pairs={{0,8},{4,20},{8,0},{12,28},{16,24},{20,4},{24,16},{28,12},{1,9},{5... | collective-permute-start | bytes 3145736 | tf_op jit(solution)/shard_map/ppermute | solution.py:76
  103.6 27.5 %collective-permute-start.20 = (bf16[256,2048]{1,0:T(8,128)(2,1)}, bf16[256,2048]{1,0:T(8,128)(2,1)}, u32[]{:S(2)}, u32[]{:S(2)}) collective-permute-start(bf16[256,2048]{1,0:T(8,128)(2,1)} %collective-permute-done.7.refs_1_), channel_id=1, source_target_pairs={{0,16},{4,12},{8,24},{12,4},{16,0},{20,28},{24,8},{28,20},{1,17},{... | collective-permute-start | bytes 3145736 | tf_op jit(solution)/shard_map/ppermute | solution.py:76
  177.7 219.0 %reduce-scatter.5.cloned.1.call-start = ((), (), s32[]{:S(2)}) async-start(), calls=%async_computation.8 | async-start | bytes 7864320 | tf_op jit(solution)/shard_map/reduce_scatter | solution.py:1086
  177.8 17.4 %collective-permute-start.31 = (bf16[256,2048]{1,0:T(8,128)(2,1)}, bf16[256,2048]{1,0:T(8,128)(2,1)S(1)}, u32[]{:S(2)}, u32[]{:S(2)}) collective-permute-start(bf16[256,2048]{1,0:T(8,128)(2,1)} %bitcast.refs_0_), channel_id=1, source_target_pairs={{0,4},{4,0},{8,12},{12,8},{16,20},{20,16},{24,28},{28,24},{1,5},{5... | collective-permute-start | bytes 3145736 | tf_op jit(solution)/shard_map/ppermute | solution.py:89
  177.8 18.4 %collective-permute-start.32 = (bf16[256,2048]{1,0:T(8,128)(2,1)}, bf16[256,2048]{1,0:T(8,128)(2,1)S(1)}, u32[]{:S(2)}, u32[]{:S(2)}) collective-permute-start(bf16[256,2048]{1,0:T(8,128)(2,1)} %collective-permute-done.7.refs_1_), channel_id=1, source_target_pairs={{0,4},{4,0},{8,12},{12,8},{16,20},{20,16},{24,28},{28,24},{1,5},{5... | collective-permute-start | bytes 3145736 | tf_op jit(solution)/shard_map/ppermute | solution.py:89
  178.3 17.9 %collective-permute-start.33 = (bf16[256,2048]{1,0:T(8,128)(2,1)}, bf16[256,2048]{1,0:T(8,128)(2,1)S(1)}, u32[]{:S(2)}, u32[]{:S(2)}) collective-permute-start(bf16[256,2048]{1,0:T(8,128)(2,1)} %copy-done.61), channel_id=1, source_target_pairs={{0,4},{4,0},{8,12},{12,8},{16,20},{20,16},{24,28},{28,24},{1,5},{5... | collective-permute-start | bytes 3145736 | tf_op jit(solution)/shard_map/ppermute | solution.py:89
  178.4 17.9 %collective-permute-start.34 = (bf16[256,2048]{1,0:T(8,128)(2,1)}, bf16[256,2048]{1,0:T(8,128)(2,1)S(1)}, u32[]{:S(2)}, u32[]{:S(2)}) collective-permute-start(bf16[256,2048]{1,0:T(8,128)(2,1)} %collective-permute-done.20.refs_3_), channel_id=1, source_target_pairs={{0,4},{4,0},{8,12},{12,8},{16,20},{20,16},{24,28},{28,24},{1,5},{5... | collective-permute-start | bytes 3145736 | tf_op jit(solution)/shard_map/ppermute | solution.py:89
  194.7 24.8 %collective-permute-start.30 = (bf16[256,2048]{1,0:T(8,128)(2,1)S(1)}, bf16[256,2048]{1,0:T(8,128)(2,1)S(1)}, u32[]{:S(2)}, u32[]{:S(2)}) collective-permute-start(bf16[256,2048]{1,0:T(8,128)(2,1)S(1)} %multiply_convert_fusion.refs_0_), channel_id=1, source_target_pairs={{0,16},{4,12},{8,24},{12,4},{16,0},{20,28},{24,8},{28,20},{1,17},{... | collective-permute-start | bytes 3145736 | tf_op jit(solution)/shard_map/ppermute | solution.py:76
  195.2 24.3 %collective-permute-start.29 = (bf16[256,2048]{1,0:T(8,128)(2,1)S(1)}, bf16[256,2048]{1,0:T(8,128)(2,1)S(1)}, u32[]{:S(2)}, u32[]{:S(2)}) collective-permute-start(bf16[256,2048]{1,0:T(8,128)(2,1)S(1)} %multiply_convert_fusion.refs_0_), channel_id=1, source_target_pairs={{0,8},{4,20},{8,0},{12,28},{16,24},{20,4},{24,16},{28,12},{1,9},{5... | collective-permute-start | bytes 3145736 | tf_op jit(solution)/shard_map/ppermute | solution.py:76
  283.5 177.7 %reduce-scatter.7.cloned.1.call-start = ((), (), s32[]{:S(2)}) async-start(), calls=%async_computation.9 | async-start | bytes 3932160 | tf_op jit(solution)/shard_map/reduce_scatter | solution.py:1086
  365.5 24.9 %collective-permute-start.46 = (bf16[256,2048]{1,0:T(8,128)(2,1)S(1)}, bf16[256,2048]{1,0:T(8,128)(2,1)S(1)}, u32[]{:S(2)}, u32[]{:S(2)}) collective-permute-start(bf16[256,2048]{1,0:T(8,128)(2,1)S(1)} %get-tuple-element.261.refs_0_), channel_id=1, source_target_pairs={{0,16},{4,12},{8,24},{12,4},{16,0},{20,28},{24,8},{28,20},{1,17},{... | collective-permute-start | bytes 3145736 | tf_op jit(solution)/shard_map/ppermute | solution.py:76
  366.0 24.3 %collective-permute-start.45 = (bf16[256,2048]{1,0:T(8,128)(2,1)S(1)}, bf16[256,2048]{1,0:T(8,128)(2,1)S(1)}, u32[]{:S(2)}, u32[]{:S(2)}) collective-permute-start(bf16[256,2048]{1,0:T(8,128)(2,1)S(1)} %get-tuple-element.261.refs_0_), channel_id=1, source_target_pairs={{0,8},{4,20},{8,0},{12,28},{16,24},{20,4},{24,16},{28,12},{1,9},{5... | collective-permute-start | bytes 3145736 | tf_op jit(solution)/shard_map/ppermute | solution.py:76
  396.7 135.4 %reduce-scatter.9.cloned.1.call-start = ((), (), s32[]{:S(2)}) async-start(), calls=%async_computation.10 | async-start | bytes 3276800 | tf_op jit(solution)/shard_map/reduce_scatter | solution.py:1086
  412.0 20.5 %collective-permute-start.56 = (bf16[256,2048]{1,0:T(8,128)(2,1)S(1)}, bf16[256,2048]{1,0:T(8,128)(2,1)S(1)}, u32[]{:S(2)}, u32[]{:S(2)}) collective-permute-start(bf16[256,2048]{1,0:T(8,128)(2,1)S(1)} %get-tuple-element.259), channel_id=1, source_target_pairs={{0,16},{4,12},{8,24},{12,4},{16,0},{20,28},{24,8},{28,20},{1,17},{... | collective-permute-start | bytes 3145736 | tf_op jit(solution)/shard_map/ppermute | solution.py:1229
  413.4 24.6 %collective-permute-start.57 = (bf16[256,2048]{1,0:T(8,128)(2,1)S(1)}, bf16[256,2048]{1,0:T(8,128)(2,1)S(1)}, u32[]{:S(2)}, u32[]{:S(2)}) collective-permute-start(bf16[256,2048]{1,0:T(8,128)(2,1)S(1)} %get-tuple-element.260), channel_id=1, source_target_pairs={{0,16},{4,12},{8,24},{12,4},{16,0},{20,28},{24,8},{28,20},{1,17},{... | collective-permute-start | bytes 3145736 | tf_op jit(solution)/shard_map/ppermute | solution.py:1229
  428.5 26.1 %collective-permute-start.55 = (f32[2,8,384]{2,1,0:T(8,128)S(1)}, f32[2,8,384]{2,1,0:T(8,128)S(1)}, u32[]{:S(2)}, u32[]{:S(2)}) collective-permute-start(f32[2,8,384]{2,1,0:T(8,128)S(1)} %get-tuple-element.270), channel_id=1, source_target_pairs={{3,0},{7,4},{11,8},{15,12},{19,16},{23,20},{27,24},{31,28}} | collective-permute-start | bytes 73736 | tf_op jit(solution)/shard_map/ppermute | solution.py:163
  429.8 24.9 %collective-permute-start.54 = (f32[2,8,384]{2,1,0:T(8,128)S(1)}, f32[2,8,384]{2,1,0:T(8,128)S(1)}, u32[]{:S(2)}, u32[]{:S(2)}) collective-permute-start(f32[2,8,384]{2,1,0:T(8,128)S(1)} %get-tuple-element.270), channel_id=1, source_target_pairs={{2,0},{3,1},{6,4},{7,5},{10,8},{11,9},{14,12},{15,13},{18,16},{19,... | collective-permute-start | bytes 73736 | tf_op jit(solution)/shard_map/ppermute | solution.py:163
  431.1 23.6 %collective-permute-start.53 = (f32[2,8,384]{2,1,0:T(8,128)S(1)}, f32[2,8,384]{2,1,0:T(8,128)S(1)}, u32[]{:S(2)}, u32[]{:S(2)}) collective-permute-start(f32[2,8,384]{2,1,0:T(8,128)S(1)} %get-tuple-element.270), channel_id=1, source_target_pairs={{1,0},{2,1},{3,2},{5,4},{6,5},{7,6},{9,8},{10,9},{11,10},{13,12},{... | collective-permute-start | bytes 73736 | tf_op jit(solution)/shard_map/ppermute | solution.py:163
  461.2 111.5 %reduce-scatter.11.cloned.1.call-start = ((), (), s32[]{:S(2)}) async-start(), calls=%async_computation.11 | async-start | bytes 2048000 | tf_op jit(solution)/shard_map/reduce_scatter | solution.py:1086
  461.3 19.2 %collective-permute-start.58 = (bf16[256,2048]{1,0:T(8,128)(2,1)S(1)}, bf16[256,2048]{1,0:T(8,128)(2,1)}, u32[]{:S(2)}, u32[]{:S(2)}) collective-permute-start(bf16[256,2048]{1,0:T(8,128)(2,1)S(1)} %shard_map.266), channel_id=1, source_target_pairs={{0,8},{4,20},{8,0},{12,28},{16,24},{20,4},{24,16},{28,12},{1,9},{5... | collective-permute-start | bytes 3145736 | tf_op jit(solution)/shard_map/ppermute | solution.py:1239
  507.6 24.6 %collective-permute-start.63 = (bf16[256,2048]{1,0:T(8,128)(2,1)}, bf16[256,2048]{1,0:T(8,128)(2,1)S(1)}, u32[]{:S(2)}, u32[]{:S(2)}) collective-permute-start(bf16[256,2048]{1,0:T(8,128)(2,1)} %get-tuple-element.310), channel_id=1, source_target_pairs={{0,16},{4,12},{8,24},{12,4},{16,0},{20,28},{24,8},{28,20},{1,17},{... | collective-permute-start | bytes 3145736 | tf_op jit(solution)/shard_map/ppermute | solution.py:122
  (146 other events, 2013.0 us)
Sparse Core Ops, SparseCore 0:
  16.8 83.2 all-gather.3
  101.6 114.5 all-gather.5
  217.7 63.6 all-gather.7
  283.6 113.0 reduce-scatter.4
  398.9 62.3 reduce-scatter.6
  463.4 54.2 reduce-scatter.8
  532.3 37.4 reduce-scatter.10

commit v5 on v4

--- a/solution.py
+++ b/solution.py
@@ -100,7 +100,7 @@
 def scatter_tail(terms, stages, waits, late=()):
     for place, pairs in enumerate(reversed(stages)):
         split = len(terms) // 2
-        sent = add_rows(terms[split:])
+        sent = add_rows(terms[split:], 60)
         if late:
             sent, late = lax.optimization_barrier((sent, late))
             terms = [[*those, (one[None], 0)] for those, one in zip(terms, late)] + terms[split:]
@@ -112,7 +112,7 @@
     return terms[0]
 
 
-def scatter_terms(make, count, wait, low_wait=None):
+def scatter_terms(make, count, wait, ahead=None):
     stages, twin = plane_stages(lax.axis_size("dp"))
     quarter = count // 4
     theirs = make([3], quarter, ())[0]
@@ -122,18 +122,17 @@
     got = [lax.ppermute(part, "dp", stages[-1]) for part in sent]
     split = quarter // 2
     theirs, near = make([2, 0], quarter, (sent,))
-    theirs, near, got[split:] = lax.optimization_barrier((theirs, near, got[split:]))
+    extra = () if ahead is None else ahead(theirs)
+    theirs, near, got[split:], extra = lax.optimization_barrier((theirs, near, got[split:], extra))
     there = lax.ppermute(theirs, "dp", twin)
     terms = [[(near, k), (there, k)] for k in range(quarter)]
     terms = terms[:split] + [[*terms[k], (got[k][None], 0)] for k in range(split, quarter)]
     late = got[:split]
-    if low_wait is not None:
-        late = low_wait(sent, late)
-    return scatter_tail(terms, stages[:-1], [wait] if wait else [], late)
+    return scatter_tail(terms, stages[:-1], [wait] if wait else [], late), extra
 
 
 def scatter_rows(make, count, wait):
-    return total_of(scatter_terms(make, count, wait))
+    return total_of(scatter_terms(make, count, wait)[0])
 
 
 def beside(work, done):
@@ -945,7 +944,7 @@
         at += count
 
 
-def add_rows(sums):
+def add_rows(sums, memory=12):
     arrays = [array for terms in sums for array, _ in terms]
     places = [index for terms in sums for _, index in terms]
     _, rows, width = arrays[0].shape
@@ -964,7 +963,7 @@
         [jax.ShapeDtypeStruct((rows, width), BF16)] * len(sums),
         [],
         1 + 0.6 * len(arrays),
-        12,
+        memory,
     )(*arrays)
 
 
@@ -994,7 +993,7 @@
     kernel = last_kernel if gain is not None else lambda count, *refs: last_kernel(
         count, *refs[:count], None, refs[count], None, refs[count + 1]
     )
-    return stream(
+    return call(
         functools.partial(kernel, len(terms)),
         (steps,),
         [spec(place) for _, place in terms]
@@ -1002,7 +1001,9 @@
         + ([] if gain is None else [resident(gain.shape)]),
         block,
         jax.ShapeDtypeStruct((tall, model), BF16),
+        [],
         6.0,
+        60,
     )(*[array for array, _ in terms], *extra, base, *([] if gain is None else [gain]))
 
 
@@ -1169,12 +1170,12 @@
     g_one = gain_rows[:, :part].reshape(1, model)
     g_two = gain_rows[:, part:].reshape(1, model)
 
-    h_all, h_one, same = first_norm(x_pieces, tops, g_one, width)
+    h_all, h_one, same = first_norm(after(x_pieces, shards), tops, g_one, width)
     c_pieces, (same, entered) = gather_rows(
-        after(cot_low, *x_pieces),
+        after(cot_low, x_pieces[half - 1]),
         [
             ((1, 2), lambda sent, done: same),
-            ((3,), lambda sent, done: mixer_enter(after(h_all, shards), done[0], w_in, extra, block)),
+            ((3,), lambda sent, done: mixer_enter(h_all, done[0], w_in, extra, block)),
         ],
     )
     (u_ext, y_pre, conv, recur, enter, keep, cum, local, ends, w_z, par) = entered
@@ -1281,14 +1282,15 @@
         return finish_grads(after(grad_one, sent), grad_two, grad_mix, model)
 
     ready = []
-    d_h_one = scatter_terms(d_leaving, count, beside(finished, ready), beside(u_grad, kept))
+    d_h_one, grad_u = scatter_terms(d_leaving, count, beside(finished, ready), u_grad)
     grad_mlp_in, grad_mlp_out, grad_out = ready.pop()
-    grad_u = seq_scatter(after(kept.pop(), grad_mix))
+    grad_u = seq_scatter(after(grad_u, grad_mix))
     input_grad = last_rows(d_h_one, d_x_one, x_low, g_one)
     d_gain_one = sum(gain_terms) / g_one
     d_gains = jnp.concatenate([d_gain_one.reshape(n_dev, part), d_gain_two.reshape(n_dev, part)], 1)
-    d_gains = lax.all_to_all(after(d_gains, input_grad), ("dp", "seq"), 0, 0, tiled=True).sum(0)
+    d_gains = lax.all_to_all(after(d_gains, d_h_one[-1][0]), ("dp", "seq"), 0, 0, tiled=True)
     grad_mix_in, grad_gate_w, rows = part_grads(after(grad_mix, grad_out), grad_u, model, wide, block)
+    d_gains = after(d_gains, grad_mix_in).sum(0)
     return (
         layer_out,
         input_grad.reshape(1, run_len, model),

time: 594 us -> 583 us (0.981)
  waiting for transfers between devices: 189 us -> 157 us
  Pallas kernels: 220 us -> 230 us
  starting transfers between devices: 58.4 us -> 65.7 us
    ppermute x6, waiting for transfers between devices: 38.8 us -> 25.3 us  [scatter_terms(): got = [lax.ppermute(part, 'dp', stages[-1]) for part in sent]]
    ppermute x15, waiting for transfers between devices: 75.4 us -> 63.7 us  [arrival(): return lax.ppermute(held[m ^ 1 << top], 'dp', stages[top])]
    pallas_call x8, Pallas kernels: 7.55 us -> 18.2 us  [add_rows(): call(functools.partial(add_kernel, counts), (steps,), [spec(place) for pl...]
    reduce_scatter x4, waiting for transfers between devices: 12.8 us -> 3.27 us  [seq_scatter(): return lax.psum_scatter(whole, 'seq', scatter_dimension=0, tiled=True)]
    all_to_all x1, waiting for transfers between devices: 7.1 us -> 0.01 us  [per_device(): lax.all_to_all(after(d_gains, d_h_one[-1][0]), ('dp', 'seq'), 0, 0, tiled...]
    unnamed x213 -> x209, local copies, waits for them, and re-layouts: 63.2 us -> 62.4 us
  transfers between devices with their start and end apart: 73 -> 73, of which waited for: 32 -> 32; matrix products, arithmetic and copies ran while one was open for 5% -> 6% of each run, Pallas kernels for 37% -> 40%
where the time goes in v5:
time: 583 us; the launch traced here: 574 us
  Pallas kernels  230 us (39%)
  waiting for transfers between devices  157 us (27%)
  local copies, waits for them, and re-layouts  72.9 us (13%)
  starting transfers between devices  65.7 us (11%)
  other arithmetic  31 us (5%)
  between operations  16.1 us (3%)
    ppermute x15, waiting for transfers between devices, arrival(): return lax.ppermute(held[m ^ 1 << top], 'dp', stages[top])  63.7 us
    unnamed x209, local copies, waits for them, and re-layouts  62.4 us
    pallas_call x7, Pallas kernels, rows_times(): call(functools.partial(rows_times_kernel, len(lefts), gained), (groups, s...  44.4 us
    pallas_call x2, Pallas kernels, mlp_part(): call(functools.partial(mlp_kernel, count, first), (hidden // tile,), [ANY...  34 us
    pallas_call x2, Pallas kernels, mlp_grads(): call(mlp_grads_kernel, (model // tile,), [resident((inner, tall))] * 3 +...  31 us
    ppermute x6, waiting for transfers between devices, scatter_terms(): got = [lax.ppermute(part, 'dp', stages[-1]) for part in sent]  25.3 us
    ppermute x3, waiting for transfers between devices, scatter_tail(): got = [lax.ppermute(part, 'dp', pairs) for part in sent]  23 us
    ppermute x15, starting transfers between devices, arrival(): return lax.ppermute(held[m ^ 1 << top], 'dp', stages[top])  18.8 us
  transfers between devices with their start and end apart: 73, of which 32 were waited for; matrix products, arithmetic and copies ran while one was open for 6% of the time, Pallas kernels for 40%

profile of v5, /device:TPU:0, one launch (start us, length us, event | category | flops | bytes accessed | tf_op | source)
XLA Modules:
  0.0 573.6 jit_solution(8676485423309664829)
XLA Ops:
  72.1 10.9 %shard_map.246 = (bf16[8,272,2048]{2,1,0:T(8,128)(2,1)}, bf16[8,256,2048]{2,1,0:T(8,128)(2,1)}, bf16[8,256,384]{2,1,0:T(8,128)(2,1)}) custom-call(bf16[256,2048]{1,0:T(8,128)(2,1)} %bitcast.1.refs_0_.refs_4_, bf16[256,2048]{1,0:T(8,128)(2,1)} %collective-permute-done.refs_1_, bf16[256,2048]{1,0:T(8,128)(2,1)} %collective-permute-done.4.refs_2_, ...), custom_call_target="tpu_custom_call" | custom-call | flops 2786882048 | bytes 1024 | tf_op jit(solution)/shard_map/pallas_call | solution.py:257
  83.0 9.3 %collective-permute-done.3.refs_2_ = bf16[256,2048]{1,0:T(8,128)(2,1)S(1)} collective-permute-done((bf16[256,2048]{1,0:T(8,128)(2,1)S(1)}, bf16[256,2048]{1,0:T(8,128)(2,1)S(1)}, u32[]{:S(2)}, u32[]{:S(2)}) %collective-permute-start.3) | collective-permute-done | bytes 1048608 | tf_op jit(solution)/shard_map/ppermute | solution.py:76
  101.7 16.3 %shard_map.247 = (bf16[8,272,384]{2,1,0:T(8,128)(2,1)S(1)}, f32[8,256,384]{2,1,0:T(8,128)S(1)}, bf16[8,256,384]{2,1,0:T(8,128)(2,1)S(1)}, f32[8,256,384]{2,1,0:T...) custom-call(bf16[8,272,2048]{2,1,0:T(8,128)(2,1)} %get-tuple-element, ...), custom_call_target="tpu_custom_call" | custom-call | flops 5024426496 | bytes 1024 | tf_op jit(solution)/shard_map/pallas_call | solution.py:437
  142.5 5.6 shard_map.251
  149.5 6.3 %collective-permute-done.25 = bf16[256,2048]{1,0:T(8,128)(2,1)S(1)} collective-permute-done((bf16[256,2048]{1,0:T(8,128)(2,1)S(1)}, bf16[256,2048]{1,0:T(8,128)(2,1)S(1)}, u32[]{:S(2)}, u32[]{:S(2)}) %collective-permute-start.25) | collective-permute-done | bytes 1048608 | tf_op jit(solution)/shard_map/ppermute | solution.py:122
  165.3 5.6 collective-permute-done.27
  173.6 12.4 %collective-permute-done.28 = bf16[256,2048]{1,0:T(8,128)(2,1)} collective-permute-done((bf16[256,2048]{1,0:T(8,128)(2,1)}, bf16[256,2048]{1,0:T(8,128)(2,1)}, u32[]{:S(2)}, u32[]{:S(2)}) %collective-permute-start.28) | collective-permute-done | bytes 1048608 | tf_op jit(solution)/shard_map/ppermute | solution.py:108
  197.3 17.3 %collective-permute-done.30.refs_2_ = bf16[256,2048]{1,0:T(8,128)(2,1)S(1)} collective-permute-done((bf16[256,2048]{1,0:T(8,128)(2,1)S(1)}, bf16[256,2048]{1,0:T(8,128)(2,1)S(1)}, u32[]{:S(2)}, u32[]{:S(2)}) %collective-permute-start.30) | collective-permute-done | bytes 1048608 | tf_op jit(solution)/shard_map/ppermute | solution.py:76
  216.1 13.4 %collective-permute-done.35.refs_3_ = bf16[256,2048]{1,0:T(8,128)(2,1)S(1)} collective-permute-done((bf16[256,2048]{1,0:T(8,128)(2,1)}, bf16[256,2048]{1,0:T(8,128)(2,1)S(1)}, u32[]{:S(2)}, u32[]{:S(2)}) %collective-permute-start.35) | collective-permute-done | bytes 1048608 | tf_op jit(solution)/shard_map/ppermute | solution.py:76
  232.3 20.6 %shard_map.254 = (bf16[8,256,512]{2,1,0:T(8,128)(2,1)S(1)}, bf16[8,256,512]{2,1,0:T(8,128)(2,1)}, bf16[8,256,512]{2,1,0:T(8,128)(2,1)}, bf16[8,256,2048]{2,1,0:T(8,128)(2,1)}) custom-call(bf16[256,2048]{1,0:T(8,128)(2,1)S(1)} %multiply_convert_fusion.refs_0_, bf16[256,2048]{1,0:T(8,128)(2,1)} %collective-permute-done.29.refs_1_, ...), custom_call_target="tpu_custom_call" | custom-call | flops 5576969728 | bytes 1024 | tf_op jit(solution)/shard_map/pallas_call | solution.py:830
  256.1 18.8 %shard_map.255 = bf16[512,6144]{1,0:T(8,128)(2,1)S(1)} custom-call(bf16[2048,512]{1,0:T(8,128)(2,1)S(1)} %bitcast.112, bf16[2048,512]{1,0:T(8,128)(2,1)S(1)} %bitcast.113, bf16[2048,512]{1,0:T(8,128)(2,1)S(1)} %bitcast.118, bf16[2048,2048]{1,0:T(8,128)(2,1)} %bitcast.129, bf16[2048,2048]{1,0:T(8,128)(2,1)} %bitcast.110), custom_call_target="tpu_custom_call" | custom-call | flops 5832525312 | bytes 1024 | tf_op jit(solution)/shard_map/pallas_call | solution.py:889
  279.6 13.4 %shard_map.256 = (bf16[8,256,256]{2,1,0:T(8,128)(2,1)}, bf16[8,256,256]{2,1,0:T(8,128)(2,1)}, bf16[8,256,256]{2,1,0:T(8,128)(2,1)}) custom-call(bf16[8,256,2048]{2,1,0:T(8,128)(2,1)} %get-tuple-element.244.refs_0_, bf16[8,256,2048]{2,1,0:T(8,128)(2,1)} %copy-done.7, bf16[256,6144]{1,0:T(8,128)(2,1)} %all-gather.8.cloned.1.call-done.refs_2_.refs_3_.refs_4_.refs_6_.refs_7_, ...), custom_call_target="tpu_custom_call" | custom-call | flops 3044040448 | bytes 1024 | tf_op jit(solution)/shard_map/pallas_call | solution.py:830
  301.5 4.7 shard_map.257
  306.2 4.7 shard_map.258.refs_0_.refs_2_
  314.1 9.8 %shard_map.260 = (bf16[2,256,2048]{2,1,0:T(8,128)(2,1)S(1)}, bf16[2,256,2048]{2,1,0:T(8,128)(2,1)S(1)}) custom-call(bf16[8,256,512]{2,1,0:T(8,128)(2,1)S(1)} %copy-done.20, bf16[8,256,512]{2,1,0:T(8,128)(2,1)S(1)} %copy-done.22, bf16[8,256,256]{2,1,0:T(8,128)(2,1)S(1)} %copy-done.28, bf16[8,256,256]{2,1,0:T(8,128)(2,1)S(1)} %copy-done.31, ...), custom_call_target="tpu_custom_call" | custom-call | flops 3299596032 | bytes 1024 | tf_op jit(solution)/shard_map/pallas_call | solution.py:725
  336.8 5.7 %collective-permute-done.43 = bf16[256,2048]{1,0:T(8,128)(2,1)} collective-permute-done((bf16[256,2048]{1,0:T(8,128)(2,1)}, bf16[256,2048]{1,0:T(8,128)(2,1)}, u32[]{:S(2)}, u32[]{:S(2)}) %collective-permute-start.43) | collective-permute-done | bytes 1048608 | tf_op jit(solution)/shard_map/ppermute | solution.py:122
  349.7 10.0 %shard_map.262 = (bf16[4,256,2048]{2,1,0:T(8,128)(2,1)S(1)}, bf16[4,256,2048]{2,1,0:T(8,128)(2,1)S(1)}) custom-call(bf16[8,256,512]{2,1,0:T(8,128)(2,1)S(1)} %copy-done.36, bf16[8,256,256]{2,1,0:T(8,128)(2,1)S(1)} %copy-done.48, bf16[512,6144]{1,0:T(8,128)(2,1)S(1)} %copy-done.4, bf16[256,6144]{1,0:T(8,128)(2,1)S(1)} %copy-done.5), custom_call_target="tpu_custom_call" | custom-call | flops 3299596032 | bytes 1024 | tf_op jit(solution)/shard_map/pallas_call | solution.py:725
  371.1 12.3 %shard_map.263 = bf16[256,6144]{1,0:T(8,128)(2,1)} custom-call(bf16[2048,256]{1,0:T(8,128)(2,1)S(1)} %bitcast.116, bf16[2048,256]{1,0:T(8,128)(2,1)S(1)} %bitcast.117, bf16[2048,256]{1,0:T(8,128)(2,1)S(1)} %bitcast.126, bf16[2048,2048]{1,0:T(8,128)(2,1)} %bitcast.130, bf16[2048,2048]{1,0:T(8,128)(2,1)} %bitcast.111), custom_call_target="tpu_custom_call" | custom-call | flops 3299596032 | bytes 1024 | tf_op jit(solution)/shard_map/pallas_call | solution.py:889
  383.3 11.3 %collective-permute-done.46.refs_2_ = bf16[256,2048]{1,0:T(8,128)(2,1)S(1)} collective-permute-done((bf16[256,2048]{1,0:T(8,128)(2,1)S(1)}, bf16[256,2048]{1,0:T(8,128)(2,1)S(1)}, u32[]{:S(2)}, u32[]{:S(2)}) %collective-permute-start.46) | collective-permute-done | bytes 1048608 | tf_op jit(solution)/shard_map/ppermute | solution.py:76
  396.3 6.3 %collective-permute-done.48.refs_1_.refs_3_ = bf16[4,256,2048]{2,1,0:T(8,128)(2,1)S(1)} collective-permute-done((bf16[4,256,2048]{2,1,0:T(8,128)(2,1)}, bf16[4,256,2048]{2,1,0:T(8,128)(2,1)S(1)}, u32[]{:S(2)}, u32[]{:S(2)}) %collective-permute-start.48) | collective-permute-done | bytes 4194336 | tf_op jit(solution)/shard_map/ppermute | solution.py:1221
  412.6 13.8 %shard_map.265 = (bf16[8,256,384]{2,1,0:T(8,128)(2,1)S(1)}, bf16[8,256,384]{2,1,0:T(8,128)(2,1)S(1)}, f32[8,256,384]{2,1,0:T(8,128)S(1)}, f32[8,256,384]{2,1,0:T...) custom-call(bf16[256,2048]{1,0:T(8,128)(2,1)S(1)} %get-tuple-element.275.refs_0_, ...), custom_call_target="tpu_custom_call" | custom-call | flops 5024426496 | bytes 1024 | tf_op jit(solution)/shard_map/pallas_call | solution.py:569
  430.4 5.6 collective-permute-done.57
  440.9 5.8 %shard_map.267.refs_0_ = bf16[320,4096]{1,0:T(8,128)(2,1)} custom-call(bf16[2048,384]{1,0:T(8,128)(2,1)S(1)} %bitcast.114, bf16[2048,2048]{1,0:T(8,128)(2,1)S(1)} %bitcast.106), custom_call_target="tpu_custom_call" | custom-call | flops 2033131392 | bytes 1024 | tf_op jit(solution)/shard_map/pallas_call | solution.py:925
  446.7 5.9 %shard_map.268 = bf16[320,4096]{1,0:T(8,128)(2,1)} custom-call(bf16[2048,384]{1,0:T(8,128)(2,1)S(1)} %bitcast.127, bf16[2048,2048]{1,0:T(8,128)(2,1)S(1)} %bitcast.121, bf16[320,4096]{1,0:T(8,128)(2,1)} %shard_map.267.refs_0_), custom_call_target="tpu_custom_call", output_to_operand_aliasing={{}: (2, {})} | custom-call | flops 2033131392 | bytes 1024 | tf_op jit(solution)/shard_map/pallas_call | solution.py:925
  457.5 17.5 %shard_map.269 = (bf16[8,256,384]{2,1,0:T(8,128)(2,1)}, f32[8,16,384]{2,1,0:T(8,128)}, bf16[320,2560]{1,0:T(8,128)(2,1)}) custom-call(f32[2,8,384]{2,1,0:T(8,128)} %copy-done.63, f32[2,8,384]{2,1,0:T(8,128)} %copy-done.62, f32[2,8,384]{2,1,0:T(8,128)} %copy-done.61, f32[2,8,384]{2,1,0:T(8,128)} %copy-done.87, f32[2,8,384]{2,1,0:T(8,128)} %copy-done.86, ...), custom_call_target="tpu_custom_call" | custom-call | flops 5024426496 | bytes 1024 | tf_op jit(solution)/shard_map/pallas_call | solution.py:674
  477.9 4.6 shard_map.270
  482.5 5.0 collective-permute-done.59
  504.4 7.9 %shard_map.274 = (bf16[2,256,2048]{2,1,0:T(8,128)(2,1)S(1)}, bf16[2,256,2048]{2,1,0:T(8,128)(2,1)S(1)}, f32[2,1,2048]{2,1,0:T(1,128)S(1)}) custom-call(bf16[8,256,384]{2,1,0:T(8,128)(2,1)S(1)} %copy-done.24, bf16[8,256,384]{2,1,0:T(8,128)(2,1)S(1)} %fusion.11.refs_1_, bf16[320,6528]{1,0:T(8,128)(2,1)S(1)} %copy-done.2, bf16[320,6528]{1,0:T(8,128)(2,1)S(1)} %copy-done.2, ...), custom_call_target="tpu_custom_call" | custom-call | flops 1822053888 | bytes 1024 | tf_op jit(solution)/shard_map/pallas_call | solution.py:725
  515.0 5.2 shard_map.275
  531.1 5.5 collective-permute-done.63
  541.1 10.6 %collective-permute-done.64 = bf16[256,2048]{1,0:T(8,128)(2,1)} collective-permute-done((bf16[256,2048]{1,0:T(8,128)(2,1)}, bf16[256,2048]{1,0:T(8,128)(2,1)}, u32[]{:S(2)}, u32[]{:S(2)}) %collective-permute-start.64) | collective-permute-done | bytes 1048608 | tf_op jit(solution)/shard_map/ppermute | solution.py:108
  555.6 5.4 shard_map.278
  (463 shorter events, 250.3 us)
Async XLA Ops:
  7.2 90.9 %all-gather.4.cloned.1.call-start = ((), (), s32[]{:S(2)}) async-start(), calls=%async_computation.5 | async-start | bytes 5222400 | tf_op jit(solution)/shard_map/all_gather | solution.py:1083
  14.7 214.8 %all-gather.6.cloned.1.call-start = ((), (), s32[]{:S(2)}) async-start(), calls=%async_computation.6 | async-start | bytes 7864320 | tf_op jit(solution)/shard_map/all_gather | solution.py:1083
  21.8 46.6 %collective-permute-start.5 = (bf16[256,2048]{1,0:T(8,128)(2,1)}, bf16[256,2048]{1,0:T(8,128)(2,1)}, u32[]{:S(2)}, u32[]{:S(2)}) collective-permute-start(bf16[256,2048]{1,0:T(8,128)(2,1)} %bitcast.1.refs_0_.refs_4_), channel_id=1, source_target_pairs={{0,4},{4,0},{8,12},{12,8},{16,20},{20,16},{24,28},{28,24},{1,5},{5... | collective-permute-start | bytes 3145736 | tf_op jit(solution)/shard_map/ppermute | solution.py:89
  21.8 44.4 %collective-permute-start.4 = (bf16[256,2048]{1,0:T(8,128)(2,1)}, bf16[256,2048]{1,0:T(8,128)(2,1)}, u32[]{:S(2)}, u32[]{:S(2)}) collective-permute-start(bf16[256,2048]{1,0:T(8,128)(2,1)} %bitcast.1.refs_0_.refs_4_), channel_id=1, source_target_pairs={{0,16},{4,12},{8,24},{12,4},{16,0},{20,28},{24,8},{28,20},{1,17},{... | collective-permute-start | bytes 3145736 | tf_op jit(solution)/shard_map/ppermute | solution.py:76
  24.4 24.0 %collective-permute-start = (bf16[256,2048]{1,0:T(8,128)(2,1)}, bf16[256,2048]{1,0:T(8,128)(2,1)}, u32[]{:S(2)}, u32[]{:S(2)}) collective-permute-start(bf16[256,2048]{1,0:T(8,128)(2,1)} %bitcast.1.refs_0_.refs_4_), channel_id=1, source_target_pairs={{0,8},{4,20},{8,0},{12,28},{16,24},{20,4},{24,16},{28,12},{1,9},{5... | collective-permute-start | bytes 3145736 | tf_op jit(solution)/shard_map/ppermute | solution.py:76
  32.1 27.6 %collective-permute-start.16 = (bf16[16,2048]{1,0:T(8,128)(2,1)S(1)}, bf16[16,2048]{1,0:T(8,128)(2,1)S(1)}, u32[]{:S(2)}, u32[]{:S(2)}) collective-permute-start(bf16[16,2048]{1,0:T(8,128)(2,1)S(1)} %fusion.10.refs_8_), channel_id=1, source_target_pairs={{0,4},{4,0},{8,12},{12,8},{16,20},{20,16},{24,28},{28,24},{1,5},{5... | collective-permute-start | bytes 196616 | tf_op jit(solution)/shard_map/ppermute | solution.py:89
  32.2 22.4 %collective-permute-start.14 = (bf16[16,2048]{1,0:T(8,128)(2,1)S(1)}, bf16[16,2048]{1,0:T(8,128)(2,1)}, u32[]{:S(2)}, u32[]{:S(2)}) collective-permute-start(bf16[16,2048]{1,0:T(8,128)(2,1)S(1)} %fusion.10.refs_8_), channel_id=1, source_target_pairs={{0,16},{4,12},{8,24},{12,4},{16,0},{20,28},{24,8},{28,20},{1,17},{... | collective-permute-start | bytes 196616 | tf_op jit(solution)/shard_map/ppermute | solution.py:76
  48.4 18.2 %collective-permute-start.1 = (bf16[256,2048]{1,0:T(8,128)(2,1)}, bf16[256,2048]{1,0:T(8,128)(2,1)}, u32[]{:S(2)}, u32[]{:S(2)}) collective-permute-start(bf16[256,2048]{1,0:T(8,128)(2,1)} %collective-permute-done.refs_1_), channel_id=1, source_target_pairs={{0,16},{4,12},{8,24},{12,4},{16,0},{20,28},{24,8},{28,20},{1,17},{... | collective-permute-start | bytes 3145736 | tf_op jit(solution)/shard_map/ppermute | solution.py:76
  54.6 225.0 %all-gather.8.cloned.1.call-start = ((), (), s32[]{:S(2)}) async-start(), calls=%async_computation.7 | async-start | bytes 3932160 | tf_op jit(solution)/shard_map/all_gather | solution.py:1083
  66.8 25.6 %collective-permute-start.3 = (bf16[256,2048]{1,0:T(8,128)(2,1)S(1)}, bf16[256,2048]{1,0:T(8,128)(2,1)S(1)}, u32[]{:S(2)}, u32[]{:S(2)}) collective-permute-start(bf16[256,2048]{1,0:T(8,128)(2,1)S(1)} %bitcast.122), channel_id=1, source_target_pairs={{0,16},{4,12},{8,24},{12,4},{16,0},{20,28},{24,8},{28,20},{1,17},{... | collective-permute-start | bytes 3145736 | tf_op jit(solution)/shard_map/ppermute | solution.py:76
  68.4 24.0 %collective-permute-start.2 = (bf16[256,2048]{1,0:T(8,128)(2,1)S(1)}, bf16[256,2048]{1,0:T(8,128)(2,1)S(1)}, u32[]{:S(2)}, u32[]{:S(2)}) collective-permute-start(bf16[256,2048]{1,0:T(8,128)(2,1)S(1)} %bitcast.123), channel_id=1, source_target_pairs={{0,8},{4,20},{8,0},{12,28},{16,24},{20,4},{24,16},{28,12},{1,9},{5... | collective-permute-start | bytes 3145736 | tf_op jit(solution)/shard_map/ppermute | solution.py:76
  92.4 30.7 %collective-permute-start.20 = (bf16[256,2048]{1,0:T(8,128)(2,1)S(1)}, bf16[256,2048]{1,0:T(8,128)(2,1)}, u32[]{:S(2)}, u32[]{:S(2)}) collective-permute-start(bf16[256,2048]{1,0:T(8,128)(2,1)S(1)} %collective-permute-done.2.refs_1_), channel_id=1, source_target_pairs={{0,16},{4,12},{8,24},{12,4},{16,0},{20,28},{24,8},{28,20},{1,17},{... | collective-permute-start | bytes 3145736 | tf_op jit(solution)/shard_map/ppermute | solution.py:76
  172.5 222.2 %reduce-scatter.5.cloned.1.call-start = ((), (), s32[]{:S(2)}) async-start(), calls=%async_computation.8 | async-start | bytes 7864320 | tf_op jit(solution)/shard_map/reduce_scatter | solution.py:1087
  172.6 18.3 %collective-permute-start.31 = (bf16[256,2048]{1,0:T(8,128)(2,1)S(1)}, bf16[256,2048]{1,0:T(8,128)(2,1)S(1)}, u32[]{:S(2)}, u32[]{:S(2)}) collective-permute-start(bf16[256,2048]{1,0:T(8,128)(2,1)S(1)} %bitcast.124), channel_id=1, source_target_pairs={{0,4},{4,0},{8,12},{12,8},{16,20},{20,16},{24,28},{28,24},{1,5},{5... | collective-permute-start | bytes 3145736 | tf_op jit(solution)/shard_map/ppermute | solution.py:89
  172.6 19.4 %collective-permute-start.32 = (bf16[256,2048]{1,0:T(8,128)(2,1)}, bf16[256,2048]{1,0:T(8,128)(2,1)S(1)}, u32[]{:S(2)}, u32[]{:S(2)}) collective-permute-start(bf16[256,2048]{1,0:T(8,128)(2,1)} %copy-done.58), channel_id=1, source_target_pairs={{0,4},{4,0},{8,12},{12,8},{16,20},{20,16},{24,28},{28,24},{1,5},{5... | collective-permute-start | bytes 3145736 | tf_op jit(solution)/shard_map/ppermute | solution.py:89
  173.1 18.9 %collective-permute-start.33 = (bf16[256,2048]{1,0:T(8,128)(2,1)}, bf16[256,2048]{1,0:T(8,128)(2,1)S(1)}, u32[]{:S(2)}, u32[]{:S(2)}) collective-permute-start(bf16[256,2048]{1,0:T(8,128)(2,1)} %copy-done.56), channel_id=1, source_target_pairs={{0,4},{4,0},{8,12},{12,8},{16,20},{20,16},{24,28},{28,24},{1,5},{5... | collective-permute-start | bytes 3145736 | tf_op jit(solution)/shard_map/ppermute | solution.py:89
  173.2 18.8 %collective-permute-start.34 = (bf16[256,2048]{1,0:T(8,128)(2,1)}, bf16[256,2048]{1,0:T(8,128)(2,1)S(1)}, u32[]{:S(2)}, u32[]{:S(2)}) collective-permute-start(bf16[256,2048]{1,0:T(8,128)(2,1)} %collective-permute-done.20.refs_3_), channel_id=1, source_target_pairs={{0,4},{4,0},{8,12},{12,8},{16,20},{20,16},{24,28},{28,24},{1,5},{5... | collective-permute-start | bytes 3145736 | tf_op jit(solution)/shard_map/ppermute | solution.py:89
  189.3 25.2 %collective-permute-start.30 = (bf16[256,2048]{1,0:T(8,128)(2,1)S(1)}, bf16[256,2048]{1,0:T(8,128)(2,1)S(1)}, u32[]{:S(2)}, u32[]{:S(2)}) collective-permute-start(bf16[256,2048]{1,0:T(8,128)(2,1)S(1)} %multiply_convert_fusion.refs_0_), channel_id=1, source_target_pairs={{0,16},{4,12},{8,24},{12,4},{16,0},{20,28},{24,8},{28,20},{1,17},{... | collective-permute-start | bytes 3145736 | tf_op jit(solution)/shard_map/ppermute | solution.py:76
  190.9 23.6 %collective-permute-start.29 = (bf16[256,2048]{1,0:T(8,128)(2,1)S(1)}, bf16[256,2048]{1,0:T(8,128)(2,1)}, u32[]{:S(2)}, u32[]{:S(2)}) collective-permute-start(bf16[256,2048]{1,0:T(8,128)(2,1)S(1)} %multiply_convert_fusion.refs_0_), channel_id=1, source_target_pairs={{0,8},{4,20},{8,0},{12,28},{16,24},{20,4},{24,16},{28,12},{1,9},{5... | collective-permute-start | bytes 3145736 | tf_op jit(solution)/shard_map/ppermute | solution.py:76
  278.9 177.0 %reduce-scatter.7.cloned.1.call-start = ((), (), s32[]{:S(2)}) async-start(), calls=%async_computation.9 | async-start | bytes 3932160 | tf_op jit(solution)/shard_map/reduce_scatter | solution.py:1087
  342.6 19.1 %collective-permute-start.44 = (bf16[256,2048]{1,0:T(8,128)(2,1)}, bf16[256,2048]{1,0:T(8,128)(2,1)S(1)}, u32[]{:S(2)}, u32[]{:S(2)}) collective-permute-start(bf16[256,2048]{1,0:T(8,128)(2,1)} %shard_map.261), channel_id=1, source_target_pairs={{0,8},{4,20},{8,0},{12,28},{16,24},{20,4},{24,16},{28,12},{1,9},{5... | collective-permute-start | bytes 3145736 | tf_op jit(solution)/shard_map/ppermute | solution.py:108
  369.1 25.6 %collective-permute-start.46 = (bf16[256,2048]{1,0:T(8,128)(2,1)S(1)}, bf16[256,2048]{1,0:T(8,128)(2,1)S(1)}, u32[]{:S(2)}, u32[]{:S(2)}) collective-permute-start(bf16[256,2048]{1,0:T(8,128)(2,1)S(1)} %get-tuple-element.275.refs_0_), channel_id=1, source_target_pairs={{0,16},{4,12},{8,24},{12,4},{16,0},{20,28},{24,8},{28,20},{1,17},{... | collective-permute-start | bytes 3145736 | tf_op jit(solution)/shard_map/ppermute | solution.py:76
  370.5 24.2 %collective-permute-start.45 = (bf16[256,2048]{1,0:T(8,128)(2,1)S(1)}, bf16[256,2048]{1,0:T(8,128)(2,1)S(1)}, u32[]{:S(2)}, u32[]{:S(2)}) collective-permute-start(bf16[256,2048]{1,0:T(8,128)(2,1)S(1)} %get-tuple-element.275.refs_0_), channel_id=1, source_target_pairs={{0,8},{4,20},{8,0},{12,28},{16,24},{20,4},{24,16},{28,12},{1,9},{5... | collective-permute-start | bytes 3145736 | tf_op jit(solution)/shard_map/ppermute | solution.py:76
  394.7 126.6 %reduce-scatter.9.cloned.1.call-start = ((), (), s32[]{:S(2)}) async-start(), calls=%async_computation.10 | async-start | bytes 3276800 | tf_op jit(solution)/shard_map/reduce_scatter | solution.py:1087
  409.9 20.5 %collective-permute-start.56 = (bf16[256,2048]{1,0:T(8,128)(2,1)S(1)}, bf16[256,2048]{1,0:T(8,128)(2,1)S(1)}, u32[]{:S(2)}, u32[]{:S(2)}) collective-permute-start(bf16[256,2048]{1,0:T(8,128)(2,1)S(1)} %get-tuple-element.273), channel_id=1, source_target_pairs={{0,16},{4,12},{8,24},{12,4},{16,0},{20,28},{24,8},{28,20},{1,17},{... | collective-permute-start | bytes 3145736 | tf_op jit(solution)/shard_map/ppermute | solution.py:1230
  410.5 25.5 %collective-permute-start.57 = (bf16[256,2048]{1,0:T(8,128)(2,1)S(1)}, bf16[256,2048]{1,0:T(8,128)(2,1)S(1)}, u32[]{:S(2)}, u32[]{:S(2)}) collective-permute-start(bf16[256,2048]{1,0:T(8,128)(2,1)S(1)} %get-tuple-element.274), channel_id=1, source_target_pairs={{0,16},{4,12},{8,24},{12,4},{16,0},{20,28},{24,8},{28,20},{1,17},{... | collective-permute-start | bytes 3145736 | tf_op jit(solution)/shard_map/ppermute | solution.py:1230
  426.5 26.1 %collective-permute-start.55 = (f32[2,8,384]{2,1,0:T(8,128)S(1)}, f32[2,8,384]{2,1,0:T(8,128)S(1)}, u32[]{:S(2)}, u32[]{:S(2)}) collective-permute-start(f32[2,8,384]{2,1,0:T(8,128)S(1)} %get-tuple-element.284), channel_id=1, source_target_pairs={{3,0},{7,4},{11,8},{15,12},{19,16},{23,20},{27,24},{31,28}} | collective-permute-start | bytes 73736 | tf_op jit(solution)/shard_map/ppermute | solution.py:162
  427.8 24.8 %collective-permute-start.54 = (f32[2,8,384]{2,1,0:T(8,128)S(1)}, f32[2,8,384]{2,1,0:T(8,128)S(1)}, u32[]{:S(2)}, u32[]{:S(2)}) collective-permute-start(f32[2,8,384]{2,1,0:T(8,128)S(1)} %get-tuple-element.284), channel_id=1, source_target_pairs={{2,0},{3,1},{6,4},{7,5},{10,8},{11,9},{14,12},{15,13},{18,16},{19,... | collective-permute-start | bytes 73736 | tf_op jit(solution)/shard_map/ppermute | solution.py:162
  429.1 23.5 %collective-permute-start.53 = (f32[2,8,384]{2,1,0:T(8,128)S(1)}, f32[2,8,384]{2,1,0:T(8,128)S(1)}, u32[]{:S(2)}, u32[]{:S(2)}) collective-permute-start(f32[2,8,384]{2,1,0:T(8,128)S(1)} %get-tuple-element.284), channel_id=1, source_target_pairs={{1,0},{2,1},{3,2},{5,4},{6,5},{7,6},{9,8},{10,9},{11,10},{13,12},{... | collective-permute-start | bytes 73736 | tf_op jit(solution)/shard_map/ppermute | solution.py:162
  455.9 105.0 %reduce-scatter.11.cloned.1.call-start = ((), (), s32[]{:S(2)}) async-start(), calls=%async_computation.11 | async-start | bytes 2048000 | tf_op jit(solution)/shard_map/reduce_scatter | solution.py:1087
  456.0 19.1 %collective-permute-start.58 = (bf16[256,2048]{1,0:T(8,128)(2,1)S(1)}, bf16[256,2048]{1,0:T(8,128)(2,1)S(1)}, u32[]{:S(2)}, u32[]{:S(2)}) collective-permute-start(bf16[256,2048]{1,0:T(8,128)(2,1)S(1)} %shard_map.266), channel_id=1, source_target_pairs={{0,8},{4,20},{8,0},{12,28},{16,24},{20,4},{24,16},{28,12},{1,9},{5... | collective-permute-start | bytes 3145736 | tf_op jit(solution)/shard_map/ppermute | solution.py:1240
  502.9 18.4 %collective-permute-start.61 = (bf16[256,2048]{1,0:T(8,128)(2,1)}, bf16[256,2048]{1,0:T(8,128)(2,1)}, u32[]{:S(2)}, u32[]{:S(2)}) collective-permute-start(bf16[256,2048]{1,0:T(8,128)(2,1)} %get-tuple-element.325), channel_id=1, source_target_pairs={{0,16},{4,12},{8,24},{12,4},{16,0},{20,28},{24,8},{28,20},{1,17},{... | collective-permute-start | bytes 3145736 | tf_op jit(solution)/shard_map/ppermute | solution.py:122
  (144 other events, 1985.1 us)
Sparse Core Ops, SparseCore 0:
  14.8 83.2 all-gather.3
  99.7 114.6 all-gather.5
  215.9 63.6 all-gather.7
  281.7 109.3 reduce-scatter.4
  394.8 61.0 reduce-scatter.6
  458.0 54.1 reduce-scatter.8
  521.5 35.5 reduce-scatter.10

commit v6 on v5

--- a/solution.py
+++ b/solution.py
@@ -305,6 +305,7 @@
     wu,
     wy,
     small,
+    raw,
     u_out,
     y_out,
     conv_out,
@@ -333,10 +334,7 @@
         for gate in (0, 1):
             spread = dot_nt(params[:, gate * block : gate * block + block], fold)
             wz[gate * width : gate * width + width, :] = jnp.where(inside, spread, 0.0).astype(BF16)
-        row = lax.broadcasted_iota(jnp.int32, (width, width), 0)
-        column = lax.broadcasted_iota(jnp.int32, (width, width), 1)
-        same = jnp.where(row == column, 1.0, 0.0).astype(BF16)
-        turned = dot_tn(params[:, 2 * block : 2 * block + 8], same)
+        turned = raw[...]
         par[0:8, :] = turned
         par[8:16, :] = turned
         par[7:8, :] = -SHARP * softplus(turned[7:8, :])
@@ -420,7 +418,7 @@
     )
 
 
-def mixer_enter(h_all, same, w_in, extra, block):
+def mixer_enter(h_all, same, w_in, raw, extra, block):
     count, tall, model = h_all.shape
     rows = tall - HALO
     chan = w_in.shape[0]
@@ -443,13 +441,14 @@
             pl.BlockSpec((chan, model), lambda step: (0, 0)),
             pl.BlockSpec((chan, model), lambda step: (0, 1)),
             pl.BlockSpec((chan, extra), lambda step: (0, 3 * model // extra)),
+            resident(raw.shape),
         ],
         [per_piece(s.shape[1:]) for s in shapes] + [resident(s.shape) for s in fixed],
         shapes + fixed,
         [pltpu.VMEM((2 * width, model), BF16), pltpu.VMEM((some, tall, 2 * width), F32)],
         SWEEP * count * rows * width,
         grown(26, count),
-    )(h_all, same, w_in, w_in, w_in)
+    )(h_all, same, w_in, w_in, w_in, raw)
 
 
 def column_tile(model):
@@ -1118,7 +1117,8 @@
     cot_low = cotangent.reshape(run_len, model)
     lead = hand_on(x_low[run_len - HALO :], 1)
     part = gain_one.shape[0]
-    gains = jnp.concatenate([gain_one, gain_two]).astype(BF16)[None]
+    vectors = [conv_w.reshape(-1), conv_bias, gate_bias.reshape(-1), decay_param]
+    gains = jnp.concatenate([gain_one, gain_two, *vectors]).astype(BF16)[None]
     my_run = lax.axis_index("seq")
     first_token = my_run * run_len
     places = lax.broadcasted_iota(jnp.int32, (n_seq, 1), 0)
@@ -1127,7 +1127,9 @@
         ring = [(source, (source + hop) % n_seq) for source in range(n_seq)]
         arrived = lax.ppermute(gains, "seq", ring)
         gain_rows = jnp.where(places == (my_run - hop) % n_seq, arrived, gain_rows)
-    gain_rows = jnp.pad(gain_rows.reshape(1, -1), ((0, 0), (0, model - 2 * part * n_seq)))
+    raw = gain_rows[:, 2 * part :].reshape(n_seq, 8, own).transpose(1, 0, 2).reshape(8, chan)
+    raw = jnp.pad(raw.astype(F32), ((0, 0), (0, width - chan)))
+    gain_rows = jnp.pad(gain_rows[:, : 2 * part].reshape(1, -1), ((0, 0), (0, model - 2 * part * n_seq)))
     padded = jnp.concatenate([jnp.full((3,), -1, jnp.int32), doc_ids.reshape(-1)])
     own_docs = lax.dynamic_slice_in_dim(padded, first_token + 3, run_len)
     same = sum(
@@ -1139,16 +1141,7 @@
     count = len(tops)
     half = count // 2
 
-    small = jnp.concatenate(
-        [
-            gate_w.reshape(own, 2 * block),
-            conv_w.T,
-            conv_bias[:, None],
-            gate_bias.T,
-            decay_param[:, None],
-        ],
-        1,
-    )
+    small = gate_w.reshape(own, 2 * block)
     extra = -(-small.shape[1] // 128) * 128
     small = jnp.pad(small, ((0, 0), (0, extra - small.shape[1])))
     w_in = jnp.concatenate([mix_in[:, 1, :], mix_in[:, 0, :], mix_out, small], 1).astype(BF16)
@@ -1175,7 +1168,7 @@
         after(cot_low, x_pieces[half - 1]),
         [
             ((1, 2), lambda sent, done: same),
-            ((3,), lambda sent, done: mixer_enter(h_all, done[0], w_in, extra, block)),
+            ((3,), lambda sent, done: mixer_enter(h_all, done[0], w_in, raw, extra, block)),
         ],
     )
     (u_ext, y_pre, conv, recur, enter, keep, cum, local, ends, w_z, par) = entered

time: 583 us -> 579 us (level)
    unnamed x209 -> x217, local copies, waits for them, and re-layouts: 62.4 us -> 62.4 us
  transfers between devices with their start and end apart: 73 -> 73, of which waited for: 32 -> 32; matrix products, arithmetic and copies ran while one was open for 6% -> 7% of each run, Pallas kernels for 40% -> 40%
where the time goes in v6:
time: 579 us; the launch traced here: 570 us
  Pallas kernels  230 us (40%)
  waiting for transfers between devices  155 us (27%)
  local copies, waits for them, and re-layouts  74.4 us (13%)
  starting transfers between devices  65 us (11%)
  other arithmetic  29.1 us (5%)
  between operations  16.1 us (3%)
    unnamed x217, local copies, waits for them, and re-layouts  62.4 us
    ppermute x15, waiting for transfers between devices, arrival(): return lax.ppermute(held[m ^ 1 << top], 'dp', stages[top])  62.1 us
    pallas_call x7, Pallas kernels, rows_times(): call(functools.partial(rows_times_kernel, len(lefts), gained), (groups, s...  44.4 us
    pallas_call x2, Pallas kernels, mlp_part(): call(functools.partial(mlp_kernel, count, first), (hidden // tile,), [ANY...  34 us
    pallas_call x2, Pallas kernels, mlp_grads(): call(mlp_grads_kernel, (model // tile,), [resident((inner, tall))] * 3 +...  31 us
    ppermute x6, waiting for transfers between devices, scatter_terms(): got = [lax.ppermute(part, 'dp', stages[-1]) for part in sent]  25.1 us
    ppermute x3, waiting for transfers between devices, scatter_tail(): got = [lax.ppermute(part, 'dp', pairs) for part in sent]  22.8 us
    pallas_call x8, Pallas kernels, add_rows(): call(functools.partial(add_kernel, counts), (steps,), [spec(place) for pl...  18.2 us
  transfers between devices with their start and end apart: 73, of which 32 were waited for; matrix products, arithmetic and copies ran while one was open for 7% of the time, Pallas kernels for 40%

profile of v6, /device:TPU:0, one launch (start us, length us, event | category | flops | bytes accessed | tf_op | source)
XLA Modules:
  0.0 570.1 jit_solution(17266579018252616250)
XLA Ops:
  69.8 10.9 %shard_map.246 = (bf16[8,272,2048]{2,1,0:T(8,128)(2,1)}, bf16[8,256,2048]{2,1,0:T(8,128)(2,1)}, bf16[8,256,384]{2,1,0:T(8,128)(2,1)}) custom-call(bf16[256,2048]{1,0:T(8,128)(2,1)} %bitcast.1.refs_0_.refs_4_, bf16[256,2048]{1,0:T(8,128)(2,1)} %collective-permute-done.refs_1_, bf16[256,2048]{1,0:T(8,128)(2,1)} %collective-permute-done.4.refs_2_, ...), custom_call_target="tpu_custom_call" | custom-call | flops 2786882048 | bytes 1024 | tf_op jit(solution)/shard_map/pallas_call | solution.py:257
  80.7 9.4 %collective-permute-done.3.refs_2_ = bf16[256,2048]{1,0:T(8,128)(2,1)S(1)} collective-permute-done((bf16[256,2048]{1,0:T(8,128)(2,1)S(1)}, bf16[256,2048]{1,0:T(8,128)(2,1)S(1)}, u32[]{:S(2)}, u32[]{:S(2)}) %collective-permute-start.3) | collective-permute-done | bytes 1048608 | tf_op jit(solution)/shard_map/ppermute | solution.py:76
  98.5 16.3 %shard_map.247 = (bf16[8,272,384]{2,1,0:T(8,128)(2,1)S(1)}, f32[8,256,384]{2,1,0:T(8,128)S(1)}, bf16[8,256,384]{2,1,0:T(8,128)(2,1)S(1)}, f32[8,256,384]{2,1,0:T...) custom-call(bf16[8,272,2048]{2,1,0:T(8,128)(2,1)} %get-tuple-element, ...), custom_call_target="tpu_custom_call" | custom-call | flops 5024426496 | bytes 1024 | tf_op jit(solution)/shard_map/pallas_call | solution.py:435
  139.4 5.6 shard_map.251
  146.3 6.1 %collective-permute-done.25 = bf16[256,2048]{1,0:T(8,128)(2,1)S(1)} collective-permute-done((bf16[256,2048]{1,0:T(8,128)(2,1)S(1)}, bf16[256,2048]{1,0:T(8,128)(2,1)S(1)}, u32[]{:S(2)}, u32[]{:S(2)}) %collective-permute-start.25) | collective-permute-done | bytes 1048608 | tf_op jit(solution)/shard_map/ppermute | solution.py:122
  162.0 5.6 collective-permute-done.27
  170.5 12.2 %collective-permute-done.28 = bf16[256,2048]{1,0:T(8,128)(2,1)} collective-permute-done((bf16[256,2048]{1,0:T(8,128)(2,1)}, bf16[256,2048]{1,0:T(8,128)(2,1)}, u32[]{:S(2)}, u32[]{:S(2)}) %collective-permute-start.28) | collective-permute-done | bytes 1048608 | tf_op jit(solution)/shard_map/ppermute | solution.py:108
  193.9 17.5 %collective-permute-done.30.refs_2_ = bf16[256,2048]{1,0:T(8,128)(2,1)S(1)} collective-permute-done((bf16[256,2048]{1,0:T(8,128)(2,1)S(1)}, bf16[256,2048]{1,0:T(8,128)(2,1)S(1)}, u32[]{:S(2)}, u32[]{:S(2)}) %collective-permute-start.30) | collective-permute-done | bytes 1048608 | tf_op jit(solution)/shard_map/ppermute | solution.py:76
  212.8 13.6 %collective-permute-done.35.refs_3_ = bf16[256,2048]{1,0:T(8,128)(2,1)S(1)} collective-permute-done((bf16[256,2048]{1,0:T(8,128)(2,1)}, bf16[256,2048]{1,0:T(8,128)(2,1)S(1)}, u32[]{:S(2)}, u32[]{:S(2)}) %collective-permute-start.35) | collective-permute-done | bytes 1048608 | tf_op jit(solution)/shard_map/ppermute | solution.py:76
  229.2 20.6 %shard_map.254 = (bf16[8,256,512]{2,1,0:T(8,128)(2,1)S(1)}, bf16[8,256,512]{2,1,0:T(8,128)(2,1)}, bf16[8,256,512]{2,1,0:T(8,128)(2,1)}, bf16[8,256,2048]{2,1,0:T(8,128)(2,1)}) custom-call(bf16[256,2048]{1,0:T(8,128)(2,1)S(1)} %multiply_convert_fusion.refs_0_, bf16[256,2048]{1,0:T(8,128)(2,1)} %collective-permute-done.29.refs_1_, ...), custom_call_target="tpu_custom_call" | custom-call | flops 5576969728 | bytes 1024 | tf_op jit(solution)/shard_map/pallas_call | solution.py:829
  253.0 18.8 %shard_map.255 = bf16[512,6144]{1,0:T(8,128)(2,1)S(1)} custom-call(bf16[2048,512]{1,0:T(8,128)(2,1)S(1)} %bitcast.108, bf16[2048,512]{1,0:T(8,128)(2,1)S(1)} %bitcast.109, bf16[2048,512]{1,0:T(8,128)(2,1)S(1)} %bitcast.114, bf16[2048,2048]{1,0:T(8,128)(2,1)} %bitcast.125, bf16[2048,2048]{1,0:T(8,128)(2,1)} %bitcast.106), custom_call_target="tpu_custom_call" | custom-call | flops 5832525312 | bytes 1024 | tf_op jit(solution)/shard_map/pallas_call | solution.py:888
  276.3 13.4 %shard_map.256 = (bf16[8,256,256]{2,1,0:T(8,128)(2,1)}, bf16[8,256,256]{2,1,0:T(8,128)(2,1)}, bf16[8,256,256]{2,1,0:T(8,128)(2,1)}) custom-call(bf16[8,256,2048]{2,1,0:T(8,128)(2,1)} %get-tuple-element.244.refs_0_, bf16[8,256,2048]{2,1,0:T(8,128)(2,1)} %copy-done.7, bf16[256,6144]{1,0:T(8,128)(2,1)} %all-gather.8.cloned.1.call-done.refs_2_.refs_3_.refs_4_.refs_6_.refs_7_, ...), custom_call_target="tpu_custom_call" | custom-call | flops 3044040448 | bytes 1024 | tf_op jit(solution)/shard_map/pallas_call | solution.py:829
  298.2 4.7 shard_map.257
  302.9 4.7 shard_map.258.refs_0_.refs_2_
  310.8 9.8 %shard_map.260 = (bf16[2,256,2048]{2,1,0:T(8,128)(2,1)S(1)}, bf16[2,256,2048]{2,1,0:T(8,128)(2,1)S(1)}) custom-call(bf16[8,256,512]{2,1,0:T(8,128)(2,1)S(1)} %copy-done.20, bf16[8,256,512]{2,1,0:T(8,128)(2,1)S(1)} %copy-done.22, bf16[8,256,256]{2,1,0:T(8,128)(2,1)S(1)} %copy-done.28, bf16[8,256,256]{2,1,0:T(8,128)(2,1)S(1)} %copy-done.31, ...), custom_call_target="tpu_custom_call" | custom-call | flops 3299596032 | bytes 1024 | tf_op jit(solution)/shard_map/pallas_call | solution.py:724
  333.5 5.7 %collective-permute-done.43 = bf16[256,2048]{1,0:T(8,128)(2,1)} collective-permute-done((bf16[256,2048]{1,0:T(8,128)(2,1)}, bf16[256,2048]{1,0:T(8,128)(2,1)}, u32[]{:S(2)}, u32[]{:S(2)}) %collective-permute-start.43) | collective-permute-done | bytes 1048608 | tf_op jit(solution)/shard_map/ppermute | solution.py:122
  346.4 10.0 %shard_map.262 = (bf16[4,256,2048]{2,1,0:T(8,128)(2,1)S(1)}, bf16[4,256,2048]{2,1,0:T(8,128)(2,1)S(1)}) custom-call(bf16[8,256,512]{2,1,0:T(8,128)(2,1)S(1)} %copy-done.36, bf16[8,256,256]{2,1,0:T(8,128)(2,1)S(1)} %copy-done.48, bf16[512,6144]{1,0:T(8,128)(2,1)S(1)} %copy-done.4, bf16[256,6144]{1,0:T(8,128)(2,1)S(1)} %copy-done.5), custom_call_target="tpu_custom_call" | custom-call | flops 3299596032 | bytes 1024 | tf_op jit(solution)/shard_map/pallas_call | solution.py:724
  367.7 12.2 %shard_map.263 = bf16[256,6144]{1,0:T(8,128)(2,1)} custom-call(bf16[2048,256]{1,0:T(8,128)(2,1)S(1)} %bitcast.112, bf16[2048,256]{1,0:T(8,128)(2,1)S(1)} %bitcast.113, bf16[2048,256]{1,0:T(8,128)(2,1)S(1)} %bitcast.122, bf16[2048,2048]{1,0:T(8,128)(2,1)} %bitcast.126, bf16[2048,2048]{1,0:T(8,128)(2,1)} %bitcast.107), custom_call_target="tpu_custom_call" | custom-call | flops 3299596032 | bytes 1024 | tf_op jit(solution)/shard_map/pallas_call | solution.py:888
  380.0 11.4 %collective-permute-done.46.refs_2_ = bf16[256,2048]{1,0:T(8,128)(2,1)S(1)} collective-permute-done((bf16[256,2048]{1,0:T(8,128)(2,1)S(1)}, bf16[256,2048]{1,0:T(8,128)(2,1)S(1)}, u32[]{:S(2)}, u32[]{:S(2)}) %collective-permute-start.46) | collective-permute-done | bytes 1048608 | tf_op jit(solution)/shard_map/ppermute | solution.py:76
  393.0 6.4 %collective-permute-done.48.refs_1_.refs_3_ = bf16[4,256,2048]{2,1,0:T(8,128)(2,1)S(1)} collective-permute-done((bf16[4,256,2048]{2,1,0:T(8,128)(2,1)}, bf16[4,256,2048]{2,1,0:T(8,128)(2,1)S(1)}, u32[]{:S(2)}, u32[]{:S(2)}) %collective-permute-start.48) | collective-permute-done | bytes 4194336 | tf_op jit(solution)/shard_map/ppermute | solution.py:1214
  409.3 13.8 %shard_map.265 = (bf16[8,256,384]{2,1,0:T(8,128)(2,1)S(1)}, bf16[8,256,384]{2,1,0:T(8,128)(2,1)S(1)}, f32[8,256,384]{2,1,0:T(8,128)S(1)}, f32[8,256,384]{2,1,0:T...) custom-call(bf16[256,2048]{1,0:T(8,128)(2,1)S(1)} %get-tuple-element.275.refs_0_, ...), custom_call_target="tpu_custom_call" | custom-call | flops 5024426496 | bytes 1024 | tf_op jit(solution)/shard_map/pallas_call | solution.py:568
  427.1 5.6 collective-permute-done.57
  437.6 5.8 %shard_map.267.refs_0_ = bf16[320,4096]{1,0:T(8,128)(2,1)} custom-call(bf16[2048,384]{1,0:T(8,128)(2,1)S(1)} %bitcast.110, bf16[2048,2048]{1,0:T(8,128)(2,1)S(1)} %bitcast.102), custom_call_target="tpu_custom_call" | custom-call | flops 2033131392 | bytes 1024 | tf_op jit(solution)/shard_map/pallas_call | solution.py:924
  443.4 5.9 %shard_map.268 = bf16[320,4096]{1,0:T(8,128)(2,1)} custom-call(bf16[2048,384]{1,0:T(8,128)(2,1)S(1)} %bitcast.123, bf16[2048,2048]{1,0:T(8,128)(2,1)S(1)} %bitcast.117, bf16[320,4096]{1,0:T(8,128)(2,1)} %shard_map.267.refs_0_), custom_call_target="tpu_custom_call", output_to_operand_aliasing={{}: (2, {})} | custom-call | flops 2033131392 | bytes 1024 | tf_op jit(solution)/shard_map/pallas_call | solution.py:924
  454.2 17.4 %shard_map.269 = (bf16[8,256,384]{2,1,0:T(8,128)(2,1)}, f32[8,16,384]{2,1,0:T(8,128)}, bf16[320,2560]{1,0:T(8,128)(2,1)}) custom-call(f32[2,8,384]{2,1,0:T(8,128)} %copy-done.63, f32[2,8,384]{2,1,0:T(8,128)} %copy-done.62, f32[2,8,384]{2,1,0:T(8,128)} %copy-done.61, f32[2,8,384]{2,1,0:T(8,128)} %copy-done.87, f32[2,8,384]{2,1,0:T(8,128)} %copy-done.86, ...), custom_call_target="tpu_custom_call" | custom-call | flops 5024426496 | bytes 1024 | tf_op jit(solution)/shard_map/pallas_call | solution.py:673
  474.5 4.6 shard_map.270
  479.1 5.0 collective-permute-done.59
  501.0 7.9 %shard_map.274 = (bf16[2,256,2048]{2,1,0:T(8,128)(2,1)S(1)}, bf16[2,256,2048]{2,1,0:T(8,128)(2,1)S(1)}, f32[2,1,2048]{2,1,0:T(1,128)S(1)}) custom-call(bf16[8,256,384]{2,1,0:T(8,128)(2,1)S(1)} %copy-done.24, bf16[8,256,384]{2,1,0:T(8,128)(2,1)S(1)} %fusion.11.refs_1_, bf16[320,6528]{1,0:T(8,128)(2,1)S(1)} %copy-done.2, bf16[320,6528]{1,0:T(8,128)(2,1)S(1)} %copy-done.2, ...), custom_call_target="tpu_custom_call" | custom-call | flops 1822053888 | bytes 1024 | tf_op jit(solution)/shard_map/pallas_call | solution.py:724
  511.6 5.2 shard_map.275
  527.7 5.5 collective-permute-done.63
  537.7 10.6 %collective-permute-done.64 = bf16[256,2048]{1,0:T(8,128)(2,1)} collective-permute-done((bf16[256,2048]{1,0:T(8,128)(2,1)}, bf16[256,2048]{1,0:T(8,128)(2,1)}, u32[]{:S(2)}, u32[]{:S(2)}) %collective-permute-start.64) | collective-permute-done | bytes 1048608 | tf_op jit(solution)/shard_map/ppermute | solution.py:108
  552.1 5.3 shard_map.278
  (477 shorter events, 246.7 us)
Async XLA Ops:
  7.2 87.7 %all-gather.4.cloned.1.call-start = ((), (), s32[]{:S(2)}) async-start(), calls=%async_computation.5 | async-start | bytes 5222400 | tf_op jit(solution)/shard_map/all_gather | solution.py:1082
  11.5 214.9 %all-gather.6.cloned.1.call-start = ((), (), s32[]{:S(2)}) async-start(), calls=%async_computation.6 | async-start | bytes 7864320 | tf_op jit(solution)/shard_map/all_gather | solution.py:1082
  18.9 46.6 %collective-permute-start.5 = (bf16[256,2048]{1,0:T(8,128)(2,1)}, bf16[256,2048]{1,0:T(8,128)(2,1)}, u32[]{:S(2)}, u32[]{:S(2)}) collective-permute-start(bf16[256,2048]{1,0:T(8,128)(2,1)} %bitcast.1.refs_0_.refs_4_), channel_id=1, source_target_pairs={{0,4},{4,0},{8,12},{12,8},{16,20},{20,16},{24,28},{28,24},{1,5},{5... | collective-permute-start | bytes 3145736 | tf_op jit(solution)/shard_map/ppermute | solution.py:89
  18.9 45.0 %collective-permute-start.4 = (bf16[256,2048]{1,0:T(8,128)(2,1)}, bf16[256,2048]{1,0:T(8,128)(2,1)}, u32[]{:S(2)}, u32[]{:S(2)}) collective-permute-start(bf16[256,2048]{1,0:T(8,128)(2,1)} %bitcast.1.refs_0_.refs_4_), channel_id=1, source_target_pairs={{0,16},{4,12},{8,24},{12,4},{16,0},{20,28},{24,8},{28,20},{1,17},{... | collective-permute-start | bytes 3145736 | tf_op jit(solution)/shard_map/ppermute | solution.py:76
  21.7 23.8 %collective-permute-start = (bf16[256,2048]{1,0:T(8,128)(2,1)}, bf16[256,2048]{1,0:T(8,128)(2,1)}, u32[]{:S(2)}, u32[]{:S(2)}) collective-permute-start(bf16[256,2048]{1,0:T(8,128)(2,1)} %bitcast.1.refs_0_.refs_4_), channel_id=1, source_target_pairs={{0,8},{4,20},{8,0},{12,28},{16,24},{20,4},{24,16},{28,12},{1,9},{5... | collective-permute-start | bytes 3145736 | tf_op jit(solution)/shard_map/ppermute | solution.py:76
  29.4 28.7 %collective-permute-start.16 = (bf16[16,2048]{1,0:T(8,128)(2,1)S(1)}, bf16[16,2048]{1,0:T(8,128)(2,1)S(1)}, u32[]{:S(2)}, u32[]{:S(2)}) collective-permute-start(bf16[16,2048]{1,0:T(8,128)(2,1)S(1)} %fusion.10.refs_8_), channel_id=1, source_target_pairs={{0,4},{4,0},{8,12},{12,8},{16,20},{20,16},{24,28},{28,24},{1,5},{5... | collective-permute-start | bytes 196616 | tf_op jit(solution)/shard_map/ppermute | solution.py:89
  29.5 23.5 %collective-permute-start.14 = (bf16[16,2048]{1,0:T(8,128)(2,1)S(1)}, bf16[16,2048]{1,0:T(8,128)(2,1)}, u32[]{:S(2)}, u32[]{:S(2)}) collective-permute-start(bf16[16,2048]{1,0:T(8,128)(2,1)S(1)} %fusion.10.refs_8_), channel_id=1, source_target_pairs={{0,16},{4,12},{8,24},{12,4},{16,0},{20,28},{24,8},{28,20},{1,17},{... | collective-permute-start | bytes 196616 | tf_op jit(solution)/shard_map/ppermute | solution.py:76
  45.5 18.8 %collective-permute-start.1 = (bf16[256,2048]{1,0:T(8,128)(2,1)}, bf16[256,2048]{1,0:T(8,128)(2,1)}, u32[]{:S(2)}, u32[]{:S(2)}) collective-permute-start(bf16[256,2048]{1,0:T(8,128)(2,1)} %collective-permute-done.refs_1_), channel_id=1, source_target_pairs={{0,16},{4,12},{8,24},{12,4},{16,0},{20,28},{24,8},{28,20},{1,17},{... | collective-permute-start | bytes 3145736 | tf_op jit(solution)/shard_map/ppermute | solution.py:76
  53.0 223.3 %all-gather.8.cloned.1.call-start = ((), (), s32[]{:S(2)}) async-start(), calls=%async_computation.7 | async-start | bytes 3932160 | tf_op jit(solution)/shard_map/all_gather | solution.py:1082
  64.5 25.6 %collective-permute-start.3 = (bf16[256,2048]{1,0:T(8,128)(2,1)S(1)}, bf16[256,2048]{1,0:T(8,128)(2,1)S(1)}, u32[]{:S(2)}, u32[]{:S(2)}) collective-permute-start(bf16[256,2048]{1,0:T(8,128)(2,1)S(1)} %bitcast.118), channel_id=1, source_target_pairs={{0,16},{4,12},{8,24},{12,4},{16,0},{20,28},{24,8},{28,20},{1,17},{... | collective-permute-start | bytes 3145736 | tf_op jit(solution)/shard_map/ppermute | solution.py:76
  65.5 24.5 %collective-permute-start.2 = (bf16[256,2048]{1,0:T(8,128)(2,1)S(1)}, bf16[256,2048]{1,0:T(8,128)(2,1)S(1)}, u32[]{:S(2)}, u32[]{:S(2)}) collective-permute-start(bf16[256,2048]{1,0:T(8,128)(2,1)S(1)} %bitcast.119), channel_id=1, source_target_pairs={{0,8},{4,20},{8,0},{12,28},{16,24},{20,4},{24,16},{28,12},{1,9},{5... | collective-permute-start | bytes 3145736 | tf_op jit(solution)/shard_map/ppermute | solution.py:76
  90.0 29.7 %collective-permute-start.20 = (bf16[256,2048]{1,0:T(8,128)(2,1)S(1)}, bf16[256,2048]{1,0:T(8,128)(2,1)}, u32[]{:S(2)}, u32[]{:S(2)}) collective-permute-start(bf16[256,2048]{1,0:T(8,128)(2,1)S(1)} %collective-permute-done.2.refs_1_), channel_id=1, source_target_pairs={{0,16},{4,12},{8,24},{12,4},{16,0},{20,28},{24,8},{28,20},{1,17},{... | collective-permute-start | bytes 3145736 | tf_op jit(solution)/shard_map/ppermute | solution.py:76
  169.3 222.0 %reduce-scatter.5.cloned.1.call-start = ((), (), s32[]{:S(2)}) async-start(), calls=%async_computation.8 | async-start | bytes 7864320 | tf_op jit(solution)/shard_map/reduce_scatter | solution.py:1086
  169.4 18.3 %collective-permute-start.31 = (bf16[256,2048]{1,0:T(8,128)(2,1)S(1)}, bf16[256,2048]{1,0:T(8,128)(2,1)S(1)}, u32[]{:S(2)}, u32[]{:S(2)}) collective-permute-start(bf16[256,2048]{1,0:T(8,128)(2,1)S(1)} %bitcast.120), channel_id=1, source_target_pairs={{0,4},{4,0},{8,12},{12,8},{16,20},{20,16},{24,28},{28,24},{1,5},{5... | collective-permute-start | bytes 3145736 | tf_op jit(solution)/shard_map/ppermute | solution.py:89
  169.5 19.2 %collective-permute-start.32 = (bf16[256,2048]{1,0:T(8,128)(2,1)}, bf16[256,2048]{1,0:T(8,128)(2,1)S(1)}, u32[]{:S(2)}, u32[]{:S(2)}) collective-permute-start(bf16[256,2048]{1,0:T(8,128)(2,1)} %copy-done.58), channel_id=1, source_target_pairs={{0,4},{4,0},{8,12},{12,8},{16,20},{20,16},{24,28},{28,24},{1,5},{5... | collective-permute-start | bytes 3145736 | tf_op jit(solution)/shard_map/ppermute | solution.py:89
  170.0 18.7 %collective-permute-start.33 = (bf16[256,2048]{1,0:T(8,128)(2,1)}, bf16[256,2048]{1,0:T(8,128)(2,1)S(1)}, u32[]{:S(2)}, u32[]{:S(2)}) collective-permute-start(bf16[256,2048]{1,0:T(8,128)(2,1)} %copy-done.56), channel_id=1, source_target_pairs={{0,4},{4,0},{8,12},{12,8},{16,20},{20,16},{24,28},{28,24},{1,5},{5... | collective-permute-start | bytes 3145736 | tf_op jit(solution)/shard_map/ppermute | solution.py:89
  170.0 18.6 %collective-permute-start.34 = (bf16[256,2048]{1,0:T(8,128)(2,1)}, bf16[256,2048]{1,0:T(8,128)(2,1)S(1)}, u32[]{:S(2)}, u32[]{:S(2)}) collective-permute-start(bf16[256,2048]{1,0:T(8,128)(2,1)} %collective-permute-done.20.refs_3_), channel_id=1, source_target_pairs={{0,4},{4,0},{8,12},{12,8},{16,20},{20,16},{24,28},{28,24},{1,5},{5... | collective-permute-start | bytes 3145736 | tf_op jit(solution)/shard_map/ppermute | solution.py:89
  186.0 25.4 %collective-permute-start.30 = (bf16[256,2048]{1,0:T(8,128)(2,1)S(1)}, bf16[256,2048]{1,0:T(8,128)(2,1)S(1)}, u32[]{:S(2)}, u32[]{:S(2)}) collective-permute-start(bf16[256,2048]{1,0:T(8,128)(2,1)S(1)} %multiply_convert_fusion.refs_0_), channel_id=1, source_target_pairs={{0,16},{4,12},{8,24},{12,4},{16,0},{20,28},{24,8},{28,20},{1,17},{... | collective-permute-start | bytes 3145736 | tf_op jit(solution)/shard_map/ppermute | solution.py:76
  187.8 23.6 %collective-permute-start.29 = (bf16[256,2048]{1,0:T(8,128)(2,1)S(1)}, bf16[256,2048]{1,0:T(8,128)(2,1)}, u32[]{:S(2)}, u32[]{:S(2)}) collective-permute-start(bf16[256,2048]{1,0:T(8,128)(2,1)S(1)} %multiply_convert_fusion.refs_0_), channel_id=1, source_target_pairs={{0,8},{4,20},{8,0},{12,28},{16,24},{20,4},{24,16},{28,12},{1,9},{5... | collective-permute-start | bytes 3145736 | tf_op jit(solution)/shard_map/ppermute | solution.py:76
  275.7 176.8 %reduce-scatter.7.cloned.1.call-start = ((), (), s32[]{:S(2)}) async-start(), calls=%async_computation.9 | async-start | bytes 3932160 | tf_op jit(solution)/shard_map/reduce_scatter | solution.py:1086
  339.2 19.1 %collective-permute-start.44 = (bf16[256,2048]{1,0:T(8,128)(2,1)}, bf16[256,2048]{1,0:T(8,128)(2,1)S(1)}, u32[]{:S(2)}, u32[]{:S(2)}) collective-permute-start(bf16[256,2048]{1,0:T(8,128)(2,1)} %shard_map.261), channel_id=1, source_target_pairs={{0,8},{4,20},{8,0},{12,28},{16,24},{20,4},{24,16},{28,12},{1,9},{5... | collective-permute-start | bytes 3145736 | tf_op jit(solution)/shard_map/ppermute | solution.py:108
  365.7 25.6 %collective-permute-start.46 = (bf16[256,2048]{1,0:T(8,128)(2,1)S(1)}, bf16[256,2048]{1,0:T(8,128)(2,1)S(1)}, u32[]{:S(2)}, u32[]{:S(2)}) collective-permute-start(bf16[256,2048]{1,0:T(8,128)(2,1)S(1)} %get-tuple-element.275.refs_0_), channel_id=1, source_target_pairs={{0,16},{4,12},{8,24},{12,4},{16,0},{20,28},{24,8},{28,20},{1,17},{... | collective-permute-start | bytes 3145736 | tf_op jit(solution)/shard_map/ppermute | solution.py:76
  367.2 24.2 %collective-permute-start.45 = (bf16[256,2048]{1,0:T(8,128)(2,1)S(1)}, bf16[256,2048]{1,0:T(8,128)(2,1)S(1)}, u32[]{:S(2)}, u32[]{:S(2)}) collective-permute-start(bf16[256,2048]{1,0:T(8,128)(2,1)S(1)} %get-tuple-element.275.refs_0_), channel_id=1, source_target_pairs={{0,8},{4,20},{8,0},{12,28},{16,24},{20,4},{24,16},{28,12},{1,9},{5... | collective-permute-start | bytes 3145736 | tf_op jit(solution)/shard_map/ppermute | solution.py:76
  391.4 126.6 %reduce-scatter.9.cloned.1.call-start = ((), (), s32[]{:S(2)}) async-start(), calls=%async_computation.10 | async-start | bytes 3276800 | tf_op jit(solution)/shard_map/reduce_scatter | solution.py:1086
  406.6 20.5 %collective-permute-start.56 = (bf16[256,2048]{1,0:T(8,128)(2,1)S(1)}, bf16[256,2048]{1,0:T(8,128)(2,1)S(1)}, u32[]{:S(2)}, u32[]{:S(2)}) collective-permute-start(bf16[256,2048]{1,0:T(8,128)(2,1)S(1)} %get-tuple-element.273), channel_id=1, source_target_pairs={{0,16},{4,12},{8,24},{12,4},{16,0},{20,28},{24,8},{28,20},{1,17},{... | collective-permute-start | bytes 3145736 | tf_op jit(solution)/shard_map/ppermute | solution.py:1223
  407.1 25.5 %collective-permute-start.57 = (bf16[256,2048]{1,0:T(8,128)(2,1)S(1)}, bf16[256,2048]{1,0:T(8,128)(2,1)S(1)}, u32[]{:S(2)}, u32[]{:S(2)}) collective-permute-start(bf16[256,2048]{1,0:T(8,128)(2,1)S(1)} %get-tuple-element.274), channel_id=1, source_target_pairs={{0,16},{4,12},{8,24},{12,4},{16,0},{20,28},{24,8},{28,20},{1,17},{... | collective-permute-start | bytes 3145736 | tf_op jit(solution)/shard_map/ppermute | solution.py:1223
  423.2 26.1 %collective-permute-start.55 = (f32[2,8,384]{2,1,0:T(8,128)S(1)}, f32[2,8,384]{2,1,0:T(8,128)S(1)}, u32[]{:S(2)}, u32[]{:S(2)}) collective-permute-start(f32[2,8,384]{2,1,0:T(8,128)S(1)} %get-tuple-element.284), channel_id=1, source_target_pairs={{3,0},{7,4},{11,8},{15,12},{19,16},{23,20},{27,24},{31,28}} | collective-permute-start | bytes 73736 | tf_op jit(solution)/shard_map/ppermute | solution.py:162
  424.5 24.8 %collective-permute-start.54 = (f32[2,8,384]{2,1,0:T(8,128)S(1)}, f32[2,8,384]{2,1,0:T(8,128)S(1)}, u32[]{:S(2)}, u32[]{:S(2)}) collective-permute-start(f32[2,8,384]{2,1,0:T(8,128)S(1)} %get-tuple-element.284), channel_id=1, source_target_pairs={{2,0},{3,1},{6,4},{7,5},{10,8},{11,9},{14,12},{15,13},{18,16},{19,... | collective-permute-start | bytes 73736 | tf_op jit(solution)/shard_map/ppermute | solution.py:162
  425.8 23.5 %collective-permute-start.53 = (f32[2,8,384]{2,1,0:T(8,128)S(1)}, f32[2,8,384]{2,1,0:T(8,128)S(1)}, u32[]{:S(2)}, u32[]{:S(2)}) collective-permute-start(f32[2,8,384]{2,1,0:T(8,128)S(1)} %get-tuple-element.284), channel_id=1, source_target_pairs={{1,0},{2,1},{3,2},{5,4},{6,5},{7,6},{9,8},{10,9},{11,10},{13,12},{... | collective-permute-start | bytes 73736 | tf_op jit(solution)/shard_map/ppermute | solution.py:162
  452.6 104.9 %reduce-scatter.11.cloned.1.call-start = ((), (), s32[]{:S(2)}) async-start(), calls=%async_computation.11 | async-start | bytes 2048000 | tf_op jit(solution)/shard_map/reduce_scatter | solution.py:1086
  452.6 19.0 %collective-permute-start.58 = (bf16[256,2048]{1,0:T(8,128)(2,1)S(1)}, bf16[256,2048]{1,0:T(8,128)(2,1)S(1)}, u32[]{:S(2)}, u32[]{:S(2)}) collective-permute-start(bf16[256,2048]{1,0:T(8,128)(2,1)S(1)} %shard_map.266), channel_id=1, source_target_pairs={{0,8},{4,20},{8,0},{12,28},{16,24},{20,4},{24,16},{28,12},{1,9},{5... | collective-permute-start | bytes 3145736 | tf_op jit(solution)/shard_map/ppermute | solution.py:1233
  499.6 18.4 %collective-permute-start.61 = (bf16[256,2048]{1,0:T(8,128)(2,1)}, bf16[256,2048]{1,0:T(8,128)(2,1)}, u32[]{:S(2)}, u32[]{:S(2)}) collective-permute-start(bf16[256,2048]{1,0:T(8,128)(2,1)} %get-tuple-element.325), channel_id=1, source_target_pairs={{0,16},{4,12},{8,24},{12,4},{16,0},{20,28},{24,8},{28,20},{1,17},{... | collective-permute-start | bytes 3145736 | tf_op jit(solution)/shard_map/ppermute | solution.py:122
  (148 other events, 1983.1 us)
Sparse Core Ops, SparseCore 0:
  11.6 83.2 all-gather.3
  96.4 114.5 all-gather.5
  212.6 63.6 all-gather.7
  278.4 109.3 reduce-scatter.4
  391.5 60.9 reduce-scatter.6
  454.7 54.1 reduce-scatter.8
  518.1 35.5 reduce-scatter.10
